TPU v7x, 32 devices: a whole 2x2x4 slice. The times are simulated.
32 devices in a mesh: groups: 2 (over x), long: 16 (over z, y, core).
Axes of the slice: x: 2, y: 2, z: 4, core: 2. Of those that a mesh axis runs over, the one named last changes fastest.
Arguments:
- initial_state: float32 [2, 8192, 128], P(None, ('groups', 'long')), parts along dimension 1, may hold values from -6 to 6
- adjoint_state: float32 [2, 8192, 128], P(None, ('groups', 'long')), parts along dimension 1, may hold values from -6 to 6
- current_gates: float32 [8, 2, 128, 128], P('groups'), parts along dimension 0, may hold values from -0.375 to 0.375
Outputs:
- final_state: float32 [2, 8192, 128], P(None, ('groups', 'long')), parts along dimension 1
- final_adjoint: float32 [2, 8192, 128], P(None, ('groups', 'long')), parts along dimension 1
There are 2 independent parts, one for each index of `groups`. A program takes and returns all parts, laid end to end along the dimension named above; each array names one. Nothing has to cross between parts.
All inputs are finite; a program needn't handle non-finite values.
Results may differ from a plain program's by a relative error of at most 0.00017.
Values sent between devices are 32-bit elements; how exact they have to be, the bound alone decides.
No kernel may reach another device: no remote copies, remote signals or barrier semaphores. Data moves between devices by JAX's collectives and lax.ppermute only.
A program may use at most 64 MiB of HBM per device.

v0:
```python
import jax
import jax.numpy as jnp
from jax import lax
from jax.sharding import PartitionSpec as P

SECTIONS = 4
NS_ITERS = 8


HIGHEST = lax.Precision.HIGHEST


def partner(x, axis, distance):
    return lax.ppermute(x, axis, [(i, i ^ 1 << distance) for i in range(lax.axis_size(axis))])


def matmul_high(left_side, right_side):
    return jnp.dot(left_side, right_side, precision=HIGHEST, preferred_element_type=jnp.float32)


def rows_product(left_side, right_side):
    return lax.dot_general(
        left_side,
        right_side,
        (((0,), (0,)), ((), ())),
        precision=HIGHEST,
        preferred_element_type=jnp.float32,
    )


def lanes_product(left_side, right_side):
    return lax.dot_general(
        left_side,
        right_side,
        (((1,), (1,)), ((), ())),
        precision=HIGHEST,
        preferred_element_type=jnp.float32,
    )


def polar_factor(summed_real, summed_imag, sweeps):
    norm_scale = lax.rsqrt(jnp.sum(summed_real * summed_real + summed_imag * summed_imag) + 1e-06)
    iterate_real = summed_real * norm_scale
    iterate_imag = summed_imag * norm_scale
    for sweep_index in range(sweeps):
        gram_real = rows_product(iterate_real, iterate_real) + rows_product(
            iterate_imag, iterate_imag
        )
        gram_imag = rows_product(iterate_real, iterate_imag) - rows_product(
            iterate_imag, iterate_real
        )
        product_real = matmul_high(iterate_real, gram_real) - matmul_high(iterate_imag, gram_imag)
        product_imag = matmul_high(iterate_real, gram_imag) + matmul_high(iterate_imag, gram_real)
        iterate_real = 1.5 * iterate_real - 0.5 * product_real
        iterate_imag = 1.5 * iterate_imag - 0.5 * product_imag
    return (iterate_real, iterate_imag)


def gate_rows(fields):
    count, rows, lanes = fields.shape
    viewed = fields.reshape(count, 2, rows // 2, 2, lanes // 2)
    return viewed.transpose(0, 2, 3, 1, 4).reshape(count, rows, lanes)


def slab_rows(fields):
    count, rows, lanes = fields.shape
    viewed = fields.reshape(count, rows // 2, 2, 2, lanes // 2)
    return viewed.transpose(0, 3, 1, 2, 4).reshape(count, rows, lanes)


def apply_lanes(field, gate_real, gate_imag):
    out_real = lanes_product(field[0], gate_real) - lanes_product(field[1], gate_imag)
    out_imag = lanes_product(field[0], gate_imag) + lanes_product(field[1], gate_real)
    return jnp.stack([out_real, out_imag])


def partial_environment(adjoint_field, state_field):
    outer_real = rows_product(adjoint_field[0], state_field[0]) + rows_product(
        adjoint_field[1], state_field[1]
    )
    outer_imag = rows_product(adjoint_field[1], state_field[0]) - rows_product(
        adjoint_field[0], state_field[1]
    )
    return (outer_real, outer_imag)


def split_pair(fields, is_lower):
    half_rows = fields.shape[1] // 2
    top_rows = fields[:, :half_rows]
    bottom_rows = fields[:, half_rows:]
    return (jnp.where(is_lower, top_rows, bottom_rows), jnp.where(is_lower, bottom_rows, top_rows))


def join_pair(kept_rows, received, is_lower):
    return jnp.concatenate(
        [jnp.where(is_lower, kept_rows, received), jnp.where(is_lower, received, kept_rows)], axis=1
    )


def shards(initial_state, adjoint_state, current_gates):
    bit_count = lax.axis_size("long").bit_length() - 1
    partner_bits = [bit_count - 1, bit_count // 2, 0, 1]
    device_index = lax.axis_index("long")
    state_now = initial_state
    adjoint_now = adjoint_state
    for section_index in range(SECTIONS):
        partner_bit = partner_bits[section_index % 4]
        is_lower = device_index // 2**partner_bit % 2 == 0
        old_real = current_gates[section_index, 0]
        old_imag = current_gates[section_index, 1]
        adjoint_kept, adjoint_sent = split_pair(adjoint_now, is_lower)
        adjoint_back = partner(adjoint_sent, "long", partner_bit)
        state_kept, state_sent = split_pair(state_now, is_lower)
        state_back = partner(state_sent, "long", partner_bit)
        state_in = gate_rows(join_pair(state_kept, state_back, is_lower))
        adjoint_out = apply_lanes(
            gate_rows(join_pair(adjoint_kept, adjoint_back, is_lower)), old_real, old_imag
        )
        part_real, part_imag = partial_environment(adjoint_out, state_in)
        summed_real, summed_imag = lax.psum((part_real, part_imag), "long")
        gate_real, gate_imag = polar_factor(summed_real, summed_imag, NS_ITERS)
        state_out = apply_lanes(state_in, gate_real, gate_imag)
        state_now = slab_rows(state_out)
        adjoint_now = slab_rows(adjoint_out)
    for back_index in range(SECTIONS - 1, -1, -1):
        partner_bit = partner_bits[back_index % 4]
        is_lower = device_index // 2**partner_bit % 2 == 0
        adjoint_kept, adjoint_sent = split_pair(adjoint_now, is_lower)
        adjoint_back = partner(adjoint_sent, "long", partner_bit)
        adjoint_now = join_pair(adjoint_kept, adjoint_back, is_lower)
    for back_index in range(SECTIONS - 1, -1, -1):
        partner_bit = partner_bits[back_index % 4]
        is_lower = device_index // 2**partner_bit % 2 == 0
        state_kept, state_sent = split_pair(state_now, is_lower)
        state_back = partner(state_sent, "long", partner_bit)
        state_now = join_pair(state_kept, state_back, is_lower)
    return (state_now, adjoint_now)


def solution(mesh):
    return jax.shard_map(
        shards,
        mesh=mesh,
        in_specs=(
            P(None, ("groups", "long"), None),
            P(None, ("groups", "long"), None),
            P("groups", None, None, None),
        ),
        out_specs=(P(None, ("groups", "long"), None), P(None, ("groups", "long"), None)),
        check_vma=False,
    )
```

profile of v0, /device:TPU:0, one launch (start us, length us, event | category | flops | bytes accessed | tf_op | source)
XLA Modules:
  0.0 532.8 jit_solution(13859174522461109207)
XLA Ops:
  7.2 1.0 fusion.264
  8.5 4.1 collective-permute-start.1
  12.8 0.9 collective-permute-start
  13.8 8.8 %collective-permute-done.1 = f32[2,128,128]{1,2,0:T(8,128)S(1)} collective-permute-done((f32[2,128,128]{1,2,0:T(8,128)S(1)}, f32[2,128,128]{1,2,0:T(8,128)S(1)}, u32[]{:S(2)}, u32[]{:S(2)}) %collective-permute-start.1) | collective-permute-done | bytes 131104 | tf_op jit(solution)/shard_map/ppermute | solution.py:14
  23.2 0.6 copy-done.8
  26.3 0.4 fusion.267
  26.7 0.4 fusion.266
  27.6 1.0 convolution_add_fusion.75
  28.7 1.0 convolution_subtract_fusion.75
  30.0 0.3 copy.23
  30.8 0.8 collective-permute-start.3
  31.6 87.4 %all-reduce.15.cloned.1.call-done = (f32[128,128]{1,0:T(8,128)}, f32[128,128]{1,0:T(8,128)}) async-done(((f32[128,128]{1,0:T(8,128)}, f32[128,128]{1,0:T(8,128)}), (f32[128,128]{1,0:T(8,128)}, f32[128,128]{1,0:T(8,128)})) %all-reduce.15.cloned.1.call-update) | async-done | bytes 131088 | tf_op jit(solution)/shard_map/psum | solution.py:120
  119.0 1.5 add_reduce_fusion.3
  121.5 0.5 copy-done.5
  139.7 0.3 copy.21
  140.2 4.2 collective-permute-start.2
  145.1 0.7 fusion.144
  149.0 0.4 fusion.298
  149.4 0.4 fusion.299
  150.2 1.0 convolution_add_fusion.58
  151.2 1.0 convolution_subtract_fusion.58
  155.2 0.3 copy.35
  155.7 82.4 %all-reduce.13.cloned.1.call-done = (f32[128,128]{1,0:T(8,128)}, f32[128,128]{1,0:T(8,128)}) async-done(((f32[128,128]{1,0:T(8,128)}, f32[128,128]{1,0:T(8,128)}), (f32[128,128]{1,0:T(8,128)}, f32[128,128]{1,0:T(8,128)})) %all-reduce.13.cloned.1.call-update) | async-done | bytes 131088 | tf_op jit(solution)/shard_map/psum | solution.py:120
  238.1 1.5 add_reduce_fusion.2
  240.6 0.5 copy-done.4
  256.8 0.5 fusion.329
  259.0 0.3 copy.27
  259.6 0.5 collective-permute-start.4
  260.1 0.6 collective-permute-start.7
  260.7 0.4 collective-permute-done.4
  261.7 0.4 fusion.330
  262.1 0.4 fusion.331
  262.8 1.0 convolution_add_fusion.41
  263.9 1.0 convolution_subtract_fusion.41
  264.9 0.7 collective-permute-done.7
  267.6 88.3 %all-reduce.11.cloned.1.call-done = (f32[128,128]{1,0:T(8,128)}, f32[128,128]{1,0:T(8,128)}) async-done(((f32[128,128]{1,0:T(8,128)}, f32[128,128]{1,0:T(8,128)}), (f32[128,128]{1,0:T(8,128)}, f32[128,128]{1,0:T(8,128)})) %all-reduce.11.cloned.1.call-update) | async-done | bytes 131088 | tf_op jit(solution)/shard_map/psum | solution.py:120
  355.9 1.5 add_reduce_fusion.1
  358.4 0.5 copy-done.6
  377.2 1.0 collective-permute-start.6
  378.5 0.4 stack.94
  379.4 0.3 copy.40
  379.9 3.3 collective-permute-done.6
  383.7 0.4 fusion.362
  384.1 0.4 fusion.363
  384.9 1.0 convolution_add_fusion.24
  385.9 1.0 convolution_subtract_fusion.24
  387.0 0.6 collective-permute-start.12
  387.6 87.5 %all-reduce.9.cloned.1.call-done = (f32[128,128]{1,0:T(8,128)}, f32[128,128]{1,0:T(8,128)}) async-done(((f32[128,128]{1,0:T(8,128)}, f32[128,128]{1,0:T(8,128)}), (f32[128,128]{1,0:T(8,128)}, f32[128,128]{1,0:T(8,128)})) %all-reduce.9.cloned.1.call-update) | async-done | bytes 131088 | tf_op jit(solution)/shard_map/psum | solution.py:120
  475.1 1.5 add_reduce_fusion
  477.6 0.5 copy-done.7
  492.9 0.5 fusion.392
  496.1 0.3 copy.39
  496.7 1.0 collective-permute-start.8
  497.8 4.8 collective-permute-done.8
  502.7 3.4 collective-permute-start.14
  506.1 1.3 collective-permute-start.10
  507.4 3.0 collective-permute-done.14
  510.5 1.5 collective-permute-start.15
  512.0 1.1 collective-permute-done.10
  513.1 1.5 collective-permute-start.11
  514.6 8.7 %collective-permute-done.15 = f32[2,128,128]{1,2,0:T(8,128)S(1)} collective-permute-done((f32[2,128,128]{1,2,0:T(8,128)S(1)}, f32[2,128,128]{1,2,0:T(8,128)S(1)}, u32[]{:S(2)}, u32[]{:S(2)}) %collective-permute-start.15) | collective-permute-done | bytes 131104 | tf_op jit(solution)/shard_map/ppermute | solution.py:14
  523.3 0.8 copy.42
  524.2 0.8 collective-permute-done.11
  525.0 0.8 copy.41
  (440 shorter events, 87.5 us)
Async XLA Ops:
  7.2 111.8 %all-reduce.15.cloned.1.call-start = ((), (), s32[]{:S(2)}) async-start(), calls=%async_computation.3 | async-start | bytes 262144 | tf_op jit(solution)/shard_map/psum | solution.py:120
  8.4 4.1 copy-start.9
  8.5 14.0 %collective-permute-start.1 = (f32[2,128,128]{1,2,0:T(8,128)S(1)}, f32[2,128,128]{1,2,0:T(8,128)S(1)}, u32[]{:S(2)}, u32[]{:S(2)}) collective-permute-start(f32[2,128,128]{1,2,0:T(8,128)S(1)} %broadcast_select_fusion.42), channel_id=1, source_target_pairs={{0,8},{1,9},{2,10},{3,11},{4,12},{5,13},{6,14},{7,15},{8,0},{9,1},... | collective-permute-start | bytes 393224 | tf_op jit(solution)/shard_map/ppermute | solution.py:14
  12.8 11.7 %collective-permute-start = (f32[2,128,128]{1,2,0:T(8,128)S(1)}, f32[2,128,128]{1,2,0:T(8,128)S(1)}, u32[]{:S(2)}, u32[]{:S(2)}) collective-permute-start(f32[2,128,128]{1,2,0:T(8,128)S(1)} %broadcast_select_fusion.46), channel_id=1, source_target_pairs={{0,8},{1,9},{2,10},{3,11},{4,12},{5,13},{6,14},{7,15},{8,0},{9,1},... | collective-permute-start | bytes 393224 | tf_op jit(solution)/shard_map/ppermute | solution.py:14
  22.8 1.0 copy-start.8
  30.5 207.6 %all-reduce.13.cloned.1.call-start = ((), (), s32[]{:S(2)}) async-start(), calls=%async_computation.2 | async-start | bytes 262144 | tf_op jit(solution)/shard_map/psum | solution.py:120
  30.8 113.7 %collective-permute-start.3 = (f32[2,128,128]{1,2,0:T(8,128)S(1)}, f32[2,128,128]{1,2,0:T(8,128)S(1)}, u32[]{:S(2)}, u32[]{:S(2)}) collective-permute-start(f32[2,128,128]{1,2,0:T(8,128)S(1)} %slice_select_fusion.12), channel_id=1, source_target_pairs={{0,4},{1,5},{2,6},{3,7},{4,0},{5,1},{6,2},{7,3},{8,12},{9,13},{10,... | collective-permute-start | bytes 393224 | tf_op jit(solution)/shard_map/ppermute | solution.py:14
  118.9 2.2 copy-start.1
  121.2 0.8 copy-start.5
  140.2 8.2 %collective-permute-start.2 = (f32[2,128,128]{1,2,0:T(8,128)S(1)}, f32[2,128,128]{1,2,0:T(8,128)S(1)}, u32[]{:S(2)}, u32[]{:S(2)}) collective-permute-start(f32[2,128,128]{1,2,0:T(8,128)S(1)} %slice_select_fusion.14), channel_id=1, source_target_pairs={{0,4},{1,5},{2,6},{3,7},{4,0},{5,1},{6,2},{7,3},{8,12},{9,13},{10,... | collective-permute-start | bytes 393224 | tf_op jit(solution)/shard_map/ppermute | solution.py:14
  148.3 4.0 collective-permute-start.5
  152.3 203.6 %all-reduce.11.cloned.1.call-start = ((), (), s32[]{:S(2)}) async-start(), calls=%async_computation.1 | async-start | bytes 262144 | tf_op jit(solution)/shard_map/psum | solution.py:120
  238.1 2.2 copy-start
  240.3 0.8 copy-start.4
  259.6 1.5 collective-permute-start.4
  260.1 5.5 %collective-permute-start.7 = (f32[2,128,128]{1,2,0:T(8,128)S(1)}, f32[2,128,128]{1,2,0:T(8,128)S(1)}, u32[]{:S(2)}, u32[]{:S(2)}) collective-permute-start(f32[2,128,128]{1,2,0:T(8,128)S(1)} %slice_select_fusion.4), channel_id=1, source_target_pairs={{0,2},{1,3},{2,0},{3,1},{4,6},{5,7},{6,4},{7,5},{8,10},{9,11},{10,... | collective-permute-start | bytes 393224 | tf_op jit(solution)/shard_map/ppermute | solution.py:14
  266.9 208.2 %all-reduce.9.cloned.1.call-start = ((), (), s32[]{:S(2)}) async-start(), calls=%async_computation | async-start | bytes 262144 | tf_op jit(solution)/shard_map/psum | solution.py:120
  355.9 2.2 copy-start.2
  358.1 0.8 copy-start.6
  377.2 5.9 %collective-permute-start.6 = (f32[2,128,128]{1,2,0:T(8,128)S(1)}, f32[2,128,128]{1,2,0:T(8,128)S(1)}, u32[]{:S(2)}, u32[]{:S(2)}) collective-permute-start(f32[2,128,128]{1,2,0:T(8,128)S(1)} %slice_select_fusion.6), channel_id=1, source_target_pairs={{0,2},{1,3},{2,0},{3,1},{4,6},{5,7},{6,4},{7,5},{8,10},{9,11},{10,... | collective-permute-start | bytes 393224 | tf_op jit(solution)/shard_map/ppermute | solution.py:14
  387.0 110.6 %collective-permute-start.12 = (f32[2,128,128]{1,2,0:T(8,128)S(1)}, f32[2,128,128]{1,2,0:T(8,128)S(1)}, u32[]{:S(2)}, u32[]{:S(2)}) collective-permute-start(f32[2,128,128]{1,2,0:T(8,128)S(1)} %slice_select_fusion), channel_id=1, source_target_pairs={{0,2},{1,3},{2,0},{3,1},{4,6},{5,7},{6,4},{7,5},{8,10},{9,11},{10,... | collective-permute-start | bytes 393224 | tf_op jit(solution)/shard_map/ppermute | solution.py:14
  475.1 2.2 copy-start.3
  477.3 0.8 copy-start.7
  496.7 5.9 %collective-permute-start.8 = (f32[2,128,128]{1,2,0:T(8,128)S(1)}, f32[2,128,128]{1,2,0:T(8,128)S(1)}, u32[]{:S(2)}, u32[]{:S(2)}) collective-permute-start(f32[2,128,128]{1,2,0:T(8,128)S(1)} %slice_select_fusion.2), channel_id=1, source_target_pairs={{0,2},{1,3},{2,0},{3,1},{4,6},{5,7},{6,4},{7,5},{8,10},{9,11},{10,... | collective-permute-start | bytes 393224 | tf_op jit(solution)/shard_map/ppermute | solution.py:14
  497.7 5.0 collective-permute-start.13
  502.6 3.5 collective-permute-start.9
  502.7 7.7 %collective-permute-start.14 = (f32[2,128,128]{1,2,0:T(8,128)S(1)}, f32[2,128,128]{1,2,0:T(8,128)S(1)}, u32[]{:S(2)}, u32[]{:S(2)}) collective-permute-start(f32[2,128,128]{1,2,0:T(8,128)S(1)} %get-tuple-element.15), channel_id=1, source_target_pairs={{0,4},{1,5},{2,6},{3,7},{4,0},{5,1},{6,2},{7,3},{8,12},{9,13},{10,... | collective-permute-start | bytes 393224 | tf_op jit(solution)/shard_map/ppermute | solution.py:14
  506.1 6.9 %collective-permute-start.10 = (f32[2,128,128]{1,2,0:T(8,128)S(1)}, f32[2,128,128]{1,2,0:T(8,128)S(1)}, u32[]{:S(2)}, u32[]{:S(2)}) collective-permute-start(f32[2,128,128]{1,2,0:T(8,128)S(1)} %get-tuple-element.24), channel_id=1, source_target_pairs={{0,4},{1,5},{2,6},{3,7},{4,0},{5,1},{6,2},{7,3},{8,12},{9,13},{10,... | collective-permute-start | bytes 393224 | tf_op jit(solution)/shard_map/ppermute | solution.py:14
  510.5 12.8 %collective-permute-start.15 = (f32[2,128,128]{1,2,0:T(8,128)S(1)}, f32[2,128,128]{1,2,0:T(8,128)S(1)}, u32[]{:S(2)}, u32[]{:S(2)}) collective-permute-start(f32[2,128,128]{1,2,0:T(8,128)S(1)} %get-tuple-element.12), channel_id=1, source_target_pairs={{0,8},{1,9},{2,10},{3,11},{4,12},{5,13},{6,14},{7,15},{8,0},{9,1},... | collective-permute-start | bytes 393224 | tf_op jit(solution)/shard_map/ppermute | solution.py:14
  513.1 11.9 %collective-permute-start.11 = (f32[2,128,128]{1,2,0:T(8,128)S(1)}, f32[2,128,128]{1,2,0:T(8,128)S(1)}, u32[]{:S(2)}, u32[]{:S(2)}) collective-permute-start(f32[2,128,128]{1,2,0:T(8,128)S(1)} %get-tuple-element.21), channel_id=1, source_target_pairs={{0,8},{1,9},{2,10},{3,11},{4,12},{5,13},{6,14},{7,15},{8,0},{9,1},... | collective-permute-start | bytes 393224 | tf_op jit(solution)/shard_map/ppermute | solution.py:14
Sparse Core Ops, SparseCore 0:
  30.6 88.2 all-reduce.14
  152.4 85.6 all-reduce.12
  267.1 88.7 all-reduce.10
  387.1 87.9 all-reduce.8
where the time goes:
time: 538 us; the launch traced here: 533 us
  waiting for transfers between devices  377 us (70%)
  matrix products  83.6 us (16%)
  starting transfers between devices  22 us (4%)
  local copies, waits for them, and re-layouts  20.6 us (4%)
  between operations  20.2 us (4%)
  other arithmetic  9.1 us (2%)
    psum x4, waiting for transfers between devices, shards(): summed_real, summed_imag = lax.psum((part_real, part_imag), 'long')  346 us
    dot_general x144, matrix products, rows_product(): lax.dot_general(left_side, right_side, (((0,), (0,)), ((), ())), precisio...  47.6 us
    ppermute x16, waiting for transfers between devices, partner(): lax.ppermute(x, axis, [(i, i ^ 1 << distance) for i in range(lax.axis_siz...  31.7 us
    dot_general x128, matrix products, matmul_high(): jnp.dot(left_side, right_side, precision=HIGHEST, preferred_element_type=...  26.5 us
    ppermute x16, starting transfers between devices, partner(): lax.ppermute(x, axis, [(i, i ^ 1 << distance) for i in range(lax.axis_siz...  21.6 us
  transfers between devices with their start and end apart: 20, of which 14 were waited for; matrix products, arithmetic and copies ran while one was open for 11% of the time, Pallas kernels for 0%

commit v1 on v0

v1 whole, which is shorter than its diff:
```python
import functools

import jax
import jax.numpy as jnp
import numpy as np
from jax import lax
from jax.experimental import pallas as pl
from jax.experimental.pallas import tpu as pltpu
from jax.sharding import PartitionSpec as P

SECTIONS = 4
NS_ITERS = 8

F32, BF16 = jnp.float32, jnp.bfloat16
NN = (((1,), (0,)), ((), ()))
NT = (((1,), (1,)), ((), ()))
VMEM_LIMIT = 48 * 2**20


class Layout:
    def __init__(self, size):
        bits = size.bit_length() - 1
        self.size = size
        self.partner_bits = [bits - 1, bits // 2, 0, 1]
        self.gate_bits = sorted(set(self.partner_bits))
        self.other_bits = [b for b in range(bits) if b not in self.gate_bits]
        self.local_bits = [self.gate_bits.index(b) for b in self.partner_bits]
        self.chips = 2 ** (len(self.gate_bits) - 1)

    def chip(self, index):
        return sum((index >> b & 1) << j for j, b in enumerate(self.gate_bits[1:]))

    def ring_position(self, chip):
        line, turn = chip >> 1, chip & 1
        return self.chips - 1 - line if turn else line

    def chip_at(self, position):
        position %= self.chips
        if position < self.chips // 2:
            return position << 1
        return (self.chips - 1 - position) << 1 | 1

    def shifted(self, index, step):
        chip = self.chip_at(self.ring_position(self.chip(index)) + step)
        for j, b in enumerate(self.gate_bits[1:]):
            index = index & ~(1 << b) | (chip >> j & 1) << b
        return index

    def ring(self, step):
        return [(i, self.shifted(i, step)) for i in range(self.size)]

    def flip(self, bit):
        return [(i, i ^ 1 << bit) for i in range(self.size)]

    def table(self):
        half = self.chips // 2
        steps = [0] + [s for k in range(1, half) for s in (-k, k)] + [half]
        low = self.gate_bits[0]
        return np.array(
            [[i >> low & 1] + [self.chip(self.shifted(i, s)) for s in steps] for i in range(self.size)], np.int32
        )


def gather_ring(block, layout):
    up, down = layout.ring(1), layout.ring(-1)
    half = layout.chips // 2
    from_below = from_above = block
    blocks = [block]
    for _ in range(1, half):
        from_below = lax.ppermute(from_below, "long", up)
        from_above = lax.ppermute(from_above, "long", down)
        blocks += [from_below, from_above]
    blocks += [lax.ppermute(from_below[:1], "long", up), lax.ppermute(from_above[1:], "long", down)]
    return blocks


def split(x):
    high = x.astype(BF16)
    return high, (x - high.astype(F32)).astype(BF16)


def dot(a, b, dims):
    return lax.dot_general(a, b, dims, preferred_element_type=F32)


def dot3(a, b, dims):
    return dot(a[0], b[0], dims) + (dot(a[0], b[1], dims) + dot(a[1], b[0], dims))


def turned(a):
    n = a.shape[1] // 2
    return jnp.concatenate([-a[:, n:], a[:, :n]], 1)


def as_matrix(a):
    n = a.shape[1] // 2
    return jnp.concatenate([jnp.concatenate([a[:, :n], -a[:, n:]], 1), jnp.concatenate([a[:, n:], a[:, :n]], 1)], 0)


def polar(e):
    x = e * lax.rsqrt(jnp.sum(e * e) + 1e-6)
    for _ in range(NS_ITERS):
        xs = split(x)
        rows = [jnp.concatenate([v, turned(v)], 0) for v in xs]
        h = dot3(xs, rows, NT)
        p = dot3(split(h), rows, NN)
        x = 1.5 * x - 0.5 * p
    return x


def pair_of(rest, bit):
    low = rest & ((1 << bit) - 1)
    first = (rest - low) * 2 + low
    return first, first + (1 << bit)


def load_pair(ref, rest, bit):
    d0, d1 = pair_of(rest, bit)
    return [
        jnp.concatenate([ref[k, d0, 0], ref[k, d1, 0], ref[k, d0, 1], ref[k, d1, 1]], 0) for k in range(2)
    ]


def store_pair(ref, rest, bit, y):
    d0, d1 = pair_of(rest, bit)
    n = y.shape[0] // 4
    for k, v in enumerate(split(y)):
        ref[k, d0, 0], ref[k, d1, 0] = v[:n], v[n : 2 * n]
        ref[k, d0, 1], ref[k, d1, 1] = v[2 * n : 3 * n], v[3 * n :]


def apply_gate(gate, source, target, bit):
    def body(rest, _):
        store_pair(target, rest, bit, dot3(gate, load_pair(source, rest, bit), NN))
        return 0

    lax.fori_loop(0, source.shape[1] // 2, body, 0, unroll=2)


def environment(phi, psi, bit):
    total = None
    for rest in range(psi.shape[1] // 2):
        term = dot3(load_pair(phi, rest, bit), load_pair(psi, rest, bit), NT)
        total = term if total is None else total + term
    n = total.shape[0] // 2
    return jnp.concatenate([total[:n, :n] + total[n:, n:], total[n:, :n] - total[:n, n:]], 1)


def place(table, blocks, target):
    core = table[0]
    for k in range(len(blocks) - 1):
        chip = table[1 + k]
        for slot in range(2):
            block = blocks[k + slot][0] if k == len(blocks) - 2 else blocks[k][slot]
            d = chip * 2 + (slot ^ core)
            target[0, d], target[1, d] = split(block)


def pack_kernel(table, x_ref, own_ref, sent_ref):
    core = table[0]
    n = x_ref.shape[2] // 2
    for plane in range(2):
        t = x_ref[plane].T
        low, high = t[:n], t[n:]
        own_ref[plane] = jnp.where(core == 0, low, high)
        sent_ref[plane] = jnp.where(core == 0, high, low)


def unpack_kernel(table, own_ref, got_ref, out_ref):
    core = table[0]
    for plane in range(2):
        own, got = own_ref[plane], got_ref[plane]
        low, high = jnp.where(core == 0, own, got), jnp.where(core == 0, got, own)
        out_ref[plane] = jnp.concatenate([low, high], 0).T


def adjoint_kernel(layout, table, gates_ref, *refs):
    *blocks, phis_ref, own_ref, sent_ref, first = refs
    place(table, blocks, first)
    source = first
    for s in range(SECTIONS):
        gate = as_matrix(jnp.concatenate([gates_ref[s, 0], gates_ref[s, 1]], 1))
        apply_gate(split(gate), source, phis_ref.at[s], layout.local_bits[s])
        source = phis_ref.at[s]
    core, chip = table[0], table[1]
    last = phis_ref.at[SECTIONS - 1]
    for slot, out in enumerate((own_ref, sent_ref)):
        d = chip * 2 + (slot ^ core)
        out[...] = last[0, d].astype(F32) + last[1, d].astype(F32)


def first_kernel(layout, table, phis_ref, *refs):
    *blocks, psi_ref, e_ref = refs
    place(table, blocks, psi_ref)
    e_ref[...] = environment(phis_ref.at[0], psi_ref, layout.local_bits[0])


def section_kernel(layout, section, e0_ref, e1_ref, phis_ref, psi_ref, next_ref, e_ref, phi, sem):
    copy = pltpu.make_async_copy(phis_ref.at[section + 1], phi, sem)
    copy.start()
    gate = split(as_matrix(polar(e0_ref[...] + e1_ref[...])))
    apply_gate(gate, psi_ref, next_ref, layout.local_bits[section])
    copy.wait()
    e_ref[...] = environment(phi, next_ref, layout.local_bits[section + 1])


def last_kernel(layout, table, e0_ref, e1_ref, psi_ref, own_ref, sent_ref, scratch):
    bit = layout.local_bits[SECTIONS - 1]
    scratch[...] = as_matrix(polar(e0_ref[...] + e1_ref[...]))
    core, chip = table[0], table[1]
    n = own_ref.shape[1]
    for slot, out in enumerate((own_ref, sent_ref)):
        d = chip * 2 + (slot ^ core)
        t = d >> bit & 1
        rest = (d >> bit + 1 << bit) + (d & (1 << bit) - 1)
        x = load_pair(psi_ref, rest, bit)
        for plane in range(2):
            start = pl.multiple_of(plane * 2 * n + t * n, n)
            out[plane] = dot3(split(scratch[pl.ds(start, n)]), x, NN)


SMEM = pl.BlockSpec(memory_space=pltpu.SMEM)
VMEM = pl.BlockSpec(memory_space=pltpu.VMEM)
ANY = pl.BlockSpec(memory_space=pl.ANY)


def call(kernel, name, outs, ins, specs, flops, scratch=()):
    sizes = [int(np.prod(a.shape)) * a.dtype.itemsize for a in list(ins) + list(outs)]
    return pl.pallas_call(
        kernel,
        out_shape=outs,
        in_specs=specs,
        out_specs=[VMEM] * len(outs),
        scratch_shapes=list(scratch),
        compiler_params=pltpu.CompilerParams(vmem_limit_bytes=VMEM_LIMIT),
        cost_estimate=pl.CostEstimate(flops=flops, bytes_accessed=sum(sizes), transcendentals=0),
        name=name,
    )(*ins)


def shards(initial_state, adjoint_state, current_gates):
    layout = Layout(lax.axis_size("long"))
    core_flip = layout.flip(layout.gate_bits[0])
    table = jnp.asarray(layout.table())[lax.axis_index("long")]
    rows, lanes = initial_state.shape[1:]
    c = lanes // 2
    devices = layout.chips * 2
    slab = jax.ShapeDtypeStruct((2, c, rows), F32)
    pieces = jax.ShapeDtypeStruct((2, devices, 2, c, rows), BF16)
    all_pieces = jax.ShapeDtypeStruct((SECTIONS,) + pieces.shape, BF16)
    env = jax.ShapeDtypeStruct((lanes, 2 * lanes), F32)
    apply_flops = 3 * 2 * (2 * lanes) ** 2 * (devices // 2) * rows

    def pack(x):
        own, sent = call(pack_kernel, "pack", [slab, slab], [table, x], [SMEM, VMEM], 0)
        return jnp.stack([own, lax.ppermute(sent, "long", core_flip)])

    def unpack(own, sent):
        got = lax.ppermute(sent, "long", core_flip)
        full = jax.ShapeDtypeStruct((2, rows, lanes), F32)
        return call(unpack_kernel, "unpack", [full], [table, own, got], [SMEM, VMEM, VMEM], 0)[0]

    def both(e):
        for bit in layout.other_bits:
            e = e + lax.ppermute(e, "long", layout.flip(bit))
        return e, lax.ppermute(e, "long", core_flip)

    phi_blocks = gather_ring(pack(adjoint_state), layout)
    psi_blocks = gather_ring(pack(initial_state), layout)
    phis, phi_own, phi_sent = call(
        functools.partial(adjoint_kernel, layout),
        "adjoint",
        [all_pieces, slab, slab],
        [table, current_gates] + phi_blocks,
        [SMEM] + [VMEM] * (1 + len(phi_blocks)),
        SECTIONS * apply_flops,
        [pltpu.VMEM(pieces.shape, BF16)],
    )
    final_adjoint = unpack(phi_own, phi_sent)
    psi, e = call(
        functools.partial(first_kernel, layout),
        "first",
        [pieces, env],
        [table, phis] + psi_blocks,
        [SMEM] + [VMEM] * (1 + len(psi_blocks)),
        apply_flops,
    )
    for section in range(SECTIONS - 1):
        e0, e1 = both(e)
        psi, e = call(
            functools.partial(section_kernel, layout, section),
            "section",
            [pieces, env],
            [e0, e1, phis, psi],
            [VMEM, VMEM, ANY, VMEM],
            3 * apply_flops,
            [pltpu.VMEM(pieces.shape, BF16), pltpu.SemaphoreType.DMA],
        )
    e0, e1 = both(e)
    own, sent = call(
        functools.partial(last_kernel, layout),
        "last",
        [slab, slab],
        [table, e0, e1, psi],
        [SMEM, VMEM, VMEM, VMEM],
        2 * apply_flops,
        [pltpu.VMEM((2 * lanes, 2 * lanes), F32)],
    )
    return unpack(own, sent), final_adjoint


def solution(mesh):
    return jax.shard_map(
        shards,
        mesh=mesh,
        in_specs=(
            P(None, ("groups", "long"), None),
            P(None, ("groups", "long"), None),
            P("groups", None, None, None),
        ),
        out_specs=(P(None, ("groups", "long"), None), P(None, ("groups", "long"), None)),
        check_vma=False,
    )
```

time: 538 us -> 101 us (0.19)
  waiting for transfers between devices: 377 us -> 29.3 us
  matrix products: 83.6 us -> 0 us
  Pallas kernels: 0 us -> 48.1 us
  between operations: 20.2 us -> 0.75 us
  local copies, waits for them, and re-layouts: 20.6 us -> 2.64 us
  other arithmetic: 9.1 us -> 0.04 us
    psum x4 -> x0, waiting for transfers between devices: 346 us -> none  [shards(): summed_real, summed_imag = lax.psum((part_real, part_imag), 'long')]
    dot_general x304 -> x0, matrix products: 83.6 us -> none  [the longest x144 47.6 us: rows_product(): lax.dot_general(left_side, right_side, (((0,), (0,)), ((), ())), precisio...]
    pallas_call x0 -> x10, Pallas kernels: none -> 48.1 us  [call(): pl.pallas_call(kernel, out_shape=outs, in_specs=specs, out_specs=[VMEM] *...]
    reduce_sum x4 -> x0, other arithmetic: 6.13 us -> none  [polar_factor(): jnp.sum(summed_real * summed_real + summed_imag * summed_imag) + 1e-06]
    ppermute x16 -> x24, waiting for transfers between devices: 31.7 us -> 29.3 us  [the longest x6 22.3 us: gather_ring(): from_above = lax.ppermute(from_above, 'long', down)]
    ppermute x16 -> x24, starting transfers between devices: 21.6 us -> 19.9 us  [the longest x6 13 us: gather_ring(): from_above = lax.ppermute(from_above, 'long', down)]
  transfers between devices with their start and end apart: 20 -> 24, of which waited for: 14 -> 12; matrix products, arithmetic and copies ran while one was open for 11% -> 0% of each run, Pallas kernels for 0% -> 20%
where the time goes in v1:
time: 101 us
  Pallas kernels  48.1 us (48%)
  waiting for transfers between devices  29.3 us (29%)
  starting transfers between devices  19.9 us (20%)
  local copies, waits for them, and re-layouts  2.64 us (3%)
    pallas_call x10, Pallas kernels, call(): pl.pallas_call(kernel, out_shape=outs, in_specs=specs, out_specs=[VMEM] *...  48.1 us
    ppermute x6, waiting for transfers between devices, gather_ring(): from_above = lax.ppermute(from_above, 'long', down)  22.3 us
    ppermute x6, starting transfers between devices, gather_ring(): from_above = lax.ppermute(from_above, 'long', down)  13 us
    ppermute x4, waiting for transfers between devices, both(): return (e, lax.ppermute(e, 'long', core_flip))  4.57 us
    ppermute x2, starting transfers between devices, gather_ring(): lax.ppermute(from_above[1:], 'long', down)  4.11 us
  transfers between devices with their start and end apart: 24, of which 12 were waited for; matrix products, arithmetic and copies ran while one was open for 0% of the time, Pallas kernels for 20%

profile of v1, /device:TPU:0, one launch (start us, length us, event | category | flops | bytes accessed | tf_op | source)
XLA Modules:
  0.0 100.7 jit_solution(11829144050929903157)
XLA Ops:
  0.6 0.7 dynamic-slice_bitcast_fusion.table
  1.3 0.0 copy-start
  1.3 0.9 copy-done
  2.3 0.7 pack.2
  3.0 0.5 collective-permute-start
  3.5 0.0 copy-start.1
  3.5 0.9 copy-done.1
  4.4 0.7 pack.3
  5.1 0.1 collective-permute-start.9
  5.2 0.0 collective-permute-done
  5.3 3.0 %collective-permute-start.2 = (f32[2,2,64,256]{3,2,1,0:T(8,128)S(1)}, f32[2,2,64,256]{3,2,1,0:T(8,128)S(1)}, u32[]{:S(2)}, u32[]{:S(2)}) collective-permute-start(f32[2,2,64,256]{3,2,1,0:T(8,128)S(1)} %pad_maximum_fusion.refs_0_), channel_id=1, source_target_pairs={{0,2},{1,3},{2,6},{3,7},{4,0},{5,1},{6,10},{7,11},{8,4},{9,5},{10,... | collective-permute-start | bytes 786440 | tf_op jit(solution)/shard_map/ppermute | solution.py:71
  8.3 0.1 collective-permute-start.1
  8.4 0.0 collective-permute-done.9
  8.4 2.0 %collective-permute-start.11 = (f32[2,2,64,256]{3,2,1,0:T(8,128)S(1)}, f32[2,2,64,256]{3,2,1,0:T(8,128)S(1)}, u32[]{:S(2)}, u32[]{:S(2)}) collective-permute-start(f32[2,2,64,256]{3,2,1,0:T(8,128)S(1)} %pad_maximum_fusion.1.refs_0_), channel_id=1, source_target_pairs={{0,2},{1,3},{2,6},{3,7},{4,0},{5,1},{6,10},{7,11},{8,4},{9,5},{10,... | collective-permute-start | bytes 786440 | tf_op jit(solution)/shard_map/ppermute | solution.py:71
  10.4 0.1 collective-permute-start.10
  10.5 4.9 %collective-permute-done.2.refs_2_ = f32[2,2,64,256]{3,2,1,0:T(8,128)S(1)} collective-permute-done((f32[2,2,64,256]{3,2,1,0:T(8,128)S(1)}, f32[2,2,64,256]{3,2,1,0:T(8,128)S(1)}, u32[]{:S(2)}, u32[]{:S(2)}) %collective-permute-start.2) | collective-permute-done | bytes 262176 | tf_op jit(solution)/shard_map/ppermute | solution.py:71
  15.4 2.0 %collective-permute-start.4 = (f32[2,2,64,256]{3,2,1,0:T(8,128)S(1)}, f32[2,2,64,256]{3,2,1,0:T(8,128)S(1)}, u32[]{:S(2)}, u32[]{:S(2)}) collective-permute-start(f32[2,2,64,256]{3,2,1,0:T(8,128)S(1)} %collective-permute-done.2.refs_2_), channel_id=1, source_target_pairs={{0,2},{1,3},{2,6},{3,7},{4,0},{5,1},{6,10},{7,11},{8,4},{9,5},{10,... | collective-permute-start | bytes 786440 | tf_op jit(solution)/shard_map/ppermute | solution.py:71
  17.4 0.0 collective-permute-done.1.refs_1_
  17.5 0.1 collective-permute-start.3
  17.6 3.5 %collective-permute-done.11.refs_2_ = f32[2,2,64,256]{3,2,1,0:T(8,128)S(1)} collective-permute-done((f32[2,2,64,256]{3,2,1,0:T(8,128)S(1)}, f32[2,2,64,256]{3,2,1,0:T(8,128)S(1)}, u32[]{:S(2)}, u32[]{:S(2)}) %collective-permute-start.11) | collective-permute-done | bytes 262176 | tf_op jit(solution)/shard_map/ppermute | solution.py:71
  21.1 2.0 %collective-permute-start.13 = (f32[2,2,64,256]{3,2,1,0:T(8,128)S(1)}, f32[2,2,64,256]{3,2,1,0:T(8,128)S(1)}, u32[]{:S(2)}, u32[]{:S(2)}) collective-permute-start(f32[2,2,64,256]{3,2,1,0:T(8,128)S(1)} %collective-permute-done.11.refs_2_), channel_id=1, source_target_pairs={{0,2},{1,3},{2,6},{3,7},{4,0},{5,1},{6,10},{7,11},{8,4},{9,5},{10,... | collective-permute-start | bytes 786440 | tf_op jit(solution)/shard_map/ppermute | solution.py:71
  23.1 0.0 collective-permute-done.10.refs_1_
  23.1 0.1 collective-permute-start.12
  23.2 3.5 %collective-permute-done.4.refs_4_ = f32[2,2,64,256]{3,2,1,0:T(8,128)S(1)} collective-permute-done((f32[2,2,64,256]{3,2,1,0:T(8,128)S(1)}, f32[2,2,64,256]{3,2,1,0:T(8,128)S(1)}, u32[]{:S(2)}, u32[]{:S(2)}) %collective-permute-start.4) | collective-permute-done | bytes 262176 | tf_op jit(solution)/shard_map/ppermute | solution.py:71
  26.7 2.0 %collective-permute-start.6 = (f32[2,2,64,256]{3,2,1,0:T(8,128)S(1)}, f32[2,2,64,256]{3,2,1,0:T(8,128)S(1)}, u32[]{:S(2)}, u32[]{:S(2)}) collective-permute-start(f32[2,2,64,256]{3,2,1,0:T(8,128)S(1)} %collective-permute-done.4.refs_4_), channel_id=1, source_target_pairs={{0,2},{1,3},{2,6},{3,7},{4,0},{5,1},{6,10},{7,11},{8,4},{9,5},{10,... | collective-permute-start | bytes 786440 | tf_op jit(solution)/shard_map/ppermute | solution.py:71
  28.7 0.0 collective-permute-done.3.refs_3_
  28.7 0.1 collective-permute-start.5
  28.8 3.5 %collective-permute-done.13.refs_4_ = f32[2,2,64,256]{3,2,1,0:T(8,128)S(1)} collective-permute-done((f32[2,2,64,256]{3,2,1,0:T(8,128)S(1)}, f32[2,2,64,256]{3,2,1,0:T(8,128)S(1)}, u32[]{:S(2)}, u32[]{:S(2)}) %collective-permute-start.13) | collective-permute-done | bytes 262176 | tf_op jit(solution)/shard_map/ppermute | solution.py:71
  32.3 2.0 %collective-permute-start.15 = (f32[2,2,64,256]{3,2,1,0:T(8,128)S(1)}, f32[2,2,64,256]{3,2,1,0:T(8,128)S(1)}, u32[]{:S(2)}, u32[]{:S(2)}) collective-permute-start(f32[2,2,64,256]{3,2,1,0:T(8,128)S(1)} %collective-permute-done.13.refs_4_), channel_id=1, source_target_pairs={{0,2},{1,3},{2,6},{3,7},{4,0},{5,1},{6,10},{7,11},{8,4},{9,5},{10,... | collective-permute-start | bytes 786440 | tf_op jit(solution)/shard_map/ppermute | solution.py:71
  34.3 0.0 collective-permute-done.12.refs_3_
  34.3 0.1 collective-permute-start.14
  34.4 3.5 %collective-permute-done.6.refs_6_ = f32[2,2,64,256]{3,2,1,0:T(8,128)S(1)} collective-permute-done((f32[2,2,64,256]{3,2,1,0:T(8,128)S(1)}, f32[2,2,64,256]{3,2,1,0:T(8,128)S(1)}, u32[]{:S(2)}, u32[]{:S(2)}) %collective-permute-start.6) | collective-permute-done | bytes 262176 | tf_op jit(solution)/shard_map/ppermute | solution.py:71
  37.9 2.1 %collective-permute-start.8 = (f32[1,2,64,256]{3,2,1,0:T(8,128)S(1)}, f32[1,2,64,256]{3,2,1,0:T(8,128)S(1)}, u32[]{:S(2)}, u32[]{:S(2)}) collective-permute-start(f32[1,2,64,256]{3,2,1,0:T(8,128)S(1)} %slice.17), channel_id=1, source_target_pairs={{0,2},{1,3},{2,6},{3,7},{4,0},{5,1},{6,10},{7,11},{8,4},{9,5},{10,... | collective-permute-start | bytes 393224 | tf_op jit(solution)/shard_map/ppermute | solution.py:73
  40.0 0.0 collective-permute-done.5.refs_5_
  40.0 0.1 collective-permute-start.7
  40.1 3.4 %collective-permute-done.15.refs_6_ = f32[2,2,64,256]{3,2,1,0:T(8,128)S(1)} collective-permute-done((f32[2,2,64,256]{3,2,1,0:T(8,128)S(1)}, f32[2,2,64,256]{3,2,1,0:T(8,128)S(1)}, u32[]{:S(2)}, u32[]{:S(2)}) %collective-permute-start.15) | collective-permute-done | bytes 262176 | tf_op jit(solution)/shard_map/ppermute | solution.py:71
  43.5 2.1 %collective-permute-start.17 = (f32[1,2,64,256]{3,2,1,0:T(8,128)S(1)}, f32[1,2,64,256]{3,2,1,0:T(8,128)S(1)}, u32[]{:S(2)}, u32[]{:S(2)}) collective-permute-start(f32[1,2,64,256]{3,2,1,0:T(8,128)S(1)} %slice.19), channel_id=1, source_target_pairs={{0,2},{1,3},{2,6},{3,7},{4,0},{5,1},{6,10},{7,11},{8,4},{9,5},{10,... | collective-permute-start | bytes 393224 | tf_op jit(solution)/shard_map/ppermute | solution.py:73
  45.6 0.0 collective-permute-done.14.refs_5_
  45.6 0.1 collective-permute-start.16
  45.8 0.6 collective-permute-done.8.refs_8_
  46.3 1.6 %collective-permute-done.7.refs_7_ = f32[1,2,64,256]{3,2,1,0:T(8,128)S(1)} collective-permute-done((f32[1,2,64,256]{3,2,1,0:T(8,128)S(1)}, f32[1,2,64,256]{3,2,1,0:T(8,128)S(1)}, u32[]{:S(2)}, u32[]{:S(2)}) %collective-permute-start.7) | collective-permute-done | bytes 131104 | tf_op jit(solution)/shard_map/ppermute | solution.py:73
  48.0 0.0 copy-done.2
  48.0 13.2 %adjoint.1 = (bf16[4,2,16,2,64,256]{5,4,3,2,1,0:T(8,128)(2,1)}, f32[2,64,256]{2,1,0:T(8,128)S(1)}, f32[2,64,256]{2,1,0:T(8,128)S(1)}) custom-call(s32[9]{0:T(128)S(1)} %dynamic-slice_bitcast_fusion.table, f32[4,2,128,128]{3,2,1,0:T(8,128)S(1)} %copy-done.2, f32[2,2,64,256]{3,2,1,0:T(8,128)S(1)} %pad_maximum_fusion.refs_0_, ...), custom_call_target="tpu_custom_call" | custom-call | flops 3221225472 | bytes 11272228 | tf_op jit(solution)/shard_map/adjoint/pallas_call | solution.py:229
  61.1 0.0 collective-permute-done.17.refs_8_
  61.1 0.0 collective-permute-done.16.refs_7_
  61.1 4.7 %first.1 = (bf16[2,16,2,64,256]{4,3,2,1,0:T(8,128)(2,1)S(1)}, f32[128,256]{1,0:T(8,128)S(1)}) custom-call(s32[9]{0:T(128)S(1)} %dynamic-slice_bitcast_fusion.table, bf16[4,2,16,2,64,256]{5,4,3,2,1,0:T(8,128)(2,1)} %get-tuple-element.21.phis_ref, f32[2,2,64,256]{3,2,1,0:T(8,128)S(1)} %pad_maximum_fusion.1.refs_0_, ...), custom_call_target="tpu_custom_call" | custom-call | flops 805306368 | bytes 12714020 | tf_op jit(solution)/shard_map/first/pallas_call | solution.py:229
  65.8 0.1 collective-permute-start.18
  65.9 1.3 %collective-permute-done.18.e1_ref = f32[128,256]{1,0:T(8,128)S(1)} collective-permute-done((f32[128,256]{1,0:T(8,128)S(1)}, f32[128,256]{1,0:T(8,128)S(1)}, u32[]{:S(2)}, u32[]{:S(2)}) %collective-permute-start.18) | collective-permute-done | bytes 131104 | tf_op jit(solution)/shard_map/ppermute | solution.py:266
  67.2 7.0 %section.3 = (bf16[2,16,2,64,256]{4,3,2,1,0:T(8,128)(2,1)S(1)}, f32[128,256]{1,0:T(8,128)S(1)}) custom-call(f32[128,256]{1,0:T(8,128)S(1)} %get-tuple-element.24.e0_ref, f32[128,256]{1,0:T(8,128)S(1)} %collective-permute-done.18.e1_ref, bf16[4,2,16,2,64,256]{5,4,3,2,1,0:T(8,128)(2,1)} %get-tuple-element.21.phis_ref, ...), custom_call_target="tpu_custom_call" | custom-call | flops 2415919104 | bytes 12976128 | tf_op jit(solution)/shard_map/section/pallas_call | solution.py:229
  74.2 0.2 collective-permute-start.19
  74.5 1.2 %collective-permute-done.19.e1_ref = f32[128,256]{1,0:T(8,128)S(1)} collective-permute-done((f32[128,256]{1,0:T(8,128)S(1)}, f32[128,256]{1,0:T(8,128)S(1)}, u32[]{:S(2)}, u32[]{:S(2)}) %collective-permute-start.19) | collective-permute-done | bytes 131104 | tf_op jit(solution)/shard_map/ppermute | solution.py:266
  75.7 7.0 %section.4 = (bf16[2,16,2,64,256]{4,3,2,1,0:T(8,128)(2,1)S(1)}, f32[128,256]{1,0:T(8,128)S(1)}) custom-call(f32[128,256]{1,0:T(8,128)S(1)} %get-tuple-element.26.e0_ref, f32[128,256]{1,0:T(8,128)S(1)} %collective-permute-done.19.e1_ref, bf16[4,2,16,2,64,256]{5,4,3,2,1,0:T(8,128)(2,1)} %get-tuple-element.21.phis_ref, ...), custom_call_target="tpu_custom_call" | custom-call | flops 2415919104 | bytes 12976128 | tf_op jit(solution)/shard_map/section/pallas_call | solution.py:229
  82.7 0.2 collective-permute-start.20
  82.9 1.2 %collective-permute-done.20.e1_ref = f32[128,256]{1,0:T(8,128)S(1)} collective-permute-done((f32[128,256]{1,0:T(8,128)S(1)}, f32[128,256]{1,0:T(8,128)S(1)}, u32[]{:S(2)}, u32[]{:S(2)}) %collective-permute-start.20) | collective-permute-done | bytes 131104 | tf_op jit(solution)/shard_map/ppermute | solution.py:266
  84.1 6.9 %section.5 = (bf16[2,16,2,64,256]{4,3,2,1,0:T(8,128)(2,1)S(1)}, f32[128,256]{1,0:T(8,128)S(1)}) custom-call(f32[128,256]{1,0:T(8,128)S(1)} %get-tuple-element.28.e0_ref, f32[128,256]{1,0:T(8,128)S(1)} %collective-permute-done.20.e1_ref, bf16[4,2,16,2,64,256]{5,4,3,2,1,0:T(8,128)(2,1)} %get-tuple-element.21.phis_ref, ...), custom_call_target="tpu_custom_call" | custom-call | flops 2415919104 | bytes 12976128 | tf_op jit(solution)/shard_map/section/pallas_call | solution.py:229
  91.0 0.2 collective-permute-start.21
  91.2 0.4 collective-permute-start.23
  91.6 0.8 collective-permute-done.21.e1_ref
  92.4 5.3 %last.1 = (f32[2,64,256]{2,1,0:T(8,128)S(1)}, f32[2,64,256]{2,1,0:T(8,128)S(1)}) custom-call(s32[9]{0:T(128)S(1)} %dynamic-slice_bitcast_fusion.table, f32[128,256]{1,0:T(8,128)S(1)} %get-tuple-element.30.e0_ref, f32[128,256]{1,0:T(8,128)S(1)} %collective-permute-done.21.e1_ref, bf16[2,16,2,64,256]{4,3,2,1,0:T(8,128)(2,1)S(1)} %get-tuple-element.31.psi_ref), custom_call_target="tpu_custom_call" | custom-call | flops 1610612736 | bytes 2621476 | tf_op jit(solution)/shard_map/last/pallas_call | solution.py:229
  97.7 0.2 collective-permute-start.22
  97.9 0.0 collective-permute-done.23.got_ref
  97.9 1.4 %unpack.3 = f32[2,256,128]{2,1,0:T(8,128)} custom-call(s32[9]{0:T(128)S(1)} %dynamic-slice_bitcast_fusion.table, f32[2,64,256]{2,1,0:T(8,128)S(1)} %get-tuple-element.34.own_ref, f32[2,64,256]{2,1,0:T(8,128)S(1)} %collective-permute-done.23.got_ref), custom_call_target="tpu_custom_call" | custom-call | bytes 524324 | tf_op jit(solution)/shard_map/unpack/pallas_call | solution.py:229
  99.3 0.0 collective-permute-done.22.got_ref
  99.3 1.4 %unpack.2 = f32[2,256,128]{2,1,0:T(8,128)} custom-call(s32[9]{0:T(128)S(1)} %dynamic-slice_bitcast_fusion.table, f32[2,64,256]{2,1,0:T(8,128)S(1)} %get-tuple-element.32.own_ref, f32[2,64,256]{2,1,0:T(8,128)S(1)} %collective-permute-done.22.got_ref), custom_call_target="tpu_custom_call" | custom-call | bytes 524324 | tf_op jit(solution)/shard_map/unpack/pallas_call | solution.py:229
  (7 shorter events, 0.1 us)
Async XLA Ops:
  1.3 0.9 copy-start
  3.0 2.3 %collective-permute-start = (f32[2,64,256]{2,1,0:T(8,128)S(1)}, f32[2,64,256]{2,1,0:T(8,128)S(1)}, u32[]{:S(2)}, u32[]{:S(2)}) collective-permute-start(f32[2,64,256]{2,1,0:T(8,128)S(1)} %get-tuple-element.20), channel_id=1, source_target_pairs={{0,1},{1,0},{2,3},{3,2},{4,5},{5,4},{6,7},{7,6},{8,9},{9,8},{10,11... | collective-permute-start | bytes 393224 | tf_op jit(solution)/shard_map/ppermute | solution.py:256
  3.5 0.9 copy-start.1
  4.4 43.5 %copy-start.2 = (f32[4,2,128,128]{3,2,1,0:T(8,128)S(1)}, f32[4,2,128,128]{3,2,1,0:T(8,128)}, u32[]{:S(2)}) copy-start(f32[4,2,128,128]{3,2,1,0:T(8,128)} %gates_ref.1) | copy-start | bytes 1572868
  5.1 3.3 %collective-permute-start.9 = (f32[2,64,256]{2,1,0:T(8,128)S(1)}, f32[2,64,256]{2,1,0:T(8,128)S(1)}, u32[]{:S(2)}, u32[]{:S(2)}) collective-permute-start(f32[2,64,256]{2,1,0:T(8,128)S(1)} %get-tuple-element.23), channel_id=1, source_target_pairs={{0,1},{1,0},{2,3},{3,2},{4,5},{5,4},{6,7},{7,6},{8,9},{9,8},{10,11... | collective-permute-start | bytes 393224 | tf_op jit(solution)/shard_map/ppermute | solution.py:256
  5.3 10.2 %collective-permute-start.2 = (f32[2,2,64,256]{3,2,1,0:T(8,128)S(1)}, f32[2,2,64,256]{3,2,1,0:T(8,128)S(1)}, u32[]{:S(2)}, u32[]{:S(2)}) collective-permute-start(f32[2,2,64,256]{3,2,1,0:T(8,128)S(1)} %pad_maximum_fusion.refs_0_), channel_id=1, source_target_pairs={{0,2},{1,3},{2,6},{3,7},{4,0},{5,1},{6,10},{7,11},{8,4},{9,5},{10,... | collective-permute-start | bytes 786440 | tf_op jit(solution)/shard_map/ppermute | solution.py:71
  8.3 9.2 %collective-permute-start.1 = (f32[2,2,64,256]{3,2,1,0:T(8,128)S(1)}, f32[2,2,64,256]{3,2,1,0:T(8,128)S(1)}, u32[]{:S(2)}, u32[]{:S(2)}) collective-permute-start(f32[2,2,64,256]{3,2,1,0:T(8,128)S(1)} %pad_maximum_fusion.refs_0_), channel_id=1, source_target_pairs={{0,4},{1,5},{2,0},{3,1},{4,8},{5,9},{6,2},{7,3},{8,12},{9,13},{10,... | collective-permute-start | bytes 786440 | tf_op jit(solution)/shard_map/ppermute | solution.py:70
  8.4 12.6 %collective-permute-start.11 = (f32[2,2,64,256]{3,2,1,0:T(8,128)S(1)}, f32[2,2,64,256]{3,2,1,0:T(8,128)S(1)}, u32[]{:S(2)}, u32[]{:S(2)}) collective-permute-start(f32[2,2,64,256]{3,2,1,0:T(8,128)S(1)} %pad_maximum_fusion.1.refs_0_), channel_id=1, source_target_pairs={{0,2},{1,3},{2,6},{3,7},{4,0},{5,1},{6,10},{7,11},{8,4},{9,5},{10,... | collective-permute-start | bytes 786440 | tf_op jit(solution)/shard_map/ppermute | solution.py:71
  10.4 12.7 %collective-permute-start.10 = (f32[2,2,64,256]{3,2,1,0:T(8,128)S(1)}, f32[2,2,64,256]{3,2,1,0:T(8,128)S(1)}, u32[]{:S(2)}, u32[]{:S(2)}) collective-permute-start(f32[2,2,64,256]{3,2,1,0:T(8,128)S(1)} %pad_maximum_fusion.1.refs_0_), channel_id=1, source_target_pairs={{0,4},{1,5},{2,0},{3,1},{4,8},{5,9},{6,2},{7,3},{8,12},{9,13},{10,... | collective-permute-start | bytes 786440 | tf_op jit(solution)/shard_map/ppermute | solution.py:70
  15.4 11.2 %collective-permute-start.4 = (f32[2,2,64,256]{3,2,1,0:T(8,128)S(1)}, f32[2,2,64,256]{3,2,1,0:T(8,128)S(1)}, u32[]{:S(2)}, u32[]{:S(2)}) collective-permute-start(f32[2,2,64,256]{3,2,1,0:T(8,128)S(1)} %collective-permute-done.2.refs_2_), channel_id=1, source_target_pairs={{0,2},{1,3},{2,6},{3,7},{4,0},{5,1},{6,10},{7,11},{8,4},{9,5},{10,... | collective-permute-start | bytes 786440 | tf_op jit(solution)/shard_map/ppermute | solution.py:71
  17.5 11.2 %collective-permute-start.3 = (f32[2,2,64,256]{3,2,1,0:T(8,128)S(1)}, f32[2,2,64,256]{3,2,1,0:T(8,128)S(1)}, u32[]{:S(2)}, u32[]{:S(2)}) collective-permute-start(f32[2,2,64,256]{3,2,1,0:T(8,128)S(1)} %collective-permute-done.1.refs_1_), channel_id=1, source_target_pairs={{0,4},{1,5},{2,0},{3,1},{4,8},{5,9},{6,2},{7,3},{8,12},{9,13},{10,... | collective-permute-start | bytes 786440 | tf_op jit(solution)/shard_map/ppermute | solution.py:70
  21.1 11.2 %collective-permute-start.13 = (f32[2,2,64,256]{3,2,1,0:T(8,128)S(1)}, f32[2,2,64,256]{3,2,1,0:T(8,128)S(1)}, u32[]{:S(2)}, u32[]{:S(2)}) collective-permute-start(f32[2,2,64,256]{3,2,1,0:T(8,128)S(1)} %collective-permute-done.11.refs_2_), channel_id=1, source_target_pairs={{0,2},{1,3},{2,6},{3,7},{4,0},{5,1},{6,10},{7,11},{8,4},{9,5},{10,... | collective-permute-start | bytes 786440 | tf_op jit(solution)/shard_map/ppermute | solution.py:71
  23.1 11.2 %collective-permute-start.12 = (f32[2,2,64,256]{3,2,1,0:T(8,128)S(1)}, f32[2,2,64,256]{3,2,1,0:T(8,128)S(1)}, u32[]{:S(2)}, u32[]{:S(2)}) collective-permute-start(f32[2,2,64,256]{3,2,1,0:T(8,128)S(1)} %collective-permute-done.10.refs_1_), channel_id=1, source_target_pairs={{0,4},{1,5},{2,0},{3,1},{4,8},{5,9},{6,2},{7,3},{8,12},{9,13},{10,... | collective-permute-start | bytes 786440 | tf_op jit(solution)/shard_map/ppermute | solution.py:70
  26.7 11.2 %collective-permute-start.6 = (f32[2,2,64,256]{3,2,1,0:T(8,128)S(1)}, f32[2,2,64,256]{3,2,1,0:T(8,128)S(1)}, u32[]{:S(2)}, u32[]{:S(2)}) collective-permute-start(f32[2,2,64,256]{3,2,1,0:T(8,128)S(1)} %collective-permute-done.4.refs_4_), channel_id=1, source_target_pairs={{0,2},{1,3},{2,6},{3,7},{4,0},{5,1},{6,10},{7,11},{8,4},{9,5},{10,... | collective-permute-start | bytes 786440 | tf_op jit(solution)/shard_map/ppermute | solution.py:71
  28.7 11.3 %collective-permute-start.5 = (f32[2,2,64,256]{3,2,1,0:T(8,128)S(1)}, f32[2,2,64,256]{3,2,1,0:T(8,128)S(1)}, u32[]{:S(2)}, u32[]{:S(2)}) collective-permute-start(f32[2,2,64,256]{3,2,1,0:T(8,128)S(1)} %collective-permute-done.3.refs_3_), channel_id=1, source_target_pairs={{0,4},{1,5},{2,0},{3,1},{4,8},{5,9},{6,2},{7,3},{8,12},{9,13},{10,... | collective-permute-start | bytes 786440 | tf_op jit(solution)/shard_map/ppermute | solution.py:70
  32.3 11.2 %collective-permute-start.15 = (f32[2,2,64,256]{3,2,1,0:T(8,128)S(1)}, f32[2,2,64,256]{3,2,1,0:T(8,128)S(1)}, u32[]{:S(2)}, u32[]{:S(2)}) collective-permute-start(f32[2,2,64,256]{3,2,1,0:T(8,128)S(1)} %collective-permute-done.13.refs_4_), channel_id=1, source_target_pairs={{0,2},{1,3},{2,6},{3,7},{4,0},{5,1},{6,10},{7,11},{8,4},{9,5},{10,... | collective-permute-start | bytes 786440 | tf_op jit(solution)/shard_map/ppermute | solution.py:71
  34.3 11.3 %collective-permute-start.14 = (f32[2,2,64,256]{3,2,1,0:T(8,128)S(1)}, f32[2,2,64,256]{3,2,1,0:T(8,128)S(1)}, u32[]{:S(2)}, u32[]{:S(2)}) collective-permute-start(f32[2,2,64,256]{3,2,1,0:T(8,128)S(1)} %collective-permute-done.12.refs_3_), channel_id=1, source_target_pairs={{0,4},{1,5},{2,0},{3,1},{4,8},{5,9},{6,2},{7,3},{8,12},{9,13},{10,... | collective-permute-start | bytes 786440 | tf_op jit(solution)/shard_map/ppermute | solution.py:70
  37.9 8.4 %collective-permute-start.8 = (f32[1,2,64,256]{3,2,1,0:T(8,128)S(1)}, f32[1,2,64,256]{3,2,1,0:T(8,128)S(1)}, u32[]{:S(2)}, u32[]{:S(2)}) collective-permute-start(f32[1,2,64,256]{3,2,1,0:T(8,128)S(1)} %slice.17), channel_id=1, source_target_pairs={{0,2},{1,3},{2,6},{3,7},{4,0},{5,1},{6,10},{7,11},{8,4},{9,5},{10,... | collective-permute-start | bytes 393224 | tf_op jit(solution)/shard_map/ppermute | solution.py:73
  40.0 8.0 %collective-permute-start.7 = (f32[1,2,64,256]{3,2,1,0:T(8,128)S(1)}, f32[1,2,64,256]{3,2,1,0:T(8,128)S(1)}, u32[]{:S(2)}, u32[]{:S(2)}) collective-permute-start(f32[1,2,64,256]{3,2,1,0:T(8,128)S(1)} %slice.16), channel_id=1, source_target_pairs={{0,4},{1,5},{2,0},{3,1},{4,8},{5,9},{6,2},{7,3},{8,12},{9,13},{10,... | collective-permute-start | bytes 393224 | tf_op jit(solution)/shard_map/ppermute | solution.py:73
  43.5 17.6 %collective-permute-start.17 = (f32[1,2,64,256]{3,2,1,0:T(8,128)S(1)}, f32[1,2,64,256]{3,2,1,0:T(8,128)S(1)}, u32[]{:S(2)}, u32[]{:S(2)}) collective-permute-start(f32[1,2,64,256]{3,2,1,0:T(8,128)S(1)} %slice.19), channel_id=1, source_target_pairs={{0,2},{1,3},{2,6},{3,7},{4,0},{5,1},{6,10},{7,11},{8,4},{9,5},{10,... | collective-permute-start | bytes 393224 | tf_op jit(solution)/shard_map/ppermute | solution.py:73
  45.6 15.5 %collective-permute-start.16 = (f32[1,2,64,256]{3,2,1,0:T(8,128)S(1)}, f32[1,2,64,256]{3,2,1,0:T(8,128)S(1)}, u32[]{:S(2)}, u32[]{:S(2)}) collective-permute-start(f32[1,2,64,256]{3,2,1,0:T(8,128)S(1)} %slice.18), channel_id=1, source_target_pairs={{0,4},{1,5},{2,0},{3,1},{4,8},{5,9},{6,2},{7,3},{8,12},{9,13},{10,... | collective-permute-start | bytes 393224 | tf_op jit(solution)/shard_map/ppermute | solution.py:73
  65.8 1.4 %collective-permute-start.18 = (f32[128,256]{1,0:T(8,128)S(1)}, f32[128,256]{1,0:T(8,128)S(1)}, u32[]{:S(2)}, u32[]{:S(2)}) collective-permute-start(f32[128,256]{1,0:T(8,128)S(1)} %get-tuple-element.24.e0_ref), channel_id=1, source_target_pairs={{0,1},{1,0},{2,3},{3,2},{4,5},{5,4},{6,7},{7,6},{8,9},{9,8},{10,11... | collective-permute-start | bytes 393224 | tf_op jit(solution)/shard_map/ppermute | solution.py:266
  74.2 1.4 %collective-permute-start.19 = (f32[128,256]{1,0:T(8,128)S(1)}, f32[128,256]{1,0:T(8,128)S(1)}, u32[]{:S(2)}, u32[]{:S(2)}) collective-permute-start(f32[128,256]{1,0:T(8,128)S(1)} %get-tuple-element.26.e0_ref), channel_id=1, source_target_pairs={{0,1},{1,0},{2,3},{3,2},{4,5},{5,4},{6,7},{7,6},{8,9},{9,8},{10,11... | collective-permute-start | bytes 393224 | tf_op jit(solution)/shard_map/ppermute | solution.py:266
  82.7 1.4 %collective-permute-start.20 = (f32[128,256]{1,0:T(8,128)S(1)}, f32[128,256]{1,0:T(8,128)S(1)}, u32[]{:S(2)}, u32[]{:S(2)}) collective-permute-start(f32[128,256]{1,0:T(8,128)S(1)} %get-tuple-element.28.e0_ref), channel_id=1, source_target_pairs={{0,1},{1,0},{2,3},{3,2},{4,5},{5,4},{6,7},{7,6},{8,9},{9,8},{10,11... | collective-permute-start | bytes 393224 | tf_op jit(solution)/shard_map/ppermute | solution.py:266
  91.0 1.4 %collective-permute-start.21 = (f32[128,256]{1,0:T(8,128)S(1)}, f32[128,256]{1,0:T(8,128)S(1)}, u32[]{:S(2)}, u32[]{:S(2)}) collective-permute-start(f32[128,256]{1,0:T(8,128)S(1)} %get-tuple-element.30.e0_ref), channel_id=1, source_target_pairs={{0,1},{1,0},{2,3},{3,2},{4,5},{5,4},{6,7},{7,6},{8,9},{9,8},{10,11... | collective-permute-start | bytes 393224 | tf_op jit(solution)/shard_map/ppermute | solution.py:266
  91.2 6.7 %collective-permute-start.23 = (f32[2,64,256]{2,1,0:T(8,128)S(1)}, f32[2,64,256]{2,1,0:T(8,128)S(1)}, u32[]{:S(2)}, u32[]{:S(2)}) collective-permute-start(f32[2,64,256]{2,1,0:T(8,128)S(1)} %get-tuple-element.35), channel_id=1, source_target_pairs={{0,1},{1,0},{2,3},{3,2},{4,5},{5,4},{6,7},{7,6},{8,9},{9,8},{10,11... | collective-permute-start | bytes 393224 | tf_op jit(solution)/shard_map/ppermute | solution.py:259
  97.7 1.6 %collective-permute-start.22 = (f32[2,64,256]{2,1,0:T(8,128)S(1)}, f32[2,64,256]{2,1,0:T(8,128)S(1)}, u32[]{:S(2)}, u32[]{:S(2)}) collective-permute-start(f32[2,64,256]{2,1,0:T(8,128)S(1)} %get-tuple-element.33), channel_id=1, source_target_pairs={{0,1},{1,0},{2,3},{3,2},{4,5},{5,4},{6,7},{7,6},{8,9},{9,8},{10,11... | collective-permute-start | bytes 393224 | tf_op jit(solution)/shard_map/ppermute | solution.py:259

commit v2 on v1

v2 whole, which is shorter than its diff:
```python
import functools

import jax
import jax.numpy as jnp
import numpy as np
from jax import lax
from jax.experimental import pallas as pl
from jax.experimental.pallas import tpu as pltpu
from jax.sharding import PartitionSpec as P

SECTIONS = 4
NS_ITERS = 8

F32, BF16 = jnp.float32, jnp.bfloat16
NN = (((1,), (0,)), ((), ()))
NT = (((1,), (1,)), ((), ()))
VMEM_LIMIT = 24 * 2**20


class Layout:
    def __init__(self, size):
        bits = size.bit_length() - 1
        self.size = size
        self.partner_bits = [bits - 1, bits // 2, 0, 1]
        self.gate_bits = sorted(set(self.partner_bits))
        self.other_bits = [b for b in range(bits) if b not in self.gate_bits]
        self.local_bits = [self.gate_bits.index(b) for b in self.partner_bits]
        self.chips = 2 ** (len(self.gate_bits) - 1)

    def chip(self, index):
        return sum((index >> b & 1) << j for j, b in enumerate(self.gate_bits[1:]))

    def ring_position(self, chip):
        line, turn = chip >> 1, chip & 1
        return self.chips - 1 - line if turn else line

    def chip_at(self, position):
        position %= self.chips
        if position < self.chips // 2:
            return position << 1
        return (self.chips - 1 - position) << 1 | 1

    def shifted(self, index, step):
        chip = self.chip_at(self.ring_position(self.chip(index)) + step)
        for j, b in enumerate(self.gate_bits[1:]):
            index = index & ~(1 << b) | (chip >> j & 1) << b
        return index

    def ring(self, step):
        return [(i, self.shifted(i, step)) for i in range(self.size)]

    def flip(self, bit):
        return [(i, i ^ 1 << bit) for i in range(self.size)]

    def place_of(self, index):
        position = self.ring_position_traced(self.chip(index))
        half = self.chips // 2
        steps = [0] + [s for k in range(1, half) for s in (-k, k)] + [half]
        return index >> self.gate_bits[0] & 1, [self.chip_at_traced(position + s) for s in steps]

    def ring_position_traced(self, chip):
        line, turn = chip >> 1, chip & 1
        return jnp.where(turn == 1, self.chips - 1 - line, line)

    def chip_at_traced(self, position):
        position = position & self.chips - 1
        return jnp.where(position < self.chips // 2, position << 1, (self.chips - 1 - position) << 1 | 1)


def gather_ring(block, layout):
    up, down = layout.ring(1), layout.ring(-1)
    half = layout.chips // 2
    from_below = from_above = block
    blocks = [block]
    for _ in range(1, half):
        from_below = lax.ppermute(from_below, "long", up)
        from_above = lax.ppermute(from_above, "long", down)
        blocks += [from_below, from_above]
    blocks += [lax.ppermute(from_below[:1], "long", up), lax.ppermute(from_above[1:], "long", down)]
    return blocks


def split(x):
    high = x.astype(BF16)
    return high, (x - high.astype(F32)).astype(BF16)


def dot(a, b, dims):
    return lax.dot_general(a, b, dims, preferred_element_type=F32)


def dot3(a, b, dims):
    return dot(a[0], b[0], dims) + (dot(a[0], b[1], dims) + dot(a[1], b[0], dims))


def turned(a):
    n = a.shape[1] // 2
    return jnp.concatenate([-a[:, n:], a[:, :n]], 1)


def as_matrix(a):
    n = a.shape[1] // 2
    return jnp.concatenate([jnp.concatenate([a[:, :n], -a[:, n:]], 1), jnp.concatenate([a[:, n:], a[:, :n]], 1)], 0)


def polar(e, beside=lambda k: None):
    x = e * lax.rsqrt(jnp.sum(e * e) + 1e-6)
    for k in range(NS_ITERS):
        xs = split(x)
        rows = [jnp.concatenate([v, turned(v)], 0) for v in xs]
        h = dot3(xs, rows, NT)
        beside(k)
        p = dot3(split(h), rows, NN)
        x = 1.5 * x - 0.5 * p
    return x


def pair_of(rest, bit):
    low = rest & ((1 << bit) - 1)
    first = (rest - low) * 2 + low
    return first, first + (1 << bit)


def load_pair(ref, rest, bit):
    d0, d1 = pair_of(rest, bit)
    return [
        jnp.concatenate([ref[k, d0, 0], ref[k, d1, 0], ref[k, d0, 1], ref[k, d1, 1]], 0) for k in range(2)
    ]


def store_pair(ref, rest, bit, y):
    d0, d1 = pair_of(rest, bit)
    n = y.shape[0] // 4
    for k, v in enumerate(split(y)):
        ref[k, d0, 0], ref[k, d1, 0] = v[:n], v[n : 2 * n]
        ref[k, d0, 1], ref[k, d1, 1] = v[2 * n : 3 * n], v[3 * n :]


def apply_at(gate, source, target, bit, rest):
    store_pair(target, rest, bit, dot3(gate, load_pair(source, rest, bit), NN))


def folded(total):
    n = total.shape[0] // 2
    return jnp.concatenate([total[:n, :n] + total[n:, n:], total[n:, :n] - total[:n, n:]], 1)


def environment(phi, psi, bit, rests):
    terms = [dot3(load_pair(phi, rest, bit), load_pair(psi, rest, bit), NT) for rest in rests]
    return sum(terms[1:], terms[0])


def gate_matrix(gates_ref, section):
    return split(as_matrix(jnp.concatenate([gates_ref[section, 0], gates_ref[section, 1]], 1)))


def place(block, target, d):
    target[0, d], target[1, d] = split(block)


def joined(ref, d):
    return ref[0, d].astype(F32) + ref[1, d].astype(F32)


def unpacked(core, own, other, out_ref):
    for plane in range(2):
        low = jnp.where(core == 0, own[plane], other[plane])
        high = jnp.where(core == 0, other[plane], own[plane])
        out_ref[plane] = jnp.concatenate([low, high], 0).T


def pack_kernel(layout, x_ref, y_ref, x_own_ref, x_sent_ref, y_own_ref, y_sent_ref):
    core, _ = layout.place_of(lax.axis_index("long"))
    n = x_ref.shape[2] // 2
    for ref, own_ref, sent_ref in ((x_ref, x_own_ref, x_sent_ref), (y_ref, y_own_ref, y_sent_ref)):
        for plane in range(2):
            t = ref[plane].T
            low, high = t[:n], t[n:]
            own_ref[plane] = jnp.where(core == 0, low, high)
            sent_ref[plane] = jnp.where(core == 0, high, low)


def rests_of(layout, chip, bit):
    low = chip & (1 << bit - 1) - 1
    base = (chip >> bit << bit - 1) + low
    return [base * 2 + slot for slot in range(2)]


def near_kernel(layout, gates_ref, *refs):
    *blocks, phi_ref, psi_ref, total_ref, raw = refs
    core, chips = layout.place_of(lax.axis_index("long"))
    bit = layout.local_bits[0]
    half = len(blocks) // 2
    for source, target in ((blocks[:half], raw), (blocks[half:], psi_ref)):
        for block, chip in zip(source, chips):
            for slot in range(2):
                place(block[slot], target, chip * 2 + (slot ^ core))
    gate = gate_matrix(gates_ref, 0)
    far = chips[-1]
    others = [far ^ k for k in range(1, layout.chips) if not k >> bit - 1 & 1]
    rests = [r for chip in others for r in rests_of(layout, chip, bit)]
    for rest in rests:
        apply_at(gate, raw, phi_ref, bit, rest)
    total_ref[...] = environment(phi_ref, psi_ref, bit, rests)
    mate = (far ^ 1 << bit - 1) * 2
    for slot in range(2):
        for k in range(2):
            phi_ref[k, mate + slot] = raw[k, mate + slot]


def far_kernel(layout, gates_ref, *refs):
    *blocks, total_ref, phi_in, psi_in, phi_ref, psi_ref, e_ref = refs
    core, chips = layout.place_of(lax.axis_index("long"))
    bit = layout.local_bits[0]
    far = chips[-1]
    for source, target in ((blocks[:2], phi_ref), (blocks[2:], psi_ref)):
        for slot in range(2):
            place(source[slot][0], target, far * 2 + (slot ^ core))
    gate = gate_matrix(gates_ref, 0)
    rests = rests_of(layout, far, bit)
    for rest in rests:
        apply_at(gate, phi_ref, phi_ref, bit, rest)
    e_ref[...] = folded(total_ref[...] + environment(phi_ref, psi_ref, bit, rests))


def section_kernel(layout, section, gates_ref, e0_ref, e1_ref, phi_ref, psi_ref, phi_next, psi_next, e_ref, *ends):
    adjoint_gate = gate_matrix(gates_ref, section + 1)
    bit, next_bit = layout.local_bits[section], layout.local_bits[section + 1]
    rests = range(psi_ref.shape[1] // 2)

    def beside(k):
        for rest in rests[k * len(rests) // NS_ITERS : (k + 1) * len(rests) // NS_ITERS]:
            apply_at(adjoint_gate, phi_ref, phi_next, next_bit, rest)

    gate = split(as_matrix(polar(e0_ref[...] + e1_ref[...], beside)))
    for rest in rests:
        apply_at(gate, psi_ref, psi_next, bit, rest)
    e_ref[...] = folded(environment(phi_next, psi_next, next_bit, rests))
    if ends:
        core, chips = layout.place_of(lax.axis_index("long"))
        phi_own, phi_sent, psi_own, psi_sent = ends
        for slot, phi_out, psi_out in ((0, phi_own, psi_own), (1, phi_sent, psi_sent)):
            d = chips[0] * 2 + (slot ^ core)
            phi_out[...] = joined(phi_next, d)
            for t, d_t in enumerate(last_pair(layout, d)):
                psi_out[t] = joined(psi_next, d_t)


def last_pair(layout, d):
    bit = layout.local_bits[SECTIONS - 1]
    first = d & ~(1 << bit)
    return first, first + (1 << bit)


def last_polar_kernel(layout, e0_ref, e1_ref, phi_own, phi_got, gate_ref, adjoint_ref):
    core, _ = layout.place_of(lax.axis_index("long"))
    gate_ref[...] = as_matrix(polar(e0_ref[...] + e1_ref[...]))
    unpacked(core, phi_own, phi_got, adjoint_ref)


def last_apply_kernel(layout, gate_ref, psi_own, psi_got, state_ref):
    core, chips = layout.place_of(lax.axis_index("long"))
    t = chips[0] * 2 + core >> layout.local_bits[SECTIONS - 1] & 1
    n = psi_own.shape[2]
    rows = [gate_ref[pl.ds(pl.multiple_of((plane * 2 + t) * n, n), n)] for plane in range(2)]
    gate = split(jnp.concatenate(rows, 0))
    halves = []
    for psi in (psi_own, psi_got):
        x = jnp.concatenate([psi[0, 0], psi[1, 0], psi[0, 1], psi[1, 1]], 0)
        y = dot3(gate, split(x), NN)
        halves.append([y[:n], y[n:]])
    unpacked(core, halves[0], halves[1], state_ref)


def call(kernel, name, outs, ins, flops, scratch=(), aliases=None):
    sizes = [int(np.prod(a.shape)) * a.dtype.itemsize for a in list(ins) + list(outs)]
    spec = pl.BlockSpec(memory_space=pltpu.VMEM)
    return pl.pallas_call(
        kernel,
        out_shape=outs,
        in_specs=[spec] * len(ins),
        out_specs=[spec] * len(outs),
        scratch_shapes=list(scratch),
        input_output_aliases=aliases or {},
        compiler_params=pltpu.CompilerParams(vmem_limit_bytes=VMEM_LIMIT),
        cost_estimate=pl.CostEstimate(flops=flops, bytes_accessed=sum(sizes), transcendentals=0),
        name=name,
    )(*ins)


def shards(initial_state, adjoint_state, current_gates):
    layout = Layout(lax.axis_size("long"))
    core_flip = layout.flip(layout.gate_bits[0])
    rows, lanes = initial_state.shape[1:]
    c = lanes // 2
    devices = layout.chips * 2
    whole = jax.ShapeDtypeStruct(initial_state.shape, F32)
    slab = jax.ShapeDtypeStruct((2, c, rows), F32)
    two_slabs = jax.ShapeDtypeStruct((2, 2, c, rows), F32)
    pieces = jax.ShapeDtypeStruct((2, devices, 2, c, rows), BF16)
    env = jax.ShapeDtypeStruct((lanes, 2 * lanes), F32)
    square = jax.ShapeDtypeStruct((2 * lanes, 2 * lanes), F32)
    apply_flops = 3 * 2 * (2 * lanes) ** 2 * (devices // 2) * rows

    def kernel(body, *args):
        return functools.partial(body, layout, *args)

    def both(e):
        for bit in layout.other_bits:
            e = e + lax.ppermute(e, "long", layout.flip(bit))
        return e, lax.ppermute(e, "long", core_flip)

    phi_own, phi_sent, psi_own, psi_sent = call(
        kernel(pack_kernel), "pack", [slab] * 4, [adjoint_state, initial_state], 0
    )
    *phi_near, phi_a, phi_b = gather_ring(jnp.stack([phi_own, lax.ppermute(phi_sent, "long", core_flip)]), layout)
    *psi_near, psi_a, psi_b = gather_ring(jnp.stack([psi_own, lax.ppermute(psi_sent, "long", core_flip)]), layout)
    phi, psi, total = call(
        kernel(near_kernel),
        "near",
        [pieces, pieces, square],
        [current_gates] + phi_near + psi_near,
        2 * apply_flops,
        [pltpu.VMEM(pieces.shape, BF16)],
    )
    phi, psi, e = call(
        kernel(far_kernel),
        "far",
        [pieces, pieces, env],
        [current_gates, phi_a, phi_b, psi_a, psi_b, total, phi, psi],
        apply_flops // 2,
        aliases={6: 0, 7: 1},
    )
    for section in range(SECTIONS - 1):
        e0, e1 = both(e)
        ends = [slab, slab, two_slabs, two_slabs] if section == SECTIONS - 2 else []
        phi, psi, e, *ends = call(
            kernel(section_kernel, section),
            "section",
            [pieces, pieces, env] + ends,
            [current_gates, e0, e1, phi, psi],
            4 * apply_flops,
        )
    phi_own, phi_sent, psi_own, psi_sent = ends
    e0, e1 = both(e)
    phi_got = lax.ppermute(phi_sent, "long", core_flip)
    psi_got = lax.ppermute(psi_sent, "long", core_flip)
    gate, final_adjoint = call(
        kernel(last_polar_kernel), "last_polar", [square, whole], [e0, e1, phi_own, phi_got], 2 * apply_flops
    )
    (final_state,) = call(
        kernel(last_apply_kernel), "last_apply", [whole], [gate, psi_own, psi_got], apply_flops // 4
    )
    return final_state, final_adjoint


def solution(mesh):
    return jax.shard_map(
        shards,
        mesh=mesh,
        in_specs=(
            P(None, ("groups", "long"), None),
            P(None, ("groups", "long"), None),
            P("groups", None, None, None),
        ),
        out_specs=(P(None, ("groups", "long"), None), P(None, ("groups", "long"), None)),
        check_vma=False,
    )
```

time: 101 us -> 84 us (0.83)
  Pallas kernels: 48.1 us -> 31.8 us
    pallas_call x10 -> x8, Pallas kernels: 48.1 us -> 31.8 us  [call(): pl.pallas_call(kernel, out_shape=outs, in_specs=[spec] * len(ins), out_sp...]
    ppermute x4, waiting for transfers between devices: 0.01 us -> 1.6 us  [the longest x1 0.91 us: shards(): lax.ppermute(psi_sent, 'long', core_flip)]
  transfers between devices with their start and end apart: 24 -> 24, of which waited for: 12 -> 13; matrix products, arithmetic and copies ran while one was open for 0% -> 0% of each run, Pallas kernels for 20% -> 10%
where the time goes in v2:
time: 84 us; the launch traced here: 83.9 us
  Pallas kernels  31.8 us (38%)
  waiting for transfers between devices  29.7 us (35%)
  starting transfers between devices  19.6 us (23%)
  local copies, waits for them, and re-layouts  1.93 us (2%)
    pallas_call x8, Pallas kernels, call(): pl.pallas_call(kernel, out_shape=outs, in_specs=[spec] * len(ins), out_sp...  31.8 us
    ppermute x6, waiting for transfers between devices, gather_ring(): from_above = lax.ppermute(from_above, 'long', down)  22.3 us
    ppermute x6, starting transfers between devices, gather_ring(): from_above = lax.ppermute(from_above, 'long', down)  12.9 us
    ppermute x2, starting transfers between devices, gather_ring(): lax.ppermute(from_above[1:], 'long', down)  4.11 us
    ppermute x4, waiting for transfers between devices, both(): return (e, lax.ppermute(e, 'long', core_flip))  3.92 us
    unnamed x6, local copies, waits for them, and re-layouts  1.9 us
    ppermute x2, waiting for transfers between devices, gather_ring(): lax.ppermute(from_below[:1], 'long', up)  1.73 us
  transfers between devices with their start and end apart: 24, of which 13 were waited for; matrix products, arithmetic and copies ran while one was open for 0% of the time, Pallas kernels for 10%

profile of v2, /device:TPU:0, one launch (start us, length us, event | category | flops | bytes accessed | tf_op | source)
XLA Modules:
  0.0 83.9 jit_solution(16805802473329929310)
XLA Ops:
  0.6 0.0 copy-start.1
  0.6 0.9 %copy-done.1 = f32[2,256,128]{2,1,0:T(8,128)S(1)} copy-done((f32[2,256,128]{2,1,0:T(8,128)S(1)}, f32[2,256,128]{2,1,0:T(8,128)}, u32[]{:S(2)}) %copy-start.1) | copy-done | bytes 262168
  1.6 0.0 copy-start.2
  1.6 0.9 %copy-done.2 = f32[2,256,128]{2,1,0:T(8,128)S(1)} copy-done((f32[2,256,128]{2,1,0:T(8,128)S(1)}, f32[2,256,128]{2,1,0:T(8,128)}, u32[]{:S(2)}) %copy-start.2) | copy-done | bytes 262168
  2.5 0.0 copy-start
  2.5 0.2 pack.1
  2.7 0.5 collective-permute-start.9
  3.3 0.1 collective-permute-start
  3.3 0.9 %collective-permute-done.9 = f32[2,64,256]{2,1,0:T(8,128)S(1)} collective-permute-done((f32[2,64,256]{2,1,0:T(8,128)S(1)}, f32[2,64,256]{2,1,0:T(8,128)S(1)}, u32[]{:S(2)}, u32[]{:S(2)}) %collective-permute-start.9) | collective-permute-done | bytes 131104 | tf_op jit(solution)/shard_map/ppermute | solution.py:317
  4.3 2.9 %collective-permute-start.14 = (f32[2,2,64,256]{3,2,1,0:T(8,128)S(1)}, f32[2,2,64,256]{3,2,1,0:T(8,128)S(1)}, u32[]{:S(2)}, u32[]{:S(2)}) collective-permute-start(f32[2,2,64,256]{3,2,1,0:T(8,128)S(1)} %pad_maximum_fusion.1.refs_7_), channel_id=1, source_target_pairs={{0,2},{1,3},{2,6},{3,7},{4,0},{5,1},{6,10},{7,11},{8,4},{9,5},{10,... | collective-permute-start | bytes 786440 | tf_op jit(solution)/shard_map/ppermute | solution.py:77
  7.2 0.1 collective-permute-start.10
  7.3 0.0 collective-permute-done
  7.3 2.0 %collective-permute-start.5 = (f32[2,2,64,256]{3,2,1,0:T(8,128)S(1)}, f32[2,2,64,256]{3,2,1,0:T(8,128)S(1)}, u32[]{:S(2)}, u32[]{:S(2)}) collective-permute-start(f32[2,2,64,256]{3,2,1,0:T(8,128)S(1)} %pad_maximum_fusion.refs_0_), channel_id=1, source_target_pairs={{0,2},{1,3},{2,6},{3,7},{4,0},{5,1},{6,10},{7,11},{8,4},{9,5},{10,... | collective-permute-start | bytes 786440 | tf_op jit(solution)/shard_map/ppermute | solution.py:77
  9.3 0.1 collective-permute-start.1
  9.4 4.9 %collective-permute-done.14.refs_9_ = f32[2,2,64,256]{3,2,1,0:T(8,128)S(1)} collective-permute-done((f32[2,2,64,256]{3,2,1,0:T(8,128)S(1)}, f32[2,2,64,256]{3,2,1,0:T(8,128)S(1)}, u32[]{:S(2)}, u32[]{:S(2)}) %collective-permute-start.14) | collective-permute-done | bytes 262176 | tf_op jit(solution)/shard_map/ppermute | solution.py:77
  14.3 2.0 %collective-permute-start.15 = (f32[2,2,64,256]{3,2,1,0:T(8,128)S(1)}, f32[2,2,64,256]{3,2,1,0:T(8,128)S(1)}, u32[]{:S(2)}, u32[]{:S(2)}) collective-permute-start(f32[2,2,64,256]{3,2,1,0:T(8,128)S(1)} %collective-permute-done.14.refs_9_), channel_id=1, source_target_pairs={{0,2},{1,3},{2,6},{3,7},{4,0},{5,1},{6,10},{7,11},{8,4},{9,5},{10,... | collective-permute-start | bytes 786440 | tf_op jit(solution)/shard_map/ppermute | solution.py:77
  16.3 0.0 collective-permute-done.10.refs_8_
  16.4 0.1 collective-permute-start.11
  16.5 3.5 %collective-permute-done.5.refs_2_ = f32[2,2,64,256]{3,2,1,0:T(8,128)S(1)} collective-permute-done((f32[2,2,64,256]{3,2,1,0:T(8,128)S(1)}, f32[2,2,64,256]{3,2,1,0:T(8,128)S(1)}, u32[]{:S(2)}, u32[]{:S(2)}) %collective-permute-start.5) | collective-permute-done | bytes 262176 | tf_op jit(solution)/shard_map/ppermute | solution.py:77
  20.0 2.0 %collective-permute-start.6 = (f32[2,2,64,256]{3,2,1,0:T(8,128)S(1)}, f32[2,2,64,256]{3,2,1,0:T(8,128)S(1)}, u32[]{:S(2)}, u32[]{:S(2)}) collective-permute-start(f32[2,2,64,256]{3,2,1,0:T(8,128)S(1)} %collective-permute-done.5.refs_2_), channel_id=1, source_target_pairs={{0,2},{1,3},{2,6},{3,7},{4,0},{5,1},{6,10},{7,11},{8,4},{9,5},{10,... | collective-permute-start | bytes 786440 | tf_op jit(solution)/shard_map/ppermute | solution.py:77
  22.0 0.0 collective-permute-done.1.refs_1_
  22.0 0.1 collective-permute-start.2
  22.1 3.5 %collective-permute-done.15.refs_11_ = f32[2,2,64,256]{3,2,1,0:T(8,128)S(1)} collective-permute-done((f32[2,2,64,256]{3,2,1,0:T(8,128)S(1)}, f32[2,2,64,256]{3,2,1,0:T(8,128)S(1)}, u32[]{:S(2)}, u32[]{:S(2)}) %collective-permute-start.15) | collective-permute-done | bytes 262176 | tf_op jit(solution)/shard_map/ppermute | solution.py:77
  25.6 2.0 %collective-permute-start.16 = (f32[2,2,64,256]{3,2,1,0:T(8,128)S(1)}, f32[2,2,64,256]{3,2,1,0:T(8,128)S(1)}, u32[]{:S(2)}, u32[]{:S(2)}) collective-permute-start(f32[2,2,64,256]{3,2,1,0:T(8,128)S(1)} %collective-permute-done.15.refs_11_), channel_id=1, source_target_pairs={{0,2},{1,3},{2,6},{3,7},{4,0},{5,1},{6,10},{7,11},{8,4},{9,5},{10,... | collective-permute-start | bytes 786440 | tf_op jit(solution)/shard_map/ppermute | solution.py:77
  27.6 0.0 collective-permute-done.11.refs_10_
  27.6 0.1 collective-permute-start.12
  27.7 3.5 %collective-permute-done.6.refs_4_ = f32[2,2,64,256]{3,2,1,0:T(8,128)S(1)} collective-permute-done((f32[2,2,64,256]{3,2,1,0:T(8,128)S(1)}, f32[2,2,64,256]{3,2,1,0:T(8,128)S(1)}, u32[]{:S(2)}, u32[]{:S(2)}) %collective-permute-start.6) | collective-permute-done | bytes 262176 | tf_op jit(solution)/shard_map/ppermute | solution.py:77
  31.2 2.0 %collective-permute-start.7 = (f32[2,2,64,256]{3,2,1,0:T(8,128)S(1)}, f32[2,2,64,256]{3,2,1,0:T(8,128)S(1)}, u32[]{:S(2)}, u32[]{:S(2)}) collective-permute-start(f32[2,2,64,256]{3,2,1,0:T(8,128)S(1)} %collective-permute-done.6.refs_4_), channel_id=1, source_target_pairs={{0,2},{1,3},{2,6},{3,7},{4,0},{5,1},{6,10},{7,11},{8,4},{9,5},{10,... | collective-permute-start | bytes 786440 | tf_op jit(solution)/shard_map/ppermute | solution.py:77
  33.2 0.0 collective-permute-done.2.refs_3_
  33.2 0.1 collective-permute-start.3
  33.3 3.5 %collective-permute-done.16.refs_13_ = f32[2,2,64,256]{3,2,1,0:T(8,128)S(1)} collective-permute-done((f32[2,2,64,256]{3,2,1,0:T(8,128)S(1)}, f32[2,2,64,256]{3,2,1,0:T(8,128)S(1)}, u32[]{:S(2)}, u32[]{:S(2)}) %collective-permute-start.16) | collective-permute-done | bytes 262176 | tf_op jit(solution)/shard_map/ppermute | solution.py:77
  36.8 2.1 %collective-permute-start.17 = (f32[1,2,64,256]{3,2,1,0:T(8,128)S(1)}, f32[1,2,64,256]{3,2,1,0:T(8,128)S(1)}, u32[]{:S(2)}, u32[]{:S(2)}) collective-permute-start(f32[1,2,64,256]{3,2,1,0:T(8,128)S(1)} %slice.19), channel_id=1, source_target_pairs={{0,2},{1,3},{2,6},{3,7},{4,0},{5,1},{6,10},{7,11},{8,4},{9,5},{10,... | collective-permute-start | bytes 393224 | tf_op jit(solution)/shard_map/ppermute | solution.py:79
  38.9 0.0 collective-permute-done.12.refs_12_
  38.9 0.1 collective-permute-start.13
  39.0 3.4 %collective-permute-done.7.refs_6_ = f32[2,2,64,256]{3,2,1,0:T(8,128)S(1)} collective-permute-done((f32[2,2,64,256]{3,2,1,0:T(8,128)S(1)}, f32[2,2,64,256]{3,2,1,0:T(8,128)S(1)}, u32[]{:S(2)}, u32[]{:S(2)}) %collective-permute-start.7) | collective-permute-done | bytes 262176 | tf_op jit(solution)/shard_map/ppermute | solution.py:77
  42.4 2.1 %collective-permute-start.8 = (f32[1,2,64,256]{3,2,1,0:T(8,128)S(1)}, f32[1,2,64,256]{3,2,1,0:T(8,128)S(1)}, u32[]{:S(2)}, u32[]{:S(2)}) collective-permute-start(f32[1,2,64,256]{3,2,1,0:T(8,128)S(1)} %slice.17), channel_id=1, source_target_pairs={{0,2},{1,3},{2,6},{3,7},{4,0},{5,1},{6,10},{7,11},{8,4},{9,5},{10,... | collective-permute-start | bytes 393224 | tf_op jit(solution)/shard_map/ppermute | solution.py:79
  44.5 0.0 collective-permute-done.3.refs_5_
  44.5 0.1 collective-permute-start.4
  44.6 0.0 copy-done
  44.7 3.1 %near.1 = (bf16[2,16,2,64,256]{4,3,2,1,0:T(8,128)(2,1)S(1)}, bf16[2,16,2,64,256]{4,3,2,1,0:T(8,128)(2,1)S(1)}, f32[256,256]{1,0:T(8,128)S(1)}) custom-call(f32[4,2,128,128]{3,2,1,0:T(8,128)S(1)} %copy-done, f32[2,2,64,256]{3,2,1,0:T(8,128)S(1)} %pad_maximum_fusion.refs_0_, f32[2,2,64,256]{3,2,1,0:T(8,128)S(1)} %collective-permute-done.1.refs_1_, ...), custom_call_target="tpu_custom_call" | custom-call | flops 1610612736 | bytes 8650752 | tf_op jit(solution)/shard_map/near/pallas_call | solution.py:278
  47.8 0.0 collective-permute-done.17.refs_3_
  47.8 0.0 collective-permute-done.13.refs_2_
  47.8 0.0 collective-permute-done.8.refs_1_
  47.8 1.7 %collective-permute-done.4.refs_0_ = f32[1,2,64,256]{3,2,1,0:T(8,128)S(1)} collective-permute-done((f32[1,2,64,256]{3,2,1,0:T(8,128)S(1)}, f32[1,2,64,256]{3,2,1,0:T(8,128)S(1)}, u32[]{:S(2)}, u32[]{:S(2)}) %collective-permute-start.4) | collective-permute-done | bytes 131104 | tf_op jit(solution)/shard_map/ppermute | solution.py:79
  49.5 1.2 %far.1 = (bf16[2,16,2,64,256]{4,3,2,1,0:T(8,128)(2,1)S(1)}, bf16[2,16,2,64,256]{4,3,2,1,0:T(8,128)(2,1)S(1)}, f32[128,256]{1,0:T(8,128)S(1)}) custom-call(f32[4,2,128,128]{3,2,1,0:T(8,128)S(1)} %copy-done, f32[1,2,64,256]{3,2,1,0:T(8,128)S(1)} %collective-permute-done.4.refs_0_, ...), custom_call_target="tpu_custom_call", output_to_operand_aliasing={{0}: (6, {}), {1}: (7, {})} | custom-call | flops 402653184 | bytes 9830400 | tf_op jit(solution)/shard_map/far/pallas_call | solution.py:278
  50.7 0.1 collective-permute-start.18
  50.8 1.3 %collective-permute-done.18.e1_ref = f32[128,256]{1,0:T(8,128)S(1)} collective-permute-done((f32[128,256]{1,0:T(8,128)S(1)}, f32[128,256]{1,0:T(8,128)S(1)}, u32[]{:S(2)}, u32[]{:S(2)}) %collective-permute-start.18) | collective-permute-done | bytes 131104 | tf_op jit(solution)/shard_map/ppermute | solution.py:311
  52.1 6.9 %section.3 = (bf16[2,16,2,64,256]{4,3,2,1,0:T(8,128)(2,1)S(1)}, bf16[2,16,2,64,256]{4,3,2,1,0:T(8,128)(2,1)S(1)}, f32[128,256]{1,0:T(8,128)S(1)}) custom-call(f32[4,2,128,128]{3,2,1,0:T(8,128)S(1)} %copy-done, f32[128,256]{1,0:T(8,128)S(1)} %get-tuple-element.32.e0_ref, f32[128,256]{1,0:T(8,128)S(1)} %collective-permute-done.18.e1_ref, ...), custom_call_target="tpu_custom_call" | custom-call | flops 3221225472 | bytes 9306112 | tf_op jit(solution)/shard_map/section/pallas_call | solution.py:278
  59.0 0.2 collective-permute-start.19
  59.2 1.2 %collective-permute-done.19.e1_ref = f32[128,256]{1,0:T(8,128)S(1)} collective-permute-done((f32[128,256]{1,0:T(8,128)S(1)}, f32[128,256]{1,0:T(8,128)S(1)}, u32[]{:S(2)}, u32[]{:S(2)}) %collective-permute-start.19) | collective-permute-done | bytes 131104 | tf_op jit(solution)/shard_map/ppermute | solution.py:311
  60.4 6.9 %section.4 = (bf16[2,16,2,64,256]{4,3,2,1,0:T(8,128)(2,1)S(1)}, bf16[2,16,2,64,256]{4,3,2,1,0:T(8,128)(2,1)S(1)}, f32[128,256]{1,0:T(8,128)S(1)}) custom-call(f32[4,2,128,128]{3,2,1,0:T(8,128)S(1)} %copy-done, f32[128,256]{1,0:T(8,128)S(1)} %get-tuple-element.35.e0_ref, f32[128,256]{1,0:T(8,128)S(1)} %collective-permute-done.19.e1_ref, ...), custom_call_target="tpu_custom_call" | custom-call | flops 3221225472 | bytes 9306112 | tf_op jit(solution)/shard_map/section/pallas_call | solution.py:278
  67.3 0.2 collective-permute-start.20
  67.5 1.2 %collective-permute-done.20.e1_ref = f32[128,256]{1,0:T(8,128)S(1)} collective-permute-done((f32[128,256]{1,0:T(8,128)S(1)}, f32[128,256]{1,0:T(8,128)S(1)}, u32[]{:S(2)}, u32[]{:S(2)}) %collective-permute-start.20) | collective-permute-done | bytes 131104 | tf_op jit(solution)/shard_map/ppermute | solution.py:311
  68.7 7.4 %section.5 = (bf16[2,16,2,64,256]{4,3,2,1,0:T(8,128)(2,1)}, bf16[2,16,2,64,256]{4,3,2,1,0:T(8,128)(2,1)}, f32[128,256]{1,0:T(8,128)S(1)}, f32[2,64,256]{2,1,0:T(...) custom-call(f32[4,2,128,128]{3,2,1,0:T(8,128)S(1)} %copy-done, ...), custom_call_target="tpu_custom_call" | custom-call | flops 3221225472 | bytes 10092544 | tf_op jit(solution)/shard_map/section/pallas_call | solution.py:278
  76.2 0.1 collective-permute-start.22
  76.3 0.4 collective-permute-start.21
  76.7 0.1 collective-permute-start.23
  76.8 0.7 collective-permute-done.22.phi_got
  77.5 0.2 collective-permute-done.21.e1_ref
  77.7 5.0 %last_polar.1 = (f32[256,256]{1,0:T(8,128)S(1)}, f32[2,256,128]{2,1,0:T(8,128)}) custom-call(f32[128,256]{1,0:T(8,128)S(1)} %get-tuple-element.41.e0_ref, f32[128,256]{1,0:T(8,128)S(1)} %collective-permute-done.21.e1_ref, f32[2,64,256]{2,1,0:T(8,128)S(1)} %get-tuple-element.42.phi_own, f32[2,64,256]{2,1,0:T(8,128)S(1)} %collective-permute-done.22.phi_got), custom_call_target="tpu_custom_call" | custom-call | flops 1610612736 | bytes 1048576 | tf_op jit(solution)/shard_map/last_polar/pallas_call | solution.py:278
  82.7 0.0 collective-permute-done.23.psi_got
  82.7 1.1 %last_apply.1 = f32[2,256,128]{2,1,0:T(8,128)} custom-call(f32[256,256]{1,0:T(8,128)S(1)} %get-tuple-element.44.gate_ref, f32[2,2,64,256]{3,2,1,0:T(8,128)S(1)} %get-tuple-element.45.psi_own, f32[2,2,64,256]{3,2,1,0:T(8,128)S(1)} %collective-permute-done.23.psi_got), custom_call_target="tpu_custom_call" | custom-call | flops 201326592 | bytes 1048576 | tf_op jit(solution)/shard_map/last_apply/pallas_call | solution.py:278
  (6 shorter events, 0.1 us)
Async XLA Ops:
  0.6 1.0 %copy-start.1 = (f32[2,256,128]{2,1,0:T(8,128)S(1)}, f32[2,256,128]{2,1,0:T(8,128)}, u32[]{:S(2)}) copy-start(f32[2,256,128]{2,1,0:T(8,128)} %x_ref.1) | copy-start | bytes 786436
  1.6 0.9 %copy-start.2 = (f32[2,256,128]{2,1,0:T(8,128)S(1)}, f32[2,256,128]{2,1,0:T(8,128)}, u32[]{:S(2)}) copy-start(f32[2,256,128]{2,1,0:T(8,128)} %y_ref.1) | copy-start | bytes 786436
  2.5 42.1 %copy-start = (f32[4,2,128,128]{3,2,1,0:T(8,128)S(1)}, f32[4,2,128,128]{3,2,1,0:T(8,128)}, u32[]{:S(2)}) copy-start(f32[4,2,128,128]{3,2,1,0:T(8,128)} %gates_ref.9) | copy-start | bytes 1572868
  2.7 1.5 %collective-permute-start.9 = (f32[2,64,256]{2,1,0:T(8,128)S(1)}, f32[2,64,256]{2,1,0:T(8,128)S(1)}, u32[]{:S(2)}, u32[]{:S(2)}) collective-permute-start(f32[2,64,256]{2,1,0:T(8,128)S(1)} %get-tuple-element.28), channel_id=1, source_target_pairs={{0,1},{1,0},{2,3},{3,2},{4,5},{5,4},{6,7},{7,6},{8,9},{9,8},{10,11... | collective-permute-start | bytes 393224 | tf_op jit(solution)/shard_map/ppermute | solution.py:317
  3.3 4.1 %collective-permute-start = (f32[2,64,256]{2,1,0:T(8,128)S(1)}, f32[2,64,256]{2,1,0:T(8,128)S(1)}, u32[]{:S(2)}, u32[]{:S(2)}) collective-permute-start(f32[2,64,256]{2,1,0:T(8,128)S(1)} %get-tuple-element.26), channel_id=1, source_target_pairs={{0,1},{1,0},{2,3},{3,2},{4,5},{5,4},{6,7},{7,6},{8,9},{9,8},{10,11... | collective-permute-start | bytes 393224 | tf_op jit(solution)/shard_map/ppermute | solution.py:316
  4.3 10.1 %collective-permute-start.14 = (f32[2,2,64,256]{3,2,1,0:T(8,128)S(1)}, f32[2,2,64,256]{3,2,1,0:T(8,128)S(1)}, u32[]{:S(2)}, u32[]{:S(2)}) collective-permute-start(f32[2,2,64,256]{3,2,1,0:T(8,128)S(1)} %pad_maximum_fusion.1.refs_7_), channel_id=1, source_target_pairs={{0,2},{1,3},{2,6},{3,7},{4,0},{5,1},{6,10},{7,11},{8,4},{9,5},{10,... | collective-permute-start | bytes 786440 | tf_op jit(solution)/shard_map/ppermute | solution.py:77
  7.2 9.2 %collective-permute-start.10 = (f32[2,2,64,256]{3,2,1,0:T(8,128)S(1)}, f32[2,2,64,256]{3,2,1,0:T(8,128)S(1)}, u32[]{:S(2)}, u32[]{:S(2)}) collective-permute-start(f32[2,2,64,256]{3,2,1,0:T(8,128)S(1)} %pad_maximum_fusion.1.refs_7_), channel_id=1, source_target_pairs={{0,4},{1,5},{2,0},{3,1},{4,8},{5,9},{6,2},{7,3},{8,12},{9,13},{10,... | collective-permute-start | bytes 786440 | tf_op jit(solution)/shard_map/ppermute | solution.py:76
  7.3 12.6 %collective-permute-start.5 = (f32[2,2,64,256]{3,2,1,0:T(8,128)S(1)}, f32[2,2,64,256]{3,2,1,0:T(8,128)S(1)}, u32[]{:S(2)}, u32[]{:S(2)}) collective-permute-start(f32[2,2,64,256]{3,2,1,0:T(8,128)S(1)} %pad_maximum_fusion.refs_0_), channel_id=1, source_target_pairs={{0,2},{1,3},{2,6},{3,7},{4,0},{5,1},{6,10},{7,11},{8,4},{9,5},{10,... | collective-permute-start | bytes 786440 | tf_op jit(solution)/shard_map/ppermute | solution.py:77
  9.3 12.7 %collective-permute-start.1 = (f32[2,2,64,256]{3,2,1,0:T(8,128)S(1)}, f32[2,2,64,256]{3,2,1,0:T(8,128)S(1)}, u32[]{:S(2)}, u32[]{:S(2)}) collective-permute-start(f32[2,2,64,256]{3,2,1,0:T(8,128)S(1)} %pad_maximum_fusion.refs_0_), channel_id=1, source_target_pairs={{0,4},{1,5},{2,0},{3,1},{4,8},{5,9},{6,2},{7,3},{8,12},{9,13},{10,... | collective-permute-start | bytes 786440 | tf_op jit(solution)/shard_map/ppermute | solution.py:76
  14.3 11.2 %collective-permute-start.15 = (f32[2,2,64,256]{3,2,1,0:T(8,128)S(1)}, f32[2,2,64,256]{3,2,1,0:T(8,128)S(1)}, u32[]{:S(2)}, u32[]{:S(2)}) collective-permute-start(f32[2,2,64,256]{3,2,1,0:T(8,128)S(1)} %collective-permute-done.14.refs_9_), channel_id=1, source_target_pairs={{0,2},{1,3},{2,6},{3,7},{4,0},{5,1},{6,10},{7,11},{8,4},{9,5},{10,... | collective-permute-start | bytes 786440 | tf_op jit(solution)/shard_map/ppermute | solution.py:77
  16.4 11.2 %collective-permute-start.11 = (f32[2,2,64,256]{3,2,1,0:T(8,128)S(1)}, f32[2,2,64,256]{3,2,1,0:T(8,128)S(1)}, u32[]{:S(2)}, u32[]{:S(2)}) collective-permute-start(f32[2,2,64,256]{3,2,1,0:T(8,128)S(1)} %collective-permute-done.10.refs_8_), channel_id=1, source_target_pairs={{0,4},{1,5},{2,0},{3,1},{4,8},{5,9},{6,2},{7,3},{8,12},{9,13},{10,... | collective-permute-start | bytes 786440 | tf_op jit(solution)/shard_map/ppermute | solution.py:76
  20.0 11.2 %collective-permute-start.6 = (f32[2,2,64,256]{3,2,1,0:T(8,128)S(1)}, f32[2,2,64,256]{3,2,1,0:T(8,128)S(1)}, u32[]{:S(2)}, u32[]{:S(2)}) collective-permute-start(f32[2,2,64,256]{3,2,1,0:T(8,128)S(1)} %collective-permute-done.5.refs_2_), channel_id=1, source_target_pairs={{0,2},{1,3},{2,6},{3,7},{4,0},{5,1},{6,10},{7,11},{8,4},{9,5},{10,... | collective-permute-start | bytes 786440 | tf_op jit(solution)/shard_map/ppermute | solution.py:77
  22.0 11.2 %collective-permute-start.2 = (f32[2,2,64,256]{3,2,1,0:T(8,128)S(1)}, f32[2,2,64,256]{3,2,1,0:T(8,128)S(1)}, u32[]{:S(2)}, u32[]{:S(2)}) collective-permute-start(f32[2,2,64,256]{3,2,1,0:T(8,128)S(1)} %collective-permute-done.1.refs_1_), channel_id=1, source_target_pairs={{0,4},{1,5},{2,0},{3,1},{4,8},{5,9},{6,2},{7,3},{8,12},{9,13},{10,... | collective-permute-start | bytes 786440 | tf_op jit(solution)/shard_map/ppermute | solution.py:76
  25.6 11.2 %collective-permute-start.16 = (f32[2,2,64,256]{3,2,1,0:T(8,128)S(1)}, f32[2,2,64,256]{3,2,1,0:T(8,128)S(1)}, u32[]{:S(2)}, u32[]{:S(2)}) collective-permute-start(f32[2,2,64,256]{3,2,1,0:T(8,128)S(1)} %collective-permute-done.15.refs_11_), channel_id=1, source_target_pairs={{0,2},{1,3},{2,6},{3,7},{4,0},{5,1},{6,10},{7,11},{8,4},{9,5},{10,... | collective-permute-start | bytes 786440 | tf_op jit(solution)/shard_map/ppermute | solution.py:77
  27.6 11.3 %collective-permute-start.12 = (f32[2,2,64,256]{3,2,1,0:T(8,128)S(1)}, f32[2,2,64,256]{3,2,1,0:T(8,128)S(1)}, u32[]{:S(2)}, u32[]{:S(2)}) collective-permute-start(f32[2,2,64,256]{3,2,1,0:T(8,128)S(1)} %collective-permute-done.11.refs_10_), channel_id=1, source_target_pairs={{0,4},{1,5},{2,0},{3,1},{4,8},{5,9},{6,2},{7,3},{8,12},{9,13},{10,... | collective-permute-start | bytes 786440 | tf_op jit(solution)/shard_map/ppermute | solution.py:76
  31.2 11.2 %collective-permute-start.7 = (f32[2,2,64,256]{3,2,1,0:T(8,128)S(1)}, f32[2,2,64,256]{3,2,1,0:T(8,128)S(1)}, u32[]{:S(2)}, u32[]{:S(2)}) collective-permute-start(f32[2,2,64,256]{3,2,1,0:T(8,128)S(1)} %collective-permute-done.6.refs_4_), channel_id=1, source_target_pairs={{0,2},{1,3},{2,6},{3,7},{4,0},{5,1},{6,10},{7,11},{8,4},{9,5},{10,... | collective-permute-start | bytes 786440 | tf_op jit(solution)/shard_map/ppermute | solution.py:77
  33.2 11.3 %collective-permute-start.3 = (f32[2,2,64,256]{3,2,1,0:T(8,128)S(1)}, f32[2,2,64,256]{3,2,1,0:T(8,128)S(1)}, u32[]{:S(2)}, u32[]{:S(2)}) collective-permute-start(f32[2,2,64,256]{3,2,1,0:T(8,128)S(1)} %collective-permute-done.2.refs_3_), channel_id=1, source_target_pairs={{0,4},{1,5},{2,0},{3,1},{4,8},{5,9},{6,2},{7,3},{8,12},{9,13},{10,... | collective-permute-start | bytes 786440 | tf_op jit(solution)/shard_map/ppermute | solution.py:76
  36.8 11.0 %collective-permute-start.17 = (f32[1,2,64,256]{3,2,1,0:T(8,128)S(1)}, f32[1,2,64,256]{3,2,1,0:T(8,128)S(1)}, u32[]{:S(2)}, u32[]{:S(2)}) collective-permute-start(f32[1,2,64,256]{3,2,1,0:T(8,128)S(1)} %slice.19), channel_id=1, source_target_pairs={{0,2},{1,3},{2,6},{3,7},{4,0},{5,1},{6,10},{7,11},{8,4},{9,5},{10,... | collective-permute-start | bytes 393224 | tf_op jit(solution)/shard_map/ppermute | solution.py:79
  38.9 8.9 %collective-permute-start.13 = (f32[1,2,64,256]{3,2,1,0:T(8,128)S(1)}, f32[1,2,64,256]{3,2,1,0:T(8,128)S(1)}, u32[]{:S(2)}, u32[]{:S(2)}) collective-permute-start(f32[1,2,64,256]{3,2,1,0:T(8,128)S(1)} %slice.18), channel_id=1, source_target_pairs={{0,4},{1,5},{2,0},{3,1},{4,8},{5,9},{6,2},{7,3},{8,12},{9,13},{10,... | collective-permute-start | bytes 393224 | tf_op jit(solution)/shard_map/ppermute | solution.py:79
  42.4 5.4 %collective-permute-start.8 = (f32[1,2,64,256]{3,2,1,0:T(8,128)S(1)}, f32[1,2,64,256]{3,2,1,0:T(8,128)S(1)}, u32[]{:S(2)}, u32[]{:S(2)}) collective-permute-start(f32[1,2,64,256]{3,2,1,0:T(8,128)S(1)} %slice.17), channel_id=1, source_target_pairs={{0,2},{1,3},{2,6},{3,7},{4,0},{5,1},{6,10},{7,11},{8,4},{9,5},{10,... | collective-permute-start | bytes 393224 | tf_op jit(solution)/shard_map/ppermute | solution.py:79
  44.5 5.0 %collective-permute-start.4 = (f32[1,2,64,256]{3,2,1,0:T(8,128)S(1)}, f32[1,2,64,256]{3,2,1,0:T(8,128)S(1)}, u32[]{:S(2)}, u32[]{:S(2)}) collective-permute-start(f32[1,2,64,256]{3,2,1,0:T(8,128)S(1)} %slice.16), channel_id=1, source_target_pairs={{0,4},{1,5},{2,0},{3,1},{4,8},{5,9},{6,2},{7,3},{8,12},{9,13},{10,... | collective-permute-start | bytes 393224 | tf_op jit(solution)/shard_map/ppermute | solution.py:79
  50.7 1.4 %collective-permute-start.18 = (f32[128,256]{1,0:T(8,128)S(1)}, f32[128,256]{1,0:T(8,128)S(1)}, u32[]{:S(2)}, u32[]{:S(2)}) collective-permute-start(f32[128,256]{1,0:T(8,128)S(1)} %get-tuple-element.32.e0_ref), channel_id=1, source_target_pairs={{0,1},{1,0},{2,3},{3,2},{4,5},{5,4},{6,7},{7,6},{8,9},{9,8},{10,11... | collective-permute-start | bytes 393224 | tf_op jit(solution)/shard_map/ppermute | solution.py:311
  59.0 1.4 %collective-permute-start.19 = (f32[128,256]{1,0:T(8,128)S(1)}, f32[128,256]{1,0:T(8,128)S(1)}, u32[]{:S(2)}, u32[]{:S(2)}) collective-permute-start(f32[128,256]{1,0:T(8,128)S(1)} %get-tuple-element.35.e0_ref), channel_id=1, source_target_pairs={{0,1},{1,0},{2,3},{3,2},{4,5},{5,4},{6,7},{7,6},{8,9},{9,8},{10,11... | collective-permute-start | bytes 393224 | tf_op jit(solution)/shard_map/ppermute | solution.py:311
  67.3 1.4 %collective-permute-start.20 = (f32[128,256]{1,0:T(8,128)S(1)}, f32[128,256]{1,0:T(8,128)S(1)}, u32[]{:S(2)}, u32[]{:S(2)}) collective-permute-start(f32[128,256]{1,0:T(8,128)S(1)} %get-tuple-element.38.e0_ref), channel_id=1, source_target_pairs={{0,1},{1,0},{2,3},{3,2},{4,5},{5,4},{6,7},{7,6},{8,9},{9,8},{10,11... | collective-permute-start | bytes 393224 | tf_op jit(solution)/shard_map/ppermute | solution.py:311
  76.2 1.3 %collective-permute-start.22 = (f32[2,64,256]{2,1,0:T(8,128)S(1)}, f32[2,64,256]{2,1,0:T(8,128)S(1)}, u32[]{:S(2)}, u32[]{:S(2)}) collective-permute-start(f32[2,64,256]{2,1,0:T(8,128)S(1)} %get-tuple-element.43), channel_id=1, source_target_pairs={{0,1},{1,0},{2,3},{3,2},{4,5},{5,4},{6,7},{7,6},{8,9},{9,8},{10,11... | collective-permute-start | bytes 393224 | tf_op jit(solution)/shard_map/ppermute | solution.py:346
  76.3 1.4 %collective-permute-start.21 = (f32[128,256]{1,0:T(8,128)S(1)}, f32[128,256]{1,0:T(8,128)S(1)}, u32[]{:S(2)}, u32[]{:S(2)}) collective-permute-start(f32[128,256]{1,0:T(8,128)S(1)} %get-tuple-element.41.e0_ref), channel_id=1, source_target_pairs={{0,1},{1,0},{2,3},{3,2},{4,5},{5,4},{6,7},{7,6},{8,9},{9,8},{10,11... | collective-permute-start | bytes 393224 | tf_op jit(solution)/shard_map/ppermute | solution.py:311
  76.7 6.0 %collective-permute-start.23 = (f32[2,2,64,256]{3,2,1,0:T(8,128)S(1)}, f32[2,2,64,256]{3,2,1,0:T(8,128)S(1)}, u32[]{:S(2)}, u32[]{:S(2)}) collective-permute-start(f32[2,2,64,256]{3,2,1,0:T(8,128)S(1)} %get-tuple-element.46), channel_id=1, source_target_pairs={{0,1},{1,0},{2,3},{3,2},{4,5},{5,4},{6,7},{7,6},{8,9},{9,8},{10,11... | collective-permute-start | bytes 786440 | tf_op jit(solution)/shard_map/ppermute | solution.py:347

commit v3 on v2

v3 whole, which is shorter than its diff:
```python
import functools

import jax
import jax.numpy as jnp
import numpy as np
from jax import lax
from jax.experimental import pallas as pl
from jax.experimental.pallas import tpu as pltpu
from jax.sharding import PartitionSpec as P

SECTIONS = 4
NS_ITERS = 8

F32, BF16 = jnp.float32, jnp.bfloat16
NN = (((1,), (0,)), ((), ()))
NT = (((1,), (1,)), ((), ()))
VMEM_LIMIT = 24 * 2**20


class Layout:
    def __init__(self, size):
        bits = size.bit_length() - 1
        self.size = size
        self.partner_bits = [bits - 1, bits // 2, 0, 1]
        self.gate_bits = sorted(set(self.partner_bits))
        self.other_bits = [b for b in range(bits) if b not in self.gate_bits]
        self.local_bits = [self.gate_bits.index(b) for b in self.partner_bits]
        self.chips = 2 ** (len(self.gate_bits) - 1)

    def chip(self, index):
        return sum((index >> b & 1) << j for j, b in enumerate(self.gate_bits[1:]))

    def ring_position(self, chip):
        line, turn = chip >> 1, chip & 1
        return self.chips - 1 - line if turn else line

    def chip_at(self, position):
        position %= self.chips
        if position < self.chips // 2:
            return position << 1
        return (self.chips - 1 - position) << 1 | 1

    def shifted(self, index, step):
        chip = self.chip_at(self.ring_position(self.chip(index)) + step)
        for j, b in enumerate(self.gate_bits[1:]):
            index = index & ~(1 << b) | (chip >> j & 1) << b
        return index

    def ring(self, step, flipped=0):
        return [(i, self.shifted(i, step) ^ flipped << self.gate_bits[0]) for i in range(self.size)]

    def flip(self, bit):
        return [(i, i ^ 1 << bit) for i in range(self.size)]

    def place_of(self, index):
        position = self.ring_position_traced(self.chip(index))
        half = self.chips // 2
        steps = [0] + [s for k in range(1, half) for s in (-k, k)] + [half]
        return index >> self.gate_bits[0] & 1, [self.chip_at_traced(position + s) for s in steps]

    def ring_position_traced(self, chip):
        line, turn = chip >> 1, chip & 1
        return jnp.where(turn == 1, self.chips - 1 - line, line)

    def chip_at_traced(self, position):
        position = position & self.chips - 1
        return jnp.where(position < self.chips // 2, position << 1, (self.chips - 1 - position) << 1 | 1)


def gather_ring(home, layout, before_last=lambda ends: ends):
    half = layout.chips // 2
    blocks, ends = [home], [home, home]
    for _ in range(1, half):
        ends = [lax.ppermute(end, "long", layout.ring(step)) for end, step in zip(ends, (1, -1))]
        blocks += ends
    ends = before_last(ends)
    opposite = [lax.ppermute(ends[k][k : k + 1], "long", layout.ring(1 - 2 * k)) for k in range(2)]
    return blocks, opposite


def split(x):
    high = x.astype(BF16)
    return high, (x - high.astype(F32)).astype(BF16)


def dot(a, b, dims):
    return lax.dot_general(a, b, dims, preferred_element_type=F32)


def dot3(a, b, dims):
    return dot(a[0], b[0], dims) + (dot(a[0], b[1], dims) + dot(a[1], b[0], dims))


def turned(a):
    n = a.shape[1] // 2
    return jnp.concatenate([-a[:, n:], a[:, :n]], 1)


def as_matrix(a):
    n = a.shape[1] // 2
    return jnp.concatenate([jnp.concatenate([a[:, :n], -a[:, n:]], 1), jnp.concatenate([a[:, n:], a[:, :n]], 1)], 0)


def polar(e):
    x = e * lax.rsqrt(jnp.sum(e * e) + 1e-6)
    for _ in range(NS_ITERS):
        xs = split(x)
        rows = [jnp.concatenate([v, turned(v)], 0) for v in xs]
        turns = [v[v.shape[0] // 2 :] for v in rows]
        h = split(jnp.concatenate([dot3(xs, xs, NT), dot3(xs, turns, NT)], 1))
        both = dot(jnp.concatenate(h, 0), rows[0], NN)
        n = x.shape[0]
        x = 1.5 * x - 0.5 * (both[:n] + both[n:] + dot(h[0], rows[1], NN))
    return x


def load_pair(ref, pair):
    return [jnp.concatenate([ref[k, d, plane] for plane in range(2) for d in pair], 0) for k in range(2)]


def store_pair(ref, pair, y):
    n = y.shape[0] // 4
    for k, v in enumerate(split(y)):
        for plane in range(2):
            for t, d in enumerate(pair):
                ref[k, d, plane] = v[(2 * plane + t) * n : (2 * plane + t + 1) * n]


def apply_at(gate, source, target, pair):
    store_pair(target, pair, dot3(gate, load_pair(source, pair), NN))


def folded(total):
    n = total.shape[0] // 2
    return jnp.concatenate([total[:n, :n] + total[n:, n:], total[n:, :n] - total[:n, n:]], 1)


def environment(phi, psi, pairs):
    terms = [dot3(load_pair(phi, pair), load_pair(psi, pair), NT) for pair in pairs]
    return sum(terms[1:], terms[0])


def gate_matrix(gates_ref, section):
    return split(as_matrix(jnp.concatenate([gates_ref[section, 0], gates_ref[section, 1]], 1)))


def place(block, target, d):
    target[0, d], target[1, d] = split(block)


def joined(ref, d):
    return ref[0, d].astype(F32) + ref[1, d].astype(F32)


def unpacked(core, own, other, out_ref):
    for plane in range(2):
        low = jnp.where(core == 0, own[plane], other[plane])
        high = jnp.where(core == 0, other[plane], own[plane])
        out_ref[plane] = jnp.concatenate([low, high], 0).T


def pack_kernel(layout, *refs):
    core, _ = layout.place_of(lax.axis_index("long"))
    n = refs[0].shape[2] // 2
    for x_ref, own_ref, sent_ref in ((refs[0], *refs[2:4]), (refs[1], *refs[4:6])):
        for plane in range(2):
            t = x_ref[plane].T
            low, high = t[:n], t[n:]
            own_ref[plane] = jnp.where(core == 0, low, high)
            sent_ref[plane] = jnp.where(core == 0, high, low)


TURN = 1


def all_pairs(layout, bit):
    return [(d, d + (1 << bit)) for d in range(2 * layout.chips) if not d >> bit & 1]


def line_pairs(layout, bit, turn):
    return [tuple(d + (turn << TURN) for d in pair) for pair in all_pairs(layout, bit) if not pair[0] >> TURN & 1]


def chip_pairs(bit, chip):
    firsts = [(chip * 2 + slot) & ~(1 << bit) for slot in range(2)]
    return [(d, d + (1 << bit)) for d in firsts]


def near_pairs(layout, far):
    bit = layout.local_bits[0]
    others = [far ^ k for k in range(1, layout.chips) if not k >> bit - 1 & 1]
    return [pair for chip in others for pair in chip_pairs(bit, chip)]


def place_blocks(blocks, chips, core, target):
    for block, chip in zip(blocks, chips):
        for slot in range(2):
            place(block[slot], target, chip * 2 + (slot ^ core))


def place_far(halves, chip, core, target):
    for slot in range(2):
        place(halves[slot][0], target, chip * 2 + (slot ^ core))


def line_kernel(layout, gates_ref, *refs):
    *blocks, phi0_ref, phi1_ref, phi2_ref = refs
    core, chips = layout.place_of(lax.axis_index("long"))
    place_blocks(blocks, chips, core, phi0_ref)
    gate = gate_matrix(gates_ref, 0)
    for pair in near_pairs(layout, chips[-1]):
        apply_at(gate, phi0_ref, phi0_ref, pair)
    for s, source, target in ((1, phi0_ref, phi1_ref), (2, phi1_ref, phi2_ref)):
        gate = gate_matrix(gates_ref, s)
        for pair in line_pairs(layout, layout.local_bits[s], chips[0] & 1):
            apply_at(gate, source, target, pair)


def near_kernel(layout, gates_ref, *refs):
    *blocks, phi_a, phi_b, phi_in, phi_ref, psi_ref, total_ref = refs
    core, chips = layout.place_of(lax.axis_index("long"))
    far = chips[-1]
    place_blocks(blocks, chips, core, psi_ref)
    total_ref[...] = environment(phi_ref, psi_ref, near_pairs(layout, far))
    place_far((phi_a, phi_b), far, core, phi_ref)
    gate = gate_matrix(gates_ref, 0)
    for pair in chip_pairs(layout.local_bits[0], far):
        apply_at(gate, phi_ref, phi_ref, pair)


def far_kernel(layout, psi_a, psi_b, total_ref, phi_ref, psi_in, psi_ref, e_ref):
    core, chips = layout.place_of(lax.axis_index("long"))
    far = chips[-1]
    place_far((psi_a, psi_b), far, core, psi_ref)
    e_ref[...] = folded(total_ref[...] + environment(phi_ref, psi_ref, chip_pairs(layout.local_bits[0], far)))


def other_line_kernel(layout, section, gates_ref, phi_ref, next_in, next_ref):
    _, chips = layout.place_of(lax.axis_index("long"))
    gate = gate_matrix(gates_ref, section)
    for pair in line_pairs(layout, layout.local_bits[section], 1 - (chips[0] & 1)):
        apply_at(gate, phi_ref, next_ref, pair)


def last_adjoint_kernel(layout, gates_ref, phi_ref, next_ref, own_ref, sent_ref):
    core, chips = layout.place_of(lax.axis_index("long"))
    gate = gate_matrix(gates_ref, SECTIONS - 1)
    for pair in all_pairs(layout, layout.local_bits[SECTIONS - 1]):
        apply_at(gate, phi_ref, next_ref, pair)
    for slot, out in enumerate((own_ref, sent_ref)):
        out[...] = joined(next_ref, chips[0] * 2 + (slot ^ core))


def ends_kernel(layout, psi_ref, own_ref, sent_ref):
    core, chips = layout.place_of(lax.axis_index("long"))
    for slot, out in enumerate((own_ref, sent_ref)):
        for t, d in enumerate(last_pair(layout, chips[0] * 2 + (slot ^ core))):
            out[t] = joined(psi_ref, d)


def section_kernel(layout, section, e0_ref, e1_ref, phi_ref, psi_ref, psi_next, e_ref):
    gate = split(as_matrix(polar(e0_ref[...] + e1_ref[...])))
    for pair in all_pairs(layout, layout.local_bits[section]):
        apply_at(gate, psi_ref, psi_next, pair)
    e_ref[...] = folded(environment(phi_ref, psi_next, all_pairs(layout, layout.local_bits[section + 1])))


def last_pair(layout, d):
    bit = layout.local_bits[SECTIONS - 1]
    first = d & ~(1 << bit)
    return first, first + (1 << bit)


def last_polar_kernel(layout, e0_ref, e1_ref, phi_own, phi_got, gate_ref, adjoint_ref):
    core, _ = layout.place_of(lax.axis_index("long"))
    gate_ref[...] = as_matrix(polar(e0_ref[...] + e1_ref[...]))
    unpacked(core, phi_own, phi_got, adjoint_ref)


def last_apply_kernel(layout, gate_ref, psi_own, psi_got, state_ref):
    core, chips = layout.place_of(lax.axis_index("long"))
    t = chips[0] * 2 + core >> layout.local_bits[SECTIONS - 1] & 1
    n = psi_own.shape[2]
    rows = [gate_ref[pl.ds(pl.multiple_of((plane * 2 + t) * n, n), n)] for plane in range(2)]
    gate = split(jnp.concatenate(rows, 0))
    halves = []
    for psi in (psi_own, psi_got):
        x = jnp.concatenate([psi[0, 0], psi[1, 0], psi[0, 1], psi[1, 1]], 0)
        y = dot3(gate, split(x), NN)
        halves.append([y[:n], y[n:]])
    unpacked(core, halves[0], halves[1], state_ref)


def call(kernel, name, outs, ins, flops, scratch=(), aliases=None):
    sizes = [int(np.prod(a.shape)) * a.dtype.itemsize for a in list(ins) + list(outs)]
    spec = pl.BlockSpec(memory_space=pltpu.VMEM)
    return pl.pallas_call(
        kernel,
        out_shape=outs,
        in_specs=[spec] * len(ins),
        out_specs=[spec] * len(outs),
        scratch_shapes=list(scratch),
        input_output_aliases=aliases or {},
        compiler_params=pltpu.CompilerParams(vmem_limit_bytes=VMEM_LIMIT),
        cost_estimate=pl.CostEstimate(flops=flops, bytes_accessed=sum(sizes), transcendentals=0),
        name=name,
    )(*ins)


def shards(initial_state, adjoint_state, current_gates):
    layout = Layout(lax.axis_size("long"))
    core_flip = layout.flip(layout.gate_bits[0])
    rows, lanes = initial_state.shape[1:]
    c = lanes // 2
    devices = layout.chips * 2
    whole = jax.ShapeDtypeStruct(initial_state.shape, F32)
    slab = jax.ShapeDtypeStruct((2, c, rows), F32)
    two_slabs = jax.ShapeDtypeStruct((2, 2, c, rows), F32)
    pieces = jax.ShapeDtypeStruct((2, devices, 2, c, rows), BF16)
    env = jax.ShapeDtypeStruct((lanes, 2 * lanes), F32)
    square = jax.ShapeDtypeStruct((2 * lanes, 2 * lanes), F32)
    apply_flops = 3 * 2 * (2 * lanes) ** 2 * (devices // 2) * rows

    def kernel(body, *args):
        return functools.partial(body, layout, *args)

    def both(e):
        for bit in layout.other_bits:
            e = e + lax.ppermute(e, "long", layout.flip(bit))
        return e, lax.ppermute(e, "long", core_flip)

    def home(own, sent):
        return jnp.stack([own, lax.ppermute(sent, "long", core_flip)])

    phi_own, phi_sent, psi_own, psi_sent = call(
        kernel(pack_kernel),
        "pack",
        [slab] * 4,
        [adjoint_state, initial_state],
        0,
    )
    phi_home = home(phi_own, phi_sent)
    phi_home, psi_own, psi_sent = lax.optimization_barrier((phi_home, psi_own, psi_sent))
    phi_near, phi_far = gather_ring(phi_home, layout)
    phis = list(
        call(kernel(line_kernel), "line", [pieces] * 3, [current_gates] + phi_near, 7 * apply_flops // 4)
    )

    def after_line(ends):
        return [ends[0], lax.optimization_barrier((ends[1], phis[0]))[0]]

    psi_near, psi_far = gather_ring(home(psi_own, psi_sent), layout, after_line)
    ins = [current_gates] + psi_near + phi_far + [phis[0]]
    phis[0], psi, total = call(
        kernel(near_kernel), "near", [pieces, pieces, square], ins, apply_flops, aliases={len(ins) - 1: 0}
    )
    psi, e = call(
        kernel(far_kernel), "far", [pieces, env], psi_far + [total, phis[0], psi], apply_flops // 4, aliases={4: 0}
    )
    for section in range(SECTIONS - 1):
        e0, e1 = both(e)
        if section < SECTIONS - 2:
            (phi,) = call(
                kernel(other_line_kernel, section + 1),
                "other_line",
                [pieces],
                [current_gates, phis[section], phis[section + 1]],
                apply_flops // 2,
                aliases={2: 0},
            )
            phis[section + 1] = phi
        else:
            phi, phi_own, phi_sent = call(
                kernel(last_adjoint_kernel),
                "last_adjoint",
                [pieces, slab, slab],
                [current_gates, phis[section]],
                apply_flops,
            )
        psi, e = call(kernel(section_kernel, section), "section", [pieces, env], [e0, e1, phi, psi], 3 * apply_flops)
    e0, e1 = both(e)
    psi_own, psi_sent = call(kernel(ends_kernel), "ends", [two_slabs, two_slabs], [psi], 0)
    phi_got = lax.ppermute(phi_sent, "long", core_flip)
    psi_got = lax.ppermute(psi_sent, "long", core_flip)
    gate, final_adjoint = call(
        kernel(last_polar_kernel), "last_polar", [square, whole], [e0, e1, phi_own, phi_got], 2 * apply_flops
    )
    (final_state,) = call(
        kernel(last_apply_kernel), "last_apply", [whole], [gate, psi_own, psi_got], apply_flops // 4
    )
    return final_state, final_adjoint


def solution(mesh):
    return jax.shard_map(
        shards,
        mesh=mesh,
        in_specs=(
            P(None, ("groups", "long"), None),
            P(None, ("groups", "long"), None),
            P("groups", None, None, None),
        ),
        out_specs=(P(None, ("groups", "long"), None), P(None, ("groups", "long"), None)),
        check_vma=False,
    )
```

time: 84 us -> 80.1 us (0.954)
  waiting for transfers between devices: 29.7 us -> 25.9 us
    ppermute x4, waiting for transfers between devices: 3.92 us -> 2.06 us  [both(): return (e, lax.ppermute(e, 'long', core_flip))]
    ppermute x18, waiting for transfers between devices: 25.1 us -> 23.8 us  [the longest x12 21.4 us: gather_ring(): lax.ppermute(end, 'long', layout.ring(step))]
    pallas_call x8 -> x13, Pallas kernels: 31.8 us -> 31.3 us  [call(): pl.pallas_call(kernel, out_shape=outs, in_specs=[spec] * len(ins), out_sp...]
  transfers between devices with their start and end apart: 24 -> 24, of which waited for: 13 -> 13; matrix products, arithmetic and copies ran while one was open for 0% -> 0% of each run, Pallas kernels for 10% -> 22%
where the time goes in v3:
time: 80.1 us; the launch traced here: 79.9 us
  Pallas kernels  31.3 us (39%)
  waiting for transfers between devices  25.9 us (32%)
  starting transfers between devices  19.9 us (25%)
  local copies, waits for them, and re-layouts  1.94 us (2%)
  between operations  0.81 us (1%)
    pallas_call x13, Pallas kernels, call(): pl.pallas_call(kernel, out_shape=outs, in_specs=[spec] * len(ins), out_sp...  31.3 us
    ppermute x12, waiting for transfers between devices, gather_ring(): lax.ppermute(end, 'long', layout.ring(step))  21.4 us
    ppermute x12, starting transfers between devices, gather_ring(): lax.ppermute(end, 'long', layout.ring(step))  13 us
    ppermute x4, starting transfers between devices, gather_ring(): lax.ppermute(ends[k][k:k + 1], 'long', layout.ring(1 - 2 * k))  4.42 us
    ppermute x4, waiting for transfers between devices, both(): return (e, lax.ppermute(e, 'long', core_flip))  2.06 us
    unnamed x6, local copies, waits for them, and re-layouts  1.9 us
  transfers between devices with their start and end apart: 24, of which 13 were waited for; matrix products, arithmetic and copies ran while one was open for 0% of the time, Pallas kernels for 22%

profile of v3, /device:TPU:0, one launch (start us, length us, event | category | flops | bytes accessed | tf_op | source)
XLA Modules:
  0.0 79.9 jit_solution(5039379619850658866)
XLA Ops:
  0.6 0.0 copy-start.1
  0.6 0.9 %copy-done.1 = f32[2,256,128]{2,1,0:T(8,128)S(1)} copy-done((f32[2,256,128]{2,1,0:T(8,128)S(1)}, f32[2,256,128]{2,1,0:T(8,128)}, u32[]{:S(2)}) %copy-start.1) | copy-done | bytes 262168
  1.6 0.9 %copy-done.2 = f32[2,256,128]{2,1,0:T(8,128)S(1)} copy-done((f32[2,256,128]{2,1,0:T(8,128)S(1)}, f32[2,256,128]{2,1,0:T(8,128)}, u32[]{:S(2)}) %copy-start.2) | copy-done | bytes 262168
  2.5 0.2 pack.1
  2.7 0.5 collective-permute-start
  3.3 1.0 %collective-permute-done = f32[2,64,256]{2,1,0:T(8,128)S(1)} collective-permute-done((f32[2,64,256]{2,1,0:T(8,128)S(1)}, f32[2,64,256]{2,1,0:T(8,128)S(1)}, u32[]{:S(2)}, u32[]{:S(2)}) %collective-permute-start) | collective-permute-done | bytes 131104 | tf_op jit(solution)/shard_map/ppermute | solution.py:333
  4.3 0.4 collective-permute-start.1
  4.7 2.7 %collective-permute-start.9 = (f32[2,2,64,256]{3,2,1,0:T(8,128)S(1)}, f32[2,2,64,256]{3,2,1,0:T(8,128)S(1)}, u32[]{:S(2)}, u32[]{:S(2)}) collective-permute-start(f32[2,2,64,256]{3,2,1,0:T(8,128)S(1)} %pad_maximum_fusion.refs_0_), channel_id=1, source_target_pairs={{0,4},{1,5},{2,0},{3,1},{4,8},{5,9},{6,2},{7,3},{8,12},{9,13},{10,... | collective-permute-start | bytes 786440 | tf_op jit(solution)/shard_map/ppermute | solution.py:74
  7.4 0.0 collective-permute-start.10
  7.4 0.0 collective-permute-done.1
  7.5 2.0 %collective-permute-start.6 = (f32[2,2,64,256]{3,2,1,0:T(8,128)S(1)}, f32[2,2,64,256]{3,2,1,0:T(8,128)S(1)}, u32[]{:S(2)}, u32[]{:S(2)}) collective-permute-start(f32[2,2,64,256]{3,2,1,0:T(8,128)S(1)} %pad_maximum_fusion.1.refs_0_), channel_id=1, source_target_pairs={{0,2},{1,3},{2,6},{3,7},{4,0},{5,1},{6,10},{7,11},{8,4},{9,5},{10,... | collective-permute-start | bytes 786440 | tf_op jit(solution)/shard_map/ppermute | solution.py:74
  9.5 0.1 collective-permute-start.2
  9.6 4.9 %collective-permute-done.9.refs_1_ = f32[2,2,64,256]{3,2,1,0:T(8,128)S(1)} collective-permute-done((f32[2,2,64,256]{3,2,1,0:T(8,128)S(1)}, f32[2,2,64,256]{3,2,1,0:T(8,128)S(1)}, u32[]{:S(2)}, u32[]{:S(2)}) %collective-permute-start.9) | collective-permute-done | bytes 262176 | tf_op jit(solution)/shard_map/ppermute | solution.py:74
  14.5 2.0 %collective-permute-start.11 = (f32[2,2,64,256]{3,2,1,0:T(8,128)S(1)}, f32[2,2,64,256]{3,2,1,0:T(8,128)S(1)}, u32[]{:S(2)}, u32[]{:S(2)}) collective-permute-start(f32[2,2,64,256]{3,2,1,0:T(8,128)S(1)} %collective-permute-done.9.refs_1_), channel_id=1, source_target_pairs={{0,4},{1,5},{2,0},{3,1},{4,8},{5,9},{6,2},{7,3},{8,12},{9,13},{10,... | collective-permute-start | bytes 786440 | tf_op jit(solution)/shard_map/ppermute | solution.py:74
  16.6 0.0 collective-permute-done.10.refs_2_
  16.6 0.0 collective-permute-start.12
  16.6 5.6 %collective-permute-done.6.refs_2_ = f32[2,2,64,256]{3,2,1,0:T(8,128)S(1)} collective-permute-done((f32[2,2,64,256]{3,2,1,0:T(8,128)S(1)}, f32[2,2,64,256]{3,2,1,0:T(8,128)S(1)}, u32[]{:S(2)}, u32[]{:S(2)}) %collective-permute-start.6) | collective-permute-done | bytes 262176 | tf_op jit(solution)/shard_map/ppermute | solution.py:74
  22.2 0.0 collective-permute-start.7
  22.2 0.0 collective-permute-done.2.refs_1_
  22.2 2.0 %collective-permute-start.3 = (f32[2,2,64,256]{3,2,1,0:T(8,128)S(1)}, f32[2,2,64,256]{3,2,1,0:T(8,128)S(1)}, u32[]{:S(2)}, u32[]{:S(2)}) collective-permute-start(f32[2,2,64,256]{3,2,1,0:T(8,128)S(1)} %collective-permute-done.2.refs_1_), channel_id=1, source_target_pairs={{0,4},{1,5},{2,0},{3,1},{4,8},{5,9},{6,2},{7,3},{8,12},{9,13},{10,... | collective-permute-start | bytes 786440 | tf_op jit(solution)/shard_map/ppermute | solution.py:74
  24.2 1.5 %collective-permute-done.11.refs_3_ = f32[2,2,64,256]{3,2,1,0:T(8,128)S(1)} collective-permute-done((f32[2,2,64,256]{3,2,1,0:T(8,128)S(1)}, f32[2,2,64,256]{3,2,1,0:T(8,128)S(1)}, u32[]{:S(2)}, u32[]{:S(2)}) %collective-permute-start.11) | collective-permute-done | bytes 262176 | tf_op jit(solution)/shard_map/ppermute | solution.py:74
  25.7 2.0 %collective-permute-start.13 = (f32[2,2,64,256]{3,2,1,0:T(8,128)S(1)}, f32[2,2,64,256]{3,2,1,0:T(8,128)S(1)}, u32[]{:S(2)}, u32[]{:S(2)}) collective-permute-start(f32[2,2,64,256]{3,2,1,0:T(8,128)S(1)} %collective-permute-done.11.refs_3_), channel_id=1, source_target_pairs={{0,4},{1,5},{2,0},{3,1},{4,8},{5,9},{6,2},{7,3},{8,12},{9,13},{10,... | collective-permute-start | bytes 786440 | tf_op jit(solution)/shard_map/ppermute | solution.py:74
  27.8 0.0 collective-permute-done.12.refs_4_
  27.8 0.0 collective-permute-start.14
  27.8 5.6 %collective-permute-done.7.refs_4_ = f32[2,2,64,256]{3,2,1,0:T(8,128)S(1)} collective-permute-done((f32[2,2,64,256]{3,2,1,0:T(8,128)S(1)}, f32[2,2,64,256]{3,2,1,0:T(8,128)S(1)}, u32[]{:S(2)}, u32[]{:S(2)}) %collective-permute-start.7) | collective-permute-done | bytes 262176 | tf_op jit(solution)/shard_map/ppermute | solution.py:74
  33.4 0.0 collective-permute-start.8
  33.4 0.0 collective-permute-done.3.refs_3_
  33.5 2.0 %collective-permute-start.4 = (f32[2,2,64,256]{3,2,1,0:T(8,128)S(1)}, f32[2,2,64,256]{3,2,1,0:T(8,128)S(1)}, u32[]{:S(2)}, u32[]{:S(2)}) collective-permute-start(f32[2,2,64,256]{3,2,1,0:T(8,128)S(1)} %collective-permute-done.3.refs_3_), channel_id=1, source_target_pairs={{0,4},{1,5},{2,0},{3,1},{4,8},{5,9},{6,2},{7,3},{8,12},{9,13},{10,... | collective-permute-start | bytes 786440 | tf_op jit(solution)/shard_map/ppermute | solution.py:74
  35.5 1.6 %collective-permute-done.13.refs_5_ = f32[2,2,64,256]{3,2,1,0:T(8,128)S(1)} collective-permute-done((f32[2,2,64,256]{3,2,1,0:T(8,128)S(1)}, f32[2,2,64,256]{3,2,1,0:T(8,128)S(1)}, u32[]{:S(2)}, u32[]{:S(2)}) %collective-permute-start.13) | collective-permute-done | bytes 262176 | tf_op jit(solution)/shard_map/ppermute | solution.py:74
  37.1 2.1 %collective-permute-start.16 = (f32[1,2,64,256]{3,2,1,0:T(8,128)S(1)}, f32[1,2,64,256]{3,2,1,0:T(8,128)S(1)}, u32[]{:S(2)}, u32[]{:S(2)}) collective-permute-start(f32[1,2,64,256]{3,2,1,0:T(8,128)S(1)} %slice.17), channel_id=1, source_target_pairs={{0,4},{1,5},{2,0},{3,1},{4,8},{5,9},{6,2},{7,3},{8,12},{9,13},{10,... | collective-permute-start | bytes 393224 | tf_op jit(solution)/shard_map/ppermute | solution.py:77
  39.2 0.0 collective-permute-done.14.refs_6_
  39.2 0.1 collective-permute-start.17
  39.3 3.4 %line.1 = (bf16[2,16,2,64,256]{4,3,2,1,0:T(8,128)(2,1)S(1)}, bf16[2,16,2,64,256]{4,3,2,1,0:T(8,128)(2,1)S(1)}, bf16[2,16,2,64,256]{4,3,2,1,0:T(8,128)(2,1)S(1)}) custom-call(f32[4,2,128,128]{3,2,1,0:T(8,128)S(1)} %copy-done, f32[2,2,64,256]{3,2,1,0:T(8,128)S(1)} %pad_maximum_fusion.refs_0_, f32[2,2,64,256]{3,2,1,0:T(8,128)S(1)} %collective-permute-done.9.refs_1_, ...), custom_call_target="tpu_custom_call" | custom-call | flops 1409286144 | bytes 8650752 | tf_op jit(solution)/shard_map/line/pallas_call | solution.py:297
  42.7 2.0 %collective-permute-done.8.refs_6_ = f32[2,2,64,256]{3,2,1,0:T(8,128)S(1)} collective-permute-done((f32[2,2,64,256]{3,2,1,0:T(8,128)S(1)}, f32[2,2,64,256]{3,2,1,0:T(8,128)S(1)}, u32[]{:S(2)}, u32[]{:S(2)}) %collective-permute-start.8) | collective-permute-done | bytes 262176 | tf_op jit(solution)/shard_map/ppermute | solution.py:74
  44.7 0.1 collective-permute-start.15
  44.8 0.0 collective-permute-done.4.refs_5_
  44.8 2.2 %collective-permute-start.5 = (f32[1,2,64,256]{3,2,1,0:T(8,128)S(1)}, f32[1,2,64,256]{3,2,1,0:T(8,128)S(1)}, u32[]{:S(2)}, u32[]{:S(2)}) collective-permute-start(f32[1,2,64,256]{3,2,1,0:T(8,128)S(1)} %slice.16), channel_id=1, source_target_pairs={{0,4},{1,5},{2,0},{3,1},{4,8},{5,9},{6,2},{7,3},{8,12},{9,13},{10,... | collective-permute-start | bytes 393224 | tf_op jit(solution)/shard_map/ppermute | solution.py:77
  47.0 0.0 collective-permute-done.16.refs_7_
  47.0 0.5 collective-permute-done.17.refs_8_
  47.5 1.5 %near.1 = (bf16[2,16,2,64,256]{4,3,2,1,0:T(8,128)(2,1)S(1)}, bf16[2,16,2,64,256]{4,3,2,1,0:T(8,128)(2,1)S(1)}, f32[256,256]{1,0:T(8,128)S(1)}) custom-call(f32[4,2,128,128]{3,2,1,0:T(8,128)S(1)} %copy-done, f32[2,2,64,256]{3,2,1,0:T(8,128)S(1)} %pad_maximum_fusion.1.refs_0_, ...), custom_call_target="tpu_custom_call", output_to_operand_aliasing={{0}: (10, {})} | custom-call | flops 805306368 | bytes 9175040 | tf_op jit(solution)/shard_map/near/pallas_call | solution.py:297
  49.0 0.7 collective-permute-done.15.psi_b
  49.7 0.3 collective-permute-done.5.psi_a
  50.0 0.4 far.1
  50.4 0.1 collective-permute-start.18
  50.5 0.6 other_line.2.phi_ref
  51.1 0.7 collective-permute-done.18.e1_ref
  51.9 6.3 %section.3 = (bf16[2,16,2,64,256]{4,3,2,1,0:T(8,128)(2,1)S(1)}, f32[128,256]{1,0:T(8,128)S(1)}) custom-call(f32[128,256]{1,0:T(8,128)S(1)} %get-tuple-element.43.e0_ref, f32[128,256]{1,0:T(8,128)S(1)} %collective-permute-done.18.e1_ref, bf16[2,16,2,64,256]{4,3,2,1,0:T(8,128)(2,1)S(1)} %other_line.2.phi_ref, ...), custom_call_target="tpu_custom_call" | custom-call | flops 2415919104 | bytes 6684672 | tf_op jit(solution)/shard_map/section/pallas_call | solution.py:297
  58.2 0.2 collective-permute-start.19
  58.4 0.6 other_line.3.phi_ref
  59.0 0.6 collective-permute-done.19.e1_ref
  59.6 6.0 %section.4 = (bf16[2,16,2,64,256]{4,3,2,1,0:T(8,128)(2,1)S(1)}, f32[128,256]{1,0:T(8,128)S(1)}) custom-call(f32[128,256]{1,0:T(8,128)S(1)} %get-tuple-element.46.e0_ref, f32[128,256]{1,0:T(8,128)S(1)} %collective-permute-done.19.e1_ref, bf16[2,16,2,64,256]{4,3,2,1,0:T(8,128)(2,1)S(1)} %other_line.3.phi_ref, ...), custom_call_target="tpu_custom_call" | custom-call | flops 2415919104 | bytes 6684672 | tf_op jit(solution)/shard_map/section/pallas_call | solution.py:297
  65.6 0.2 collective-permute-start.20
  65.8 1.0 %last_adjoint.1 = (bf16[2,16,2,64,256]{4,3,2,1,0:T(8,128)(2,1)S(1)}, f32[2,64,256]{2,1,0:T(8,128)S(1)}, f32[2,64,256]{2,1,0:T(8,128)S(1)}) custom-call(f32[4,2,128,128]{3,2,1,0:T(8,128)S(1)} %copy-done, bf16[2,16,2,64,256]{4,3,2,1,0:T(8,128)(2,1)S(1)} %other_line.3.phi_ref), custom_call_target="tpu_custom_call" | custom-call | flops 805306368 | bytes 4980736 | tf_op jit(solution)/shard_map/last_adjoint/pallas_call | solution.py:297
  66.8 0.4 collective-permute-start.22
  67.3 0.0 collective-permute-done.20.e1_ref
  67.3 5.8 %section.5 = (bf16[2,16,2,64,256]{4,3,2,1,0:T(8,128)(2,1)S(1)}, f32[128,256]{1,0:T(8,128)S(1)}) custom-call(f32[128,256]{1,0:T(8,128)S(1)} %get-tuple-element.49.e0_ref, f32[128,256]{1,0:T(8,128)S(1)} %collective-permute-done.20.e1_ref, bf16[2,16,2,64,256]{4,3,2,1,0:T(8,128)(2,1)S(1)} %get-tuple-element.50.phi_ref, ...), custom_call_target="tpu_custom_call" | custom-call | flops 2415919104 | bytes 6684672 | tf_op jit(solution)/shard_map/section/pallas_call | solution.py:297
  73.1 0.2 collective-permute-start.21
  73.3 0.1 ends.1
  73.4 0.4 collective-permute-start.23
  73.8 0.0 collective-permute-done.22.phi_got
  73.8 0.7 collective-permute-done.21.e1_ref
  74.5 4.3 %last_polar.1 = (f32[256,256]{1,0:T(8,128)S(1)}, f32[2,256,128]{2,1,0:T(8,128)}) custom-call(f32[128,256]{1,0:T(8,128)S(1)} %get-tuple-element.52.e0_ref, f32[128,256]{1,0:T(8,128)S(1)} %collective-permute-done.21.e1_ref, f32[2,64,256]{2,1,0:T(8,128)S(1)} %get-tuple-element.53.phi_own, f32[2,64,256]{2,1,0:T(8,128)S(1)} %collective-permute-done.22.phi_got), custom_call_target="tpu_custom_call" | custom-call | flops 1610612736 | bytes 1048576 | tf_op jit(solution)/shard_map/last_polar/pallas_call | solution.py:297
  78.8 0.0 collective-permute-done.23.psi_got
  78.8 1.1 %last_apply.1 = f32[2,256,128]{2,1,0:T(8,128)} custom-call(f32[256,256]{1,0:T(8,128)S(1)} %get-tuple-element.55.gate_ref, f32[2,2,64,256]{3,2,1,0:T(8,128)S(1)} %get-tuple-element.57.psi_own, f32[2,2,64,256]{3,2,1,0:T(8,128)S(1)} %collective-permute-done.23.psi_got), custom_call_target="tpu_custom_call" | custom-call | flops 201326592 | bytes 1048576 | tf_op jit(solution)/shard_map/last_apply/pallas_call | solution.py:297
  (9 shorter events, 0.1 us)
Async XLA Ops:
  0.6 1.0 %copy-start.1 = (f32[2,256,128]{2,1,0:T(8,128)S(1)}, f32[2,256,128]{2,1,0:T(8,128)}, u32[]{:S(2)}) copy-start(f32[2,256,128]{2,1,0:T(8,128)} %refs_0_.1) | copy-start | bytes 786436
  1.6 0.9 %copy-start.2 = (f32[2,256,128]{2,1,0:T(8,128)S(1)}, f32[2,256,128]{2,1,0:T(8,128)}, u32[]{:S(2)}) copy-start(f32[2,256,128]{2,1,0:T(8,128)} %refs_1_.1) | copy-start | bytes 786436
  2.5 36.7 %copy-start = (f32[4,2,128,128]{3,2,1,0:T(8,128)S(1)}, f32[4,2,128,128]{3,2,1,0:T(8,128)}, u32[]{:S(2)}) copy-start(f32[4,2,128,128]{3,2,1,0:T(8,128)} %gates_ref.9) | copy-start | bytes 1572868
  2.7 1.5 %collective-permute-start = (f32[2,64,256]{2,1,0:T(8,128)S(1)}, f32[2,64,256]{2,1,0:T(8,128)S(1)}, u32[]{:S(2)}, u32[]{:S(2)}) collective-permute-start(f32[2,64,256]{2,1,0:T(8,128)S(1)} %get-tuple-element.32), channel_id=1, source_target_pairs={{0,1},{1,0},{2,3},{3,2},{4,5},{5,4},{6,7},{7,6},{8,9},{9,8},{10,11... | collective-permute-start | bytes 393224 | tf_op jit(solution)/shard_map/ppermute | solution.py:333
  4.3 3.2 %collective-permute-start.1 = (f32[2,64,256]{2,1,0:T(8,128)S(1)}, f32[2,64,256]{2,1,0:T(8,128)S(1)}, u32[]{:S(2)}, u32[]{:S(2)}) collective-permute-start(f32[2,64,256]{2,1,0:T(8,128)S(1)} %get-tuple-element.36), channel_id=1, source_target_pairs={{0,1},{1,0},{2,3},{3,2},{4,5},{5,4},{6,7},{7,6},{8,9},{9,8},{10,11... | collective-permute-start | bytes 393224 | tf_op jit(solution)/shard_map/ppermute | solution.py:333
  4.7 9.8 %collective-permute-start.9 = (f32[2,2,64,256]{3,2,1,0:T(8,128)S(1)}, f32[2,2,64,256]{3,2,1,0:T(8,128)S(1)}, u32[]{:S(2)}, u32[]{:S(2)}) collective-permute-start(f32[2,2,64,256]{3,2,1,0:T(8,128)S(1)} %pad_maximum_fusion.refs_0_), channel_id=1, source_target_pairs={{0,4},{1,5},{2,0},{3,1},{4,8},{5,9},{6,2},{7,3},{8,12},{9,13},{10,... | collective-permute-start | bytes 786440 | tf_op jit(solution)/shard_map/ppermute | solution.py:74
  7.4 9.2 %collective-permute-start.10 = (f32[2,2,64,256]{3,2,1,0:T(8,128)S(1)}, f32[2,2,64,256]{3,2,1,0:T(8,128)S(1)}, u32[]{:S(2)}, u32[]{:S(2)}) collective-permute-start(f32[2,2,64,256]{3,2,1,0:T(8,128)S(1)} %pad_maximum_fusion.refs_0_), channel_id=1, source_target_pairs={{0,2},{1,3},{2,6},{3,7},{4,0},{5,1},{6,10},{7,11},{8,4},{9,5},{10,... | collective-permute-start | bytes 786440 | tf_op jit(solution)/shard_map/ppermute | solution.py:74
  7.5 14.8 %collective-permute-start.6 = (f32[2,2,64,256]{3,2,1,0:T(8,128)S(1)}, f32[2,2,64,256]{3,2,1,0:T(8,128)S(1)}, u32[]{:S(2)}, u32[]{:S(2)}) collective-permute-start(f32[2,2,64,256]{3,2,1,0:T(8,128)S(1)} %pad_maximum_fusion.1.refs_0_), channel_id=1, source_target_pairs={{0,2},{1,3},{2,6},{3,7},{4,0},{5,1},{6,10},{7,11},{8,4},{9,5},{10,... | collective-permute-start | bytes 786440 | tf_op jit(solution)/shard_map/ppermute | solution.py:74
  9.5 12.7 %collective-permute-start.2 = (f32[2,2,64,256]{3,2,1,0:T(8,128)S(1)}, f32[2,2,64,256]{3,2,1,0:T(8,128)S(1)}, u32[]{:S(2)}, u32[]{:S(2)}) collective-permute-start(f32[2,2,64,256]{3,2,1,0:T(8,128)S(1)} %pad_maximum_fusion.1.refs_0_), channel_id=1, source_target_pairs={{0,4},{1,5},{2,0},{3,1},{4,8},{5,9},{6,2},{7,3},{8,12},{9,13},{10,... | collective-permute-start | bytes 786440 | tf_op jit(solution)/shard_map/ppermute | solution.py:74
  14.5 11.2 %collective-permute-start.11 = (f32[2,2,64,256]{3,2,1,0:T(8,128)S(1)}, f32[2,2,64,256]{3,2,1,0:T(8,128)S(1)}, u32[]{:S(2)}, u32[]{:S(2)}) collective-permute-start(f32[2,2,64,256]{3,2,1,0:T(8,128)S(1)} %collective-permute-done.9.refs_1_), channel_id=1, source_target_pairs={{0,4},{1,5},{2,0},{3,1},{4,8},{5,9},{6,2},{7,3},{8,12},{9,13},{10,... | collective-permute-start | bytes 786440 | tf_op jit(solution)/shard_map/ppermute | solution.py:74
  16.6 11.2 %collective-permute-start.12 = (f32[2,2,64,256]{3,2,1,0:T(8,128)S(1)}, f32[2,2,64,256]{3,2,1,0:T(8,128)S(1)}, u32[]{:S(2)}, u32[]{:S(2)}) collective-permute-start(f32[2,2,64,256]{3,2,1,0:T(8,128)S(1)} %collective-permute-done.10.refs_2_), channel_id=1, source_target_pairs={{0,2},{1,3},{2,6},{3,7},{4,0},{5,1},{6,10},{7,11},{8,4},{9,5},{10,... | collective-permute-start | bytes 786440 | tf_op jit(solution)/shard_map/ppermute | solution.py:74
  22.2 11.2 %collective-permute-start.7 = (f32[2,2,64,256]{3,2,1,0:T(8,128)S(1)}, f32[2,2,64,256]{3,2,1,0:T(8,128)S(1)}, u32[]{:S(2)}, u32[]{:S(2)}) collective-permute-start(f32[2,2,64,256]{3,2,1,0:T(8,128)S(1)} %collective-permute-done.6.refs_2_), channel_id=1, source_target_pairs={{0,2},{1,3},{2,6},{3,7},{4,0},{5,1},{6,10},{7,11},{8,4},{9,5},{10,... | collective-permute-start | bytes 786440 | tf_op jit(solution)/shard_map/ppermute | solution.py:74
  22.2 11.2 %collective-permute-start.3 = (f32[2,2,64,256]{3,2,1,0:T(8,128)S(1)}, f32[2,2,64,256]{3,2,1,0:T(8,128)S(1)}, u32[]{:S(2)}, u32[]{:S(2)}) collective-permute-start(f32[2,2,64,256]{3,2,1,0:T(8,128)S(1)} %collective-permute-done.2.refs_1_), channel_id=1, source_target_pairs={{0,4},{1,5},{2,0},{3,1},{4,8},{5,9},{6,2},{7,3},{8,12},{9,13},{10,... | collective-permute-start | bytes 786440 | tf_op jit(solution)/shard_map/ppermute | solution.py:74
  25.7 11.3 %collective-permute-start.13 = (f32[2,2,64,256]{3,2,1,0:T(8,128)S(1)}, f32[2,2,64,256]{3,2,1,0:T(8,128)S(1)}, u32[]{:S(2)}, u32[]{:S(2)}) collective-permute-start(f32[2,2,64,256]{3,2,1,0:T(8,128)S(1)} %collective-permute-done.11.refs_3_), channel_id=1, source_target_pairs={{0,4},{1,5},{2,0},{3,1},{4,8},{5,9},{6,2},{7,3},{8,12},{9,13},{10,... | collective-permute-start | bytes 786440 | tf_op jit(solution)/shard_map/ppermute | solution.py:74
  27.8 11.3 %collective-permute-start.14 = (f32[2,2,64,256]{3,2,1,0:T(8,128)S(1)}, f32[2,2,64,256]{3,2,1,0:T(8,128)S(1)}, u32[]{:S(2)}, u32[]{:S(2)}) collective-permute-start(f32[2,2,64,256]{3,2,1,0:T(8,128)S(1)} %collective-permute-done.12.refs_4_), channel_id=1, source_target_pairs={{0,2},{1,3},{2,6},{3,7},{4,0},{5,1},{6,10},{7,11},{8,4},{9,5},{10,... | collective-permute-start | bytes 786440 | tf_op jit(solution)/shard_map/ppermute | solution.py:74
  33.4 11.2 %collective-permute-start.8 = (f32[2,2,64,256]{3,2,1,0:T(8,128)S(1)}, f32[2,2,64,256]{3,2,1,0:T(8,128)S(1)}, u32[]{:S(2)}, u32[]{:S(2)}) collective-permute-start(f32[2,2,64,256]{3,2,1,0:T(8,128)S(1)} %collective-permute-done.7.refs_4_), channel_id=1, source_target_pairs={{0,2},{1,3},{2,6},{3,7},{4,0},{5,1},{6,10},{7,11},{8,4},{9,5},{10,... | collective-permute-start | bytes 786440 | tf_op jit(solution)/shard_map/ppermute | solution.py:74
  33.5 11.3 %collective-permute-start.4 = (f32[2,2,64,256]{3,2,1,0:T(8,128)S(1)}, f32[2,2,64,256]{3,2,1,0:T(8,128)S(1)}, u32[]{:S(2)}, u32[]{:S(2)}) collective-permute-start(f32[2,2,64,256]{3,2,1,0:T(8,128)S(1)} %collective-permute-done.3.refs_3_), channel_id=1, source_target_pairs={{0,4},{1,5},{2,0},{3,1},{4,8},{5,9},{6,2},{7,3},{8,12},{9,13},{10,... | collective-permute-start | bytes 786440 | tf_op jit(solution)/shard_map/ppermute | solution.py:74
  37.1 9.9 %collective-permute-start.16 = (f32[1,2,64,256]{3,2,1,0:T(8,128)S(1)}, f32[1,2,64,256]{3,2,1,0:T(8,128)S(1)}, u32[]{:S(2)}, u32[]{:S(2)}) collective-permute-start(f32[1,2,64,256]{3,2,1,0:T(8,128)S(1)} %slice.17), channel_id=1, source_target_pairs={{0,4},{1,5},{2,0},{3,1},{4,8},{5,9},{6,2},{7,3},{8,12},{9,13},{10,... | collective-permute-start | bytes 393224 | tf_op jit(solution)/shard_map/ppermute | solution.py:77
  39.2 8.3 %collective-permute-start.17 = (f32[1,2,64,256]{3,2,1,0:T(8,128)S(1)}, f32[1,2,64,256]{3,2,1,0:T(8,128)S(1)}, u32[]{:S(2)}, u32[]{:S(2)}) collective-permute-start(f32[1,2,64,256]{3,2,1,0:T(8,128)S(1)} %slice.18), channel_id=1, source_target_pairs={{0,2},{1,3},{2,6},{3,7},{4,0},{5,1},{6,10},{7,11},{8,4},{9,5},{10,... | collective-permute-start | bytes 393224 | tf_op jit(solution)/shard_map/ppermute | solution.py:77
  44.7 5.0 %collective-permute-start.15 = (f32[1,2,64,256]{3,2,1,0:T(8,128)S(1)}, f32[1,2,64,256]{3,2,1,0:T(8,128)S(1)}, u32[]{:S(2)}, u32[]{:S(2)}) collective-permute-start(f32[1,2,64,256]{3,2,1,0:T(8,128)S(1)} %slice.13), channel_id=1, source_target_pairs={{0,2},{1,3},{2,6},{3,7},{4,0},{5,1},{6,10},{7,11},{8,4},{9,5},{10,... | collective-permute-start | bytes 393224 | tf_op jit(solution)/shard_map/ppermute | solution.py:77
  44.8 5.2 %collective-permute-start.5 = (f32[1,2,64,256]{3,2,1,0:T(8,128)S(1)}, f32[1,2,64,256]{3,2,1,0:T(8,128)S(1)}, u32[]{:S(2)}, u32[]{:S(2)}) collective-permute-start(f32[1,2,64,256]{3,2,1,0:T(8,128)S(1)} %slice.16), channel_id=1, source_target_pairs={{0,4},{1,5},{2,0},{3,1},{4,8},{5,9},{6,2},{7,3},{8,12},{9,13},{10,... | collective-permute-start | bytes 393224 | tf_op jit(solution)/shard_map/ppermute | solution.py:77
  50.4 1.4 %collective-permute-start.18 = (f32[128,256]{1,0:T(8,128)S(1)}, f32[128,256]{1,0:T(8,128)S(1)}, u32[]{:S(2)}, u32[]{:S(2)}) collective-permute-start(f32[128,256]{1,0:T(8,128)S(1)} %get-tuple-element.43.e0_ref), channel_id=1, source_target_pairs={{0,1},{1,0},{2,3},{3,2},{4,5},{5,4},{6,7},{7,6},{8,9},{9,8},{10,11... | collective-permute-start | bytes 393224 | tf_op jit(solution)/shard_map/ppermute | solution.py:330
  58.2 1.4 %collective-permute-start.19 = (f32[128,256]{1,0:T(8,128)S(1)}, f32[128,256]{1,0:T(8,128)S(1)}, u32[]{:S(2)}, u32[]{:S(2)}) collective-permute-start(f32[128,256]{1,0:T(8,128)S(1)} %get-tuple-element.46.e0_ref), channel_id=1, source_target_pairs={{0,1},{1,0},{2,3},{3,2},{4,5},{5,4},{6,7},{7,6},{8,9},{9,8},{10,11... | collective-permute-start | bytes 393224 | tf_op jit(solution)/shard_map/ppermute | solution.py:330
  65.6 1.7 %collective-permute-start.20 = (f32[128,256]{1,0:T(8,128)S(1)}, f32[128,256]{1,0:T(8,128)S(1)}, u32[]{:S(2)}, u32[]{:S(2)}) collective-permute-start(f32[128,256]{1,0:T(8,128)S(1)} %get-tuple-element.49.e0_ref), channel_id=1, source_target_pairs={{0,1},{1,0},{2,3},{3,2},{4,5},{5,4},{6,7},{7,6},{8,9},{9,8},{10,11... | collective-permute-start | bytes 393224 | tf_op jit(solution)/shard_map/ppermute | solution.py:330
  66.8 6.9 %collective-permute-start.22 = (f32[2,64,256]{2,1,0:T(8,128)S(1)}, f32[2,64,256]{2,1,0:T(8,128)S(1)}, u32[]{:S(2)}, u32[]{:S(2)}) collective-permute-start(f32[2,64,256]{2,1,0:T(8,128)S(1)} %get-tuple-element.54), channel_id=1, source_target_pairs={{0,1},{1,0},{2,3},{3,2},{4,5},{5,4},{6,7},{7,6},{8,9},{9,8},{10,11... | collective-permute-start | bytes 393224 | tf_op jit(solution)/shard_map/ppermute | solution.py:383
  73.1 1.4 %collective-permute-start.21 = (f32[128,256]{1,0:T(8,128)S(1)}, f32[128,256]{1,0:T(8,128)S(1)}, u32[]{:S(2)}, u32[]{:S(2)}) collective-permute-start(f32[128,256]{1,0:T(8,128)S(1)} %get-tuple-element.52.e0_ref), channel_id=1, source_target_pairs={{0,1},{1,0},{2,3},{3,2},{4,5},{5,4},{6,7},{7,6},{8,9},{9,8},{10,11... | collective-permute-start | bytes 393224 | tf_op jit(solution)/shard_map/ppermute | solution.py:330
  73.4 5.4 %collective-permute-start.23 = (f32[2,2,64,256]{3,2,1,0:T(8,128)S(1)}, f32[2,2,64,256]{3,2,1,0:T(8,128)S(1)}, u32[]{:S(2)}, u32[]{:S(2)}) collective-permute-start(f32[2,2,64,256]{3,2,1,0:T(8,128)S(1)} %get-tuple-element.58), channel_id=1, source_target_pairs={{0,1},{1,0},{2,3},{3,2},{4,5},{5,4},{6,7},{7,6},{8,9},{9,8},{10,11... | collective-permute-start | bytes 786440 | tf_op jit(solution)/shard_map/ppermute | solution.py:384

commit v4 on v3

--- a/solution.py
+++ b/solution.py
@@ -46,8 +46,8 @@
             index = index & ~(1 << b) | (chip >> j & 1) << b
         return index
 
-    def ring(self, step, flipped=0):
-        return [(i, self.shifted(i, step) ^ flipped << self.gate_bits[0]) for i in range(self.size)]
+    def ring(self, step):
+        return [(i, self.shifted(i, step)) for i in range(self.size)]
 
     def flip(self, bit):
         return [(i, i ^ 1 << bit) for i in range(self.size)]
@@ -67,15 +67,19 @@
         return jnp.where(position < self.chips // 2, position << 1, (self.chips - 1 - position) << 1 | 1)
 
 
-def gather_ring(home, layout, before_last=lambda ends: ends):
-    half = layout.chips // 2
+STEPS = (1, -1)
+
+
+def gather_ring(home, layout):
     blocks, ends = [home], [home, home]
-    for _ in range(1, half):
-        ends = [lax.ppermute(end, "long", layout.ring(step)) for end, step in zip(ends, (1, -1))]
+    for _ in range(1, layout.chips // 2):
+        ends = [lax.ppermute(end, "long", layout.ring(step)) for end, step in zip(ends, STEPS)]
         blocks += ends
-    ends = before_last(ends)
-    opposite = [lax.ppermute(ends[k][k : k + 1], "long", layout.ring(1 - 2 * k)) for k in range(2)]
-    return blocks, opposite
+    return blocks, [ends[0][:1], ends[1][1:]]
+
+
+def last_step(tail, layout):
+    return [lax.ppermute(end, "long", layout.ring(step)) for end, step in zip(tail, STEPS)]
 
 
 def split(x):
@@ -101,15 +105,17 @@
     return jnp.concatenate([jnp.concatenate([a[:, :n], -a[:, n:]], 1), jnp.concatenate([a[:, n:], a[:, :n]], 1)], 0)
 
 
-def polar(e):
+def polar(e, beside=lambda gap: None):
     x = e * lax.rsqrt(jnp.sum(e * e) + 1e-6)
-    for _ in range(NS_ITERS):
+    n = x.shape[0]
+    for k in range(NS_ITERS):
         xs = split(x)
-        rows = [jnp.concatenate([v, turned(v)], 0) for v in xs]
-        turns = [v[v.shape[0] // 2 :] for v in rows]
+        turns = [turned(v) for v in xs]
+        beside(2 * k)
         h = split(jnp.concatenate([dot3(xs, xs, NT), dot3(xs, turns, NT)], 1))
+        beside(2 * k + 1)
+        rows = [jnp.concatenate(pair, 0) for pair in zip(xs, turns)]
         both = dot(jnp.concatenate(h, 0), rows[0], NN)
-        n = x.shape[0]
         x = 1.5 * x - 0.5 * (both[:n] + both[n:] + dot(h[0], rows[1], NN))
     return x
 
@@ -159,15 +165,14 @@
         out_ref[plane] = jnp.concatenate([low, high], 0).T
 
 
-def pack_kernel(layout, *refs):
+def pack_kernel(layout, x_ref, own_ref, sent_ref):
     core, _ = layout.place_of(lax.axis_index("long"))
-    n = refs[0].shape[2] // 2
-    for x_ref, own_ref, sent_ref in ((refs[0], *refs[2:4]), (refs[1], *refs[4:6])):
-        for plane in range(2):
-            t = x_ref[plane].T
-            low, high = t[:n], t[n:]
-            own_ref[plane] = jnp.where(core == 0, low, high)
-            sent_ref[plane] = jnp.where(core == 0, high, low)
+    n = x_ref.shape[2] // 2
+    for plane in range(2):
+        t = x_ref[plane].T
+        low, high = t[:n], t[n:]
+        own_ref[plane] = jnp.where(core == 0, low, high)
+        sent_ref[plane] = jnp.where(core == 0, high, low)
 
 
 TURN = 1
@@ -203,13 +208,17 @@
         place(halves[slot][0], target, chip * 2 + (slot ^ core))
 
 
-def line_kernel(layout, gates_ref, *refs):
-    *blocks, phi0_ref, phi1_ref, phi2_ref = refs
-    core, chips = layout.place_of(lax.axis_index("long"))
-    place_blocks(blocks, chips, core, phi0_ref)
+def first_gate_kernel(layout, gates_ref, *refs):
+    *blocks, phi_ref = refs
+    core, chips = layout.place_of(lax.axis_index("long"))
+    place_blocks(blocks, chips, core, phi_ref)
     gate = gate_matrix(gates_ref, 0)
     for pair in near_pairs(layout, chips[-1]):
-        apply_at(gate, phi0_ref, phi0_ref, pair)
+        apply_at(gate, phi_ref, phi_ref, pair)
+
+
+def line_kernel(layout, gates_ref, phi0_ref, phi1_ref, phi2_ref):
+    _, chips = layout.place_of(lax.axis_index("long"))
     for s, source, target in ((1, phi0_ref, phi1_ref), (2, phi1_ref, phi2_ref)):
         gate = gate_matrix(gates_ref, s)
         for pair in line_pairs(layout, layout.local_bits[s], chips[0] & 1):
@@ -251,30 +260,91 @@
         out[...] = joined(next_ref, chips[0] * 2 + (slot ^ core))
 
 
-def ends_kernel(layout, psi_ref, own_ref, sent_ref):
-    core, chips = layout.place_of(lax.axis_index("long"))
-    for slot, out in enumerate((own_ref, sent_ref)):
-        for t, d in enumerate(last_pair(layout, chips[0] * 2 + (slot ^ core))):
-            out[t] = joined(psi_ref, d)
-
-
-def section_kernel(layout, section, e0_ref, e1_ref, phi_ref, psi_ref, psi_next, e_ref):
-    gate = split(as_matrix(polar(e0_ref[...] + e1_ref[...])))
-    for pair in all_pairs(layout, layout.local_bits[section]):
-        apply_at(gate, psi_ref, psi_next, pair)
-    e_ref[...] = folded(environment(phi_ref, psi_next, all_pairs(layout, layout.local_bits[section + 1])))
-
-
 def last_pair(layout, d):
     bit = layout.local_bits[SECTIONS - 1]
     first = d & ~(1 << bit)
     return first, first + (1 << bit)
 
 
-def last_polar_kernel(layout, e0_ref, e1_ref, phi_own, phi_got, gate_ref, adjoint_ref):
+def insert_bits(rest, bits):
+    for bit in sorted(bits):
+        rest = (rest >> bit << bit + 1) + (rest & (1 << bit) - 1)
+    return rest
+
+
+def load_quad(ref, rest, bits, plane):
+    d = insert_bits(rest, bits)
+    quad = [d + (t1 << bits[0]) + (t0 << bits[1]) for t1 in range(2) for t0 in range(2)]
+    return [jnp.concatenate([ref[k, q, plane] for q in quad], 0) for k in range(2)]
+
+
+def section_kernel(layout, section, e0_ref, e1_ref, phi_ref, psi_ref, gate_ref, e_ref, joint, left):
+    bits = layout.local_bits[section + 1], layout.local_bits[section]
+    rests = psi_ref.shape[1] // 4
+    q = joint.shape[0] // 2
+    c = q // 4
+    units = [(rest, p, u) for rest in range(rests) for p in range(2) for u in range(2)]
+    gaps = 2 * NS_ITERS - 2
+
+    def add(rest, p, u):
+        term = dot3(load_quad(phi_ref, rest, bits, p), load_quad(psi_ref, rest, bits, u), NT)
+        at = (slice(p * q, p * q + q), slice(u * q, u * q + q))
+        joint[at] = term if rest == 0 else joint[at] + term
+
+    def arrange(p):
+        real = joint[:q, :q] + joint[q:, q:] if p == 0 else joint[q:, :q] - joint[:q, q:]
+        for k, v in enumerate(split(real)):
+            for u1 in range(2):
+                for t1 in range(2):
+                    for t0 in range(2):
+                        rows = slice((u1 * 2 + t1) * c, (u1 * 2 + t1 + 1) * c)
+                        lanes = slice((p * 2 + t0) * 2 * c, (p * 2 + t0 + 1) * 2 * c)
+                        left[k, rows, lanes] = v[(t1 * 2 + t0) * c : (t1 * 2 + t0 + 1) * c, u1 * 2 * c : (u1 + 1) * 2 * c]
+
+    def beside(gap):
+        for unit in units[gap * len(units) // gaps : (gap + 1) * len(units) // gaps] if gap < gaps else ():
+            add(*unit)
+        if gap >= gaps:
+            arrange(gap - gaps)
+
+    x = polar(e0_ref[...] + e1_ref[...], beside)
+    right = []
+    for v in split(x):
+        r0, r1, i0, i1 = v[:c, : 2 * c], v[c:, : 2 * c], v[:c, 2 * c :], v[c:, 2 * c :]
+        right.append(
+            jnp.concatenate([jnp.concatenate([r0, r1, i0, i1], 1), jnp.concatenate([-i0, -i1, r0, r1], 1)], 0)
+        )
+    out = dot3((left[0], left[1]), right, NT)
+    first, second = out[: 2 * c], out[2 * c :]
+    e_ref[...] = jnp.concatenate([first[:, :c], second[:, :c], first[:, c:], second[:, c:]], 1)
+    gate_ref[0], gate_ref[1] = split(as_matrix(x))
+
+
+def apply_kernel(layout, section, gate_ref, psi_ref, next_ref):
+    gate = gate_ref[0], gate_ref[1]
+    for pair in all_pairs(layout, layout.local_bits[section]):
+        apply_at(gate, psi_ref, next_ref, pair)
+
+
+def ends_kernel(layout, gate_ref, psi_ref, own_ref, sent_ref):
+    core, chips = layout.place_of(lax.axis_index("long"))
+    gate = gate_ref[0], gate_ref[1]
+    n = own_ref.shape[2]
+    for t, first in enumerate(last_pair(layout, chips[0] * 2)):
+        y = dot3(gate, load_pair(psi_ref, (first, first + 1)), NN)
+        for plane in range(2):
+            low, high = y[2 * plane * n : (2 * plane + 1) * n], y[(2 * plane + 1) * n : (2 * plane + 2) * n]
+            own_ref[t, plane] = jnp.where(core == 0, low, high)
+            sent_ref[t, plane] = jnp.where(core == 0, high, low)
+
+
+def last_polar_kernel(e0_ref, e1_ref, gate_ref):
+    gate_ref[...] = as_matrix(polar(e0_ref[...] + e1_ref[...]))
+
+
+def unpack_kernel(layout, own_ref, got_ref, out_ref):
     core, _ = layout.place_of(lax.axis_index("long"))
-    gate_ref[...] = as_matrix(polar(e0_ref[...] + e1_ref[...]))
-    unpacked(core, phi_own, phi_got, adjoint_ref)
+    unpacked(core, own_ref, got_ref, out_ref)
 
 
 def last_apply_kernel(layout, gate_ref, psi_own, psi_got, state_ref):
@@ -332,59 +402,68 @@
     def home(own, sent):
         return jnp.stack([own, lax.ppermute(sent, "long", core_flip)])
 
-    phi_own, phi_sent, psi_own, psi_sent = call(
-        kernel(pack_kernel),
-        "pack",
-        [slab] * 4,
-        [adjoint_state, initial_state],
-        0,
-    )
-    phi_home = home(phi_own, phi_sent)
+    def pack(state):
+        return call(kernel(pack_kernel), "pack", [slab] * 2, [state], 0)
+
+    def after(x, *others):
+        return lax.optimization_barrier((x, *others))[0]
+
+    phi_home = home(*pack(adjoint_state))
+    psi_own, psi_sent = pack(initial_state)
     phi_home, psi_own, psi_sent = lax.optimization_barrier((phi_home, psi_own, psi_sent))
-    phi_near, phi_far = gather_ring(phi_home, layout)
-    phis = list(
-        call(kernel(line_kernel), "line", [pieces] * 3, [current_gates] + phi_near, 7 * apply_flops // 4)
-    )
-
-    def after_line(ends):
-        return [ends[0], lax.optimization_barrier((ends[1], phis[0]))[0]]
-
-    psi_near, psi_far = gather_ring(home(psi_own, psi_sent), layout, after_line)
+    phi_near, phi_tail = gather_ring(phi_home, layout)
+    phis = [call(kernel(first_gate_kernel), "first_gate", [pieces], [current_gates] + phi_near, apply_flops)[0]]
+    phi_far = last_step(phi_tail, layout)
+    phis += call(kernel(line_kernel), "line", [pieces] * 2, [current_gates, phis[0]], apply_flops)
+    psi_near, psi_tail = gather_ring(home(psi_own, psi_sent), layout)
+    psi_far = last_step([psi_tail[0], after(psi_tail[1], phis[1])], layout)
     ins = [current_gates] + psi_near + phi_far + [phis[0]]
     phis[0], psi, total = call(
         kernel(near_kernel), "near", [pieces, pieces, square], ins, apply_flops, aliases={len(ins) - 1: 0}
     )
+
+    def other_line(section):
+        ins = [current_gates, phis[section - 1], phis[section]]
+        return call(
+            kernel(other_line_kernel, section), "other_line", [pieces], ins, apply_flops // 2, aliases={2: 0}
+        )[0]
+
+    phis[1] = other_line(1)
+    phis[2] = other_line(2)
+    total = after(total, phis[2])
     psi, e = call(
         kernel(far_kernel), "far", [pieces, env], psi_far + [total, phis[0], psi], apply_flops // 4, aliases={4: 0}
     )
+    gate_pair = jax.ShapeDtypeStruct((2,) + square.shape, BF16)
     for section in range(SECTIONS - 1):
         e0, e1 = both(e)
-        if section < SECTIONS - 2:
-            (phi,) = call(
-                kernel(other_line_kernel, section + 1),
-                "other_line",
-                [pieces],
-                [current_gates, phis[section], phis[section + 1]],
-                apply_flops // 2,
-                aliases={2: 0},
-            )
-            phis[section + 1] = phi
-        else:
+        if section == 0:
             phi, phi_own, phi_sent = call(
                 kernel(last_adjoint_kernel),
                 "last_adjoint",
                 [pieces, slab, slab],
-                [current_gates, phis[section]],
+                [current_gates, phis[2]],
                 apply_flops,
             )
-        psi, e = call(kernel(section_kernel, section), "section", [pieces, env], [e0, e1, phi, psi], 3 * apply_flops)
+            phis.append(phi)
+            psi = after(psi, phi)
+        else:
+            (psi,) = call(kernel(apply_kernel, section - 1), "apply", [pieces], [gate, psi], apply_flops)
+        if section == 1:
+            phi_got = lax.ppermute(after(phi_sent, e), "long", core_flip)
+        gate, e = call(
+            kernel(section_kernel, section),
+            "section",
+            [gate_pair, env],
+            [e0, e1, phis[section + 1], psi],
+            4 * apply_flops,
+            [pltpu.VMEM((4 * lanes, 4 * lanes), F32), pltpu.VMEM((2, 2 * lanes, 4 * lanes), BF16)],
+        )
     e0, e1 = both(e)
-    psi_own, psi_sent = call(kernel(ends_kernel), "ends", [two_slabs, two_slabs], [psi], 0)
-    phi_got = lax.ppermute(phi_sent, "long", core_flip)
+    psi_own, psi_sent = call(kernel(ends_kernel), "ends", [two_slabs, two_slabs], [gate, psi], apply_flops // 4)
     psi_got = lax.ppermute(psi_sent, "long", core_flip)
-    gate, final_adjoint = call(
-        kernel(last_polar_kernel), "last_polar", [square, whole], [e0, e1, phi_own, phi_got], 2 * apply_flops
-    )
+    (final_adjoint,) = call(kernel(unpack_kernel), "unpack", [whole], [after(phi_own, e), phi_got], 0)
+    (gate,) = call(last_polar_kernel, "last_polar", [square], [e0, e1], 2 * apply_flops)
     (final_state,) = call(
         kernel(last_apply_kernel), "last_apply", [whole], [gate, psi_own, psi_got], apply_flops // 4
     )

time: 80.1 us -> 76.5 us (0.955)
  waiting for transfers between devices: 25.9 us -> 22.3 us
    ppermute x4, waiting for transfers between devices: 2.06 us -> 0.48 us  [both(): return (e, lax.ppermute(e, 'long', core_flip))]
    ppermute x5, waiting for transfers between devices: 1.48 us -> 0.47 us  [the longest x4 0.47 us: last_step(): lax.ppermute(end, 'long', layout.ring(step))]
    ppermute x2, waiting for transfers between devices: 0.99 us -> 0.01 us  [home(): return jnp.stack([own, lax.ppermute(sent, 'long', core_flip)])]
    pallas_call x13 -> x18, Pallas kernels: 31.3 us -> 31.3 us  [call(): pl.pallas_call(kernel, out_shape=outs, in_specs=[spec] * len(ins), out_sp...]
  transfers between devices with their start and end apart: 24 -> 24, of which waited for: 13 -> 9; matrix products, arithmetic and copies ran while one was open for 0% -> 0% of each run, Pallas kernels for 22% -> 25%
where the time goes in v4:
time: 76.5 us; the launch traced here: 76.3 us
  Pallas kernels  31.3 us (41%)
  waiting for transfers between devices  22.3 us (29%)
  starting transfers between devices  19.9 us (26%)
  local copies, waits for them, and re-layouts  1.93 us (3%)
  between operations  0.86 us (1%)
    pallas_call x18, Pallas kernels, call(): pl.pallas_call(kernel, out_shape=outs, in_specs=[spec] * len(ins), out_sp...  31.3 us
    ppermute x12, waiting for transfers between devices, gather_ring(): lax.ppermute(end, 'long', layout.ring(step))  21.4 us
    ppermute x12, starting transfers between devices, gather_ring(): lax.ppermute(end, 'long', layout.ring(step))  13 us
    ppermute x4, starting transfers between devices, last_step(): lax.ppermute(end, 'long', layout.ring(step))  4.46 us
    unnamed x6, local copies, waits for them, and re-layouts  1.9 us
  transfers between devices with their start and end apart: 24, of which 9 were waited for; matrix products, arithmetic and copies ran while one was open for 0% of the time, Pallas kernels for 25%

profile of v4, /device:TPU:0, one launch (start us, length us, event | category | flops | bytes accessed | tf_op | source)
XLA Modules:
  0.0 76.3 jit_solution(1633825087694345507)
XLA Ops:
  0.6 0.9 %copy-done.1 = f32[2,256,128]{2,1,0:T(8,128)S(1)} copy-done((f32[2,256,128]{2,1,0:T(8,128)S(1)}, f32[2,256,128]{2,1,0:T(8,128)}, u32[]{:S(2)}) %copy-start.1) | copy-done | bytes 262168
  1.6 0.1 pack.2
  1.7 0.5 collective-permute-start
  2.2 0.9 %copy-done.2 = f32[2,256,128]{2,1,0:T(8,128)S(1)} copy-done((f32[2,256,128]{2,1,0:T(8,128)S(1)}, f32[2,256,128]{2,1,0:T(8,128)}, u32[]{:S(2)}) %copy-start.2) | copy-done | bytes 262168
  3.2 0.1 pack.3
  3.3 0.0 collective-permute-done
  3.4 0.3 collective-permute-start.1
  3.7 2.8 %collective-permute-start.10 = (f32[2,2,64,256]{3,2,1,0:T(8,128)S(1)}, f32[2,2,64,256]{3,2,1,0:T(8,128)S(1)}, u32[]{:S(2)}, u32[]{:S(2)}) collective-permute-start(f32[2,2,64,256]{3,2,1,0:T(8,128)S(1)} %pad_maximum_fusion.refs_0_), channel_id=1, source_target_pairs={{0,2},{1,3},{2,6},{3,7},{4,0},{5,1},{6,10},{7,11},{8,4},{9,5},{10,... | collective-permute-start | bytes 786440 | tf_op jit(solution)/shard_map/ppermute | solution.py:76
  6.5 0.1 collective-permute-start.9
  6.5 0.0 collective-permute-done.1
  6.5 2.1 %collective-permute-start.2 = (f32[2,2,64,256]{3,2,1,0:T(8,128)S(1)}, f32[2,2,64,256]{3,2,1,0:T(8,128)S(1)}, u32[]{:S(2)}, u32[]{:S(2)}) collective-permute-start(f32[2,2,64,256]{3,2,1,0:T(8,128)S(1)} %pad_maximum_fusion.1.refs_0_), channel_id=1, source_target_pairs={{0,4},{1,5},{2,0},{3,1},{4,8},{5,9},{6,2},{7,3},{8,12},{9,13},{10,... | collective-permute-start | bytes 786440 | tf_op jit(solution)/shard_map/ppermute | solution.py:76
  8.6 0.0 collective-permute-start.6
  8.6 5.0 %collective-permute-done.10.refs_2_ = f32[2,2,64,256]{3,2,1,0:T(8,128)S(1)} collective-permute-done((f32[2,2,64,256]{3,2,1,0:T(8,128)S(1)}, f32[2,2,64,256]{3,2,1,0:T(8,128)S(1)}, u32[]{:S(2)}, u32[]{:S(2)}) %collective-permute-start.10) | collective-permute-done | bytes 262176 | tf_op jit(solution)/shard_map/ppermute | solution.py:76
  13.6 2.0 %collective-permute-start.12 = (f32[2,2,64,256]{3,2,1,0:T(8,128)S(1)}, f32[2,2,64,256]{3,2,1,0:T(8,128)S(1)}, u32[]{:S(2)}, u32[]{:S(2)}) collective-permute-start(f32[2,2,64,256]{3,2,1,0:T(8,128)S(1)} %collective-permute-done.10.refs_2_), channel_id=1, source_target_pairs={{0,2},{1,3},{2,6},{3,7},{4,0},{5,1},{6,10},{7,11},{8,4},{9,5},{10,... | collective-permute-start | bytes 786440 | tf_op jit(solution)/shard_map/ppermute | solution.py:76
  15.6 0.0 collective-permute-done.9.refs_1_
  15.6 0.0 collective-permute-start.11
  15.7 5.6 %collective-permute-done.2.refs_1_ = f32[2,2,64,256]{3,2,1,0:T(8,128)S(1)} collective-permute-done((f32[2,2,64,256]{3,2,1,0:T(8,128)S(1)}, f32[2,2,64,256]{3,2,1,0:T(8,128)S(1)}, u32[]{:S(2)}, u32[]{:S(2)}) %collective-permute-start.2) | collective-permute-done | bytes 262176 | tf_op jit(solution)/shard_map/ppermute | solution.py:76
  21.3 0.0 collective-permute-start.3
  21.3 0.0 collective-permute-done.6.refs_2_
  21.3 2.0 %collective-permute-start.7 = (f32[2,2,64,256]{3,2,1,0:T(8,128)S(1)}, f32[2,2,64,256]{3,2,1,0:T(8,128)S(1)}, u32[]{:S(2)}, u32[]{:S(2)}) collective-permute-start(f32[2,2,64,256]{3,2,1,0:T(8,128)S(1)} %collective-permute-done.6.refs_2_), channel_id=1, source_target_pairs={{0,2},{1,3},{2,6},{3,7},{4,0},{5,1},{6,10},{7,11},{8,4},{9,5},{10,... | collective-permute-start | bytes 786440 | tf_op jit(solution)/shard_map/ppermute | solution.py:76
  23.3 1.5 %collective-permute-done.12.refs_4_ = f32[2,2,64,256]{3,2,1,0:T(8,128)S(1)} collective-permute-done((f32[2,2,64,256]{3,2,1,0:T(8,128)S(1)}, f32[2,2,64,256]{3,2,1,0:T(8,128)S(1)}, u32[]{:S(2)}, u32[]{:S(2)}) %collective-permute-start.12) | collective-permute-done | bytes 262176 | tf_op jit(solution)/shard_map/ppermute | solution.py:76
  24.8 2.0 %collective-permute-start.14 = (f32[2,2,64,256]{3,2,1,0:T(8,128)S(1)}, f32[2,2,64,256]{3,2,1,0:T(8,128)S(1)}, u32[]{:S(2)}, u32[]{:S(2)}) collective-permute-start(f32[2,2,64,256]{3,2,1,0:T(8,128)S(1)} %collective-permute-done.12.refs_4_), channel_id=1, source_target_pairs={{0,2},{1,3},{2,6},{3,7},{4,0},{5,1},{6,10},{7,11},{8,4},{9,5},{10,... | collective-permute-start | bytes 786440 | tf_op jit(solution)/shard_map/ppermute | solution.py:76
  26.8 0.0 collective-permute-done.11.refs_3_
  26.9 0.0 collective-permute-start.13
  26.9 5.6 %collective-permute-done.3.refs_3_ = f32[2,2,64,256]{3,2,1,0:T(8,128)S(1)} collective-permute-done((f32[2,2,64,256]{3,2,1,0:T(8,128)S(1)}, f32[2,2,64,256]{3,2,1,0:T(8,128)S(1)}, u32[]{:S(2)}, u32[]{:S(2)}) %collective-permute-start.3) | collective-permute-done | bytes 262176 | tf_op jit(solution)/shard_map/ppermute | solution.py:76
  32.5 0.0 collective-permute-start.4
  32.5 0.0 collective-permute-done.7.refs_4_
  32.5 2.0 %collective-permute-start.8 = (f32[2,2,64,256]{3,2,1,0:T(8,128)S(1)}, f32[2,2,64,256]{3,2,1,0:T(8,128)S(1)}, u32[]{:S(2)}, u32[]{:S(2)}) collective-permute-start(f32[2,2,64,256]{3,2,1,0:T(8,128)S(1)} %collective-permute-done.7.refs_4_), channel_id=1, source_target_pairs={{0,2},{1,3},{2,6},{3,7},{4,0},{5,1},{6,10},{7,11},{8,4},{9,5},{10,... | collective-permute-start | bytes 786440 | tf_op jit(solution)/shard_map/ppermute | solution.py:76
  34.5 1.7 %collective-permute-done.14.refs_6_ = f32[2,2,64,256]{3,2,1,0:T(8,128)S(1)} collective-permute-done((f32[2,2,64,256]{3,2,1,0:T(8,128)S(1)}, f32[2,2,64,256]{3,2,1,0:T(8,128)S(1)}, u32[]{:S(2)}, u32[]{:S(2)}) %collective-permute-start.14) | collective-permute-done | bytes 262176 | tf_op jit(solution)/shard_map/ppermute | solution.py:76
  36.2 2.0 %collective-permute-start.17 = (f32[1,2,64,256]{3,2,1,0:T(8,128)S(1)}, f32[1,2,64,256]{3,2,1,0:T(8,128)S(1)}, u32[]{:S(2)}, u32[]{:S(2)}) collective-permute-start(f32[1,2,64,256]{3,2,1,0:T(8,128)S(1)} %slice.19), channel_id=1, source_target_pairs={{0,2},{1,3},{2,6},{3,7},{4,0},{5,1},{6,10},{7,11},{8,4},{9,5},{10,... | collective-permute-start | bytes 393224 | tf_op jit(solution)/shard_map/ppermute | solution.py:82
  38.2 0.0 collective-permute-done.13.refs_5_
  38.2 0.1 collective-permute-start.16
  38.4 2.4 %first_gate.1.phi0_ref.refs_9_ = bf16[2,16,2,64,256]{4,3,2,1,0:T(8,128)(2,1)S(1)} custom-call(f32[4,2,128,128]{3,2,1,0:T(8,128)S(1)} %copy-done, f32[2,2,64,256]{3,2,1,0:T(8,128)S(1)} %pad_maximum_fusion.refs_0_, f32[2,2,64,256]{3,2,1,0:T(8,128)S(1)} %collective-permute-done.9.refs_1_, f32[2,2,64,256]{3,2,1,0:T(8,128)S(1)} %collective-permute-done.10.refs_2_, ...), custom_call_target="tpu_custom_call" | custom-call | flops 805306368 | bytes 4456448 | tf_op jit(solution)/shard_map/first_gate/pallas_call | solution.py:367
  40.8 1.0 %line.1 = (bf16[2,16,2,64,256]{4,3,2,1,0:T(8,128)(2,1)S(1)}, bf16[2,16,2,64,256]{4,3,2,1,0:T(8,128)(2,1)S(1)}) custom-call(f32[4,2,128,128]{3,2,1,0:T(8,128)S(1)} %copy-done, bf16[2,16,2,64,256]{4,3,2,1,0:T(8,128)(2,1)S(1)} %first_gate.1.phi0_ref.refs_9_), custom_call_target="tpu_custom_call" | custom-call | flops 805306368 | bytes 6815744 | tf_op jit(solution)/shard_map/line/pallas_call | solution.py:367
  41.8 1.9 %collective-permute-done.4.refs_5_ = f32[2,2,64,256]{3,2,1,0:T(8,128)S(1)} collective-permute-done((f32[2,2,64,256]{3,2,1,0:T(8,128)S(1)}, f32[2,2,64,256]{3,2,1,0:T(8,128)S(1)}, u32[]{:S(2)}, u32[]{:S(2)}) %collective-permute-start.4) | collective-permute-done | bytes 262176 | tf_op jit(solution)/shard_map/ppermute | solution.py:76
  43.7 0.1 collective-permute-start.5
  43.9 0.0 collective-permute-done.8.refs_6_
  43.9 2.2 %collective-permute-start.15 = (f32[1,2,64,256]{3,2,1,0:T(8,128)S(1)}, f32[1,2,64,256]{3,2,1,0:T(8,128)S(1)}, u32[]{:S(2)}, u32[]{:S(2)}) collective-permute-start(f32[1,2,64,256]{3,2,1,0:T(8,128)S(1)} %slice.17), channel_id=1, source_target_pairs={{0,2},{1,3},{2,6},{3,7},{4,0},{5,1},{6,10},{7,11},{8,4},{9,5},{10,... | collective-permute-start | bytes 393224 | tf_op jit(solution)/shard_map/ppermute | solution.py:82
  46.1 0.5 collective-permute-done.16.refs_7_
  46.5 1.5 %near.1 = (bf16[2,16,2,64,256]{4,3,2,1,0:T(8,128)(2,1)S(1)}, bf16[2,16,2,64,256]{4,3,2,1,0:T(8,128)(2,1)S(1)}, f32[256,256]{1,0:T(8,128)S(1)}) custom-call(f32[4,2,128,128]{3,2,1,0:T(8,128)S(1)} %copy-done, f32[2,2,64,256]{3,2,1,0:T(8,128)S(1)} %pad_maximum_fusion.1.refs_0_, ...), custom_call_target="tpu_custom_call", output_to_operand_aliasing={{0}: (10, {})} | custom-call | flops 805306368 | bytes 9175040 | tf_op jit(solution)/shard_map/near/pallas_call | solution.py:367
  48.0 0.6 other_line.2.phi_ref
  48.6 0.6 other_line.3.phi_ref
  49.2 0.0 collective-permute-done.15.psi_b
  49.2 0.4 far.1
  49.7 0.1 collective-permute-start.18
  49.8 1.0 %last_adjoint.1 = (bf16[2,16,2,64,256]{4,3,2,1,0:T(8,128)(2,1)S(1)}, f32[2,64,256]{2,1,0:T(8,128)S(1)}, f32[2,64,256]{2,1,0:T(8,128)S(1)}) custom-call(f32[4,2,128,128]{3,2,1,0:T(8,128)S(1)} %copy-done, bf16[2,16,2,64,256]{4,3,2,1,0:T(8,128)(2,1)S(1)} %other_line.3.phi_ref), custom_call_target="tpu_custom_call" | custom-call | flops 805306368 | bytes 4980736 | tf_op jit(solution)/shard_map/last_adjoint/pallas_call | solution.py:367
  50.8 0.3 collective-permute-done.18.e1_ref
  51.1 5.1 %section.3 = (bf16[2,256,256]{2,1,0:T(8,128)(2,1)S(1)}, f32[128,256]{1,0:T(8,128)S(1)}) custom-call(f32[128,256]{1,0:T(8,128)S(1)} %get-tuple-element.46.e0_ref, f32[128,256]{1,0:T(8,128)S(1)} %collective-permute-done.18.e1_ref, bf16[2,16,2,64,256]{4,3,2,1,0:T(8,128)(2,1)S(1)} %other_line.2.phi_ref, bf16[2,16,2,64,256]{4,3,2,1,0:T(8,128)(2,1)S(1)} %get-tuple-element.49.psi_ref), custom_call_target="tpu_custom_call" | custom-call | flops 3221225472 | bytes 4849664 | tf_op jit(solution)/shard_map/section/pallas_call | solution.py:367
  56.2 0.3 collective-permute-start.19
  56.5 1.0 %apply.2.psi_ref = bf16[2,16,2,64,256]{4,3,2,1,0:T(8,128)(2,1)S(1)} custom-call(bf16[2,256,256]{2,1,0:T(8,128)(2,1)S(1)} %get-tuple-element.51.gate_ref, bf16[2,16,2,64,256]{4,3,2,1,0:T(8,128)(2,1)S(1)} %get-tuple-element.49.psi_ref), custom_call_target="tpu_custom_call" | custom-call | flops 805306368 | bytes 4456448 | tf_op jit(solution)/shard_map/apply/pallas_call | solution.py:367
  57.5 0.2 collective-permute-done.19.e1_ref
  57.6 5.1 %section.4 = (bf16[2,256,256]{2,1,0:T(8,128)(2,1)S(1)}, f32[128,256]{1,0:T(8,128)S(1)}) custom-call(f32[128,256]{1,0:T(8,128)S(1)} %get-tuple-element.50.e0_ref, f32[128,256]{1,0:T(8,128)S(1)} %collective-permute-done.19.e1_ref, bf16[2,16,2,64,256]{4,3,2,1,0:T(8,128)(2,1)S(1)} %other_line.3.phi_ref, bf16[2,16,2,64,256]{4,3,2,1,0:T(8,128)(2,1)S(1)} %apply.2.psi_ref), custom_call_target="tpu_custom_call" | custom-call | flops 3221225472 | bytes 4849664 | tf_op jit(solution)/shard_map/section/pallas_call | solution.py:367
  62.8 0.3 collective-permute-start.20
  63.0 0.3 collective-permute-start.23
  63.3 1.0 %apply.3.psi_ref = bf16[2,16,2,64,256]{4,3,2,1,0:T(8,128)(2,1)S(1)} custom-call(bf16[2,256,256]{2,1,0:T(8,128)(2,1)S(1)} %get-tuple-element.53.gate_ref, bf16[2,16,2,64,256]{4,3,2,1,0:T(8,128)(2,1)S(1)} %apply.2.psi_ref), custom_call_target="tpu_custom_call" | custom-call | flops 805306368 | bytes 4456448 | tf_op jit(solution)/shard_map/apply/pallas_call | solution.py:367
  64.3 0.0 collective-permute-done.20.e1_ref
  64.3 5.3 %section.5 = (bf16[2,256,256]{2,1,0:T(8,128)(2,1)S(1)}, f32[128,256]{1,0:T(8,128)S(1)}) custom-call(f32[128,256]{1,0:T(8,128)S(1)} %get-tuple-element.52.e0_ref, f32[128,256]{1,0:T(8,128)S(1)} %collective-permute-done.20.e1_ref, bf16[2,16,2,64,256]{4,3,2,1,0:T(8,128)(2,1)S(1)} %get-tuple-element.48.phi_ref, bf16[2,16,2,64,256]{4,3,2,1,0:T(8,128)(2,1)S(1)} %apply.3.psi_ref), custom_call_target="tpu_custom_call" | custom-call | flops 3221225472 | bytes 4849664 | tf_op jit(solution)/shard_map/section/pallas_call | solution.py:367
  69.7 0.3 collective-permute-start.21
  69.9 0.4 ends.1
  70.3 0.4 collective-permute-start.22
  70.7 0.0 collective-permute-done.23.got_ref
  70.7 0.8 %unpack.1 = f32[2,256,128]{2,1,0:T(8,128)} custom-call(f32[2,64,256]{2,1,0:T(8,128)S(1)} %get-tuple-element.59.own_ref, f32[2,64,256]{2,1,0:T(8,128)S(1)} %collective-permute-done.23.got_ref), custom_call_target="tpu_custom_call" | custom-call | bytes 524288 | tf_op jit(solution)/shard_map/unpack/pallas_call | solution.py:367
  71.5 3.6 %last_polar.1.gate_ref = f32[256,256]{1,0:T(8,128)S(1)} custom-call(f32[128,256]{1,0:T(8,128)S(1)} %get-tuple-element.54.e0_ref, f32[128,256]{1,0:T(8,128)S(1)} %collective-permute-done.21.e1_ref), custom_call_target="tpu_custom_call" | custom-call | flops 1610612736 | bytes 524288 | tf_op jit(solution)/shard_map/last_polar/pallas_call | solution.py:367
  75.2 1.1 %last_apply.1 = f32[2,256,128]{2,1,0:T(8,128)} custom-call(f32[256,256]{1,0:T(8,128)S(1)} %last_polar.1.gate_ref, f32[2,2,64,256]{3,2,1,0:T(8,128)S(1)} %get-tuple-element.56.psi_own, f32[2,2,64,256]{3,2,1,0:T(8,128)S(1)} %collective-permute-done.22.psi_got), custom_call_target="tpu_custom_call" | custom-call | flops 201326592 | bytes 1048576 | tf_op jit(solution)/shard_map/last_apply/pallas_call | solution.py:367
  (14 shorter events, 0.1 us)
Async XLA Ops:
  0.6 1.0 %copy-start.1 = (f32[2,256,128]{2,1,0:T(8,128)S(1)}, f32[2,256,128]{2,1,0:T(8,128)}, u32[]{:S(2)}) copy-start(f32[2,256,128]{2,1,0:T(8,128)} %x_ref.2) | copy-start | bytes 786436
  1.6 36.8 %copy-start = (f32[4,2,128,128]{3,2,1,0:T(8,128)S(1)}, f32[4,2,128,128]{3,2,1,0:T(8,128)}, u32[]{:S(2)}) copy-start(f32[4,2,128,128]{3,2,1,0:T(8,128)} %gates_ref.11) | copy-start | bytes 1572868
  1.7 1.6 %collective-permute-start = (f32[2,64,256]{2,1,0:T(8,128)S(1)}, f32[2,64,256]{2,1,0:T(8,128)S(1)}, u32[]{:S(2)}, u32[]{:S(2)}) collective-permute-start(f32[2,64,256]{2,1,0:T(8,128)S(1)} %get-tuple-element.33), channel_id=1, source_target_pairs={{0,1},{1,0},{2,3},{3,2},{4,5},{5,4},{6,7},{7,6},{8,9},{9,8},{10,11... | collective-permute-start | bytes 393224 | tf_op jit(solution)/shard_map/ppermute | solution.py:403
  2.2 0.9 %copy-start.2 = (f32[2,256,128]{2,1,0:T(8,128)S(1)}, f32[2,256,128]{2,1,0:T(8,128)}, u32[]{:S(2)}) copy-start(f32[2,256,128]{2,1,0:T(8,128)} %x_ref.3) | copy-start | bytes 786436
  3.4 3.2 %collective-permute-start.1 = (f32[2,64,256]{2,1,0:T(8,128)S(1)}, f32[2,64,256]{2,1,0:T(8,128)S(1)}, u32[]{:S(2)}, u32[]{:S(2)}) collective-permute-start(f32[2,64,256]{2,1,0:T(8,128)S(1)} %get-tuple-element.37), channel_id=1, source_target_pairs={{0,1},{1,0},{2,3},{3,2},{4,5},{5,4},{6,7},{7,6},{8,9},{9,8},{10,11... | collective-permute-start | bytes 393224 | tf_op jit(solution)/shard_map/ppermute | solution.py:403
  3.7 9.9 %collective-permute-start.10 = (f32[2,2,64,256]{3,2,1,0:T(8,128)S(1)}, f32[2,2,64,256]{3,2,1,0:T(8,128)S(1)}, u32[]{:S(2)}, u32[]{:S(2)}) collective-permute-start(f32[2,2,64,256]{3,2,1,0:T(8,128)S(1)} %pad_maximum_fusion.refs_0_), channel_id=1, source_target_pairs={{0,2},{1,3},{2,6},{3,7},{4,0},{5,1},{6,10},{7,11},{8,4},{9,5},{10,... | collective-permute-start | bytes 786440 | tf_op jit(solution)/shard_map/ppermute | solution.py:76
  6.5 9.2 %collective-permute-start.9 = (f32[2,2,64,256]{3,2,1,0:T(8,128)S(1)}, f32[2,2,64,256]{3,2,1,0:T(8,128)S(1)}, u32[]{:S(2)}, u32[]{:S(2)}) collective-permute-start(f32[2,2,64,256]{3,2,1,0:T(8,128)S(1)} %pad_maximum_fusion.refs_0_), channel_id=1, source_target_pairs={{0,4},{1,5},{2,0},{3,1},{4,8},{5,9},{6,2},{7,3},{8,12},{9,13},{10,... | collective-permute-start | bytes 786440 | tf_op jit(solution)/shard_map/ppermute | solution.py:76
  6.5 14.7 %collective-permute-start.2 = (f32[2,2,64,256]{3,2,1,0:T(8,128)S(1)}, f32[2,2,64,256]{3,2,1,0:T(8,128)S(1)}, u32[]{:S(2)}, u32[]{:S(2)}) collective-permute-start(f32[2,2,64,256]{3,2,1,0:T(8,128)S(1)} %pad_maximum_fusion.1.refs_0_), channel_id=1, source_target_pairs={{0,4},{1,5},{2,0},{3,1},{4,8},{5,9},{6,2},{7,3},{8,12},{9,13},{10,... | collective-permute-start | bytes 786440 | tf_op jit(solution)/shard_map/ppermute | solution.py:76
  8.6 12.7 %collective-permute-start.6 = (f32[2,2,64,256]{3,2,1,0:T(8,128)S(1)}, f32[2,2,64,256]{3,2,1,0:T(8,128)S(1)}, u32[]{:S(2)}, u32[]{:S(2)}) collective-permute-start(f32[2,2,64,256]{3,2,1,0:T(8,128)S(1)} %pad_maximum_fusion.1.refs_0_), channel_id=1, source_target_pairs={{0,2},{1,3},{2,6},{3,7},{4,0},{5,1},{6,10},{7,11},{8,4},{9,5},{10,... | collective-permute-start | bytes 786440 | tf_op jit(solution)/shard_map/ppermute | solution.py:76
  13.6 11.2 %collective-permute-start.12 = (f32[2,2,64,256]{3,2,1,0:T(8,128)S(1)}, f32[2,2,64,256]{3,2,1,0:T(8,128)S(1)}, u32[]{:S(2)}, u32[]{:S(2)}) collective-permute-start(f32[2,2,64,256]{3,2,1,0:T(8,128)S(1)} %collective-permute-done.10.refs_2_), channel_id=1, source_target_pairs={{0,2},{1,3},{2,6},{3,7},{4,0},{5,1},{6,10},{7,11},{8,4},{9,5},{10,... | collective-permute-start | bytes 786440 | tf_op jit(solution)/shard_map/ppermute | solution.py:76
  15.6 11.2 %collective-permute-start.11 = (f32[2,2,64,256]{3,2,1,0:T(8,128)S(1)}, f32[2,2,64,256]{3,2,1,0:T(8,128)S(1)}, u32[]{:S(2)}, u32[]{:S(2)}) collective-permute-start(f32[2,2,64,256]{3,2,1,0:T(8,128)S(1)} %collective-permute-done.9.refs_1_), channel_id=1, source_target_pairs={{0,4},{1,5},{2,0},{3,1},{4,8},{5,9},{6,2},{7,3},{8,12},{9,13},{10,... | collective-permute-start | bytes 786440 | tf_op jit(solution)/shard_map/ppermute | solution.py:76
  21.3 11.2 %collective-permute-start.3 = (f32[2,2,64,256]{3,2,1,0:T(8,128)S(1)}, f32[2,2,64,256]{3,2,1,0:T(8,128)S(1)}, u32[]{:S(2)}, u32[]{:S(2)}) collective-permute-start(f32[2,2,64,256]{3,2,1,0:T(8,128)S(1)} %collective-permute-done.2.refs_1_), channel_id=1, source_target_pairs={{0,4},{1,5},{2,0},{3,1},{4,8},{5,9},{6,2},{7,3},{8,12},{9,13},{10,... | collective-permute-start | bytes 786440 | tf_op jit(solution)/shard_map/ppermute | solution.py:76
  21.3 11.2 %collective-permute-start.7 = (f32[2,2,64,256]{3,2,1,0:T(8,128)S(1)}, f32[2,2,64,256]{3,2,1,0:T(8,128)S(1)}, u32[]{:S(2)}, u32[]{:S(2)}) collective-permute-start(f32[2,2,64,256]{3,2,1,0:T(8,128)S(1)} %collective-permute-done.6.refs_2_), channel_id=1, source_target_pairs={{0,2},{1,3},{2,6},{3,7},{4,0},{5,1},{6,10},{7,11},{8,4},{9,5},{10,... | collective-permute-start | bytes 786440 | tf_op jit(solution)/shard_map/ppermute | solution.py:76
  24.8 11.4 %collective-permute-start.14 = (f32[2,2,64,256]{3,2,1,0:T(8,128)S(1)}, f32[2,2,64,256]{3,2,1,0:T(8,128)S(1)}, u32[]{:S(2)}, u32[]{:S(2)}) collective-permute-start(f32[2,2,64,256]{3,2,1,0:T(8,128)S(1)} %collective-permute-done.12.refs_4_), channel_id=1, source_target_pairs={{0,2},{1,3},{2,6},{3,7},{4,0},{5,1},{6,10},{7,11},{8,4},{9,5},{10,... | collective-permute-start | bytes 786440 | tf_op jit(solution)/shard_map/ppermute | solution.py:76
  26.9 11.3 %collective-permute-start.13 = (f32[2,2,64,256]{3,2,1,0:T(8,128)S(1)}, f32[2,2,64,256]{3,2,1,0:T(8,128)S(1)}, u32[]{:S(2)}, u32[]{:S(2)}) collective-permute-start(f32[2,2,64,256]{3,2,1,0:T(8,128)S(1)} %collective-permute-done.11.refs_3_), channel_id=1, source_target_pairs={{0,4},{1,5},{2,0},{3,1},{4,8},{5,9},{6,2},{7,3},{8,12},{9,13},{10,... | collective-permute-start | bytes 786440 | tf_op jit(solution)/shard_map/ppermute | solution.py:76
  32.5 11.2 %collective-permute-start.4 = (f32[2,2,64,256]{3,2,1,0:T(8,128)S(1)}, f32[2,2,64,256]{3,2,1,0:T(8,128)S(1)}, u32[]{:S(2)}, u32[]{:S(2)}) collective-permute-start(f32[2,2,64,256]{3,2,1,0:T(8,128)S(1)} %collective-permute-done.3.refs_3_), channel_id=1, source_target_pairs={{0,4},{1,5},{2,0},{3,1},{4,8},{5,9},{6,2},{7,3},{8,12},{9,13},{10,... | collective-permute-start | bytes 786440 | tf_op jit(solution)/shard_map/ppermute | solution.py:76
  32.5 11.4 %collective-permute-start.8 = (f32[2,2,64,256]{3,2,1,0:T(8,128)S(1)}, f32[2,2,64,256]{3,2,1,0:T(8,128)S(1)}, u32[]{:S(2)}, u32[]{:S(2)}) collective-permute-start(f32[2,2,64,256]{3,2,1,0:T(8,128)S(1)} %collective-permute-done.7.refs_4_), channel_id=1, source_target_pairs={{0,2},{1,3},{2,6},{3,7},{4,0},{5,1},{6,10},{7,11},{8,4},{9,5},{10,... | collective-permute-start | bytes 786440 | tf_op jit(solution)/shard_map/ppermute | solution.py:76
  36.2 9.9 %collective-permute-start.17 = (f32[1,2,64,256]{3,2,1,0:T(8,128)S(1)}, f32[1,2,64,256]{3,2,1,0:T(8,128)S(1)}, u32[]{:S(2)}, u32[]{:S(2)}) collective-permute-start(f32[1,2,64,256]{3,2,1,0:T(8,128)S(1)} %slice.19), channel_id=1, source_target_pairs={{0,2},{1,3},{2,6},{3,7},{4,0},{5,1},{6,10},{7,11},{8,4},{9,5},{10,... | collective-permute-start | bytes 393224 | tf_op jit(solution)/shard_map/ppermute | solution.py:82
  38.2 8.3 %collective-permute-start.16 = (f32[1,2,64,256]{3,2,1,0:T(8,128)S(1)}, f32[1,2,64,256]{3,2,1,0:T(8,128)S(1)}, u32[]{:S(2)}, u32[]{:S(2)}) collective-permute-start(f32[1,2,64,256]{3,2,1,0:T(8,128)S(1)} %slice.18), channel_id=1, source_target_pairs={{0,4},{1,5},{2,0},{3,1},{4,8},{5,9},{6,2},{7,3},{8,12},{9,13},{10,... | collective-permute-start | bytes 393224 | tf_op jit(solution)/shard_map/ppermute | solution.py:82
  43.7 5.5 %collective-permute-start.5 = (f32[1,2,64,256]{3,2,1,0:T(8,128)S(1)}, f32[1,2,64,256]{3,2,1,0:T(8,128)S(1)}, u32[]{:S(2)}, u32[]{:S(2)}) collective-permute-start(f32[1,2,64,256]{3,2,1,0:T(8,128)S(1)} %slice.16), channel_id=1, source_target_pairs={{0,4},{1,5},{2,0},{3,1},{4,8},{5,9},{6,2},{7,3},{8,12},{9,13},{10,... | collective-permute-start | bytes 393224 | tf_op jit(solution)/shard_map/ppermute | solution.py:82
  43.9 5.3 %collective-permute-start.15 = (f32[1,2,64,256]{3,2,1,0:T(8,128)S(1)}, f32[1,2,64,256]{3,2,1,0:T(8,128)S(1)}, u32[]{:S(2)}, u32[]{:S(2)}) collective-permute-start(f32[1,2,64,256]{3,2,1,0:T(8,128)S(1)} %slice.17), channel_id=1, source_target_pairs={{0,2},{1,3},{2,6},{3,7},{4,0},{5,1},{6,10},{7,11},{8,4},{9,5},{10,... | collective-permute-start | bytes 393224 | tf_op jit(solution)/shard_map/ppermute | solution.py:82
  49.7 1.4 %collective-permute-start.18 = (f32[128,256]{1,0:T(8,128)S(1)}, f32[128,256]{1,0:T(8,128)S(1)}, u32[]{:S(2)}, u32[]{:S(2)}) collective-permute-start(f32[128,256]{1,0:T(8,128)S(1)} %get-tuple-element.46.e0_ref), channel_id=1, source_target_pairs={{0,1},{1,0},{2,3},{3,2},{4,5},{5,4},{6,7},{7,6},{8,9},{9,8},{10,11... | collective-permute-start | bytes 393224 | tf_op jit(solution)/shard_map/ppermute | solution.py:400
  56.2 1.4 %collective-permute-start.19 = (f32[128,256]{1,0:T(8,128)S(1)}, f32[128,256]{1,0:T(8,128)S(1)}, u32[]{:S(2)}, u32[]{:S(2)}) collective-permute-start(f32[128,256]{1,0:T(8,128)S(1)} %get-tuple-element.50.e0_ref), channel_id=1, source_target_pairs={{0,1},{1,0},{2,3},{3,2},{4,5},{5,4},{6,7},{7,6},{8,9},{9,8},{10,11... | collective-permute-start | bytes 393224 | tf_op jit(solution)/shard_map/ppermute | solution.py:400
  62.8 1.6 %collective-permute-start.20 = (f32[128,256]{1,0:T(8,128)S(1)}, f32[128,256]{1,0:T(8,128)S(1)}, u32[]{:S(2)}, u32[]{:S(2)}) collective-permute-start(f32[128,256]{1,0:T(8,128)S(1)} %get-tuple-element.52.e0_ref), channel_id=1, source_target_pairs={{0,1},{1,0},{2,3},{3,2},{4,5},{5,4},{6,7},{7,6},{8,9},{9,8},{10,11... | collective-permute-start | bytes 393224 | tf_op jit(solution)/shard_map/ppermute | solution.py:400
  63.0 7.7 %collective-permute-start.23 = (f32[2,64,256]{2,1,0:T(8,128)S(1)}, f32[2,64,256]{2,1,0:T(8,128)S(1)}, u32[]{:S(2)}, u32[]{:S(2)}) collective-permute-start(f32[2,64,256]{2,1,0:T(8,128)S(1)} %get-tuple-element.61), channel_id=1, source_target_pairs={{0,1},{1,0},{2,3},{3,2},{4,5},{5,4},{6,7},{7,6},{8,9},{9,8},{10,11... | collective-permute-start | bytes 393224 | tf_op jit(solution)/shard_map/ppermute | solution.py:453
  69.7 1.9 %collective-permute-start.21 = (f32[128,256]{1,0:T(8,128)S(1)}, f32[128,256]{1,0:T(8,128)S(1)}, u32[]{:S(2)}, u32[]{:S(2)}) collective-permute-start(f32[128,256]{1,0:T(8,128)S(1)} %get-tuple-element.54.e0_ref), channel_id=1, source_target_pairs={{0,1},{1,0},{2,3},{3,2},{4,5},{5,4},{6,7},{7,6},{8,9},{9,8},{10,11... | collective-permute-start | bytes 393224 | tf_op jit(solution)/shard_map/ppermute | solution.py:400
  70.3 4.9 %collective-permute-start.22 = (f32[2,2,64,256]{3,2,1,0:T(8,128)S(1)}, f32[2,2,64,256]{3,2,1,0:T(8,128)S(1)}, u32[]{:S(2)}, u32[]{:S(2)}) collective-permute-start(f32[2,2,64,256]{3,2,1,0:T(8,128)S(1)} %get-tuple-element.57), channel_id=1, source_target_pairs={{0,1},{1,0},{2,3},{3,2},{4,5},{5,4},{6,7},{7,6},{8,9},{9,8},{10,11... | collective-permute-start | bytes 786440 | tf_op jit(solution)/shard_map/ppermute | solution.py:464

commit v5 on v4

--- a/solution.py
+++ b/solution.py
@@ -158,11 +158,8 @@
     return ref[0, d].astype(F32) + ref[1, d].astype(F32)
 
 
-def unpacked(core, own, other, out_ref):
-    for plane in range(2):
-        low = jnp.where(core == 0, own[plane], other[plane])
-        high = jnp.where(core == 0, other[plane], own[plane])
-        out_ref[plane] = jnp.concatenate([low, high], 0).T
+def unpacked(core, own, other):
+    return jnp.concatenate([jnp.where(core == 0, own, other), jnp.where(core == 0, other, own)], 0).T
 
 
 def pack_kernel(layout, x_ref, own_ref, sent_ref):
@@ -283,12 +280,13 @@
     rests = psi_ref.shape[1] // 4
     q = joint.shape[0] // 2
     c = q // 4
-    units = [(rest, p, u) for rest in range(rests) for p in range(2) for u in range(2)]
+    units = [(rest, u) for rest in range(rests) for u in range(2)]
     gaps = 2 * NS_ITERS - 2
 
-    def add(rest, p, u):
-        term = dot3(load_quad(phi_ref, rest, bits, p), load_quad(psi_ref, rest, bits, u), NT)
-        at = (slice(p * q, p * q + q), slice(u * q, u * q + q))
+    def add(rest, u):
+        planes = [load_quad(phi_ref, rest, bits, p) for p in range(2)]
+        term = dot3([jnp.concatenate(v, 0) for v in zip(*planes)], load_quad(psi_ref, rest, bits, u), NT)
+        at = (slice(None), slice(u * q, u * q + q))
         joint[at] = term if rest == 0 else joint[at] + term
 
     def arrange(p):
@@ -338,37 +336,42 @@
             sent_ref[t, plane] = jnp.where(core == 0, high, low)
 
 
-def last_polar_kernel(e0_ref, e1_ref, gate_ref):
+def last_polar_kernel(e0_ref, e1_ref, adjoint_ref, gate_ref, out_ref, sem):
+    copy = pltpu.make_async_copy(adjoint_ref, out_ref, sem)
+    copy.start()
     gate_ref[...] = as_matrix(polar(e0_ref[...] + e1_ref[...]))
+    copy.wait()
 
 
 def unpack_kernel(layout, own_ref, got_ref, out_ref):
     core, _ = layout.place_of(lax.axis_index("long"))
-    unpacked(core, own_ref, got_ref, out_ref)
-
-
-def last_apply_kernel(layout, gate_ref, psi_own, psi_got, state_ref):
+    for plane in range(2):
+        out_ref[plane] = unpacked(core, own_ref[plane], got_ref[plane])
+
+
+def last_apply_kernel(layout, gate_ref, psi_own, psi_got, out_ref, state, sems):
     core, chips = layout.place_of(lax.axis_index("long"))
     t = chips[0] * 2 + core >> layout.local_bits[SECTIONS - 1] & 1
     n = psi_own.shape[2]
-    rows = [gate_ref[pl.ds(pl.multiple_of((plane * 2 + t) * n, n), n)] for plane in range(2)]
-    gate = split(jnp.concatenate(rows, 0))
-    halves = []
-    for psi in (psi_own, psi_got):
-        x = jnp.concatenate([psi[0, 0], psi[1, 0], psi[0, 1], psi[1, 1]], 0)
-        y = dot3(gate, split(x), NN)
-        halves.append([y[:n], y[n:]])
-    unpacked(core, halves[0], halves[1], state_ref)
-
-
-def call(kernel, name, outs, ins, flops, scratch=(), aliases=None):
+    inputs = [split(jnp.concatenate([psi[0, 0], psi[1, 0], psi[0, 1], psi[1, 1]], 0)) for psi in (psi_own, psi_got)]
+    copies = []
+    for plane in range(2):
+        gate = split(gate_ref[pl.ds(pl.multiple_of((plane * 2 + t) * n, n), n)])
+        state[plane] = unpacked(core, *[dot3(gate, x, NN) for x in inputs])
+        copies.append(pltpu.make_async_copy(state.at[plane], out_ref.at[plane], sems.at[plane]))
+        copies[plane].start()
+    for copy in copies:
+        copy.wait()
+
+
+def call(kernel, name, outs, ins, flops, scratch=(), aliases=None, out_spaces={}):
     sizes = [int(np.prod(a.shape)) * a.dtype.itemsize for a in list(ins) + list(outs)]
     spec = pl.BlockSpec(memory_space=pltpu.VMEM)
     return pl.pallas_call(
         kernel,
         out_shape=outs,
         in_specs=[spec] * len(ins),
-        out_specs=[spec] * len(outs),
+        out_specs=[pl.BlockSpec(memory_space=out_spaces.get(k, pltpu.VMEM)) for k in range(len(outs))],
         scratch_shapes=list(scratch),
         input_output_aliases=aliases or {},
         compiler_params=pltpu.CompilerParams(vmem_limit_bytes=VMEM_LIMIT),
@@ -462,10 +465,24 @@
     e0, e1 = both(e)
     psi_own, psi_sent = call(kernel(ends_kernel), "ends", [two_slabs, two_slabs], [gate, psi], apply_flops // 4)
     psi_got = lax.ppermute(psi_sent, "long", core_flip)
-    (final_adjoint,) = call(kernel(unpack_kernel), "unpack", [whole], [after(phi_own, e), phi_got], 0)
-    (gate,) = call(last_polar_kernel, "last_polar", [square], [e0, e1], 2 * apply_flops)
+    (adjoint,) = call(kernel(unpack_kernel), "unpack", [whole], [after(phi_own, e), phi_got], 0)
+    gate, final_adjoint = call(
+        last_polar_kernel,
+        "last_polar",
+        [square, whole],
+        [e0, e1, adjoint],
+        2 * apply_flops,
+        [pltpu.SemaphoreType.DMA],
+        out_spaces={1: pl.ANY},
+    )
     (final_state,) = call(
-        kernel(last_apply_kernel), "last_apply", [whole], [gate, psi_own, psi_got], apply_flops // 4
+        kernel(last_apply_kernel),
+        "last_apply",
+        [whole],
+        [gate, psi_own, psi_got],
+        apply_flops // 4,
+        [pltpu.VMEM(initial_state.shape, F32), pltpu.SemaphoreType.DMA((2,))],
+        out_spaces={0: pl.ANY},
     )
     return final_state, final_adjoint
 

time: 76.5 us -> 76.2 us (level)
  transfers between devices with their start and end apart: 24 -> 24, of which waited for: 9 -> 10; matrix products, arithmetic and copies ran while one was open for 0% -> 0% of each run, Pallas kernels for 25% -> 25%
where the time goes in v5:
time: 76.2 us; the launch traced here: 76 us
  Pallas kernels  30.6 us (40%)
  waiting for transfers between devices  22.6 us (30%)
  starting transfers between devices  19.9 us (26%)
  local copies, waits for them, and re-layouts  1.93 us (3%)
  between operations  1.05 us (1%)
    pallas_call x18, Pallas kernels, call(): pl.pallas_call(kernel, out_shape=outs, in_specs=[spec] * len(ins), out_sp...  30.6 us
    ppermute x12, waiting for transfers between devices, gather_ring(): lax.ppermute(end, 'long', layout.ring(step))  21.4 us
    ppermute x12, starting transfers between devices, gather_ring(): lax.ppermute(end, 'long', layout.ring(step))  13 us
    ppermute x4, starting transfers between devices, last_step(): lax.ppermute(end, 'long', layout.ring(step))  4.46 us
    unnamed x6, local copies, waits for them, and re-layouts  1.9 us
  transfers between devices with their start and end apart: 24, of which 10 were waited for; matrix products, arithmetic and copies ran while one was open for 0% of the time, Pallas kernels for 25%

profile of v5, /device:TPU:0, one launch (start us, length us, event | category | flops | bytes accessed | tf_op | source)
XLA Modules:
  0.0 76.0 jit_solution(8908322971209587815)
XLA Ops:
  0.6 0.9 %copy-done.1 = f32[2,256,128]{2,1,0:T(8,128)S(1)} copy-done((f32[2,256,128]{2,1,0:T(8,128)S(1)}, f32[2,256,128]{2,1,0:T(8,128)}, u32[]{:S(2)}) %copy-start.1) | copy-done | bytes 262168
  1.6 0.1 pack.2
  1.7 0.5 collective-permute-start
  2.2 0.9 %copy-done.2 = f32[2,256,128]{2,1,0:T(8,128)S(1)} copy-done((f32[2,256,128]{2,1,0:T(8,128)S(1)}, f32[2,256,128]{2,1,0:T(8,128)}, u32[]{:S(2)}) %copy-start.2) | copy-done | bytes 262168
  3.2 0.1 pack.3
  3.3 0.0 collective-permute-done
  3.4 0.3 collective-permute-start.1
  3.7 2.8 %collective-permute-start.10 = (f32[2,2,64,256]{3,2,1,0:T(8,128)S(1)}, f32[2,2,64,256]{3,2,1,0:T(8,128)S(1)}, u32[]{:S(2)}, u32[]{:S(2)}) collective-permute-start(f32[2,2,64,256]{3,2,1,0:T(8,128)S(1)} %pad_maximum_fusion.refs_0_), channel_id=1, source_target_pairs={{0,2},{1,3},{2,6},{3,7},{4,0},{5,1},{6,10},{7,11},{8,4},{9,5},{10,... | collective-permute-start | bytes 786440 | tf_op jit(solution)/shard_map/ppermute | solution.py:76
  6.5 0.1 collective-permute-start.9
  6.5 0.0 collective-permute-done.1
  6.5 2.1 %collective-permute-start.2 = (f32[2,2,64,256]{3,2,1,0:T(8,128)S(1)}, f32[2,2,64,256]{3,2,1,0:T(8,128)S(1)}, u32[]{:S(2)}, u32[]{:S(2)}) collective-permute-start(f32[2,2,64,256]{3,2,1,0:T(8,128)S(1)} %pad_maximum_fusion.1.refs_0_), channel_id=1, source_target_pairs={{0,4},{1,5},{2,0},{3,1},{4,8},{5,9},{6,2},{7,3},{8,12},{9,13},{10,... | collective-permute-start | bytes 786440 | tf_op jit(solution)/shard_map/ppermute | solution.py:76
  8.6 0.0 collective-permute-start.6
  8.6 5.0 %collective-permute-done.10.refs_2_ = f32[2,2,64,256]{3,2,1,0:T(8,128)S(1)} collective-permute-done((f32[2,2,64,256]{3,2,1,0:T(8,128)S(1)}, f32[2,2,64,256]{3,2,1,0:T(8,128)S(1)}, u32[]{:S(2)}, u32[]{:S(2)}) %collective-permute-start.10) | collective-permute-done | bytes 262176 | tf_op jit(solution)/shard_map/ppermute | solution.py:76
  13.6 2.0 %collective-permute-start.12 = (f32[2,2,64,256]{3,2,1,0:T(8,128)S(1)}, f32[2,2,64,256]{3,2,1,0:T(8,128)S(1)}, u32[]{:S(2)}, u32[]{:S(2)}) collective-permute-start(f32[2,2,64,256]{3,2,1,0:T(8,128)S(1)} %collective-permute-done.10.refs_2_), channel_id=1, source_target_pairs={{0,2},{1,3},{2,6},{3,7},{4,0},{5,1},{6,10},{7,11},{8,4},{9,5},{10,... | collective-permute-start | bytes 786440 | tf_op jit(solution)/shard_map/ppermute | solution.py:76
  15.6 0.0 collective-permute-done.9.refs_1_
  15.6 0.0 collective-permute-start.11
  15.7 5.6 %collective-permute-done.2.refs_1_ = f32[2,2,64,256]{3,2,1,0:T(8,128)S(1)} collective-permute-done((f32[2,2,64,256]{3,2,1,0:T(8,128)S(1)}, f32[2,2,64,256]{3,2,1,0:T(8,128)S(1)}, u32[]{:S(2)}, u32[]{:S(2)}) %collective-permute-start.2) | collective-permute-done | bytes 262176 | tf_op jit(solution)/shard_map/ppermute | solution.py:76
  21.3 0.0 collective-permute-start.3
  21.3 0.0 collective-permute-done.6.refs_2_
  21.3 2.0 %collective-permute-start.7 = (f32[2,2,64,256]{3,2,1,0:T(8,128)S(1)}, f32[2,2,64,256]{3,2,1,0:T(8,128)S(1)}, u32[]{:S(2)}, u32[]{:S(2)}) collective-permute-start(f32[2,2,64,256]{3,2,1,0:T(8,128)S(1)} %collective-permute-done.6.refs_2_), channel_id=1, source_target_pairs={{0,2},{1,3},{2,6},{3,7},{4,0},{5,1},{6,10},{7,11},{8,4},{9,5},{10,... | collective-permute-start | bytes 786440 | tf_op jit(solution)/shard_map/ppermute | solution.py:76
  23.3 1.5 %collective-permute-done.12.refs_4_ = f32[2,2,64,256]{3,2,1,0:T(8,128)S(1)} collective-permute-done((f32[2,2,64,256]{3,2,1,0:T(8,128)S(1)}, f32[2,2,64,256]{3,2,1,0:T(8,128)S(1)}, u32[]{:S(2)}, u32[]{:S(2)}) %collective-permute-start.12) | collective-permute-done | bytes 262176 | tf_op jit(solution)/shard_map/ppermute | solution.py:76
  24.8 2.0 %collective-permute-start.14 = (f32[2,2,64,256]{3,2,1,0:T(8,128)S(1)}, f32[2,2,64,256]{3,2,1,0:T(8,128)S(1)}, u32[]{:S(2)}, u32[]{:S(2)}) collective-permute-start(f32[2,2,64,256]{3,2,1,0:T(8,128)S(1)} %collective-permute-done.12.refs_4_), channel_id=1, source_target_pairs={{0,2},{1,3},{2,6},{3,7},{4,0},{5,1},{6,10},{7,11},{8,4},{9,5},{10,... | collective-permute-start | bytes 786440 | tf_op jit(solution)/shard_map/ppermute | solution.py:76
  26.8 0.0 collective-permute-done.11.refs_3_
  26.9 0.0 collective-permute-start.13
  26.9 5.6 %collective-permute-done.3.refs_3_ = f32[2,2,64,256]{3,2,1,0:T(8,128)S(1)} collective-permute-done((f32[2,2,64,256]{3,2,1,0:T(8,128)S(1)}, f32[2,2,64,256]{3,2,1,0:T(8,128)S(1)}, u32[]{:S(2)}, u32[]{:S(2)}) %collective-permute-start.3) | collective-permute-done | bytes 262176 | tf_op jit(solution)/shard_map/ppermute | solution.py:76
  32.5 0.0 collective-permute-start.4
  32.5 0.0 collective-permute-done.7.refs_4_
  32.5 2.0 %collective-permute-start.8 = (f32[2,2,64,256]{3,2,1,0:T(8,128)S(1)}, f32[2,2,64,256]{3,2,1,0:T(8,128)S(1)}, u32[]{:S(2)}, u32[]{:S(2)}) collective-permute-start(f32[2,2,64,256]{3,2,1,0:T(8,128)S(1)} %collective-permute-done.7.refs_4_), channel_id=1, source_target_pairs={{0,2},{1,3},{2,6},{3,7},{4,0},{5,1},{6,10},{7,11},{8,4},{9,5},{10,... | collective-permute-start | bytes 786440 | tf_op jit(solution)/shard_map/ppermute | solution.py:76
  34.5 1.7 %collective-permute-done.14.refs_6_ = f32[2,2,64,256]{3,2,1,0:T(8,128)S(1)} collective-permute-done((f32[2,2,64,256]{3,2,1,0:T(8,128)S(1)}, f32[2,2,64,256]{3,2,1,0:T(8,128)S(1)}, u32[]{:S(2)}, u32[]{:S(2)}) %collective-permute-start.14) | collective-permute-done | bytes 262176 | tf_op jit(solution)/shard_map/ppermute | solution.py:76
  36.2 2.0 %collective-permute-start.17 = (f32[1,2,64,256]{3,2,1,0:T(8,128)S(1)}, f32[1,2,64,256]{3,2,1,0:T(8,128)S(1)}, u32[]{:S(2)}, u32[]{:S(2)}) collective-permute-start(f32[1,2,64,256]{3,2,1,0:T(8,128)S(1)} %slice.19), channel_id=1, source_target_pairs={{0,2},{1,3},{2,6},{3,7},{4,0},{5,1},{6,10},{7,11},{8,4},{9,5},{10,... | collective-permute-start | bytes 393224 | tf_op jit(solution)/shard_map/ppermute | solution.py:82
  38.2 0.1 collective-permute-start.16
  38.4 2.4 %first_gate.1.phi0_ref.refs_9_ = bf16[2,16,2,64,256]{4,3,2,1,0:T(8,128)(2,1)S(1)} custom-call(f32[4,2,128,128]{3,2,1,0:T(8,128)S(1)} %copy-done, f32[2,2,64,256]{3,2,1,0:T(8,128)S(1)} %pad_maximum_fusion.refs_0_, f32[2,2,64,256]{3,2,1,0:T(8,128)S(1)} %collective-permute-done.9.refs_1_, f32[2,2,64,256]{3,2,1,0:T(8,128)S(1)} %collective-permute-done.10.refs_2_, ...), custom_call_target="tpu_custom_call" | custom-call | flops 805306368 | bytes 4456448 | tf_op jit(solution)/shard_map/first_gate/pallas_call | solution.py:370
  40.8 1.0 %line.1 = (bf16[2,16,2,64,256]{4,3,2,1,0:T(8,128)(2,1)S(1)}, bf16[2,16,2,64,256]{4,3,2,1,0:T(8,128)(2,1)S(1)}) custom-call(f32[4,2,128,128]{3,2,1,0:T(8,128)S(1)} %copy-done, bf16[2,16,2,64,256]{4,3,2,1,0:T(8,128)(2,1)S(1)} %first_gate.1.phi0_ref.refs_9_), custom_call_target="tpu_custom_call" | custom-call | flops 805306368 | bytes 6815744 | tf_op jit(solution)/shard_map/line/pallas_call | solution.py:370
  41.8 1.9 %collective-permute-done.4.refs_5_ = f32[2,2,64,256]{3,2,1,0:T(8,128)S(1)} collective-permute-done((f32[2,2,64,256]{3,2,1,0:T(8,128)S(1)}, f32[2,2,64,256]{3,2,1,0:T(8,128)S(1)}, u32[]{:S(2)}, u32[]{:S(2)}) %collective-permute-start.4) | collective-permute-done | bytes 262176 | tf_op jit(solution)/shard_map/ppermute | solution.py:76
  43.7 0.1 collective-permute-start.5
  43.9 0.0 collective-permute-done.8.refs_6_
  43.9 2.2 %collective-permute-start.15 = (f32[1,2,64,256]{3,2,1,0:T(8,128)S(1)}, f32[1,2,64,256]{3,2,1,0:T(8,128)S(1)}, u32[]{:S(2)}, u32[]{:S(2)}) collective-permute-start(f32[1,2,64,256]{3,2,1,0:T(8,128)S(1)} %slice.17), channel_id=1, source_target_pairs={{0,2},{1,3},{2,6},{3,7},{4,0},{5,1},{6,10},{7,11},{8,4},{9,5},{10,... | collective-permute-start | bytes 393224 | tf_op jit(solution)/shard_map/ppermute | solution.py:82
  46.1 0.0 collective-permute-done.17.refs_8_
  46.1 0.5 collective-permute-done.16.refs_7_
  46.5 1.5 %near.1 = (bf16[2,16,2,64,256]{4,3,2,1,0:T(8,128)(2,1)S(1)}, bf16[2,16,2,64,256]{4,3,2,1,0:T(8,128)(2,1)S(1)}, f32[256,256]{1,0:T(8,128)S(1)}) custom-call(f32[4,2,128,128]{3,2,1,0:T(8,128)S(1)} %copy-done, f32[2,2,64,256]{3,2,1,0:T(8,128)S(1)} %pad_maximum_fusion.1.refs_0_, ...), custom_call_target="tpu_custom_call", output_to_operand_aliasing={{0}: (10, {})} | custom-call | flops 805306368 | bytes 9175040 | tf_op jit(solution)/shard_map/near/pallas_call | solution.py:370
  48.0 0.6 other_line.2.phi_ref
  48.6 0.6 other_line.3.phi_ref
  49.2 0.0 collective-permute-done.5.psi_a
  49.2 0.4 far.1
  49.7 0.1 collective-permute-start.18
  49.8 1.0 %last_adjoint.1 = (bf16[2,16,2,64,256]{4,3,2,1,0:T(8,128)(2,1)S(1)}, f32[2,64,256]{2,1,0:T(8,128)S(1)}, f32[2,64,256]{2,1,0:T(8,128)S(1)}) custom-call(f32[4,2,128,128]{3,2,1,0:T(8,128)S(1)} %copy-done, bf16[2,16,2,64,256]{4,3,2,1,0:T(8,128)(2,1)S(1)} %other_line.3.phi_ref), custom_call_target="tpu_custom_call" | custom-call | flops 805306368 | bytes 4980736 | tf_op jit(solution)/shard_map/last_adjoint/pallas_call | solution.py:370
  50.8 0.3 collective-permute-done.18.e1_ref
  51.1 5.1 %section.3 = (bf16[2,256,256]{2,1,0:T(8,128)(2,1)S(1)}, f32[128,256]{1,0:T(8,128)S(1)}) custom-call(f32[128,256]{1,0:T(8,128)S(1)} %get-tuple-element.48.e0_ref, f32[128,256]{1,0:T(8,128)S(1)} %collective-permute-done.18.e1_ref, bf16[2,16,2,64,256]{4,3,2,1,0:T(8,128)(2,1)S(1)} %other_line.2.phi_ref, bf16[2,16,2,64,256]{4,3,2,1,0:T(8,128)(2,1)S(1)} %get-tuple-element.51.psi_ref), custom_call_target="tpu_custom_call" | custom-call | flops 3221225472 | bytes 4849664 | tf_op jit(solution)/shard_map/section/pallas_call | solution.py:370
  56.2 0.3 collective-permute-start.19
  56.5 1.0 %apply.2.psi_ref = bf16[2,16,2,64,256]{4,3,2,1,0:T(8,128)(2,1)S(1)} custom-call(bf16[2,256,256]{2,1,0:T(8,128)(2,1)S(1)} %get-tuple-element.53.gate_ref, bf16[2,16,2,64,256]{4,3,2,1,0:T(8,128)(2,1)S(1)} %get-tuple-element.51.psi_ref), custom_call_target="tpu_custom_call" | custom-call | flops 805306368 | bytes 4456448 | tf_op jit(solution)/shard_map/apply/pallas_call | solution.py:370
  57.5 0.2 collective-permute-done.19.e1_ref
  57.6 5.1 %section.4 = (bf16[2,256,256]{2,1,0:T(8,128)(2,1)S(1)}, f32[128,256]{1,0:T(8,128)S(1)}) custom-call(f32[128,256]{1,0:T(8,128)S(1)} %get-tuple-element.52.e0_ref, f32[128,256]{1,0:T(8,128)S(1)} %collective-permute-done.19.e1_ref, bf16[2,16,2,64,256]{4,3,2,1,0:T(8,128)(2,1)S(1)} %other_line.3.phi_ref, bf16[2,16,2,64,256]{4,3,2,1,0:T(8,128)(2,1)S(1)} %apply.2.psi_ref), custom_call_target="tpu_custom_call" | custom-call | flops 3221225472 | bytes 4849664 | tf_op jit(solution)/shard_map/section/pallas_call | solution.py:370
  62.7 0.3 collective-permute-start.20
  63.0 0.3 collective-permute-start.22
  63.3 1.0 %apply.3.psi_ref = bf16[2,16,2,64,256]{4,3,2,1,0:T(8,128)(2,1)S(1)} custom-call(bf16[2,256,256]{2,1,0:T(8,128)(2,1)S(1)} %get-tuple-element.55.gate_ref, bf16[2,16,2,64,256]{4,3,2,1,0:T(8,128)(2,1)S(1)} %apply.2.psi_ref), custom_call_target="tpu_custom_call" | custom-call | flops 805306368 | bytes 4456448 | tf_op jit(solution)/shard_map/apply/pallas_call | solution.py:370
  64.3 5.3 %section.5 = (bf16[2,256,256]{2,1,0:T(8,128)(2,1)S(1)}, f32[128,256]{1,0:T(8,128)S(1)}) custom-call(f32[128,256]{1,0:T(8,128)S(1)} %get-tuple-element.54.e0_ref, f32[128,256]{1,0:T(8,128)S(1)} %collective-permute-done.20.e1_ref, bf16[2,16,2,64,256]{4,3,2,1,0:T(8,128)(2,1)S(1)} %get-tuple-element.50.phi_ref, bf16[2,16,2,64,256]{4,3,2,1,0:T(8,128)(2,1)S(1)} %apply.3.psi_ref), custom_call_target="tpu_custom_call" | custom-call | flops 3221225472 | bytes 4849664 | tf_op jit(solution)/shard_map/section/pallas_call | solution.py:370
  69.6 0.3 collective-permute-start.21
  69.9 0.4 ends.1
  70.2 0.4 collective-permute-start.23
  70.6 0.0 collective-permute-done.22.got_ref
  70.6 0.1 unpack.1.adjoint_ref
  70.8 0.3 collective-permute-done.21.e1_ref
  71.0 3.7 %last_polar.1 = (f32[256,256]{1,0:T(8,128)S(1)}, f32[2,256,128]{2,1,0:T(8,128)}) custom-call(f32[128,256]{1,0:T(8,128)S(1)} %get-tuple-element.56.e0_ref, f32[128,256]{1,0:T(8,128)S(1)} %collective-permute-done.21.e1_ref, f32[2,256,128]{2,1,0:T(8,128)S(1)} %unpack.1.adjoint_ref), custom_call_target="tpu_custom_call" | custom-call | flops 1610612736 | bytes 1048576 | tf_op jit(solution)/shard_map/last_polar/pallas_call | solution.py:370
  74.7 1.2 %last_apply.1 = f32[2,256,128]{2,1,0:T(8,128)} custom-call(f32[256,256]{1,0:T(8,128)S(1)} %get-tuple-element.61.gate_ref, f32[2,2,64,256]{3,2,1,0:T(8,128)S(1)} %get-tuple-element.63.psi_own, f32[2,2,64,256]{3,2,1,0:T(8,128)S(1)} %collective-permute-done.23.psi_got), custom_call_target="tpu_custom_call" | custom-call | flops 201326592 | bytes 1048576 | tf_op jit(solution)/shard_map/last_apply/pallas_call | solution.py:370
  (14 shorter events, 0.1 us)
Async XLA Ops:
  0.6 1.0 %copy-start.1 = (f32[2,256,128]{2,1,0:T(8,128)S(1)}, f32[2,256,128]{2,1,0:T(8,128)}, u32[]{:S(2)}) copy-start(f32[2,256,128]{2,1,0:T(8,128)} %x_ref.2) | copy-start | bytes 786436
  1.6 36.8 %copy-start = (f32[4,2,128,128]{3,2,1,0:T(8,128)S(1)}, f32[4,2,128,128]{3,2,1,0:T(8,128)}, u32[]{:S(2)}) copy-start(f32[4,2,128,128]{3,2,1,0:T(8,128)} %gates_ref.11) | copy-start | bytes 1572868
  1.7 1.6 %collective-permute-start = (f32[2,64,256]{2,1,0:T(8,128)S(1)}, f32[2,64,256]{2,1,0:T(8,128)S(1)}, u32[]{:S(2)}, u32[]{:S(2)}) collective-permute-start(f32[2,64,256]{2,1,0:T(8,128)S(1)} %get-tuple-element.35), channel_id=1, source_target_pairs={{0,1},{1,0},{2,3},{3,2},{4,5},{5,4},{6,7},{7,6},{8,9},{9,8},{10,11... | collective-permute-start | bytes 393224 | tf_op jit(solution)/shard_map/ppermute | solution.py:406
  2.2 0.9 %copy-start.2 = (f32[2,256,128]{2,1,0:T(8,128)S(1)}, f32[2,256,128]{2,1,0:T(8,128)}, u32[]{:S(2)}) copy-start(f32[2,256,128]{2,1,0:T(8,128)} %x_ref.3) | copy-start | bytes 786436
  3.4 3.2 %collective-permute-start.1 = (f32[2,64,256]{2,1,0:T(8,128)S(1)}, f32[2,64,256]{2,1,0:T(8,128)S(1)}, u32[]{:S(2)}, u32[]{:S(2)}) collective-permute-start(f32[2,64,256]{2,1,0:T(8,128)S(1)} %get-tuple-element.39), channel_id=1, source_target_pairs={{0,1},{1,0},{2,3},{3,2},{4,5},{5,4},{6,7},{7,6},{8,9},{9,8},{10,11... | collective-permute-start | bytes 393224 | tf_op jit(solution)/shard_map/ppermute | solution.py:406
  3.7 9.9 %collective-permute-start.10 = (f32[2,2,64,256]{3,2,1,0:T(8,128)S(1)}, f32[2,2,64,256]{3,2,1,0:T(8,128)S(1)}, u32[]{:S(2)}, u32[]{:S(2)}) collective-permute-start(f32[2,2,64,256]{3,2,1,0:T(8,128)S(1)} %pad_maximum_fusion.refs_0_), channel_id=1, source_target_pairs={{0,2},{1,3},{2,6},{3,7},{4,0},{5,1},{6,10},{7,11},{8,4},{9,5},{10,... | collective-permute-start | bytes 786440 | tf_op jit(solution)/shard_map/ppermute | solution.py:76
  6.5 9.2 %collective-permute-start.9 = (f32[2,2,64,256]{3,2,1,0:T(8,128)S(1)}, f32[2,2,64,256]{3,2,1,0:T(8,128)S(1)}, u32[]{:S(2)}, u32[]{:S(2)}) collective-permute-start(f32[2,2,64,256]{3,2,1,0:T(8,128)S(1)} %pad_maximum_fusion.refs_0_), channel_id=1, source_target_pairs={{0,4},{1,5},{2,0},{3,1},{4,8},{5,9},{6,2},{7,3},{8,12},{9,13},{10,... | collective-permute-start | bytes 786440 | tf_op jit(solution)/shard_map/ppermute | solution.py:76
  6.5 14.7 %collective-permute-start.2 = (f32[2,2,64,256]{3,2,1,0:T(8,128)S(1)}, f32[2,2,64,256]{3,2,1,0:T(8,128)S(1)}, u32[]{:S(2)}, u32[]{:S(2)}) collective-permute-start(f32[2,2,64,256]{3,2,1,0:T(8,128)S(1)} %pad_maximum_fusion.1.refs_0_), channel_id=1, source_target_pairs={{0,4},{1,5},{2,0},{3,1},{4,8},{5,9},{6,2},{7,3},{8,12},{9,13},{10,... | collective-permute-start | bytes 786440 | tf_op jit(solution)/shard_map/ppermute | solution.py:76
  8.6 12.7 %collective-permute-start.6 = (f32[2,2,64,256]{3,2,1,0:T(8,128)S(1)}, f32[2,2,64,256]{3,2,1,0:T(8,128)S(1)}, u32[]{:S(2)}, u32[]{:S(2)}) collective-permute-start(f32[2,2,64,256]{3,2,1,0:T(8,128)S(1)} %pad_maximum_fusion.1.refs_0_), channel_id=1, source_target_pairs={{0,2},{1,3},{2,6},{3,7},{4,0},{5,1},{6,10},{7,11},{8,4},{9,5},{10,... | collective-permute-start | bytes 786440 | tf_op jit(solution)/shard_map/ppermute | solution.py:76
  13.6 11.2 %collective-permute-start.12 = (f32[2,2,64,256]{3,2,1,0:T(8,128)S(1)}, f32[2,2,64,256]{3,2,1,0:T(8,128)S(1)}, u32[]{:S(2)}, u32[]{:S(2)}) collective-permute-start(f32[2,2,64,256]{3,2,1,0:T(8,128)S(1)} %collective-permute-done.10.refs_2_), channel_id=1, source_target_pairs={{0,2},{1,3},{2,6},{3,7},{4,0},{5,1},{6,10},{7,11},{8,4},{9,5},{10,... | collective-permute-start | bytes 786440 | tf_op jit(solution)/shard_map/ppermute | solution.py:76
  15.6 11.2 %collective-permute-start.11 = (f32[2,2,64,256]{3,2,1,0:T(8,128)S(1)}, f32[2,2,64,256]{3,2,1,0:T(8,128)S(1)}, u32[]{:S(2)}, u32[]{:S(2)}) collective-permute-start(f32[2,2,64,256]{3,2,1,0:T(8,128)S(1)} %collective-permute-done.9.refs_1_), channel_id=1, source_target_pairs={{0,4},{1,5},{2,0},{3,1},{4,8},{5,9},{6,2},{7,3},{8,12},{9,13},{10,... | collective-permute-start | bytes 786440 | tf_op jit(solution)/shard_map/ppermute | solution.py:76
  21.3 11.2 %collective-permute-start.3 = (f32[2,2,64,256]{3,2,1,0:T(8,128)S(1)}, f32[2,2,64,256]{3,2,1,0:T(8,128)S(1)}, u32[]{:S(2)}, u32[]{:S(2)}) collective-permute-start(f32[2,2,64,256]{3,2,1,0:T(8,128)S(1)} %collective-permute-done.2.refs_1_), channel_id=1, source_target_pairs={{0,4},{1,5},{2,0},{3,1},{4,8},{5,9},{6,2},{7,3},{8,12},{9,13},{10,... | collective-permute-start | bytes 786440 | tf_op jit(solution)/shard_map/ppermute | solution.py:76
  21.3 11.2 %collective-permute-start.7 = (f32[2,2,64,256]{3,2,1,0:T(8,128)S(1)}, f32[2,2,64,256]{3,2,1,0:T(8,128)S(1)}, u32[]{:S(2)}, u32[]{:S(2)}) collective-permute-start(f32[2,2,64,256]{3,2,1,0:T(8,128)S(1)} %collective-permute-done.6.refs_2_), channel_id=1, source_target_pairs={{0,2},{1,3},{2,6},{3,7},{4,0},{5,1},{6,10},{7,11},{8,4},{9,5},{10,... | collective-permute-start | bytes 786440 | tf_op jit(solution)/shard_map/ppermute | solution.py:76
  24.8 11.4 %collective-permute-start.14 = (f32[2,2,64,256]{3,2,1,0:T(8,128)S(1)}, f32[2,2,64,256]{3,2,1,0:T(8,128)S(1)}, u32[]{:S(2)}, u32[]{:S(2)}) collective-permute-start(f32[2,2,64,256]{3,2,1,0:T(8,128)S(1)} %collective-permute-done.12.refs_4_), channel_id=1, source_target_pairs={{0,2},{1,3},{2,6},{3,7},{4,0},{5,1},{6,10},{7,11},{8,4},{9,5},{10,... | collective-permute-start | bytes 786440 | tf_op jit(solution)/shard_map/ppermute | solution.py:76
  26.9 11.3 %collective-permute-start.13 = (f32[2,2,64,256]{3,2,1,0:T(8,128)S(1)}, f32[2,2,64,256]{3,2,1,0:T(8,128)S(1)}, u32[]{:S(2)}, u32[]{:S(2)}) collective-permute-start(f32[2,2,64,256]{3,2,1,0:T(8,128)S(1)} %collective-permute-done.11.refs_3_), channel_id=1, source_target_pairs={{0,4},{1,5},{2,0},{3,1},{4,8},{5,9},{6,2},{7,3},{8,12},{9,13},{10,... | collective-permute-start | bytes 786440 | tf_op jit(solution)/shard_map/ppermute | solution.py:76
  32.5 11.2 %collective-permute-start.4 = (f32[2,2,64,256]{3,2,1,0:T(8,128)S(1)}, f32[2,2,64,256]{3,2,1,0:T(8,128)S(1)}, u32[]{:S(2)}, u32[]{:S(2)}) collective-permute-start(f32[2,2,64,256]{3,2,1,0:T(8,128)S(1)} %collective-permute-done.3.refs_3_), channel_id=1, source_target_pairs={{0,4},{1,5},{2,0},{3,1},{4,8},{5,9},{6,2},{7,3},{8,12},{9,13},{10,... | collective-permute-start | bytes 786440 | tf_op jit(solution)/shard_map/ppermute | solution.py:76
  32.5 11.4 %collective-permute-start.8 = (f32[2,2,64,256]{3,2,1,0:T(8,128)S(1)}, f32[2,2,64,256]{3,2,1,0:T(8,128)S(1)}, u32[]{:S(2)}, u32[]{:S(2)}) collective-permute-start(f32[2,2,64,256]{3,2,1,0:T(8,128)S(1)} %collective-permute-done.7.refs_4_), channel_id=1, source_target_pairs={{0,2},{1,3},{2,6},{3,7},{4,0},{5,1},{6,10},{7,11},{8,4},{9,5},{10,... | collective-permute-start | bytes 786440 | tf_op jit(solution)/shard_map/ppermute | solution.py:76
  36.2 9.9 %collective-permute-start.17 = (f32[1,2,64,256]{3,2,1,0:T(8,128)S(1)}, f32[1,2,64,256]{3,2,1,0:T(8,128)S(1)}, u32[]{:S(2)}, u32[]{:S(2)}) collective-permute-start(f32[1,2,64,256]{3,2,1,0:T(8,128)S(1)} %slice.19), channel_id=1, source_target_pairs={{0,2},{1,3},{2,6},{3,7},{4,0},{5,1},{6,10},{7,11},{8,4},{9,5},{10,... | collective-permute-start | bytes 393224 | tf_op jit(solution)/shard_map/ppermute | solution.py:82
  38.2 8.3 %collective-permute-start.16 = (f32[1,2,64,256]{3,2,1,0:T(8,128)S(1)}, f32[1,2,64,256]{3,2,1,0:T(8,128)S(1)}, u32[]{:S(2)}, u32[]{:S(2)}) collective-permute-start(f32[1,2,64,256]{3,2,1,0:T(8,128)S(1)} %slice.18), channel_id=1, source_target_pairs={{0,4},{1,5},{2,0},{3,1},{4,8},{5,9},{6,2},{7,3},{8,12},{9,13},{10,... | collective-permute-start | bytes 393224 | tf_op jit(solution)/shard_map/ppermute | solution.py:82
  43.7 5.5 %collective-permute-start.5 = (f32[1,2,64,256]{3,2,1,0:T(8,128)S(1)}, f32[1,2,64,256]{3,2,1,0:T(8,128)S(1)}, u32[]{:S(2)}, u32[]{:S(2)}) collective-permute-start(f32[1,2,64,256]{3,2,1,0:T(8,128)S(1)} %slice.16), channel_id=1, source_target_pairs={{0,4},{1,5},{2,0},{3,1},{4,8},{5,9},{6,2},{7,3},{8,12},{9,13},{10,... | collective-permute-start | bytes 393224 | tf_op jit(solution)/shard_map/ppermute | solution.py:82
  43.9 5.3 %collective-permute-start.15 = (f32[1,2,64,256]{3,2,1,0:T(8,128)S(1)}, f32[1,2,64,256]{3,2,1,0:T(8,128)S(1)}, u32[]{:S(2)}, u32[]{:S(2)}) collective-permute-start(f32[1,2,64,256]{3,2,1,0:T(8,128)S(1)} %slice.17), channel_id=1, source_target_pairs={{0,2},{1,3},{2,6},{3,7},{4,0},{5,1},{6,10},{7,11},{8,4},{9,5},{10,... | collective-permute-start | bytes 393224 | tf_op jit(solution)/shard_map/ppermute | solution.py:82
  49.7 1.4 %collective-permute-start.18 = (f32[128,256]{1,0:T(8,128)S(1)}, f32[128,256]{1,0:T(8,128)S(1)}, u32[]{:S(2)}, u32[]{:S(2)}) collective-permute-start(f32[128,256]{1,0:T(8,128)S(1)} %get-tuple-element.48.e0_ref), channel_id=1, source_target_pairs={{0,1},{1,0},{2,3},{3,2},{4,5},{5,4},{6,7},{7,6},{8,9},{9,8},{10,11... | collective-permute-start | bytes 393224 | tf_op jit(solution)/shard_map/ppermute | solution.py:403
  56.2 1.4 %collective-permute-start.19 = (f32[128,256]{1,0:T(8,128)S(1)}, f32[128,256]{1,0:T(8,128)S(1)}, u32[]{:S(2)}, u32[]{:S(2)}) collective-permute-start(f32[128,256]{1,0:T(8,128)S(1)} %get-tuple-element.52.e0_ref), channel_id=1, source_target_pairs={{0,1},{1,0},{2,3},{3,2},{4,5},{5,4},{6,7},{7,6},{8,9},{9,8},{10,11... | collective-permute-start | bytes 393224 | tf_op jit(solution)/shard_map/ppermute | solution.py:403
  62.7 1.6 %collective-permute-start.20 = (f32[128,256]{1,0:T(8,128)S(1)}, f32[128,256]{1,0:T(8,128)S(1)}, u32[]{:S(2)}, u32[]{:S(2)}) collective-permute-start(f32[128,256]{1,0:T(8,128)S(1)} %get-tuple-element.54.e0_ref), channel_id=1, source_target_pairs={{0,1},{1,0},{2,3},{3,2},{4,5},{5,4},{6,7},{7,6},{8,9},{9,8},{10,11... | collective-permute-start | bytes 393224 | tf_op jit(solution)/shard_map/ppermute | solution.py:403
  63.0 7.7 %collective-permute-start.22 = (f32[2,64,256]{2,1,0:T(8,128)S(1)}, f32[2,64,256]{2,1,0:T(8,128)S(1)}, u32[]{:S(2)}, u32[]{:S(2)}) collective-permute-start(f32[2,64,256]{2,1,0:T(8,128)S(1)} %get-tuple-element.60), channel_id=1, source_target_pairs={{0,1},{1,0},{2,3},{3,2},{4,5},{5,4},{6,7},{7,6},{8,9},{9,8},{10,11... | collective-permute-start | bytes 393224 | tf_op jit(solution)/shard_map/ppermute | solution.py:456
  69.6 1.4 %collective-permute-start.21 = (f32[128,256]{1,0:T(8,128)S(1)}, f32[128,256]{1,0:T(8,128)S(1)}, u32[]{:S(2)}, u32[]{:S(2)}) collective-permute-start(f32[128,256]{1,0:T(8,128)S(1)} %get-tuple-element.56.e0_ref), channel_id=1, source_target_pairs={{0,1},{1,0},{2,3},{3,2},{4,5},{5,4},{6,7},{7,6},{8,9},{9,8},{10,11... | collective-permute-start | bytes 393224 | tf_op jit(solution)/shard_map/ppermute | solution.py:403
  70.2 4.4 %collective-permute-start.23 = (f32[2,2,64,256]{3,2,1,0:T(8,128)S(1)}, f32[2,2,64,256]{3,2,1,0:T(8,128)S(1)}, u32[]{:S(2)}, u32[]{:S(2)}) collective-permute-start(f32[2,2,64,256]{3,2,1,0:T(8,128)S(1)} %get-tuple-element.64), channel_id=1, source_target_pairs={{0,1},{1,0},{2,3},{3,2},{4,5},{5,4},{6,7},{7,6},{8,9},{9,8},{10,11... | collective-permute-start | bytes 786440 | tf_op jit(solution)/shard_map/ppermute | solution.py:467

commit v6 on v5

--- a/solution.py
+++ b/solution.py
@@ -106,17 +106,20 @@
 
 
 def polar(e, beside=lambda gap: None):
-    x = e * lax.rsqrt(jnp.sum(e * e) + 1e-6)
+    scale = lax.rsqrt(jnp.sum(e * e) + 1e-6)
+    x = e
     n = x.shape[0]
     for k in range(NS_ITERS):
         xs = split(x)
         turns = [turned(v) for v in xs]
         beside(2 * k)
-        h = split(jnp.concatenate([dot3(xs, xs, NT), dot3(xs, turns, NT)], 1))
+        h = jnp.concatenate([dot3(xs, xs, NT), dot3(xs, turns, NT)], 1)
+        h = split(h * (scale * scale) if k == 0 else h)
         beside(2 * k + 1)
         rows = [jnp.concatenate(pair, 0) for pair in zip(xs, turns)]
         both = dot(jnp.concatenate(h, 0), rows[0], NN)
         x = 1.5 * x - 0.5 * (both[:n] + both[n:] + dot(h[0], rows[1], NN))
+        x = x * scale if k == 0 else x
     return x
 
 
@@ -222,16 +225,23 @@
             apply_at(gate, source, target, pair)
 
 
-def near_kernel(layout, gates_ref, *refs):
-    *blocks, phi_a, phi_b, phi_in, phi_ref, psi_ref, total_ref = refs
-    core, chips = layout.place_of(lax.axis_index("long"))
-    far = chips[-1]
+def near_kernel(layout, *refs):
+    *blocks, phi_ref, psi_ref, total_ref = refs
+    core, chips = layout.place_of(lax.axis_index("long"))
     place_blocks(blocks, chips, core, psi_ref)
-    total_ref[...] = environment(phi_ref, psi_ref, near_pairs(layout, far))
-    place_far((phi_a, phi_b), far, core, phi_ref)
+    total_ref[...] = environment(phi_ref, psi_ref, near_pairs(layout, chips[-1]))
+
+
+def other_line_kernel(layout, gates_ref, far_a, far_b, phi0_in, phi1_in, phi2_in, phi0_ref, phi1_ref, phi2_ref):
+    core, chips = layout.place_of(lax.axis_index("long"))
+    place_far((far_a, far_b), chips[-1], core, phi0_ref)
     gate = gate_matrix(gates_ref, 0)
-    for pair in chip_pairs(layout.local_bits[0], far):
-        apply_at(gate, phi_ref, phi_ref, pair)
+    for pair in chip_pairs(layout.local_bits[0], chips[-1]):
+        apply_at(gate, phi0_ref, phi0_ref, pair)
+    for s, source, target in ((1, phi0_ref, phi1_ref), (2, phi1_ref, phi2_ref)):
+        gate = gate_matrix(gates_ref, s)
+        for pair in line_pairs(layout, layout.local_bits[s], 1 - (chips[0] & 1)):
+            apply_at(gate, source, target, pair)
 
 
 def far_kernel(layout, psi_a, psi_b, total_ref, phi_ref, psi_in, psi_ref, e_ref):
@@ -239,13 +249,6 @@
     far = chips[-1]
     place_far((psi_a, psi_b), far, core, psi_ref)
     e_ref[...] = folded(total_ref[...] + environment(phi_ref, psi_ref, chip_pairs(layout.local_bits[0], far)))
-
-
-def other_line_kernel(layout, section, gates_ref, phi_ref, next_in, next_ref):
-    _, chips = layout.place_of(lax.axis_index("long"))
-    gate = gate_matrix(gates_ref, section)
-    for pair in line_pairs(layout, layout.local_bits[section], 1 - (chips[0] & 1)):
-        apply_at(gate, phi_ref, next_ref, pair)
 
 
 def last_adjoint_kernel(layout, gates_ref, phi_ref, next_ref, own_ref, sent_ref):
@@ -353,11 +356,14 @@
     core, chips = layout.place_of(lax.axis_index("long"))
     t = chips[0] * 2 + core >> layout.local_bits[SECTIONS - 1] & 1
     n = psi_own.shape[2]
-    inputs = [split(jnp.concatenate([psi[0, 0], psi[1, 0], psi[0, 1], psi[1, 1]], 0)) for psi in (psi_own, psi_got)]
+    gate = split(jnp.concatenate([gate_ref[pl.ds(pl.multiple_of((plane * 2 + t) * n, n), n)] for plane in range(2)], 0))
+    halves = [
+        dot3(gate, split(jnp.concatenate([psi[0, 0], psi[1, 0], psi[0, 1], psi[1, 1]], 0)), NN)
+        for psi in (psi_own, psi_got)
+    ]
     copies = []
     for plane in range(2):
-        gate = split(gate_ref[pl.ds(pl.multiple_of((plane * 2 + t) * n, n), n)])
-        state[plane] = unpacked(core, *[dot3(gate, x, NN) for x in inputs])
+        state[plane] = unpacked(core, *[y[plane * n : (plane + 1) * n] for y in halves])
         copies.append(pltpu.make_async_copy(state.at[plane], out_ref.at[plane], sems.at[plane]))
         copies[plane].start()
     for copy in copies:
@@ -420,19 +426,17 @@
     phis += call(kernel(line_kernel), "line", [pieces] * 2, [current_gates, phis[0]], apply_flops)
     psi_near, psi_tail = gather_ring(home(psi_own, psi_sent), layout)
     psi_far = last_step([psi_tail[0], after(psi_tail[1], phis[1])], layout)
-    ins = [current_gates] + psi_near + phi_far + [phis[0]]
-    phis[0], psi, total = call(
-        kernel(near_kernel), "near", [pieces, pieces, square], ins, apply_flops, aliases={len(ins) - 1: 0}
+    psi, total = call(kernel(near_kernel), "near", [pieces, square], psi_near + [phis[0]], 3 * apply_flops // 4)
+    phis = list(
+        call(
+            kernel(other_line_kernel),
+            "other_line",
+            [pieces] * 3,
+            [current_gates] + phi_far + phis,
+            5 * apply_flops // 4,
+            aliases={3: 0, 4: 1, 5: 2},
+        )
     )
-
-    def other_line(section):
-        ins = [current_gates, phis[section - 1], phis[section]]
-        return call(
-            kernel(other_line_kernel, section), "other_line", [pieces], ins, apply_flops // 2, aliases={2: 0}
-        )[0]
-
-    phis[1] = other_line(1)
-    phis[2] = other_line(2)
     total = after(total, phis[2])
     psi, e = call(
         kernel(far_kernel), "far", [pieces, env], psi_far + [total, phis[0], psi], apply_flops // 4, aliases={4: 0}

time: 76.2 us -> 75.3 us (0.988)
    pallas_call x18 -> x17, Pallas kernels: 30.6 us -> 30 us  [call(): pl.pallas_call(kernel, out_shape=outs, in_specs=[spec] * len(ins), out_sp...]
where the time goes in v6:
time: 75.3 us; the launch traced here: 75.1 us
  Pallas kernels  30 us (40%)
  waiting for transfers between devices  22.3 us (30%)
  starting transfers between devices  19.9 us (26%)
  local copies, waits for them, and re-layouts  1.93 us (3%)
  between operations  1.05 us (1%)
    pallas_call x17, Pallas kernels, call(): pl.pallas_call(kernel, out_shape=outs, in_specs=[spec] * len(ins), out_sp...  30 us
    ppermute x12, waiting for transfers between devices, gather_ring(): lax.ppermute(end, 'long', layout.ring(step))  21.4 us
    ppermute x12, starting transfers between devices, gather_ring(): lax.ppermute(end, 'long', layout.ring(step))  13 us
    ppermute x4, starting transfers between devices, last_step(): lax.ppermute(end, 'long', layout.ring(step))  4.46 us
    unnamed x6, local copies, waits for them, and re-layouts  1.9 us
  transfers between devices with their start and end apart: 24, of which 10 were waited for; matrix products, arithmetic and copies ran while one was open for 0% of the time, Pallas kernels for 25%

profile of v6, /device:TPU:0, one launch (start us, length us, event | category | flops | bytes accessed | tf_op | source)
XLA Modules:
  0.0 75.1 jit_solution(1356729046474491251)
XLA Ops:
  0.6 0.9 %copy-done.1 = f32[2,256,128]{2,1,0:T(8,128)S(1)} copy-done((f32[2,256,128]{2,1,0:T(8,128)S(1)}, f32[2,256,128]{2,1,0:T(8,128)}, u32[]{:S(2)}) %copy-start.1) | copy-done | bytes 262168
  1.6 0.1 pack.2
  1.7 0.5 collective-permute-start
  2.2 0.9 %copy-done.2 = f32[2,256,128]{2,1,0:T(8,128)S(1)} copy-done((f32[2,256,128]{2,1,0:T(8,128)S(1)}, f32[2,256,128]{2,1,0:T(8,128)}, u32[]{:S(2)}) %copy-start.2) | copy-done | bytes 262168
  3.2 0.1 pack.3
  3.3 0.0 collective-permute-done
  3.4 0.3 collective-permute-start.1
  3.7 2.8 %collective-permute-start.10 = (f32[2,2,64,256]{3,2,1,0:T(8,128)S(1)}, f32[2,2,64,256]{3,2,1,0:T(8,128)S(1)}, u32[]{:S(2)}, u32[]{:S(2)}) collective-permute-start(f32[2,2,64,256]{3,2,1,0:T(8,128)S(1)} %pad_maximum_fusion.refs_0_), channel_id=1, source_target_pairs={{0,2},{1,3},{2,6},{3,7},{4,0},{5,1},{6,10},{7,11},{8,4},{9,5},{10,... | collective-permute-start | bytes 786440 | tf_op jit(solution)/shard_map/ppermute | solution.py:76
  6.5 0.1 collective-permute-start.9
  6.5 0.0 collective-permute-done.1
  6.5 2.1 %collective-permute-start.2 = (f32[2,2,64,256]{3,2,1,0:T(8,128)S(1)}, f32[2,2,64,256]{3,2,1,0:T(8,128)S(1)}, u32[]{:S(2)}, u32[]{:S(2)}) collective-permute-start(f32[2,2,64,256]{3,2,1,0:T(8,128)S(1)} %pad_maximum_fusion.1.refs_0_), channel_id=1, source_target_pairs={{0,4},{1,5},{2,0},{3,1},{4,8},{5,9},{6,2},{7,3},{8,12},{9,13},{10,... | collective-permute-start | bytes 786440 | tf_op jit(solution)/shard_map/ppermute | solution.py:76
  8.6 0.0 collective-permute-start.6
  8.6 5.0 %collective-permute-done.10.refs_2_ = f32[2,2,64,256]{3,2,1,0:T(8,128)S(1)} collective-permute-done((f32[2,2,64,256]{3,2,1,0:T(8,128)S(1)}, f32[2,2,64,256]{3,2,1,0:T(8,128)S(1)}, u32[]{:S(2)}, u32[]{:S(2)}) %collective-permute-start.10) | collective-permute-done | bytes 262176 | tf_op jit(solution)/shard_map/ppermute | solution.py:76
  13.6 2.0 %collective-permute-start.12 = (f32[2,2,64,256]{3,2,1,0:T(8,128)S(1)}, f32[2,2,64,256]{3,2,1,0:T(8,128)S(1)}, u32[]{:S(2)}, u32[]{:S(2)}) collective-permute-start(f32[2,2,64,256]{3,2,1,0:T(8,128)S(1)} %collective-permute-done.10.refs_2_), channel_id=1, source_target_pairs={{0,2},{1,3},{2,6},{3,7},{4,0},{5,1},{6,10},{7,11},{8,4},{9,5},{10,... | collective-permute-start | bytes 786440 | tf_op jit(solution)/shard_map/ppermute | solution.py:76
  15.6 0.0 collective-permute-done.9.refs_1_
  15.6 0.0 collective-permute-start.11
  15.7 5.6 %collective-permute-done.2.refs_1_ = f32[2,2,64,256]{3,2,1,0:T(8,128)S(1)} collective-permute-done((f32[2,2,64,256]{3,2,1,0:T(8,128)S(1)}, f32[2,2,64,256]{3,2,1,0:T(8,128)S(1)}, u32[]{:S(2)}, u32[]{:S(2)}) %collective-permute-start.2) | collective-permute-done | bytes 262176 | tf_op jit(solution)/shard_map/ppermute | solution.py:76
  21.3 0.0 collective-permute-start.3
  21.3 0.0 collective-permute-done.6.refs_2_
  21.3 2.0 %collective-permute-start.7 = (f32[2,2,64,256]{3,2,1,0:T(8,128)S(1)}, f32[2,2,64,256]{3,2,1,0:T(8,128)S(1)}, u32[]{:S(2)}, u32[]{:S(2)}) collective-permute-start(f32[2,2,64,256]{3,2,1,0:T(8,128)S(1)} %collective-permute-done.6.refs_2_), channel_id=1, source_target_pairs={{0,2},{1,3},{2,6},{3,7},{4,0},{5,1},{6,10},{7,11},{8,4},{9,5},{10,... | collective-permute-start | bytes 786440 | tf_op jit(solution)/shard_map/ppermute | solution.py:76
  23.3 1.5 %collective-permute-done.12.refs_4_ = f32[2,2,64,256]{3,2,1,0:T(8,128)S(1)} collective-permute-done((f32[2,2,64,256]{3,2,1,0:T(8,128)S(1)}, f32[2,2,64,256]{3,2,1,0:T(8,128)S(1)}, u32[]{:S(2)}, u32[]{:S(2)}) %collective-permute-start.12) | collective-permute-done | bytes 262176 | tf_op jit(solution)/shard_map/ppermute | solution.py:76
  24.8 2.0 %collective-permute-start.14 = (f32[2,2,64,256]{3,2,1,0:T(8,128)S(1)}, f32[2,2,64,256]{3,2,1,0:T(8,128)S(1)}, u32[]{:S(2)}, u32[]{:S(2)}) collective-permute-start(f32[2,2,64,256]{3,2,1,0:T(8,128)S(1)} %collective-permute-done.12.refs_4_), channel_id=1, source_target_pairs={{0,2},{1,3},{2,6},{3,7},{4,0},{5,1},{6,10},{7,11},{8,4},{9,5},{10,... | collective-permute-start | bytes 786440 | tf_op jit(solution)/shard_map/ppermute | solution.py:76
  26.8 0.0 collective-permute-done.11.refs_3_
  26.9 0.0 collective-permute-start.13
  26.9 5.6 %collective-permute-done.3.refs_3_ = f32[2,2,64,256]{3,2,1,0:T(8,128)S(1)} collective-permute-done((f32[2,2,64,256]{3,2,1,0:T(8,128)S(1)}, f32[2,2,64,256]{3,2,1,0:T(8,128)S(1)}, u32[]{:S(2)}, u32[]{:S(2)}) %collective-permute-start.3) | collective-permute-done | bytes 262176 | tf_op jit(solution)/shard_map/ppermute | solution.py:76
  32.5 0.0 collective-permute-start.4
  32.5 0.0 collective-permute-done.7.refs_4_
  32.5 2.0 %collective-permute-start.8 = (f32[2,2,64,256]{3,2,1,0:T(8,128)S(1)}, f32[2,2,64,256]{3,2,1,0:T(8,128)S(1)}, u32[]{:S(2)}, u32[]{:S(2)}) collective-permute-start(f32[2,2,64,256]{3,2,1,0:T(8,128)S(1)} %collective-permute-done.7.refs_4_), channel_id=1, source_target_pairs={{0,2},{1,3},{2,6},{3,7},{4,0},{5,1},{6,10},{7,11},{8,4},{9,5},{10,... | collective-permute-start | bytes 786440 | tf_op jit(solution)/shard_map/ppermute | solution.py:76
  34.5 1.7 %collective-permute-done.14.refs_6_ = f32[2,2,64,256]{3,2,1,0:T(8,128)S(1)} collective-permute-done((f32[2,2,64,256]{3,2,1,0:T(8,128)S(1)}, f32[2,2,64,256]{3,2,1,0:T(8,128)S(1)}, u32[]{:S(2)}, u32[]{:S(2)}) %collective-permute-start.14) | collective-permute-done | bytes 262176 | tf_op jit(solution)/shard_map/ppermute | solution.py:76
  36.2 2.0 %collective-permute-start.17 = (f32[1,2,64,256]{3,2,1,0:T(8,128)S(1)}, f32[1,2,64,256]{3,2,1,0:T(8,128)S(1)}, u32[]{:S(2)}, u32[]{:S(2)}) collective-permute-start(f32[1,2,64,256]{3,2,1,0:T(8,128)S(1)} %slice.19), channel_id=1, source_target_pairs={{0,2},{1,3},{2,6},{3,7},{4,0},{5,1},{6,10},{7,11},{8,4},{9,5},{10,... | collective-permute-start | bytes 393224 | tf_op jit(solution)/shard_map/ppermute | solution.py:82
  38.2 0.0 collective-permute-done.13.refs_5_
  38.2 0.1 collective-permute-start.16
  38.4 2.4 %first_gate.1.phi0_ref.refs_7_.phi0_in = bf16[2,16,2,64,256]{4,3,2,1,0:T(8,128)(2,1)S(1)} custom-call(f32[4,2,128,128]{3,2,1,0:T(8,128)S(1)} %copy-done, f32[2,2,64,256]{3,2,1,0:T(8,128)S(1)} %pad_maximum_fusion.refs_0_, f32[2,2,64,256]{3,2,1,0:T(8,128)S(1)} %collective-permute-done.9.refs_1_, f32[2,2,64,256]{3,2,1,0:T(8,128)S(1)} %collective-permute-done.10.refs_2_, ...), custom_call_target="tpu_custom_call" | custom-call | flops 805306368 | bytes 4456448 | tf_op jit(solution)/shard_map/first_gate/pallas_call | solution.py:376
  40.8 1.0 %line.1 = (bf16[2,16,2,64,256]{4,3,2,1,0:T(8,128)(2,1)S(1)}, bf16[2,16,2,64,256]{4,3,2,1,0:T(8,128)(2,1)S(1)}) custom-call(f32[4,2,128,128]{3,2,1,0:T(8,128)S(1)} %copy-done, bf16[2,16,2,64,256]{4,3,2,1,0:T(8,128)(2,1)S(1)} %first_gate.1.phi0_ref.refs_7_.phi0_in), custom_call_target="tpu_custom_call" | custom-call | flops 805306368 | bytes 6815744 | tf_op jit(solution)/shard_map/line/pallas_call | solution.py:376
  41.8 1.9 %collective-permute-done.4.refs_5_ = f32[2,2,64,256]{3,2,1,0:T(8,128)S(1)} collective-permute-done((f32[2,2,64,256]{3,2,1,0:T(8,128)S(1)}, f32[2,2,64,256]{3,2,1,0:T(8,128)S(1)}, u32[]{:S(2)}, u32[]{:S(2)}) %collective-permute-start.4) | collective-permute-done | bytes 262176 | tf_op jit(solution)/shard_map/ppermute | solution.py:76
  43.7 0.1 collective-permute-start.5
  43.9 2.2 %collective-permute-start.15 = (f32[1,2,64,256]{3,2,1,0:T(8,128)S(1)}, f32[1,2,64,256]{3,2,1,0:T(8,128)S(1)}, u32[]{:S(2)}, u32[]{:S(2)}) collective-permute-start(f32[1,2,64,256]{3,2,1,0:T(8,128)S(1)} %slice.17), channel_id=1, source_target_pairs={{0,2},{1,3},{2,6},{3,7},{4,0},{5,1},{6,10},{7,11},{8,4},{9,5},{10,... | collective-permute-start | bytes 393224 | tf_op jit(solution)/shard_map/ppermute | solution.py:82
  46.1 1.1 %near.1 = (bf16[2,16,2,64,256]{4,3,2,1,0:T(8,128)(2,1)S(1)}, f32[256,256]{1,0:T(8,128)S(1)}) custom-call(f32[2,2,64,256]{3,2,1,0:T(8,128)S(1)} %pad_maximum_fusion.1.refs_0_, f32[2,2,64,256]{3,2,1,0:T(8,128)S(1)} %collective-permute-done.2.refs_1_, f32[2,2,64,256]{3,2,1,0:T(8,128)S(1)} %collective-permute-done.6.refs_2_, ...), custom_call_target="tpu_custom_call" | custom-call | flops 603979776 | bytes 6291456 | tf_op jit(solution)/shard_map/near/pallas_call | solution.py:376
  47.2 0.0 collective-permute-done.17.far_b
  47.2 1.8 %other_line.1 = (bf16[2,16,2,64,256]{4,3,2,1,0:T(8,128)(2,1)S(1)}, bf16[2,16,2,64,256]{4,3,2,1,0:T(8,128)(2,1)S(1)}, bf16[2,16,2,64,256]{4,3,2,1,0:T(8,128)(2,1)S(1)}) custom-call(f32[4,2,128,128]{3,2,1,0:T(8,128)S(1)} %copy-done, f32[1,2,64,256]{3,2,1,0:T(8,128)S(1)} %collective-permute-done.16.far_a, ...), custom_call_target="tpu_custom_call", output_to_operand_aliasing={{0}: (3, {}), {1}: (4, {}), {2}: (5, {})} | custom-call | flops 1006632960 | bytes 13369344 | tf_op jit(solution)/shard_map/other_line/pallas_call | solution.py:376
  48.9 0.0 collective-permute-done.5.psi_a
  48.9 0.1 collective-permute-done.15.psi_b
  49.1 0.4 far.1
  49.5 0.1 collective-permute-start.18
  49.6 1.0 %last_adjoint.1 = (bf16[2,16,2,64,256]{4,3,2,1,0:T(8,128)(2,1)S(1)}, f32[2,64,256]{2,1,0:T(8,128)S(1)}, f32[2,64,256]{2,1,0:T(8,128)S(1)}) custom-call(f32[4,2,128,128]{3,2,1,0:T(8,128)S(1)} %copy-done, bf16[2,16,2,64,256]{4,3,2,1,0:T(8,128)(2,1)S(1)} %get-tuple-element.47.phi_ref), custom_call_target="tpu_custom_call" | custom-call | flops 805306368 | bytes 4980736 | tf_op jit(solution)/shard_map/last_adjoint/pallas_call | solution.py:376
  50.6 0.3 collective-permute-done.18.e1_ref
  51.0 4.9 %section.3 = (bf16[2,256,256]{2,1,0:T(8,128)(2,1)S(1)}, f32[128,256]{1,0:T(8,128)S(1)}) custom-call(f32[128,256]{1,0:T(8,128)S(1)} %get-tuple-element.51.e0_ref, f32[128,256]{1,0:T(8,128)S(1)} %collective-permute-done.18.e1_ref, bf16[2,16,2,64,256]{4,3,2,1,0:T(8,128)(2,1)S(1)} %get-tuple-element.52.phi_ref, ...), custom_call_target="tpu_custom_call" | custom-call | flops 3221225472 | bytes 4849664 | tf_op jit(solution)/shard_map/section/pallas_call | solution.py:376
  55.9 0.3 collective-permute-start.19
  56.1 1.0 %apply.2.psi_ref = bf16[2,16,2,64,256]{4,3,2,1,0:T(8,128)(2,1)S(1)} custom-call(bf16[2,256,256]{2,1,0:T(8,128)(2,1)S(1)} %get-tuple-element.57.gate_ref, bf16[2,16,2,64,256]{4,3,2,1,0:T(8,128)(2,1)S(1)} %get-tuple-element.55.psi_ref), custom_call_target="tpu_custom_call" | custom-call | flops 805306368 | bytes 4456448 | tf_op jit(solution)/shard_map/apply/pallas_call | solution.py:376
  57.1 0.2 collective-permute-done.19.e1_ref
  57.3 4.9 %section.4 = (bf16[2,256,256]{2,1,0:T(8,128)(2,1)S(1)}, f32[128,256]{1,0:T(8,128)S(1)}) custom-call(f32[128,256]{1,0:T(8,128)S(1)} %get-tuple-element.56.e0_ref, f32[128,256]{1,0:T(8,128)S(1)} %collective-permute-done.19.e1_ref, bf16[2,16,2,64,256]{4,3,2,1,0:T(8,128)(2,1)S(1)} %get-tuple-element.47.phi_ref, bf16[2,16,2,64,256]{4,3,2,1,0:T(8,128)(2,1)S(1)} %apply.2.psi_ref), custom_call_target="tpu_custom_call" | custom-call | flops 3221225472 | bytes 4849664 | tf_op jit(solution)/shard_map/section/pallas_call | solution.py:376
  62.2 0.2 collective-permute-start.20
  62.5 0.3 collective-permute-start.22
  62.8 1.0 %apply.3.psi_ref = bf16[2,16,2,64,256]{4,3,2,1,0:T(8,128)(2,1)S(1)} custom-call(bf16[2,256,256]{2,1,0:T(8,128)(2,1)S(1)} %get-tuple-element.59.gate_ref, bf16[2,16,2,64,256]{4,3,2,1,0:T(8,128)(2,1)S(1)} %apply.2.psi_ref), custom_call_target="tpu_custom_call" | custom-call | flops 805306368 | bytes 4456448 | tf_op jit(solution)/shard_map/apply/pallas_call | solution.py:376
  63.8 5.1 %section.5 = (bf16[2,256,256]{2,1,0:T(8,128)(2,1)S(1)}, f32[128,256]{1,0:T(8,128)S(1)}) custom-call(f32[128,256]{1,0:T(8,128)S(1)} %get-tuple-element.58.e0_ref, f32[128,256]{1,0:T(8,128)S(1)} %collective-permute-done.20.e1_ref, bf16[2,16,2,64,256]{4,3,2,1,0:T(8,128)(2,1)S(1)} %get-tuple-element.54.phi_ref, bf16[2,16,2,64,256]{4,3,2,1,0:T(8,128)(2,1)S(1)} %apply.3.psi_ref), custom_call_target="tpu_custom_call" | custom-call | flops 3221225472 | bytes 4849664 | tf_op jit(solution)/shard_map/section/pallas_call | solution.py:376
  69.0 0.2 collective-permute-start.21
  69.2 0.4 ends.1
  69.6 0.4 collective-permute-start.23
  70.0 0.0 collective-permute-done.22.got_ref
  70.0 0.1 unpack.1.adjoint_ref
  70.1 0.3 collective-permute-done.21.e1_ref
  70.4 3.5 %last_polar.1 = (f32[256,256]{1,0:T(8,128)S(1)}, f32[2,256,128]{2,1,0:T(8,128)}) custom-call(f32[128,256]{1,0:T(8,128)S(1)} %get-tuple-element.60.e0_ref, f32[128,256]{1,0:T(8,128)S(1)} %collective-permute-done.21.e1_ref, f32[2,256,128]{2,1,0:T(8,128)S(1)} %unpack.1.adjoint_ref), custom_call_target="tpu_custom_call" | custom-call | flops 1610612736 | bytes 1048576 | tf_op jit(solution)/shard_map/last_polar/pallas_call | solution.py:376
  73.9 0.0 collective-permute-done.23.psi_got
  73.9 1.1 %last_apply.1 = f32[2,256,128]{2,1,0:T(8,128)} custom-call(f32[256,256]{1,0:T(8,128)S(1)} %get-tuple-element.65.gate_ref, f32[2,2,64,256]{3,2,1,0:T(8,128)S(1)} %get-tuple-element.67.psi_own, f32[2,2,64,256]{3,2,1,0:T(8,128)S(1)} %collective-permute-done.23.psi_got), custom_call_target="tpu_custom_call" | custom-call | flops 201326592 | bytes 1048576 | tf_op jit(solution)/shard_map/last_apply/pallas_call | solution.py:376
  (13 shorter events, 0.1 us)
Async XLA Ops:
  0.6 1.0 %copy-start.1 = (f32[2,256,128]{2,1,0:T(8,128)S(1)}, f32[2,256,128]{2,1,0:T(8,128)}, u32[]{:S(2)}) copy-start(f32[2,256,128]{2,1,0:T(8,128)} %x_ref.2) | copy-start | bytes 786436
  1.6 36.8 %copy-start = (f32[4,2,128,128]{3,2,1,0:T(8,128)S(1)}, f32[4,2,128,128]{3,2,1,0:T(8,128)}, u32[]{:S(2)}) copy-start(f32[4,2,128,128]{3,2,1,0:T(8,128)} %gates_ref.7) | copy-start | bytes 1572868
  1.7 1.6 %collective-permute-start = (f32[2,64,256]{2,1,0:T(8,128)S(1)}, f32[2,64,256]{2,1,0:T(8,128)S(1)}, u32[]{:S(2)}, u32[]{:S(2)}) collective-permute-start(f32[2,64,256]{2,1,0:T(8,128)S(1)} %get-tuple-element.37), channel_id=1, source_target_pairs={{0,1},{1,0},{2,3},{3,2},{4,5},{5,4},{6,7},{7,6},{8,9},{9,8},{10,11... | collective-permute-start | bytes 393224 | tf_op jit(solution)/shard_map/ppermute | solution.py:412
  2.2 0.9 %copy-start.2 = (f32[2,256,128]{2,1,0:T(8,128)S(1)}, f32[2,256,128]{2,1,0:T(8,128)}, u32[]{:S(2)}) copy-start(f32[2,256,128]{2,1,0:T(8,128)} %x_ref.3) | copy-start | bytes 786436
  3.4 3.2 %collective-permute-start.1 = (f32[2,64,256]{2,1,0:T(8,128)S(1)}, f32[2,64,256]{2,1,0:T(8,128)S(1)}, u32[]{:S(2)}, u32[]{:S(2)}) collective-permute-start(f32[2,64,256]{2,1,0:T(8,128)S(1)} %get-tuple-element.41), channel_id=1, source_target_pairs={{0,1},{1,0},{2,3},{3,2},{4,5},{5,4},{6,7},{7,6},{8,9},{9,8},{10,11... | collective-permute-start | bytes 393224 | tf_op jit(solution)/shard_map/ppermute | solution.py:412
  3.7 9.9 %collective-permute-start.10 = (f32[2,2,64,256]{3,2,1,0:T(8,128)S(1)}, f32[2,2,64,256]{3,2,1,0:T(8,128)S(1)}, u32[]{:S(2)}, u32[]{:S(2)}) collective-permute-start(f32[2,2,64,256]{3,2,1,0:T(8,128)S(1)} %pad_maximum_fusion.refs_0_), channel_id=1, source_target_pairs={{0,2},{1,3},{2,6},{3,7},{4,0},{5,1},{6,10},{7,11},{8,4},{9,5},{10,... | collective-permute-start | bytes 786440 | tf_op jit(solution)/shard_map/ppermute | solution.py:76
  6.5 9.2 %collective-permute-start.9 = (f32[2,2,64,256]{3,2,1,0:T(8,128)S(1)}, f32[2,2,64,256]{3,2,1,0:T(8,128)S(1)}, u32[]{:S(2)}, u32[]{:S(2)}) collective-permute-start(f32[2,2,64,256]{3,2,1,0:T(8,128)S(1)} %pad_maximum_fusion.refs_0_), channel_id=1, source_target_pairs={{0,4},{1,5},{2,0},{3,1},{4,8},{5,9},{6,2},{7,3},{8,12},{9,13},{10,... | collective-permute-start | bytes 786440 | tf_op jit(solution)/shard_map/ppermute | solution.py:76
  6.5 14.7 %collective-permute-start.2 = (f32[2,2,64,256]{3,2,1,0:T(8,128)S(1)}, f32[2,2,64,256]{3,2,1,0:T(8,128)S(1)}, u32[]{:S(2)}, u32[]{:S(2)}) collective-permute-start(f32[2,2,64,256]{3,2,1,0:T(8,128)S(1)} %pad_maximum_fusion.1.refs_0_), channel_id=1, source_target_pairs={{0,4},{1,5},{2,0},{3,1},{4,8},{5,9},{6,2},{7,3},{8,12},{9,13},{10,... | collective-permute-start | bytes 786440 | tf_op jit(solution)/shard_map/ppermute | solution.py:76
  8.6 12.7 %collective-permute-start.6 = (f32[2,2,64,256]{3,2,1,0:T(8,128)S(1)}, f32[2,2,64,256]{3,2,1,0:T(8,128)S(1)}, u32[]{:S(2)}, u32[]{:S(2)}) collective-permute-start(f32[2,2,64,256]{3,2,1,0:T(8,128)S(1)} %pad_maximum_fusion.1.refs_0_), channel_id=1, source_target_pairs={{0,2},{1,3},{2,6},{3,7},{4,0},{5,1},{6,10},{7,11},{8,4},{9,5},{10,... | collective-permute-start | bytes 786440 | tf_op jit(solution)/shard_map/ppermute | solution.py:76
  13.6 11.2 %collective-permute-start.12 = (f32[2,2,64,256]{3,2,1,0:T(8,128)S(1)}, f32[2,2,64,256]{3,2,1,0:T(8,128)S(1)}, u32[]{:S(2)}, u32[]{:S(2)}) collective-permute-start(f32[2,2,64,256]{3,2,1,0:T(8,128)S(1)} %collective-permute-done.10.refs_2_), channel_id=1, source_target_pairs={{0,2},{1,3},{2,6},{3,7},{4,0},{5,1},{6,10},{7,11},{8,4},{9,5},{10,... | collective-permute-start | bytes 786440 | tf_op jit(solution)/shard_map/ppermute | solution.py:76
  15.6 11.2 %collective-permute-start.11 = (f32[2,2,64,256]{3,2,1,0:T(8,128)S(1)}, f32[2,2,64,256]{3,2,1,0:T(8,128)S(1)}, u32[]{:S(2)}, u32[]{:S(2)}) collective-permute-start(f32[2,2,64,256]{3,2,1,0:T(8,128)S(1)} %collective-permute-done.9.refs_1_), channel_id=1, source_target_pairs={{0,4},{1,5},{2,0},{3,1},{4,8},{5,9},{6,2},{7,3},{8,12},{9,13},{10,... | collective-permute-start | bytes 786440 | tf_op jit(solution)/shard_map/ppermute | solution.py:76
  21.3 11.2 %collective-permute-start.3 = (f32[2,2,64,256]{3,2,1,0:T(8,128)S(1)}, f32[2,2,64,256]{3,2,1,0:T(8,128)S(1)}, u32[]{:S(2)}, u32[]{:S(2)}) collective-permute-start(f32[2,2,64,256]{3,2,1,0:T(8,128)S(1)} %collective-permute-done.2.refs_1_), channel_id=1, source_target_pairs={{0,4},{1,5},{2,0},{3,1},{4,8},{5,9},{6,2},{7,3},{8,12},{9,13},{10,... | collective-permute-start | bytes 786440 | tf_op jit(solution)/shard_map/ppermute | solution.py:76
  21.3 11.2 %collective-permute-start.7 = (f32[2,2,64,256]{3,2,1,0:T(8,128)S(1)}, f32[2,2,64,256]{3,2,1,0:T(8,128)S(1)}, u32[]{:S(2)}, u32[]{:S(2)}) collective-permute-start(f32[2,2,64,256]{3,2,1,0:T(8,128)S(1)} %collective-permute-done.6.refs_2_), channel_id=1, source_target_pairs={{0,2},{1,3},{2,6},{3,7},{4,0},{5,1},{6,10},{7,11},{8,4},{9,5},{10,... | collective-permute-start | bytes 786440 | tf_op jit(solution)/shard_map/ppermute | solution.py:76
  24.8 11.4 %collective-permute-start.14 = (f32[2,2,64,256]{3,2,1,0:T(8,128)S(1)}, f32[2,2,64,256]{3,2,1,0:T(8,128)S(1)}, u32[]{:S(2)}, u32[]{:S(2)}) collective-permute-start(f32[2,2,64,256]{3,2,1,0:T(8,128)S(1)} %collective-permute-done.12.refs_4_), channel_id=1, source_target_pairs={{0,2},{1,3},{2,6},{3,7},{4,0},{5,1},{6,10},{7,11},{8,4},{9,5},{10,... | collective-permute-start | bytes 786440 | tf_op jit(solution)/shard_map/ppermute | solution.py:76
  26.9 11.3 %collective-permute-start.13 = (f32[2,2,64,256]{3,2,1,0:T(8,128)S(1)}, f32[2,2,64,256]{3,2,1,0:T(8,128)S(1)}, u32[]{:S(2)}, u32[]{:S(2)}) collective-permute-start(f32[2,2,64,256]{3,2,1,0:T(8,128)S(1)} %collective-permute-done.11.refs_3_), channel_id=1, source_target_pairs={{0,4},{1,5},{2,0},{3,1},{4,8},{5,9},{6,2},{7,3},{8,12},{9,13},{10,... | collective-permute-start | bytes 786440 | tf_op jit(solution)/shard_map/ppermute | solution.py:76
  32.5 11.2 %collective-permute-start.4 = (f32[2,2,64,256]{3,2,1,0:T(8,128)S(1)}, f32[2,2,64,256]{3,2,1,0:T(8,128)S(1)}, u32[]{:S(2)}, u32[]{:S(2)}) collective-permute-start(f32[2,2,64,256]{3,2,1,0:T(8,128)S(1)} %collective-permute-done.3.refs_3_), channel_id=1, source_target_pairs={{0,4},{1,5},{2,0},{3,1},{4,8},{5,9},{6,2},{7,3},{8,12},{9,13},{10,... | collective-permute-start | bytes 786440 | tf_op jit(solution)/shard_map/ppermute | solution.py:76
  32.5 11.4 %collective-permute-start.8 = (f32[2,2,64,256]{3,2,1,0:T(8,128)S(1)}, f32[2,2,64,256]{3,2,1,0:T(8,128)S(1)}, u32[]{:S(2)}, u32[]{:S(2)}) collective-permute-start(f32[2,2,64,256]{3,2,1,0:T(8,128)S(1)} %collective-permute-done.7.refs_4_), channel_id=1, source_target_pairs={{0,2},{1,3},{2,6},{3,7},{4,0},{5,1},{6,10},{7,11},{8,4},{9,5},{10,... | collective-permute-start | bytes 786440 | tf_op jit(solution)/shard_map/ppermute | solution.py:76
  36.2 11.0 %collective-permute-start.17 = (f32[1,2,64,256]{3,2,1,0:T(8,128)S(1)}, f32[1,2,64,256]{3,2,1,0:T(8,128)S(1)}, u32[]{:S(2)}, u32[]{:S(2)}) collective-permute-start(f32[1,2,64,256]{3,2,1,0:T(8,128)S(1)} %slice.19), channel_id=1, source_target_pairs={{0,2},{1,3},{2,6},{3,7},{4,0},{5,1},{6,10},{7,11},{8,4},{9,5},{10,... | collective-permute-start | bytes 393224 | tf_op jit(solution)/shard_map/ppermute | solution.py:82
  38.2 8.9 %collective-permute-start.16 = (f32[1,2,64,256]{3,2,1,0:T(8,128)S(1)}, f32[1,2,64,256]{3,2,1,0:T(8,128)S(1)}, u32[]{:S(2)}, u32[]{:S(2)}) collective-permute-start(f32[1,2,64,256]{3,2,1,0:T(8,128)S(1)} %slice.18), channel_id=1, source_target_pairs={{0,4},{1,5},{2,0},{3,1},{4,8},{5,9},{6,2},{7,3},{8,12},{9,13},{10,... | collective-permute-start | bytes 393224 | tf_op jit(solution)/shard_map/ppermute | solution.py:82
  43.7 5.2 %collective-permute-start.5 = (f32[1,2,64,256]{3,2,1,0:T(8,128)S(1)}, f32[1,2,64,256]{3,2,1,0:T(8,128)S(1)}, u32[]{:S(2)}, u32[]{:S(2)}) collective-permute-start(f32[1,2,64,256]{3,2,1,0:T(8,128)S(1)} %slice.16), channel_id=1, source_target_pairs={{0,4},{1,5},{2,0},{3,1},{4,8},{5,9},{6,2},{7,3},{8,12},{9,13},{10,... | collective-permute-start | bytes 393224 | tf_op jit(solution)/shard_map/ppermute | solution.py:82
  43.9 5.2 %collective-permute-start.15 = (f32[1,2,64,256]{3,2,1,0:T(8,128)S(1)}, f32[1,2,64,256]{3,2,1,0:T(8,128)S(1)}, u32[]{:S(2)}, u32[]{:S(2)}) collective-permute-start(f32[1,2,64,256]{3,2,1,0:T(8,128)S(1)} %slice.17), channel_id=1, source_target_pairs={{0,2},{1,3},{2,6},{3,7},{4,0},{5,1},{6,10},{7,11},{8,4},{9,5},{10,... | collective-permute-start | bytes 393224 | tf_op jit(solution)/shard_map/ppermute | solution.py:82
  49.5 1.4 %collective-permute-start.18 = (f32[128,256]{1,0:T(8,128)S(1)}, f32[128,256]{1,0:T(8,128)S(1)}, u32[]{:S(2)}, u32[]{:S(2)}) collective-permute-start(f32[128,256]{1,0:T(8,128)S(1)} %get-tuple-element.51.e0_ref), channel_id=1, source_target_pairs={{0,1},{1,0},{2,3},{3,2},{4,5},{5,4},{6,7},{7,6},{8,9},{9,8},{10,11... | collective-permute-start | bytes 393224 | tf_op jit(solution)/shard_map/ppermute | solution.py:409
  55.9 1.4 %collective-permute-start.19 = (f32[128,256]{1,0:T(8,128)S(1)}, f32[128,256]{1,0:T(8,128)S(1)}, u32[]{:S(2)}, u32[]{:S(2)}) collective-permute-start(f32[128,256]{1,0:T(8,128)S(1)} %get-tuple-element.56.e0_ref), channel_id=1, source_target_pairs={{0,1},{1,0},{2,3},{3,2},{4,5},{5,4},{6,7},{7,6},{8,9},{9,8},{10,11... | collective-permute-start | bytes 393224 | tf_op jit(solution)/shard_map/ppermute | solution.py:409
  62.2 1.6 %collective-permute-start.20 = (f32[128,256]{1,0:T(8,128)S(1)}, f32[128,256]{1,0:T(8,128)S(1)}, u32[]{:S(2)}, u32[]{:S(2)}) collective-permute-start(f32[128,256]{1,0:T(8,128)S(1)} %get-tuple-element.58.e0_ref), channel_id=1, source_target_pairs={{0,1},{1,0},{2,3},{3,2},{4,5},{5,4},{6,7},{7,6},{8,9},{9,8},{10,11... | collective-permute-start | bytes 393224 | tf_op jit(solution)/shard_map/ppermute | solution.py:409
  62.5 7.5 %collective-permute-start.22 = (f32[2,64,256]{2,1,0:T(8,128)S(1)}, f32[2,64,256]{2,1,0:T(8,128)S(1)}, u32[]{:S(2)}, u32[]{:S(2)}) collective-permute-start(f32[2,64,256]{2,1,0:T(8,128)S(1)} %get-tuple-element.64), channel_id=1, source_target_pairs={{0,1},{1,0},{2,3},{3,2},{4,5},{5,4},{6,7},{7,6},{8,9},{9,8},{10,11... | collective-permute-start | bytes 393224 | tf_op jit(solution)/shard_map/ppermute | solution.py:460
  69.0 1.4 %collective-permute-start.21 = (f32[128,256]{1,0:T(8,128)S(1)}, f32[128,256]{1,0:T(8,128)S(1)}, u32[]{:S(2)}, u32[]{:S(2)}) collective-permute-start(f32[128,256]{1,0:T(8,128)S(1)} %get-tuple-element.60.e0_ref), channel_id=1, source_target_pairs={{0,1},{1,0},{2,3},{3,2},{4,5},{5,4},{6,7},{7,6},{8,9},{9,8},{10,11... | collective-permute-start | bytes 393224 | tf_op jit(solution)/shard_map/ppermute | solution.py:409
  69.6 4.3 %collective-permute-start.23 = (f32[2,2,64,256]{3,2,1,0:T(8,128)S(1)}, f32[2,2,64,256]{3,2,1,0:T(8,128)S(1)}, u32[]{:S(2)}, u32[]{:S(2)}) collective-permute-start(f32[2,2,64,256]{3,2,1,0:T(8,128)S(1)} %get-tuple-element.68), channel_id=1, source_target_pairs={{0,1},{1,0},{2,3},{3,2},{4,5},{5,4},{6,7},{7,6},{8,9},{9,8},{10,11... | collective-permute-start | bytes 786440 | tf_op jit(solution)/shard_map/ppermute | solution.py:471

commit v7 on v6

--- a/solution.py
+++ b/solution.py
@@ -315,7 +315,8 @@
         right.append(
             jnp.concatenate([jnp.concatenate([r0, r1, i0, i1], 1), jnp.concatenate([-i0, -i1, r0, r1], 1)], 0)
         )
-    out = dot3((left[0], left[1]), right, NT)
+    two = dot(left[0], jnp.concatenate(right, 0), NT)
+    out = two[:, : 2 * c] + two[:, 2 * c :] + dot(left[1], right[0], NT)
     first, second = out[: 2 * c], out[2 * c :]
     e_ref[...] = jnp.concatenate([first[:, :c], second[:, :c], first[:, c:], second[:, c:]], 1)
     gate_ref[0], gate_ref[1] = split(as_matrix(x))

time: 75.3 us -> 75.1 us (level)
  no operation moved by 1% of the time
where the time goes in v7:
time: 75.1 us; the launch traced here: 74.9 us
  Pallas kernels  29.8 us (40%)
  waiting for transfers between devices  22.3 us (30%)
  starting transfers between devices  19.9 us (26%)
  local copies, waits for them, and re-layouts  1.93 us (3%)
  between operations  1.05 us (1%)
    pallas_call x17, Pallas kernels, call(): pl.pallas_call(kernel, out_shape=outs, in_specs=[spec] * len(ins), out_sp...  29.8 us
    ppermute x12, waiting for transfers between devices, gather_ring(): lax.ppermute(end, 'long', layout.ring(step))  21.4 us
    ppermute x12, starting transfers between devices, gather_ring(): lax.ppermute(end, 'long', layout.ring(step))  13 us
    ppermute x4, starting transfers between devices, last_step(): lax.ppermute(end, 'long', layout.ring(step))  4.46 us
    unnamed x6, local copies, waits for them, and re-layouts  1.9 us
  transfers between devices with their start and end apart: 24, of which 10 were waited for; matrix products, arithmetic and copies ran while one was open for 0% of the time, Pallas kernels for 25%

profile of v7, /device:TPU:0, one launch (start us, length us, event | category | flops | bytes accessed | tf_op | source)
XLA Modules:
  0.0 74.9 jit_solution(15074617486850253976)
XLA Ops:
  0.6 0.9 %copy-done.1 = f32[2,256,128]{2,1,0:T(8,128)S(1)} copy-done((f32[2,256,128]{2,1,0:T(8,128)S(1)}, f32[2,256,128]{2,1,0:T(8,128)}, u32[]{:S(2)}) %copy-start.1) | copy-done | bytes 262168
  1.6 0.1 pack.2
  1.7 0.5 collective-permute-start
  2.2 0.9 %copy-done.2 = f32[2,256,128]{2,1,0:T(8,128)S(1)} copy-done((f32[2,256,128]{2,1,0:T(8,128)S(1)}, f32[2,256,128]{2,1,0:T(8,128)}, u32[]{:S(2)}) %copy-start.2) | copy-done | bytes 262168
  3.2 0.1 pack.3
  3.3 0.0 collective-permute-done
  3.4 0.3 collective-permute-start.1
  3.7 2.8 %collective-permute-start.10 = (f32[2,2,64,256]{3,2,1,0:T(8,128)S(1)}, f32[2,2,64,256]{3,2,1,0:T(8,128)S(1)}, u32[]{:S(2)}, u32[]{:S(2)}) collective-permute-start(f32[2,2,64,256]{3,2,1,0:T(8,128)S(1)} %pad_maximum_fusion.refs_0_), channel_id=1, source_target_pairs={{0,2},{1,3},{2,6},{3,7},{4,0},{5,1},{6,10},{7,11},{8,4},{9,5},{10,... | collective-permute-start | bytes 786440 | tf_op jit(solution)/shard_map/ppermute | solution.py:76
  6.5 0.1 collective-permute-start.9
  6.5 0.0 collective-permute-done.1
  6.5 2.1 %collective-permute-start.2 = (f32[2,2,64,256]{3,2,1,0:T(8,128)S(1)}, f32[2,2,64,256]{3,2,1,0:T(8,128)S(1)}, u32[]{:S(2)}, u32[]{:S(2)}) collective-permute-start(f32[2,2,64,256]{3,2,1,0:T(8,128)S(1)} %pad_maximum_fusion.1.refs_0_), channel_id=1, source_target_pairs={{0,4},{1,5},{2,0},{3,1},{4,8},{5,9},{6,2},{7,3},{8,12},{9,13},{10,... | collective-permute-start | bytes 786440 | tf_op jit(solution)/shard_map/ppermute | solution.py:76
  8.6 0.0 collective-permute-start.6
  8.6 5.0 %collective-permute-done.10.refs_2_ = f32[2,2,64,256]{3,2,1,0:T(8,128)S(1)} collective-permute-done((f32[2,2,64,256]{3,2,1,0:T(8,128)S(1)}, f32[2,2,64,256]{3,2,1,0:T(8,128)S(1)}, u32[]{:S(2)}, u32[]{:S(2)}) %collective-permute-start.10) | collective-permute-done | bytes 262176 | tf_op jit(solution)/shard_map/ppermute | solution.py:76
  13.6 2.0 %collective-permute-start.12 = (f32[2,2,64,256]{3,2,1,0:T(8,128)S(1)}, f32[2,2,64,256]{3,2,1,0:T(8,128)S(1)}, u32[]{:S(2)}, u32[]{:S(2)}) collective-permute-start(f32[2,2,64,256]{3,2,1,0:T(8,128)S(1)} %collective-permute-done.10.refs_2_), channel_id=1, source_target_pairs={{0,2},{1,3},{2,6},{3,7},{4,0},{5,1},{6,10},{7,11},{8,4},{9,5},{10,... | collective-permute-start | bytes 786440 | tf_op jit(solution)/shard_map/ppermute | solution.py:76
  15.6 0.0 collective-permute-done.9.refs_1_
  15.6 0.0 collective-permute-start.11
  15.7 5.6 %collective-permute-done.2.refs_1_ = f32[2,2,64,256]{3,2,1,0:T(8,128)S(1)} collective-permute-done((f32[2,2,64,256]{3,2,1,0:T(8,128)S(1)}, f32[2,2,64,256]{3,2,1,0:T(8,128)S(1)}, u32[]{:S(2)}, u32[]{:S(2)}) %collective-permute-start.2) | collective-permute-done | bytes 262176 | tf_op jit(solution)/shard_map/ppermute | solution.py:76
  21.3 0.0 collective-permute-start.3
  21.3 0.0 collective-permute-done.6.refs_2_
  21.3 2.0 %collective-permute-start.7 = (f32[2,2,64,256]{3,2,1,0:T(8,128)S(1)}, f32[2,2,64,256]{3,2,1,0:T(8,128)S(1)}, u32[]{:S(2)}, u32[]{:S(2)}) collective-permute-start(f32[2,2,64,256]{3,2,1,0:T(8,128)S(1)} %collective-permute-done.6.refs_2_), channel_id=1, source_target_pairs={{0,2},{1,3},{2,6},{3,7},{4,0},{5,1},{6,10},{7,11},{8,4},{9,5},{10,... | collective-permute-start | bytes 786440 | tf_op jit(solution)/shard_map/ppermute | solution.py:76
  23.3 1.5 %collective-permute-done.12.refs_4_ = f32[2,2,64,256]{3,2,1,0:T(8,128)S(1)} collective-permute-done((f32[2,2,64,256]{3,2,1,0:T(8,128)S(1)}, f32[2,2,64,256]{3,2,1,0:T(8,128)S(1)}, u32[]{:S(2)}, u32[]{:S(2)}) %collective-permute-start.12) | collective-permute-done | bytes 262176 | tf_op jit(solution)/shard_map/ppermute | solution.py:76
  24.8 2.0 %collective-permute-start.14 = (f32[2,2,64,256]{3,2,1,0:T(8,128)S(1)}, f32[2,2,64,256]{3,2,1,0:T(8,128)S(1)}, u32[]{:S(2)}, u32[]{:S(2)}) collective-permute-start(f32[2,2,64,256]{3,2,1,0:T(8,128)S(1)} %collective-permute-done.12.refs_4_), channel_id=1, source_target_pairs={{0,2},{1,3},{2,6},{3,7},{4,0},{5,1},{6,10},{7,11},{8,4},{9,5},{10,... | collective-permute-start | bytes 786440 | tf_op jit(solution)/shard_map/ppermute | solution.py:76
  26.8 0.0 collective-permute-done.11.refs_3_
  26.9 0.0 collective-permute-start.13
  26.9 5.6 %collective-permute-done.3.refs_3_ = f32[2,2,64,256]{3,2,1,0:T(8,128)S(1)} collective-permute-done((f32[2,2,64,256]{3,2,1,0:T(8,128)S(1)}, f32[2,2,64,256]{3,2,1,0:T(8,128)S(1)}, u32[]{:S(2)}, u32[]{:S(2)}) %collective-permute-start.3) | collective-permute-done | bytes 262176 | tf_op jit(solution)/shard_map/ppermute | solution.py:76
  32.5 0.0 collective-permute-start.4
  32.5 0.0 collective-permute-done.7.refs_4_
  32.5 2.0 %collective-permute-start.8 = (f32[2,2,64,256]{3,2,1,0:T(8,128)S(1)}, f32[2,2,64,256]{3,2,1,0:T(8,128)S(1)}, u32[]{:S(2)}, u32[]{:S(2)}) collective-permute-start(f32[2,2,64,256]{3,2,1,0:T(8,128)S(1)} %collective-permute-done.7.refs_4_), channel_id=1, source_target_pairs={{0,2},{1,3},{2,6},{3,7},{4,0},{5,1},{6,10},{7,11},{8,4},{9,5},{10,... | collective-permute-start | bytes 786440 | tf_op jit(solution)/shard_map/ppermute | solution.py:76
  34.5 1.7 %collective-permute-done.14.refs_6_ = f32[2,2,64,256]{3,2,1,0:T(8,128)S(1)} collective-permute-done((f32[2,2,64,256]{3,2,1,0:T(8,128)S(1)}, f32[2,2,64,256]{3,2,1,0:T(8,128)S(1)}, u32[]{:S(2)}, u32[]{:S(2)}) %collective-permute-start.14) | collective-permute-done | bytes 262176 | tf_op jit(solution)/shard_map/ppermute | solution.py:76
  36.2 2.0 %collective-permute-start.17 = (f32[1,2,64,256]{3,2,1,0:T(8,128)S(1)}, f32[1,2,64,256]{3,2,1,0:T(8,128)S(1)}, u32[]{:S(2)}, u32[]{:S(2)}) collective-permute-start(f32[1,2,64,256]{3,2,1,0:T(8,128)S(1)} %slice.19), channel_id=1, source_target_pairs={{0,2},{1,3},{2,6},{3,7},{4,0},{5,1},{6,10},{7,11},{8,4},{9,5},{10,... | collective-permute-start | bytes 393224 | tf_op jit(solution)/shard_map/ppermute | solution.py:82
  38.2 0.0 collective-permute-done.13.refs_5_
  38.2 0.1 collective-permute-start.16
  38.4 2.4 %first_gate.1.phi0_ref.refs_7_.phi0_in = bf16[2,16,2,64,256]{4,3,2,1,0:T(8,128)(2,1)S(1)} custom-call(f32[4,2,128,128]{3,2,1,0:T(8,128)S(1)} %copy-done, f32[2,2,64,256]{3,2,1,0:T(8,128)S(1)} %pad_maximum_fusion.refs_0_, f32[2,2,64,256]{3,2,1,0:T(8,128)S(1)} %collective-permute-done.9.refs_1_, f32[2,2,64,256]{3,2,1,0:T(8,128)S(1)} %collective-permute-done.10.refs_2_, ...), custom_call_target="tpu_custom_call" | custom-call | flops 805306368 | bytes 4456448 | tf_op jit(solution)/shard_map/first_gate/pallas_call | solution.py:377
  40.8 1.0 %line.1 = (bf16[2,16,2,64,256]{4,3,2,1,0:T(8,128)(2,1)S(1)}, bf16[2,16,2,64,256]{4,3,2,1,0:T(8,128)(2,1)S(1)}) custom-call(f32[4,2,128,128]{3,2,1,0:T(8,128)S(1)} %copy-done, bf16[2,16,2,64,256]{4,3,2,1,0:T(8,128)(2,1)S(1)} %first_gate.1.phi0_ref.refs_7_.phi0_in), custom_call_target="tpu_custom_call" | custom-call | flops 805306368 | bytes 6815744 | tf_op jit(solution)/shard_map/line/pallas_call | solution.py:377
  41.8 1.9 %collective-permute-done.4.refs_5_ = f32[2,2,64,256]{3,2,1,0:T(8,128)S(1)} collective-permute-done((f32[2,2,64,256]{3,2,1,0:T(8,128)S(1)}, f32[2,2,64,256]{3,2,1,0:T(8,128)S(1)}, u32[]{:S(2)}, u32[]{:S(2)}) %collective-permute-start.4) | collective-permute-done | bytes 262176 | tf_op jit(solution)/shard_map/ppermute | solution.py:76
  43.7 0.1 collective-permute-start.5
  43.9 0.0 collective-permute-done.8.refs_6_
  43.9 2.2 %collective-permute-start.15 = (f32[1,2,64,256]{3,2,1,0:T(8,128)S(1)}, f32[1,2,64,256]{3,2,1,0:T(8,128)S(1)}, u32[]{:S(2)}, u32[]{:S(2)}) collective-permute-start(f32[1,2,64,256]{3,2,1,0:T(8,128)S(1)} %slice.17), channel_id=1, source_target_pairs={{0,2},{1,3},{2,6},{3,7},{4,0},{5,1},{6,10},{7,11},{8,4},{9,5},{10,... | collective-permute-start | bytes 393224 | tf_op jit(solution)/shard_map/ppermute | solution.py:82
  46.1 1.1 %near.1 = (bf16[2,16,2,64,256]{4,3,2,1,0:T(8,128)(2,1)S(1)}, f32[256,256]{1,0:T(8,128)S(1)}) custom-call(f32[2,2,64,256]{3,2,1,0:T(8,128)S(1)} %pad_maximum_fusion.1.refs_0_, f32[2,2,64,256]{3,2,1,0:T(8,128)S(1)} %collective-permute-done.2.refs_1_, f32[2,2,64,256]{3,2,1,0:T(8,128)S(1)} %collective-permute-done.6.refs_2_, ...), custom_call_target="tpu_custom_call" | custom-call | flops 603979776 | bytes 6291456 | tf_op jit(solution)/shard_map/near/pallas_call | solution.py:377
  47.2 0.0 collective-permute-done.16.far_a
  47.2 1.8 %other_line.1 = (bf16[2,16,2,64,256]{4,3,2,1,0:T(8,128)(2,1)S(1)}, bf16[2,16,2,64,256]{4,3,2,1,0:T(8,128)(2,1)S(1)}, bf16[2,16,2,64,256]{4,3,2,1,0:T(8,128)(2,1)S(1)}) custom-call(f32[4,2,128,128]{3,2,1,0:T(8,128)S(1)} %copy-done, f32[1,2,64,256]{3,2,1,0:T(8,128)S(1)} %collective-permute-done.16.far_a, ...), custom_call_target="tpu_custom_call", output_to_operand_aliasing={{0}: (3, {}), {1}: (4, {}), {2}: (5, {})} | custom-call | flops 1006632960 | bytes 13369344 | tf_op jit(solution)/shard_map/other_line/pallas_call | solution.py:377
  48.9 0.1 collective-permute-done.15.psi_b
  49.1 0.4 far.1
  49.5 0.1 collective-permute-start.18
  49.6 1.0 %last_adjoint.1 = (bf16[2,16,2,64,256]{4,3,2,1,0:T(8,128)(2,1)S(1)}, f32[2,64,256]{2,1,0:T(8,128)S(1)}, f32[2,64,256]{2,1,0:T(8,128)S(1)}) custom-call(f32[4,2,128,128]{3,2,1,0:T(8,128)S(1)} %copy-done, bf16[2,16,2,64,256]{4,3,2,1,0:T(8,128)(2,1)S(1)} %get-tuple-element.47.phi_ref), custom_call_target="tpu_custom_call" | custom-call | flops 805306368 | bytes 4980736 | tf_op jit(solution)/shard_map/last_adjoint/pallas_call | solution.py:377
  50.6 0.3 collective-permute-done.18.e1_ref
  51.0 4.9 %section.3 = (bf16[2,256,256]{2,1,0:T(8,128)(2,1)S(1)}, f32[128,256]{1,0:T(8,128)S(1)}) custom-call(f32[128,256]{1,0:T(8,128)S(1)} %get-tuple-element.51.e0_ref, f32[128,256]{1,0:T(8,128)S(1)} %collective-permute-done.18.e1_ref, bf16[2,16,2,64,256]{4,3,2,1,0:T(8,128)(2,1)S(1)} %get-tuple-element.52.phi_ref, ...), custom_call_target="tpu_custom_call" | custom-call | flops 3221225472 | bytes 4849664 | tf_op jit(solution)/shard_map/section/pallas_call | solution.py:377
  55.8 0.3 collective-permute-start.19
  56.1 1.0 %apply.2.psi_ref = bf16[2,16,2,64,256]{4,3,2,1,0:T(8,128)(2,1)S(1)} custom-call(bf16[2,256,256]{2,1,0:T(8,128)(2,1)S(1)} %get-tuple-element.57.gate_ref, bf16[2,16,2,64,256]{4,3,2,1,0:T(8,128)(2,1)S(1)} %get-tuple-element.55.psi_ref), custom_call_target="tpu_custom_call" | custom-call | flops 805306368 | bytes 4456448 | tf_op jit(solution)/shard_map/apply/pallas_call | solution.py:377
  57.1 0.2 collective-permute-done.19.e1_ref
  57.2 4.8 %section.4 = (bf16[2,256,256]{2,1,0:T(8,128)(2,1)S(1)}, f32[128,256]{1,0:T(8,128)S(1)}) custom-call(f32[128,256]{1,0:T(8,128)S(1)} %get-tuple-element.56.e0_ref, f32[128,256]{1,0:T(8,128)S(1)} %collective-permute-done.19.e1_ref, bf16[2,16,2,64,256]{4,3,2,1,0:T(8,128)(2,1)S(1)} %get-tuple-element.47.phi_ref, bf16[2,16,2,64,256]{4,3,2,1,0:T(8,128)(2,1)S(1)} %apply.2.psi_ref), custom_call_target="tpu_custom_call" | custom-call | flops 3221225472 | bytes 4849664 | tf_op jit(solution)/shard_map/section/pallas_call | solution.py:377
  62.1 0.3 collective-permute-start.20
  62.3 0.3 collective-permute-start.22
  62.7 1.0 %apply.3.psi_ref = bf16[2,16,2,64,256]{4,3,2,1,0:T(8,128)(2,1)S(1)} custom-call(bf16[2,256,256]{2,1,0:T(8,128)(2,1)S(1)} %get-tuple-element.59.gate_ref, bf16[2,16,2,64,256]{4,3,2,1,0:T(8,128)(2,1)S(1)} %apply.2.psi_ref), custom_call_target="tpu_custom_call" | custom-call | flops 805306368 | bytes 4456448 | tf_op jit(solution)/shard_map/apply/pallas_call | solution.py:377
  63.7 5.1 %section.5 = (bf16[2,256,256]{2,1,0:T(8,128)(2,1)S(1)}, f32[128,256]{1,0:T(8,128)S(1)}) custom-call(f32[128,256]{1,0:T(8,128)S(1)} %get-tuple-element.58.e0_ref, f32[128,256]{1,0:T(8,128)S(1)} %collective-permute-done.20.e1_ref, bf16[2,16,2,64,256]{4,3,2,1,0:T(8,128)(2,1)S(1)} %get-tuple-element.54.phi_ref, bf16[2,16,2,64,256]{4,3,2,1,0:T(8,128)(2,1)S(1)} %apply.3.psi_ref), custom_call_target="tpu_custom_call" | custom-call | flops 3221225472 | bytes 4849664 | tf_op jit(solution)/shard_map/section/pallas_call | solution.py:377
  68.7 0.3 collective-permute-start.21
  69.0 0.4 ends.1
  69.4 0.4 collective-permute-start.23
  69.8 0.0 collective-permute-done.22.got_ref
  69.8 0.1 unpack.1.adjoint_ref
  69.9 0.3 collective-permute-done.21.e1_ref
  70.2 3.5 %last_polar.1 = (f32[256,256]{1,0:T(8,128)S(1)}, f32[2,256,128]{2,1,0:T(8,128)}) custom-call(f32[128,256]{1,0:T(8,128)S(1)} %get-tuple-element.60.e0_ref, f32[128,256]{1,0:T(8,128)S(1)} %collective-permute-done.21.e1_ref, f32[2,256,128]{2,1,0:T(8,128)S(1)} %unpack.1.adjoint_ref), custom_call_target="tpu_custom_call" | custom-call | flops 1610612736 | bytes 1048576 | tf_op jit(solution)/shard_map/last_polar/pallas_call | solution.py:377
  73.6 0.0 collective-permute-done.23.psi_got
  73.6 1.1 %last_apply.1 = f32[2,256,128]{2,1,0:T(8,128)} custom-call(f32[256,256]{1,0:T(8,128)S(1)} %get-tuple-element.65.gate_ref, f32[2,2,64,256]{3,2,1,0:T(8,128)S(1)} %get-tuple-element.67.psi_own, f32[2,2,64,256]{3,2,1,0:T(8,128)S(1)} %collective-permute-done.23.psi_got), custom_call_target="tpu_custom_call" | custom-call | flops 201326592 | bytes 1048576 | tf_op jit(solution)/shard_map/last_apply/pallas_call | solution.py:377
  (13 shorter events, 0.1 us)
Async XLA Ops:
  0.6 1.0 %copy-start.1 = (f32[2,256,128]{2,1,0:T(8,128)S(1)}, f32[2,256,128]{2,1,0:T(8,128)}, u32[]{:S(2)}) copy-start(f32[2,256,128]{2,1,0:T(8,128)} %x_ref.2) | copy-start | bytes 786436
  1.6 36.8 %copy-start = (f32[4,2,128,128]{3,2,1,0:T(8,128)S(1)}, f32[4,2,128,128]{3,2,1,0:T(8,128)}, u32[]{:S(2)}) copy-start(f32[4,2,128,128]{3,2,1,0:T(8,128)} %gates_ref.7) | copy-start | bytes 1572868
  1.7 1.6 %collective-permute-start = (f32[2,64,256]{2,1,0:T(8,128)S(1)}, f32[2,64,256]{2,1,0:T(8,128)S(1)}, u32[]{:S(2)}, u32[]{:S(2)}) collective-permute-start(f32[2,64,256]{2,1,0:T(8,128)S(1)} %get-tuple-element.37), channel_id=1, source_target_pairs={{0,1},{1,0},{2,3},{3,2},{4,5},{5,4},{6,7},{7,6},{8,9},{9,8},{10,11... | collective-permute-start | bytes 393224 | tf_op jit(solution)/shard_map/ppermute | solution.py:413
  2.2 0.9 %copy-start.2 = (f32[2,256,128]{2,1,0:T(8,128)S(1)}, f32[2,256,128]{2,1,0:T(8,128)}, u32[]{:S(2)}) copy-start(f32[2,256,128]{2,1,0:T(8,128)} %x_ref.3) | copy-start | bytes 786436
  3.4 3.2 %collective-permute-start.1 = (f32[2,64,256]{2,1,0:T(8,128)S(1)}, f32[2,64,256]{2,1,0:T(8,128)S(1)}, u32[]{:S(2)}, u32[]{:S(2)}) collective-permute-start(f32[2,64,256]{2,1,0:T(8,128)S(1)} %get-tuple-element.41), channel_id=1, source_target_pairs={{0,1},{1,0},{2,3},{3,2},{4,5},{5,4},{6,7},{7,6},{8,9},{9,8},{10,11... | collective-permute-start | bytes 393224 | tf_op jit(solution)/shard_map/ppermute | solution.py:413
  3.7 9.9 %collective-permute-start.10 = (f32[2,2,64,256]{3,2,1,0:T(8,128)S(1)}, f32[2,2,64,256]{3,2,1,0:T(8,128)S(1)}, u32[]{:S(2)}, u32[]{:S(2)}) collective-permute-start(f32[2,2,64,256]{3,2,1,0:T(8,128)S(1)} %pad_maximum_fusion.refs_0_), channel_id=1, source_target_pairs={{0,2},{1,3},{2,6},{3,7},{4,0},{5,1},{6,10},{7,11},{8,4},{9,5},{10,... | collective-permute-start | bytes 786440 | tf_op jit(solution)/shard_map/ppermute | solution.py:76
  6.5 9.2 %collective-permute-start.9 = (f32[2,2,64,256]{3,2,1,0:T(8,128)S(1)}, f32[2,2,64,256]{3,2,1,0:T(8,128)S(1)}, u32[]{:S(2)}, u32[]{:S(2)}) collective-permute-start(f32[2,2,64,256]{3,2,1,0:T(8,128)S(1)} %pad_maximum_fusion.refs_0_), channel_id=1, source_target_pairs={{0,4},{1,5},{2,0},{3,1},{4,8},{5,9},{6,2},{7,3},{8,12},{9,13},{10,... | collective-permute-start | bytes 786440 | tf_op jit(solution)/shard_map/ppermute | solution.py:76
  6.5 14.7 %collective-permute-start.2 = (f32[2,2,64,256]{3,2,1,0:T(8,128)S(1)}, f32[2,2,64,256]{3,2,1,0:T(8,128)S(1)}, u32[]{:S(2)}, u32[]{:S(2)}) collective-permute-start(f32[2,2,64,256]{3,2,1,0:T(8,128)S(1)} %pad_maximum_fusion.1.refs_0_), channel_id=1, source_target_pairs={{0,4},{1,5},{2,0},{3,1},{4,8},{5,9},{6,2},{7,3},{8,12},{9,13},{10,... | collective-permute-start | bytes 786440 | tf_op jit(solution)/shard_map/ppermute | solution.py:76
  8.6 12.7 %collective-permute-start.6 = (f32[2,2,64,256]{3,2,1,0:T(8,128)S(1)}, f32[2,2,64,256]{3,2,1,0:T(8,128)S(1)}, u32[]{:S(2)}, u32[]{:S(2)}) collective-permute-start(f32[2,2,64,256]{3,2,1,0:T(8,128)S(1)} %pad_maximum_fusion.1.refs_0_), channel_id=1, source_target_pairs={{0,2},{1,3},{2,6},{3,7},{4,0},{5,1},{6,10},{7,11},{8,4},{9,5},{10,... | collective-permute-start | bytes 786440 | tf_op jit(solution)/shard_map/ppermute | solution.py:76
  13.6 11.2 %collective-permute-start.12 = (f32[2,2,64,256]{3,2,1,0:T(8,128)S(1)}, f32[2,2,64,256]{3,2,1,0:T(8,128)S(1)}, u32[]{:S(2)}, u32[]{:S(2)}) collective-permute-start(f32[2,2,64,256]{3,2,1,0:T(8,128)S(1)} %collective-permute-done.10.refs_2_), channel_id=1, source_target_pairs={{0,2},{1,3},{2,6},{3,7},{4,0},{5,1},{6,10},{7,11},{8,4},{9,5},{10,... | collective-permute-start | bytes 786440 | tf_op jit(solution)/shard_map/ppermute | solution.py:76
  15.6 11.2 %collective-permute-start.11 = (f32[2,2,64,256]{3,2,1,0:T(8,128)S(1)}, f32[2,2,64,256]{3,2,1,0:T(8,128)S(1)}, u32[]{:S(2)}, u32[]{:S(2)}) collective-permute-start(f32[2,2,64,256]{3,2,1,0:T(8,128)S(1)} %collective-permute-done.9.refs_1_), channel_id=1, source_target_pairs={{0,4},{1,5},{2,0},{3,1},{4,8},{5,9},{6,2},{7,3},{8,12},{9,13},{10,... | collective-permute-start | bytes 786440 | tf_op jit(solution)/shard_map/ppermute | solution.py:76
  21.3 11.2 %collective-permute-start.3 = (f32[2,2,64,256]{3,2,1,0:T(8,128)S(1)}, f32[2,2,64,256]{3,2,1,0:T(8,128)S(1)}, u32[]{:S(2)}, u32[]{:S(2)}) collective-permute-start(f32[2,2,64,256]{3,2,1,0:T(8,128)S(1)} %collective-permute-done.2.refs_1_), channel_id=1, source_target_pairs={{0,4},{1,5},{2,0},{3,1},{4,8},{5,9},{6,2},{7,3},{8,12},{9,13},{10,... | collective-permute-start | bytes 786440 | tf_op jit(solution)/shard_map/ppermute | solution.py:76
  21.3 11.2 %collective-permute-start.7 = (f32[2,2,64,256]{3,2,1,0:T(8,128)S(1)}, f32[2,2,64,256]{3,2,1,0:T(8,128)S(1)}, u32[]{:S(2)}, u32[]{:S(2)}) collective-permute-start(f32[2,2,64,256]{3,2,1,0:T(8,128)S(1)} %collective-permute-done.6.refs_2_), channel_id=1, source_target_pairs={{0,2},{1,3},{2,6},{3,7},{4,0},{5,1},{6,10},{7,11},{8,4},{9,5},{10,... | collective-permute-start | bytes 786440 | tf_op jit(solution)/shard_map/ppermute | solution.py:76
  24.8 11.4 %collective-permute-start.14 = (f32[2,2,64,256]{3,2,1,0:T(8,128)S(1)}, f32[2,2,64,256]{3,2,1,0:T(8,128)S(1)}, u32[]{:S(2)}, u32[]{:S(2)}) collective-permute-start(f32[2,2,64,256]{3,2,1,0:T(8,128)S(1)} %collective-permute-done.12.refs_4_), channel_id=1, source_target_pairs={{0,2},{1,3},{2,6},{3,7},{4,0},{5,1},{6,10},{7,11},{8,4},{9,5},{10,... | collective-permute-start | bytes 786440 | tf_op jit(solution)/shard_map/ppermute | solution.py:76
  26.9 11.3 %collective-permute-start.13 = (f32[2,2,64,256]{3,2,1,0:T(8,128)S(1)}, f32[2,2,64,256]{3,2,1,0:T(8,128)S(1)}, u32[]{:S(2)}, u32[]{:S(2)}) collective-permute-start(f32[2,2,64,256]{3,2,1,0:T(8,128)S(1)} %collective-permute-done.11.refs_3_), channel_id=1, source_target_pairs={{0,4},{1,5},{2,0},{3,1},{4,8},{5,9},{6,2},{7,3},{8,12},{9,13},{10,... | collective-permute-start | bytes 786440 | tf_op jit(solution)/shard_map/ppermute | solution.py:76
  32.5 11.2 %collective-permute-start.4 = (f32[2,2,64,256]{3,2,1,0:T(8,128)S(1)}, f32[2,2,64,256]{3,2,1,0:T(8,128)S(1)}, u32[]{:S(2)}, u32[]{:S(2)}) collective-permute-start(f32[2,2,64,256]{3,2,1,0:T(8,128)S(1)} %collective-permute-done.3.refs_3_), channel_id=1, source_target_pairs={{0,4},{1,5},{2,0},{3,1},{4,8},{5,9},{6,2},{7,3},{8,12},{9,13},{10,... | collective-permute-start | bytes 786440 | tf_op jit(solution)/shard_map/ppermute | solution.py:76
  32.5 11.4 %collective-permute-start.8 = (f32[2,2,64,256]{3,2,1,0:T(8,128)S(1)}, f32[2,2,64,256]{3,2,1,0:T(8,128)S(1)}, u32[]{:S(2)}, u32[]{:S(2)}) collective-permute-start(f32[2,2,64,256]{3,2,1,0:T(8,128)S(1)} %collective-permute-done.7.refs_4_), channel_id=1, source_target_pairs={{0,2},{1,3},{2,6},{3,7},{4,0},{5,1},{6,10},{7,11},{8,4},{9,5},{10,... | collective-permute-start | bytes 786440 | tf_op jit(solution)/shard_map/ppermute | solution.py:76
  36.2 11.0 %collective-permute-start.17 = (f32[1,2,64,256]{3,2,1,0:T(8,128)S(1)}, f32[1,2,64,256]{3,2,1,0:T(8,128)S(1)}, u32[]{:S(2)}, u32[]{:S(2)}) collective-permute-start(f32[1,2,64,256]{3,2,1,0:T(8,128)S(1)} %slice.19), channel_id=1, source_target_pairs={{0,2},{1,3},{2,6},{3,7},{4,0},{5,1},{6,10},{7,11},{8,4},{9,5},{10,... | collective-permute-start | bytes 393224 | tf_op jit(solution)/shard_map/ppermute | solution.py:82
  38.2 8.9 %collective-permute-start.16 = (f32[1,2,64,256]{3,2,1,0:T(8,128)S(1)}, f32[1,2,64,256]{3,2,1,0:T(8,128)S(1)}, u32[]{:S(2)}, u32[]{:S(2)}) collective-permute-start(f32[1,2,64,256]{3,2,1,0:T(8,128)S(1)} %slice.18), channel_id=1, source_target_pairs={{0,4},{1,5},{2,0},{3,1},{4,8},{5,9},{6,2},{7,3},{8,12},{9,13},{10,... | collective-permute-start | bytes 393224 | tf_op jit(solution)/shard_map/ppermute | solution.py:82
  43.7 5.2 %collective-permute-start.5 = (f32[1,2,64,256]{3,2,1,0:T(8,128)S(1)}, f32[1,2,64,256]{3,2,1,0:T(8,128)S(1)}, u32[]{:S(2)}, u32[]{:S(2)}) collective-permute-start(f32[1,2,64,256]{3,2,1,0:T(8,128)S(1)} %slice.16), channel_id=1, source_target_pairs={{0,4},{1,5},{2,0},{3,1},{4,8},{5,9},{6,2},{7,3},{8,12},{9,13},{10,... | collective-permute-start | bytes 393224 | tf_op jit(solution)/shard_map/ppermute | solution.py:82
  43.9 5.2 %collective-permute-start.15 = (f32[1,2,64,256]{3,2,1,0:T(8,128)S(1)}, f32[1,2,64,256]{3,2,1,0:T(8,128)S(1)}, u32[]{:S(2)}, u32[]{:S(2)}) collective-permute-start(f32[1,2,64,256]{3,2,1,0:T(8,128)S(1)} %slice.17), channel_id=1, source_target_pairs={{0,2},{1,3},{2,6},{3,7},{4,0},{5,1},{6,10},{7,11},{8,4},{9,5},{10,... | collective-permute-start | bytes 393224 | tf_op jit(solution)/shard_map/ppermute | solution.py:82
  49.5 1.4 %collective-permute-start.18 = (f32[128,256]{1,0:T(8,128)S(1)}, f32[128,256]{1,0:T(8,128)S(1)}, u32[]{:S(2)}, u32[]{:S(2)}) collective-permute-start(f32[128,256]{1,0:T(8,128)S(1)} %get-tuple-element.51.e0_ref), channel_id=1, source_target_pairs={{0,1},{1,0},{2,3},{3,2},{4,5},{5,4},{6,7},{7,6},{8,9},{9,8},{10,11... | collective-permute-start | bytes 393224 | tf_op jit(solution)/shard_map/ppermute | solution.py:410
  55.8 1.4 %collective-permute-start.19 = (f32[128,256]{1,0:T(8,128)S(1)}, f32[128,256]{1,0:T(8,128)S(1)}, u32[]{:S(2)}, u32[]{:S(2)}) collective-permute-start(f32[128,256]{1,0:T(8,128)S(1)} %get-tuple-element.56.e0_ref), channel_id=1, source_target_pairs={{0,1},{1,0},{2,3},{3,2},{4,5},{5,4},{6,7},{7,6},{8,9},{9,8},{10,11... | collective-permute-start | bytes 393224 | tf_op jit(solution)/shard_map/ppermute | solution.py:410
  62.1 1.6 %collective-permute-start.20 = (f32[128,256]{1,0:T(8,128)S(1)}, f32[128,256]{1,0:T(8,128)S(1)}, u32[]{:S(2)}, u32[]{:S(2)}) collective-permute-start(f32[128,256]{1,0:T(8,128)S(1)} %get-tuple-element.58.e0_ref), channel_id=1, source_target_pairs={{0,1},{1,0},{2,3},{3,2},{4,5},{5,4},{6,7},{7,6},{8,9},{9,8},{10,11... | collective-permute-start | bytes 393224 | tf_op jit(solution)/shard_map/ppermute | solution.py:410
  62.3 7.4 %collective-permute-start.22 = (f32[2,64,256]{2,1,0:T(8,128)S(1)}, f32[2,64,256]{2,1,0:T(8,128)S(1)}, u32[]{:S(2)}, u32[]{:S(2)}) collective-permute-start(f32[2,64,256]{2,1,0:T(8,128)S(1)} %get-tuple-element.64), channel_id=1, source_target_pairs={{0,1},{1,0},{2,3},{3,2},{4,5},{5,4},{6,7},{7,6},{8,9},{9,8},{10,11... | collective-permute-start | bytes 393224 | tf_op jit(solution)/shard_map/ppermute | solution.py:461
  68.7 1.4 %collective-permute-start.21 = (f32[128,256]{1,0:T(8,128)S(1)}, f32[128,256]{1,0:T(8,128)S(1)}, u32[]{:S(2)}, u32[]{:S(2)}) collective-permute-start(f32[128,256]{1,0:T(8,128)S(1)} %get-tuple-element.60.e0_ref), channel_id=1, source_target_pairs={{0,1},{1,0},{2,3},{3,2},{4,5},{5,4},{6,7},{7,6},{8,9},{9,8},{10,11... | collective-permute-start | bytes 393224 | tf_op jit(solution)/shard_map/ppermute | solution.py:410
  69.4 4.3 %collective-permute-start.23 = (f32[2,2,64,256]{3,2,1,0:T(8,128)S(1)}, f32[2,2,64,256]{3,2,1,0:T(8,128)S(1)}, u32[]{:S(2)}, u32[]{:S(2)}) collective-permute-start(f32[2,2,64,256]{3,2,1,0:T(8,128)S(1)} %get-tuple-element.68), channel_id=1, source_target_pairs={{0,1},{1,0},{2,3},{3,2},{4,5},{5,4},{6,7},{7,6},{8,9},{9,8},{10,11... | collective-permute-start | bytes 786440 | tf_op jit(solution)/shard_map/ppermute | solution.py:472

commit v8 on v7

--- a/solution.py
+++ b/solution.py
@@ -420,7 +420,7 @@
 
     phi_home = home(*pack(adjoint_state))
     psi_own, psi_sent = pack(initial_state)
-    phi_home, psi_own, psi_sent = lax.optimization_barrier((phi_home, psi_own, psi_sent))
+    psi_sent = after(psi_sent, phi_home)
     phi_near, phi_tail = gather_ring(phi_home, layout)
     phis = [call(kernel(first_gate_kernel), "first_gate", [pieces], [current_gates] + phi_near, apply_flops)[0]]
     phi_far = last_step(phi_tail, layout)

time: 75.1 us -> 75.1 us (level)
  no operation moved by 1% of the time
where the time goes in v8:
time: 75.1 us; the launch traced here: 74.9 us
  Pallas kernels  29.8 us (40%)
  waiting for transfers between devices  22.3 us (30%)
  starting transfers between devices  19.9 us (26%)
  local copies, waits for them, and re-layouts  1.93 us (3%)
  between operations  1.05 us (1%)
    pallas_call x17, Pallas kernels, call(): pl.pallas_call(kernel, out_shape=outs, in_specs=[spec] * len(ins), out_sp...  29.8 us
    ppermute x12, waiting for transfers between devices, gather_ring(): lax.ppermute(end, 'long', layout.ring(step))  21.4 us
    ppermute x12, starting transfers between devices, gather_ring(): lax.ppermute(end, 'long', layout.ring(step))  13 us
    ppermute x4, starting transfers between devices, last_step(): lax.ppermute(end, 'long', layout.ring(step))  4.46 us
    unnamed x6, local copies, waits for them, and re-layouts  1.9 us
  transfers between devices with their start and end apart: 24, of which 10 were waited for; matrix products, arithmetic and copies ran while one was open for 0% of the time, Pallas kernels for 25%

profile of v8, /device:TPU:0, one launch (start us, length us, event | category | flops | bytes accessed | tf_op | source)
XLA Modules:
  0.0 74.9 jit_solution(15074617486850253976)
XLA Ops:
  0.6 0.9 %copy-done.1 = f32[2,256,128]{2,1,0:T(8,128)S(1)} copy-done((f32[2,256,128]{2,1,0:T(8,128)S(1)}, f32[2,256,128]{2,1,0:T(8,128)}, u32[]{:S(2)}) %copy-start.1) | copy-done | bytes 262168
  1.6 0.1 pack.3
  1.7 0.5 collective-permute-start
  2.2 0.9 %copy-done.2 = f32[2,256,128]{2,1,0:T(8,128)S(1)} copy-done((f32[2,256,128]{2,1,0:T(8,128)S(1)}, f32[2,256,128]{2,1,0:T(8,128)}, u32[]{:S(2)}) %copy-start.2) | copy-done | bytes 262168
  3.2 0.1 pack.2
  3.3 0.0 collective-permute-done
  3.4 0.3 collective-permute-start.1
  3.7 2.8 %collective-permute-start.10 = (f32[2,2,64,256]{3,2,1,0:T(8,128)S(1)}, f32[2,2,64,256]{3,2,1,0:T(8,128)S(1)}, u32[]{:S(2)}, u32[]{:S(2)}) collective-permute-start(f32[2,2,64,256]{3,2,1,0:T(8,128)S(1)} %pad_maximum_fusion.refs_0_), channel_id=1, source_target_pairs={{0,2},{1,3},{2,6},{3,7},{4,0},{5,1},{6,10},{7,11},{8,4},{9,5},{10,... | collective-permute-start | bytes 786440 | tf_op jit(solution)/shard_map/ppermute | solution.py:76
  6.5 0.1 collective-permute-start.9
  6.5 0.0 collective-permute-done.1
  6.5 2.1 %collective-permute-start.2 = (f32[2,2,64,256]{3,2,1,0:T(8,128)S(1)}, f32[2,2,64,256]{3,2,1,0:T(8,128)S(1)}, u32[]{:S(2)}, u32[]{:S(2)}) collective-permute-start(f32[2,2,64,256]{3,2,1,0:T(8,128)S(1)} %pad_maximum_fusion.1.refs_0_), channel_id=1, source_target_pairs={{0,4},{1,5},{2,0},{3,1},{4,8},{5,9},{6,2},{7,3},{8,12},{9,13},{10,... | collective-permute-start | bytes 786440 | tf_op jit(solution)/shard_map/ppermute | solution.py:76
  8.6 0.0 collective-permute-start.6
  8.6 5.0 %collective-permute-done.10.refs_2_ = f32[2,2,64,256]{3,2,1,0:T(8,128)S(1)} collective-permute-done((f32[2,2,64,256]{3,2,1,0:T(8,128)S(1)}, f32[2,2,64,256]{3,2,1,0:T(8,128)S(1)}, u32[]{:S(2)}, u32[]{:S(2)}) %collective-permute-start.10) | collective-permute-done | bytes 262176 | tf_op jit(solution)/shard_map/ppermute | solution.py:76
  13.6 2.0 %collective-permute-start.12 = (f32[2,2,64,256]{3,2,1,0:T(8,128)S(1)}, f32[2,2,64,256]{3,2,1,0:T(8,128)S(1)}, u32[]{:S(2)}, u32[]{:S(2)}) collective-permute-start(f32[2,2,64,256]{3,2,1,0:T(8,128)S(1)} %collective-permute-done.10.refs_2_), channel_id=1, source_target_pairs={{0,2},{1,3},{2,6},{3,7},{4,0},{5,1},{6,10},{7,11},{8,4},{9,5},{10,... | collective-permute-start | bytes 786440 | tf_op jit(solution)/shard_map/ppermute | solution.py:76
  15.6 0.0 collective-permute-done.9.refs_1_
  15.6 0.0 collective-permute-start.11
  15.7 5.6 %collective-permute-done.2.refs_1_ = f32[2,2,64,256]{3,2,1,0:T(8,128)S(1)} collective-permute-done((f32[2,2,64,256]{3,2,1,0:T(8,128)S(1)}, f32[2,2,64,256]{3,2,1,0:T(8,128)S(1)}, u32[]{:S(2)}, u32[]{:S(2)}) %collective-permute-start.2) | collective-permute-done | bytes 262176 | tf_op jit(solution)/shard_map/ppermute | solution.py:76
  21.3 0.0 collective-permute-start.3
  21.3 0.0 collective-permute-done.6.refs_2_
  21.3 2.0 %collective-permute-start.7 = (f32[2,2,64,256]{3,2,1,0:T(8,128)S(1)}, f32[2,2,64,256]{3,2,1,0:T(8,128)S(1)}, u32[]{:S(2)}, u32[]{:S(2)}) collective-permute-start(f32[2,2,64,256]{3,2,1,0:T(8,128)S(1)} %collective-permute-done.6.refs_2_), channel_id=1, source_target_pairs={{0,2},{1,3},{2,6},{3,7},{4,0},{5,1},{6,10},{7,11},{8,4},{9,5},{10,... | collective-permute-start | bytes 786440 | tf_op jit(solution)/shard_map/ppermute | solution.py:76
  23.3 1.5 %collective-permute-done.12.refs_4_ = f32[2,2,64,256]{3,2,1,0:T(8,128)S(1)} collective-permute-done((f32[2,2,64,256]{3,2,1,0:T(8,128)S(1)}, f32[2,2,64,256]{3,2,1,0:T(8,128)S(1)}, u32[]{:S(2)}, u32[]{:S(2)}) %collective-permute-start.12) | collective-permute-done | bytes 262176 | tf_op jit(solution)/shard_map/ppermute | solution.py:76
  24.8 2.0 %collective-permute-start.14 = (f32[2,2,64,256]{3,2,1,0:T(8,128)S(1)}, f32[2,2,64,256]{3,2,1,0:T(8,128)S(1)}, u32[]{:S(2)}, u32[]{:S(2)}) collective-permute-start(f32[2,2,64,256]{3,2,1,0:T(8,128)S(1)} %collective-permute-done.12.refs_4_), channel_id=1, source_target_pairs={{0,2},{1,3},{2,6},{3,7},{4,0},{5,1},{6,10},{7,11},{8,4},{9,5},{10,... | collective-permute-start | bytes 786440 | tf_op jit(solution)/shard_map/ppermute | solution.py:76
  26.8 0.0 collective-permute-done.11.refs_3_
  26.9 0.0 collective-permute-start.13
  26.9 5.6 %collective-permute-done.3.refs_3_ = f32[2,2,64,256]{3,2,1,0:T(8,128)S(1)} collective-permute-done((f32[2,2,64,256]{3,2,1,0:T(8,128)S(1)}, f32[2,2,64,256]{3,2,1,0:T(8,128)S(1)}, u32[]{:S(2)}, u32[]{:S(2)}) %collective-permute-start.3) | collective-permute-done | bytes 262176 | tf_op jit(solution)/shard_map/ppermute | solution.py:76
  32.5 0.0 collective-permute-start.4
  32.5 0.0 collective-permute-done.7.refs_4_
  32.5 2.0 %collective-permute-start.8 = (f32[2,2,64,256]{3,2,1,0:T(8,128)S(1)}, f32[2,2,64,256]{3,2,1,0:T(8,128)S(1)}, u32[]{:S(2)}, u32[]{:S(2)}) collective-permute-start(f32[2,2,64,256]{3,2,1,0:T(8,128)S(1)} %collective-permute-done.7.refs_4_), channel_id=1, source_target_pairs={{0,2},{1,3},{2,6},{3,7},{4,0},{5,1},{6,10},{7,11},{8,4},{9,5},{10,... | collective-permute-start | bytes 786440 | tf_op jit(solution)/shard_map/ppermute | solution.py:76
  34.5 1.7 %collective-permute-done.14.refs_6_ = f32[2,2,64,256]{3,2,1,0:T(8,128)S(1)} collective-permute-done((f32[2,2,64,256]{3,2,1,0:T(8,128)S(1)}, f32[2,2,64,256]{3,2,1,0:T(8,128)S(1)}, u32[]{:S(2)}, u32[]{:S(2)}) %collective-permute-start.14) | collective-permute-done | bytes 262176 | tf_op jit(solution)/shard_map/ppermute | solution.py:76
  36.2 2.0 %collective-permute-start.17 = (f32[1,2,64,256]{3,2,1,0:T(8,128)S(1)}, f32[1,2,64,256]{3,2,1,0:T(8,128)S(1)}, u32[]{:S(2)}, u32[]{:S(2)}) collective-permute-start(f32[1,2,64,256]{3,2,1,0:T(8,128)S(1)} %slice.19), channel_id=1, source_target_pairs={{0,2},{1,3},{2,6},{3,7},{4,0},{5,1},{6,10},{7,11},{8,4},{9,5},{10,... | collective-permute-start | bytes 393224 | tf_op jit(solution)/shard_map/ppermute | solution.py:82
  38.2 0.0 collective-permute-done.13.refs_5_
  38.2 0.1 collective-permute-start.16
  38.4 2.4 %first_gate.1.phi0_ref.refs_7_.phi0_in = bf16[2,16,2,64,256]{4,3,2,1,0:T(8,128)(2,1)S(1)} custom-call(f32[4,2,128,128]{3,2,1,0:T(8,128)S(1)} %copy-done, f32[2,2,64,256]{3,2,1,0:T(8,128)S(1)} %pad_maximum_fusion.refs_0_, f32[2,2,64,256]{3,2,1,0:T(8,128)S(1)} %collective-permute-done.9.refs_1_, f32[2,2,64,256]{3,2,1,0:T(8,128)S(1)} %collective-permute-done.10.refs_2_, ...), custom_call_target="tpu_custom_call" | custom-call | flops 805306368 | bytes 4456448 | tf_op jit(solution)/shard_map/first_gate/pallas_call | solution.py:377
  40.8 1.0 %line.1 = (bf16[2,16,2,64,256]{4,3,2,1,0:T(8,128)(2,1)S(1)}, bf16[2,16,2,64,256]{4,3,2,1,0:T(8,128)(2,1)S(1)}) custom-call(f32[4,2,128,128]{3,2,1,0:T(8,128)S(1)} %copy-done, bf16[2,16,2,64,256]{4,3,2,1,0:T(8,128)(2,1)S(1)} %first_gate.1.phi0_ref.refs_7_.phi0_in), custom_call_target="tpu_custom_call" | custom-call | flops 805306368 | bytes 6815744 | tf_op jit(solution)/shard_map/line/pallas_call | solution.py:377
  41.8 1.9 %collective-permute-done.4.refs_5_ = f32[2,2,64,256]{3,2,1,0:T(8,128)S(1)} collective-permute-done((f32[2,2,64,256]{3,2,1,0:T(8,128)S(1)}, f32[2,2,64,256]{3,2,1,0:T(8,128)S(1)}, u32[]{:S(2)}, u32[]{:S(2)}) %collective-permute-start.4) | collective-permute-done | bytes 262176 | tf_op jit(solution)/shard_map/ppermute | solution.py:76
  43.7 0.1 collective-permute-start.5
  43.9 0.0 collective-permute-done.8.refs_6_
  43.9 2.2 %collective-permute-start.15 = (f32[1,2,64,256]{3,2,1,0:T(8,128)S(1)}, f32[1,2,64,256]{3,2,1,0:T(8,128)S(1)}, u32[]{:S(2)}, u32[]{:S(2)}) collective-permute-start(f32[1,2,64,256]{3,2,1,0:T(8,128)S(1)} %slice.17), channel_id=1, source_target_pairs={{0,2},{1,3},{2,6},{3,7},{4,0},{5,1},{6,10},{7,11},{8,4},{9,5},{10,... | collective-permute-start | bytes 393224 | tf_op jit(solution)/shard_map/ppermute | solution.py:82
  46.1 1.1 %near.1 = (bf16[2,16,2,64,256]{4,3,2,1,0:T(8,128)(2,1)S(1)}, f32[256,256]{1,0:T(8,128)S(1)}) custom-call(f32[2,2,64,256]{3,2,1,0:T(8,128)S(1)} %pad_maximum_fusion.1.refs_0_, f32[2,2,64,256]{3,2,1,0:T(8,128)S(1)} %collective-permute-done.2.refs_1_, f32[2,2,64,256]{3,2,1,0:T(8,128)S(1)} %collective-permute-done.6.refs_2_, ...), custom_call_target="tpu_custom_call" | custom-call | flops 603979776 | bytes 6291456 | tf_op jit(solution)/shard_map/near/pallas_call | solution.py:377
  47.2 0.0 collective-permute-done.16.far_a
  47.2 1.8 %other_line.1 = (bf16[2,16,2,64,256]{4,3,2,1,0:T(8,128)(2,1)S(1)}, bf16[2,16,2,64,256]{4,3,2,1,0:T(8,128)(2,1)S(1)}, bf16[2,16,2,64,256]{4,3,2,1,0:T(8,128)(2,1)S(1)}) custom-call(f32[4,2,128,128]{3,2,1,0:T(8,128)S(1)} %copy-done, f32[1,2,64,256]{3,2,1,0:T(8,128)S(1)} %collective-permute-done.16.far_a, ...), custom_call_target="tpu_custom_call", output_to_operand_aliasing={{0}: (3, {}), {1}: (4, {}), {2}: (5, {})} | custom-call | flops 1006632960 | bytes 13369344 | tf_op jit(solution)/shard_map/other_line/pallas_call | solution.py:377
  48.9 0.1 collective-permute-done.15.psi_b
  49.1 0.4 far.1
  49.5 0.1 collective-permute-start.18
  49.6 1.0 %last_adjoint.1 = (bf16[2,16,2,64,256]{4,3,2,1,0:T(8,128)(2,1)S(1)}, f32[2,64,256]{2,1,0:T(8,128)S(1)}, f32[2,64,256]{2,1,0:T(8,128)S(1)}) custom-call(f32[4,2,128,128]{3,2,1,0:T(8,128)S(1)} %copy-done, bf16[2,16,2,64,256]{4,3,2,1,0:T(8,128)(2,1)S(1)} %get-tuple-element.43.phi_ref), custom_call_target="tpu_custom_call" | custom-call | flops 805306368 | bytes 4980736 | tf_op jit(solution)/shard_map/last_adjoint/pallas_call | solution.py:377
  50.6 0.3 collective-permute-done.18.e1_ref
  51.0 4.9 %section.3 = (bf16[2,256,256]{2,1,0:T(8,128)(2,1)S(1)}, f32[128,256]{1,0:T(8,128)S(1)}) custom-call(f32[128,256]{1,0:T(8,128)S(1)} %get-tuple-element.47.e0_ref, f32[128,256]{1,0:T(8,128)S(1)} %collective-permute-done.18.e1_ref, bf16[2,16,2,64,256]{4,3,2,1,0:T(8,128)(2,1)S(1)} %get-tuple-element.48.phi_ref, ...), custom_call_target="tpu_custom_call" | custom-call | flops 3221225472 | bytes 4849664 | tf_op jit(solution)/shard_map/section/pallas_call | solution.py:377
  55.8 0.3 collective-permute-start.19
  56.1 1.0 %apply.2.psi_ref = bf16[2,16,2,64,256]{4,3,2,1,0:T(8,128)(2,1)S(1)} custom-call(bf16[2,256,256]{2,1,0:T(8,128)(2,1)S(1)} %get-tuple-element.53.gate_ref, bf16[2,16,2,64,256]{4,3,2,1,0:T(8,128)(2,1)S(1)} %get-tuple-element.51.psi_ref), custom_call_target="tpu_custom_call" | custom-call | flops 805306368 | bytes 4456448 | tf_op jit(solution)/shard_map/apply/pallas_call | solution.py:377
  57.1 0.2 collective-permute-done.19.e1_ref
  57.2 4.8 %section.4 = (bf16[2,256,256]{2,1,0:T(8,128)(2,1)S(1)}, f32[128,256]{1,0:T(8,128)S(1)}) custom-call(f32[128,256]{1,0:T(8,128)S(1)} %get-tuple-element.52.e0_ref, f32[128,256]{1,0:T(8,128)S(1)} %collective-permute-done.19.e1_ref, bf16[2,16,2,64,256]{4,3,2,1,0:T(8,128)(2,1)S(1)} %get-tuple-element.43.phi_ref, bf16[2,16,2,64,256]{4,3,2,1,0:T(8,128)(2,1)S(1)} %apply.2.psi_ref), custom_call_target="tpu_custom_call" | custom-call | flops 3221225472 | bytes 4849664 | tf_op jit(solution)/shard_map/section/pallas_call | solution.py:377
  62.1 0.3 collective-permute-start.20
  62.3 0.3 collective-permute-start.22
  62.7 1.0 %apply.3.psi_ref = bf16[2,16,2,64,256]{4,3,2,1,0:T(8,128)(2,1)S(1)} custom-call(bf16[2,256,256]{2,1,0:T(8,128)(2,1)S(1)} %get-tuple-element.55.gate_ref, bf16[2,16,2,64,256]{4,3,2,1,0:T(8,128)(2,1)S(1)} %apply.2.psi_ref), custom_call_target="tpu_custom_call" | custom-call | flops 805306368 | bytes 4456448 | tf_op jit(solution)/shard_map/apply/pallas_call | solution.py:377
  63.7 5.1 %section.5 = (bf16[2,256,256]{2,1,0:T(8,128)(2,1)S(1)}, f32[128,256]{1,0:T(8,128)S(1)}) custom-call(f32[128,256]{1,0:T(8,128)S(1)} %get-tuple-element.54.e0_ref, f32[128,256]{1,0:T(8,128)S(1)} %collective-permute-done.20.e1_ref, bf16[2,16,2,64,256]{4,3,2,1,0:T(8,128)(2,1)S(1)} %get-tuple-element.50.phi_ref, bf16[2,16,2,64,256]{4,3,2,1,0:T(8,128)(2,1)S(1)} %apply.3.psi_ref), custom_call_target="tpu_custom_call" | custom-call | flops 3221225472 | bytes 4849664 | tf_op jit(solution)/shard_map/section/pallas_call | solution.py:377
  68.7 0.3 collective-permute-start.21
  69.0 0.4 ends.1
  69.4 0.4 collective-permute-start.23
  69.8 0.0 collective-permute-done.22.got_ref
  69.8 0.1 unpack.1.adjoint_ref
  69.9 0.3 collective-permute-done.21.e1_ref
  70.2 3.5 %last_polar.1 = (f32[256,256]{1,0:T(8,128)S(1)}, f32[2,256,128]{2,1,0:T(8,128)}) custom-call(f32[128,256]{1,0:T(8,128)S(1)} %get-tuple-element.56.e0_ref, f32[128,256]{1,0:T(8,128)S(1)} %collective-permute-done.21.e1_ref, f32[2,256,128]{2,1,0:T(8,128)S(1)} %unpack.1.adjoint_ref), custom_call_target="tpu_custom_call" | custom-call | flops 1610612736 | bytes 1048576 | tf_op jit(solution)/shard_map/last_polar/pallas_call | solution.py:377
  73.6 0.0 collective-permute-done.23.psi_got
  73.6 1.1 %last_apply.1 = f32[2,256,128]{2,1,0:T(8,128)} custom-call(f32[256,256]{1,0:T(8,128)S(1)} %get-tuple-element.61.gate_ref, f32[2,2,64,256]{3,2,1,0:T(8,128)S(1)} %get-tuple-element.63.psi_own, f32[2,2,64,256]{3,2,1,0:T(8,128)S(1)} %collective-permute-done.23.psi_got), custom_call_target="tpu_custom_call" | custom-call | flops 201326592 | bytes 1048576 | tf_op jit(solution)/shard_map/last_apply/pallas_call | solution.py:377
  (13 shorter events, 0.1 us)
Async XLA Ops:
  0.6 1.0 %copy-start.1 = (f32[2,256,128]{2,1,0:T(8,128)S(1)}, f32[2,256,128]{2,1,0:T(8,128)}, u32[]{:S(2)}) copy-start(f32[2,256,128]{2,1,0:T(8,128)} %x_ref.3) | copy-start | bytes 786436
  1.6 36.8 %copy-start = (f32[4,2,128,128]{3,2,1,0:T(8,128)S(1)}, f32[4,2,128,128]{3,2,1,0:T(8,128)}, u32[]{:S(2)}) copy-start(f32[4,2,128,128]{3,2,1,0:T(8,128)} %gates_ref.7) | copy-start | bytes 1572868
  1.7 1.6 %collective-permute-start = (f32[2,64,256]{2,1,0:T(8,128)S(1)}, f32[2,64,256]{2,1,0:T(8,128)S(1)}, u32[]{:S(2)}, u32[]{:S(2)}) collective-permute-start(f32[2,64,256]{2,1,0:T(8,128)S(1)} %get-tuple-element.37), channel_id=1, source_target_pairs={{0,1},{1,0},{2,3},{3,2},{4,5},{5,4},{6,7},{7,6},{8,9},{9,8},{10,11... | collective-permute-start | bytes 393224 | tf_op jit(solution)/shard_map/ppermute | solution.py:413
  2.2 0.9 %copy-start.2 = (f32[2,256,128]{2,1,0:T(8,128)S(1)}, f32[2,256,128]{2,1,0:T(8,128)}, u32[]{:S(2)}) copy-start(f32[2,256,128]{2,1,0:T(8,128)} %x_ref.2) | copy-start | bytes 786436
  3.4 3.2 %collective-permute-start.1 = (f32[2,64,256]{2,1,0:T(8,128)S(1)}, f32[2,64,256]{2,1,0:T(8,128)S(1)}, u32[]{:S(2)}, u32[]{:S(2)}) collective-permute-start(f32[2,64,256]{2,1,0:T(8,128)S(1)} %get-tuple-element.38), channel_id=1, source_target_pairs={{0,1},{1,0},{2,3},{3,2},{4,5},{5,4},{6,7},{7,6},{8,9},{9,8},{10,11... | collective-permute-start | bytes 393224 | tf_op jit(solution)/shard_map/ppermute | solution.py:413
  3.7 9.9 %collective-permute-start.10 = (f32[2,2,64,256]{3,2,1,0:T(8,128)S(1)}, f32[2,2,64,256]{3,2,1,0:T(8,128)S(1)}, u32[]{:S(2)}, u32[]{:S(2)}) collective-permute-start(f32[2,2,64,256]{3,2,1,0:T(8,128)S(1)} %pad_maximum_fusion.refs_0_), channel_id=1, source_target_pairs={{0,2},{1,3},{2,6},{3,7},{4,0},{5,1},{6,10},{7,11},{8,4},{9,5},{10,... | collective-permute-start | bytes 786440 | tf_op jit(solution)/shard_map/ppermute | solution.py:76
  6.5 9.2 %collective-permute-start.9 = (f32[2,2,64,256]{3,2,1,0:T(8,128)S(1)}, f32[2,2,64,256]{3,2,1,0:T(8,128)S(1)}, u32[]{:S(2)}, u32[]{:S(2)}) collective-permute-start(f32[2,2,64,256]{3,2,1,0:T(8,128)S(1)} %pad_maximum_fusion.refs_0_), channel_id=1, source_target_pairs={{0,4},{1,5},{2,0},{3,1},{4,8},{5,9},{6,2},{7,3},{8,12},{9,13},{10,... | collective-permute-start | bytes 786440 | tf_op jit(solution)/shard_map/ppermute | solution.py:76
  6.5 14.7 %collective-permute-start.2 = (f32[2,2,64,256]{3,2,1,0:T(8,128)S(1)}, f32[2,2,64,256]{3,2,1,0:T(8,128)S(1)}, u32[]{:S(2)}, u32[]{:S(2)}) collective-permute-start(f32[2,2,64,256]{3,2,1,0:T(8,128)S(1)} %pad_maximum_fusion.1.refs_0_), channel_id=1, source_target_pairs={{0,4},{1,5},{2,0},{3,1},{4,8},{5,9},{6,2},{7,3},{8,12},{9,13},{10,... | collective-permute-start | bytes 786440 | tf_op jit(solution)/shard_map/ppermute | solution.py:76
  8.6 12.7 %collective-permute-start.6 = (f32[2,2,64,256]{3,2,1,0:T(8,128)S(1)}, f32[2,2,64,256]{3,2,1,0:T(8,128)S(1)}, u32[]{:S(2)}, u32[]{:S(2)}) collective-permute-start(f32[2,2,64,256]{3,2,1,0:T(8,128)S(1)} %pad_maximum_fusion.1.refs_0_), channel_id=1, source_target_pairs={{0,2},{1,3},{2,6},{3,7},{4,0},{5,1},{6,10},{7,11},{8,4},{9,5},{10,... | collective-permute-start | bytes 786440 | tf_op jit(solution)/shard_map/ppermute | solution.py:76
  13.6 11.2 %collective-permute-start.12 = (f32[2,2,64,256]{3,2,1,0:T(8,128)S(1)}, f32[2,2,64,256]{3,2,1,0:T(8,128)S(1)}, u32[]{:S(2)}, u32[]{:S(2)}) collective-permute-start(f32[2,2,64,256]{3,2,1,0:T(8,128)S(1)} %collective-permute-done.10.refs_2_), channel_id=1, source_target_pairs={{0,2},{1,3},{2,6},{3,7},{4,0},{5,1},{6,10},{7,11},{8,4},{9,5},{10,... | collective-permute-start | bytes 786440 | tf_op jit(solution)/shard_map/ppermute | solution.py:76
  15.6 11.2 %collective-permute-start.11 = (f32[2,2,64,256]{3,2,1,0:T(8,128)S(1)}, f32[2,2,64,256]{3,2,1,0:T(8,128)S(1)}, u32[]{:S(2)}, u32[]{:S(2)}) collective-permute-start(f32[2,2,64,256]{3,2,1,0:T(8,128)S(1)} %collective-permute-done.9.refs_1_), channel_id=1, source_target_pairs={{0,4},{1,5},{2,0},{3,1},{4,8},{5,9},{6,2},{7,3},{8,12},{9,13},{10,... | collective-permute-start | bytes 786440 | tf_op jit(solution)/shard_map/ppermute | solution.py:76
  21.3 11.2 %collective-permute-start.3 = (f32[2,2,64,256]{3,2,1,0:T(8,128)S(1)}, f32[2,2,64,256]{3,2,1,0:T(8,128)S(1)}, u32[]{:S(2)}, u32[]{:S(2)}) collective-permute-start(f32[2,2,64,256]{3,2,1,0:T(8,128)S(1)} %collective-permute-done.2.refs_1_), channel_id=1, source_target_pairs={{0,4},{1,5},{2,0},{3,1},{4,8},{5,9},{6,2},{7,3},{8,12},{9,13},{10,... | collective-permute-start | bytes 786440 | tf_op jit(solution)/shard_map/ppermute | solution.py:76
  21.3 11.2 %collective-permute-start.7 = (f32[2,2,64,256]{3,2,1,0:T(8,128)S(1)}, f32[2,2,64,256]{3,2,1,0:T(8,128)S(1)}, u32[]{:S(2)}, u32[]{:S(2)}) collective-permute-start(f32[2,2,64,256]{3,2,1,0:T(8,128)S(1)} %collective-permute-done.6.refs_2_), channel_id=1, source_target_pairs={{0,2},{1,3},{2,6},{3,7},{4,0},{5,1},{6,10},{7,11},{8,4},{9,5},{10,... | collective-permute-start | bytes 786440 | tf_op jit(solution)/shard_map/ppermute | solution.py:76
  24.8 11.4 %collective-permute-start.14 = (f32[2,2,64,256]{3,2,1,0:T(8,128)S(1)}, f32[2,2,64,256]{3,2,1,0:T(8,128)S(1)}, u32[]{:S(2)}, u32[]{:S(2)}) collective-permute-start(f32[2,2,64,256]{3,2,1,0:T(8,128)S(1)} %collective-permute-done.12.refs_4_), channel_id=1, source_target_pairs={{0,2},{1,3},{2,6},{3,7},{4,0},{5,1},{6,10},{7,11},{8,4},{9,5},{10,... | collective-permute-start | bytes 786440 | tf_op jit(solution)/shard_map/ppermute | solution.py:76
  26.9 11.3 %collective-permute-start.13 = (f32[2,2,64,256]{3,2,1,0:T(8,128)S(1)}, f32[2,2,64,256]{3,2,1,0:T(8,128)S(1)}, u32[]{:S(2)}, u32[]{:S(2)}) collective-permute-start(f32[2,2,64,256]{3,2,1,0:T(8,128)S(1)} %collective-permute-done.11.refs_3_), channel_id=1, source_target_pairs={{0,4},{1,5},{2,0},{3,1},{4,8},{5,9},{6,2},{7,3},{8,12},{9,13},{10,... | collective-permute-start | bytes 786440 | tf_op jit(solution)/shard_map/ppermute | solution.py:76
  32.5 11.2 %collective-permute-start.4 = (f32[2,2,64,256]{3,2,1,0:T(8,128)S(1)}, f32[2,2,64,256]{3,2,1,0:T(8,128)S(1)}, u32[]{:S(2)}, u32[]{:S(2)}) collective-permute-start(f32[2,2,64,256]{3,2,1,0:T(8,128)S(1)} %collective-permute-done.3.refs_3_), channel_id=1, source_target_pairs={{0,4},{1,5},{2,0},{3,1},{4,8},{5,9},{6,2},{7,3},{8,12},{9,13},{10,... | collective-permute-start | bytes 786440 | tf_op jit(solution)/shard_map/ppermute | solution.py:76
  32.5 11.4 %collective-permute-start.8 = (f32[2,2,64,256]{3,2,1,0:T(8,128)S(1)}, f32[2,2,64,256]{3,2,1,0:T(8,128)S(1)}, u32[]{:S(2)}, u32[]{:S(2)}) collective-permute-start(f32[2,2,64,256]{3,2,1,0:T(8,128)S(1)} %collective-permute-done.7.refs_4_), channel_id=1, source_target_pairs={{0,2},{1,3},{2,6},{3,7},{4,0},{5,1},{6,10},{7,11},{8,4},{9,5},{10,... | collective-permute-start | bytes 786440 | tf_op jit(solution)/shard_map/ppermute | solution.py:76
  36.2 11.0 %collective-permute-start.17 = (f32[1,2,64,256]{3,2,1,0:T(8,128)S(1)}, f32[1,2,64,256]{3,2,1,0:T(8,128)S(1)}, u32[]{:S(2)}, u32[]{:S(2)}) collective-permute-start(f32[1,2,64,256]{3,2,1,0:T(8,128)S(1)} %slice.19), channel_id=1, source_target_pairs={{0,2},{1,3},{2,6},{3,7},{4,0},{5,1},{6,10},{7,11},{8,4},{9,5},{10,... | collective-permute-start | bytes 393224 | tf_op jit(solution)/shard_map/ppermute | solution.py:82
  38.2 8.9 %collective-permute-start.16 = (f32[1,2,64,256]{3,2,1,0:T(8,128)S(1)}, f32[1,2,64,256]{3,2,1,0:T(8,128)S(1)}, u32[]{:S(2)}, u32[]{:S(2)}) collective-permute-start(f32[1,2,64,256]{3,2,1,0:T(8,128)S(1)} %slice.18), channel_id=1, source_target_pairs={{0,4},{1,5},{2,0},{3,1},{4,8},{5,9},{6,2},{7,3},{8,12},{9,13},{10,... | collective-permute-start | bytes 393224 | tf_op jit(solution)/shard_map/ppermute | solution.py:82
  43.7 5.2 %collective-permute-start.5 = (f32[1,2,64,256]{3,2,1,0:T(8,128)S(1)}, f32[1,2,64,256]{3,2,1,0:T(8,128)S(1)}, u32[]{:S(2)}, u32[]{:S(2)}) collective-permute-start(f32[1,2,64,256]{3,2,1,0:T(8,128)S(1)} %slice.16), channel_id=1, source_target_pairs={{0,4},{1,5},{2,0},{3,1},{4,8},{5,9},{6,2},{7,3},{8,12},{9,13},{10,... | collective-permute-start | bytes 393224 | tf_op jit(solution)/shard_map/ppermute | solution.py:82
  43.9 5.2 %collective-permute-start.15 = (f32[1,2,64,256]{3,2,1,0:T(8,128)S(1)}, f32[1,2,64,256]{3,2,1,0:T(8,128)S(1)}, u32[]{:S(2)}, u32[]{:S(2)}) collective-permute-start(f32[1,2,64,256]{3,2,1,0:T(8,128)S(1)} %slice.17), channel_id=1, source_target_pairs={{0,2},{1,3},{2,6},{3,7},{4,0},{5,1},{6,10},{7,11},{8,4},{9,5},{10,... | collective-permute-start | bytes 393224 | tf_op jit(solution)/shard_map/ppermute | solution.py:82
  49.5 1.4 %collective-permute-start.18 = (f32[128,256]{1,0:T(8,128)S(1)}, f32[128,256]{1,0:T(8,128)S(1)}, u32[]{:S(2)}, u32[]{:S(2)}) collective-permute-start(f32[128,256]{1,0:T(8,128)S(1)} %get-tuple-element.47.e0_ref), channel_id=1, source_target_pairs={{0,1},{1,0},{2,3},{3,2},{4,5},{5,4},{6,7},{7,6},{8,9},{9,8},{10,11... | collective-permute-start | bytes 393224 | tf_op jit(solution)/shard_map/ppermute | solution.py:410
  55.8 1.4 %collective-permute-start.19 = (f32[128,256]{1,0:T(8,128)S(1)}, f32[128,256]{1,0:T(8,128)S(1)}, u32[]{:S(2)}, u32[]{:S(2)}) collective-permute-start(f32[128,256]{1,0:T(8,128)S(1)} %get-tuple-element.52.e0_ref), channel_id=1, source_target_pairs={{0,1},{1,0},{2,3},{3,2},{4,5},{5,4},{6,7},{7,6},{8,9},{9,8},{10,11... | collective-permute-start | bytes 393224 | tf_op jit(solution)/shard_map/ppermute | solution.py:410
  62.1 1.6 %collective-permute-start.20 = (f32[128,256]{1,0:T(8,128)S(1)}, f32[128,256]{1,0:T(8,128)S(1)}, u32[]{:S(2)}, u32[]{:S(2)}) collective-permute-start(f32[128,256]{1,0:T(8,128)S(1)} %get-tuple-element.54.e0_ref), channel_id=1, source_target_pairs={{0,1},{1,0},{2,3},{3,2},{4,5},{5,4},{6,7},{7,6},{8,9},{9,8},{10,11... | collective-permute-start | bytes 393224 | tf_op jit(solution)/shard_map/ppermute | solution.py:410
  62.3 7.4 %collective-permute-start.22 = (f32[2,64,256]{2,1,0:T(8,128)S(1)}, f32[2,64,256]{2,1,0:T(8,128)S(1)}, u32[]{:S(2)}, u32[]{:S(2)}) collective-permute-start(f32[2,64,256]{2,1,0:T(8,128)S(1)} %get-tuple-element.60), channel_id=1, source_target_pairs={{0,1},{1,0},{2,3},{3,2},{4,5},{5,4},{6,7},{7,6},{8,9},{9,8},{10,11... | collective-permute-start | bytes 393224 | tf_op jit(solution)/shard_map/ppermute | solution.py:461
  68.7 1.4 %collective-permute-start.21 = (f32[128,256]{1,0:T(8,128)S(1)}, f32[128,256]{1,0:T(8,128)S(1)}, u32[]{:S(2)}, u32[]{:S(2)}) collective-permute-start(f32[128,256]{1,0:T(8,128)S(1)} %get-tuple-element.56.e0_ref), channel_id=1, source_target_pairs={{0,1},{1,0},{2,3},{3,2},{4,5},{5,4},{6,7},{7,6},{8,9},{9,8},{10,11... | collective-permute-start | bytes 393224 | tf_op jit(solution)/shard_map/ppermute | solution.py:410
  69.4 4.3 %collective-permute-start.23 = (f32[2,2,64,256]{3,2,1,0:T(8,128)S(1)}, f32[2,2,64,256]{3,2,1,0:T(8,128)S(1)}, u32[]{:S(2)}, u32[]{:S(2)}) collective-permute-start(f32[2,2,64,256]{3,2,1,0:T(8,128)S(1)} %get-tuple-element.64), channel_id=1, source_target_pairs={{0,1},{1,0},{2,3},{3,2},{4,5},{5,4},{6,7},{7,6},{8,9},{9,8},{10,11... | collective-permute-start | bytes 786440 | tf_op jit(solution)/shard_map/ppermute | solution.py:472

commit v9 on v7

--- a/solution.py
+++ b/solution.py
@@ -114,11 +114,11 @@
         turns = [turned(v) for v in xs]
         beside(2 * k)
         h = jnp.concatenate([dot3(xs, xs, NT), dot3(xs, turns, NT)], 1)
-        h = split(h * (scale * scale) if k == 0 else h)
+        h = split(h * (-0.5 * scale * scale) if k == 0 else -0.5 * h)
         beside(2 * k + 1)
         rows = [jnp.concatenate(pair, 0) for pair in zip(xs, turns)]
         both = dot(jnp.concatenate(h, 0), rows[0], NN)
-        x = 1.5 * x - 0.5 * (both[:n] + both[n:] + dot(h[0], rows[1], NN))
+        x = 1.5 * x + (both[:n] + both[n:] + dot(h[0], rows[1], NN))
         x = x * scale if k == 0 else x
     return x
 

time: 75.1 us -> 75.1 us (level)
  no operation moved by 1% of the time
where the time goes in v9:
time: 75.1 us; the launch traced here: 74.9 us
  Pallas kernels  29.7 us (40%)
  waiting for transfers between devices  22.3 us (30%)
  starting transfers between devices  19.9 us (26%)
  local copies, waits for them, and re-layouts  1.93 us (3%)
  between operations  1.05 us (1%)
    pallas_call x17, Pallas kernels, call(): pl.pallas_call(kernel, out_shape=outs, in_specs=[spec] * len(ins), out_sp...  29.7 us
    ppermute x12, waiting for transfers between devices, gather_ring(): lax.ppermute(end, 'long', layout.ring(step))  21.4 us
    ppermute x12, starting transfers between devices, gather_ring(): lax.ppermute(end, 'long', layout.ring(step))  13 us
    ppermute x4, starting transfers between devices, last_step(): lax.ppermute(end, 'long', layout.ring(step))  4.46 us
    unnamed x6, local copies, waits for them, and re-layouts  1.9 us
  transfers between devices with their start and end apart: 24, of which 10 were waited for; matrix products, arithmetic and copies ran while one was open for 0% of the time, Pallas kernels for 25%

profile of v9, /device:TPU:0, one launch (start us, length us, event | category | flops | bytes accessed | tf_op | source)
XLA Modules:
  0.0 74.9 jit_solution(2143447382126485856)
XLA Ops:
  0.6 0.9 %copy-done.1 = f32[2,256,128]{2,1,0:T(8,128)S(1)} copy-done((f32[2,256,128]{2,1,0:T(8,128)S(1)}, f32[2,256,128]{2,1,0:T(8,128)}, u32[]{:S(2)}) %copy-start.1) | copy-done | bytes 262168
  1.6 0.1 pack.2
  1.7 0.5 collective-permute-start
  2.2 0.9 %copy-done.2 = f32[2,256,128]{2,1,0:T(8,128)S(1)} copy-done((f32[2,256,128]{2,1,0:T(8,128)S(1)}, f32[2,256,128]{2,1,0:T(8,128)}, u32[]{:S(2)}) %copy-start.2) | copy-done | bytes 262168
  3.2 0.1 pack.3
  3.3 0.0 collective-permute-done
  3.4 0.3 collective-permute-start.1
  3.7 2.8 %collective-permute-start.10 = (f32[2,2,64,256]{3,2,1,0:T(8,128)S(1)}, f32[2,2,64,256]{3,2,1,0:T(8,128)S(1)}, u32[]{:S(2)}, u32[]{:S(2)}) collective-permute-start(f32[2,2,64,256]{3,2,1,0:T(8,128)S(1)} %pad_maximum_fusion.refs_0_), channel_id=1, source_target_pairs={{0,2},{1,3},{2,6},{3,7},{4,0},{5,1},{6,10},{7,11},{8,4},{9,5},{10,... | collective-permute-start | bytes 786440 | tf_op jit(solution)/shard_map/ppermute | solution.py:76
  6.5 0.1 collective-permute-start.9
  6.5 0.0 collective-permute-done.1
  6.5 2.1 %collective-permute-start.2 = (f32[2,2,64,256]{3,2,1,0:T(8,128)S(1)}, f32[2,2,64,256]{3,2,1,0:T(8,128)S(1)}, u32[]{:S(2)}, u32[]{:S(2)}) collective-permute-start(f32[2,2,64,256]{3,2,1,0:T(8,128)S(1)} %pad_maximum_fusion.1.refs_0_), channel_id=1, source_target_pairs={{0,4},{1,5},{2,0},{3,1},{4,8},{5,9},{6,2},{7,3},{8,12},{9,13},{10,... | collective-permute-start | bytes 786440 | tf_op jit(solution)/shard_map/ppermute | solution.py:76
  8.6 0.0 collective-permute-start.6
  8.6 5.0 %collective-permute-done.10.refs_2_ = f32[2,2,64,256]{3,2,1,0:T(8,128)S(1)} collective-permute-done((f32[2,2,64,256]{3,2,1,0:T(8,128)S(1)}, f32[2,2,64,256]{3,2,1,0:T(8,128)S(1)}, u32[]{:S(2)}, u32[]{:S(2)}) %collective-permute-start.10) | collective-permute-done | bytes 262176 | tf_op jit(solution)/shard_map/ppermute | solution.py:76
  13.6 2.0 %collective-permute-start.12 = (f32[2,2,64,256]{3,2,1,0:T(8,128)S(1)}, f32[2,2,64,256]{3,2,1,0:T(8,128)S(1)}, u32[]{:S(2)}, u32[]{:S(2)}) collective-permute-start(f32[2,2,64,256]{3,2,1,0:T(8,128)S(1)} %collective-permute-done.10.refs_2_), channel_id=1, source_target_pairs={{0,2},{1,3},{2,6},{3,7},{4,0},{5,1},{6,10},{7,11},{8,4},{9,5},{10,... | collective-permute-start | bytes 786440 | tf_op jit(solution)/shard_map/ppermute | solution.py:76
  15.6 0.0 collective-permute-done.9.refs_1_
  15.6 0.0 collective-permute-start.11
  15.7 5.6 %collective-permute-done.2.refs_1_ = f32[2,2,64,256]{3,2,1,0:T(8,128)S(1)} collective-permute-done((f32[2,2,64,256]{3,2,1,0:T(8,128)S(1)}, f32[2,2,64,256]{3,2,1,0:T(8,128)S(1)}, u32[]{:S(2)}, u32[]{:S(2)}) %collective-permute-start.2) | collective-permute-done | bytes 262176 | tf_op jit(solution)/shard_map/ppermute | solution.py:76
  21.3 0.0 collective-permute-start.3
  21.3 0.0 collective-permute-done.6.refs_2_
  21.3 2.0 %collective-permute-start.7 = (f32[2,2,64,256]{3,2,1,0:T(8,128)S(1)}, f32[2,2,64,256]{3,2,1,0:T(8,128)S(1)}, u32[]{:S(2)}, u32[]{:S(2)}) collective-permute-start(f32[2,2,64,256]{3,2,1,0:T(8,128)S(1)} %collective-permute-done.6.refs_2_), channel_id=1, source_target_pairs={{0,2},{1,3},{2,6},{3,7},{4,0},{5,1},{6,10},{7,11},{8,4},{9,5},{10,... | collective-permute-start | bytes 786440 | tf_op jit(solution)/shard_map/ppermute | solution.py:76
  23.3 1.5 %collective-permute-done.12.refs_4_ = f32[2,2,64,256]{3,2,1,0:T(8,128)S(1)} collective-permute-done((f32[2,2,64,256]{3,2,1,0:T(8,128)S(1)}, f32[2,2,64,256]{3,2,1,0:T(8,128)S(1)}, u32[]{:S(2)}, u32[]{:S(2)}) %collective-permute-start.12) | collective-permute-done | bytes 262176 | tf_op jit(solution)/shard_map/ppermute | solution.py:76
  24.8 2.0 %collective-permute-start.14 = (f32[2,2,64,256]{3,2,1,0:T(8,128)S(1)}, f32[2,2,64,256]{3,2,1,0:T(8,128)S(1)}, u32[]{:S(2)}, u32[]{:S(2)}) collective-permute-start(f32[2,2,64,256]{3,2,1,0:T(8,128)S(1)} %collective-permute-done.12.refs_4_), channel_id=1, source_target_pairs={{0,2},{1,3},{2,6},{3,7},{4,0},{5,1},{6,10},{7,11},{8,4},{9,5},{10,... | collective-permute-start | bytes 786440 | tf_op jit(solution)/shard_map/ppermute | solution.py:76
  26.8 0.0 collective-permute-done.11.refs_3_
  26.9 0.0 collective-permute-start.13
  26.9 5.6 %collective-permute-done.3.refs_3_ = f32[2,2,64,256]{3,2,1,0:T(8,128)S(1)} collective-permute-done((f32[2,2,64,256]{3,2,1,0:T(8,128)S(1)}, f32[2,2,64,256]{3,2,1,0:T(8,128)S(1)}, u32[]{:S(2)}, u32[]{:S(2)}) %collective-permute-start.3) | collective-permute-done | bytes 262176 | tf_op jit(solution)/shard_map/ppermute | solution.py:76
  32.5 0.0 collective-permute-start.4
  32.5 0.0 collective-permute-done.7.refs_4_
  32.5 2.0 %collective-permute-start.8 = (f32[2,2,64,256]{3,2,1,0:T(8,128)S(1)}, f32[2,2,64,256]{3,2,1,0:T(8,128)S(1)}, u32[]{:S(2)}, u32[]{:S(2)}) collective-permute-start(f32[2,2,64,256]{3,2,1,0:T(8,128)S(1)} %collective-permute-done.7.refs_4_), channel_id=1, source_target_pairs={{0,2},{1,3},{2,6},{3,7},{4,0},{5,1},{6,10},{7,11},{8,4},{9,5},{10,... | collective-permute-start | bytes 786440 | tf_op jit(solution)/shard_map/ppermute | solution.py:76
  34.5 1.7 %collective-permute-done.14.refs_6_ = f32[2,2,64,256]{3,2,1,0:T(8,128)S(1)} collective-permute-done((f32[2,2,64,256]{3,2,1,0:T(8,128)S(1)}, f32[2,2,64,256]{3,2,1,0:T(8,128)S(1)}, u32[]{:S(2)}, u32[]{:S(2)}) %collective-permute-start.14) | collective-permute-done | bytes 262176 | tf_op jit(solution)/shard_map/ppermute | solution.py:76
  36.2 2.0 %collective-permute-start.17 = (f32[1,2,64,256]{3,2,1,0:T(8,128)S(1)}, f32[1,2,64,256]{3,2,1,0:T(8,128)S(1)}, u32[]{:S(2)}, u32[]{:S(2)}) collective-permute-start(f32[1,2,64,256]{3,2,1,0:T(8,128)S(1)} %slice.19), channel_id=1, source_target_pairs={{0,2},{1,3},{2,6},{3,7},{4,0},{5,1},{6,10},{7,11},{8,4},{9,5},{10,... | collective-permute-start | bytes 393224 | tf_op jit(solution)/shard_map/ppermute | solution.py:82
  38.2 0.0 collective-permute-done.13.refs_5_
  38.2 0.1 collective-permute-start.16
  38.4 2.4 %first_gate.1.phi0_ref.refs_7_.phi0_in = bf16[2,16,2,64,256]{4,3,2,1,0:T(8,128)(2,1)S(1)} custom-call(f32[4,2,128,128]{3,2,1,0:T(8,128)S(1)} %copy-done, f32[2,2,64,256]{3,2,1,0:T(8,128)S(1)} %pad_maximum_fusion.refs_0_, f32[2,2,64,256]{3,2,1,0:T(8,128)S(1)} %collective-permute-done.9.refs_1_, f32[2,2,64,256]{3,2,1,0:T(8,128)S(1)} %collective-permute-done.10.refs_2_, ...), custom_call_target="tpu_custom_call" | custom-call | flops 805306368 | bytes 4456448 | tf_op jit(solution)/shard_map/first_gate/pallas_call | solution.py:377
  40.8 1.0 %line.1 = (bf16[2,16,2,64,256]{4,3,2,1,0:T(8,128)(2,1)S(1)}, bf16[2,16,2,64,256]{4,3,2,1,0:T(8,128)(2,1)S(1)}) custom-call(f32[4,2,128,128]{3,2,1,0:T(8,128)S(1)} %copy-done, bf16[2,16,2,64,256]{4,3,2,1,0:T(8,128)(2,1)S(1)} %first_gate.1.phi0_ref.refs_7_.phi0_in), custom_call_target="tpu_custom_call" | custom-call | flops 805306368 | bytes 6815744 | tf_op jit(solution)/shard_map/line/pallas_call | solution.py:377
  41.8 1.9 %collective-permute-done.4.refs_5_ = f32[2,2,64,256]{3,2,1,0:T(8,128)S(1)} collective-permute-done((f32[2,2,64,256]{3,2,1,0:T(8,128)S(1)}, f32[2,2,64,256]{3,2,1,0:T(8,128)S(1)}, u32[]{:S(2)}, u32[]{:S(2)}) %collective-permute-start.4) | collective-permute-done | bytes 262176 | tf_op jit(solution)/shard_map/ppermute | solution.py:76
  43.7 0.1 collective-permute-start.5
  43.9 0.0 collective-permute-done.8.refs_6_
  43.9 2.2 %collective-permute-start.15 = (f32[1,2,64,256]{3,2,1,0:T(8,128)S(1)}, f32[1,2,64,256]{3,2,1,0:T(8,128)S(1)}, u32[]{:S(2)}, u32[]{:S(2)}) collective-permute-start(f32[1,2,64,256]{3,2,1,0:T(8,128)S(1)} %slice.17), channel_id=1, source_target_pairs={{0,2},{1,3},{2,6},{3,7},{4,0},{5,1},{6,10},{7,11},{8,4},{9,5},{10,... | collective-permute-start | bytes 393224 | tf_op jit(solution)/shard_map/ppermute | solution.py:82
  46.1 1.1 %near.1 = (bf16[2,16,2,64,256]{4,3,2,1,0:T(8,128)(2,1)S(1)}, f32[256,256]{1,0:T(8,128)S(1)}) custom-call(f32[2,2,64,256]{3,2,1,0:T(8,128)S(1)} %pad_maximum_fusion.1.refs_0_, f32[2,2,64,256]{3,2,1,0:T(8,128)S(1)} %collective-permute-done.2.refs_1_, f32[2,2,64,256]{3,2,1,0:T(8,128)S(1)} %collective-permute-done.6.refs_2_, ...), custom_call_target="tpu_custom_call" | custom-call | flops 603979776 | bytes 6291456 | tf_op jit(solution)/shard_map/near/pallas_call | solution.py:377
  47.2 0.0 collective-permute-done.17.far_b
  47.2 0.0 collective-permute-done.16.far_a
  47.2 1.8 %other_line.1 = (bf16[2,16,2,64,256]{4,3,2,1,0:T(8,128)(2,1)S(1)}, bf16[2,16,2,64,256]{4,3,2,1,0:T(8,128)(2,1)S(1)}, bf16[2,16,2,64,256]{4,3,2,1,0:T(8,128)(2,1)S(1)}) custom-call(f32[4,2,128,128]{3,2,1,0:T(8,128)S(1)} %copy-done, f32[1,2,64,256]{3,2,1,0:T(8,128)S(1)} %collective-permute-done.16.far_a, ...), custom_call_target="tpu_custom_call", output_to_operand_aliasing={{0}: (3, {}), {1}: (4, {}), {2}: (5, {})} | custom-call | flops 1006632960 | bytes 13369344 | tf_op jit(solution)/shard_map/other_line/pallas_call | solution.py:377
  48.9 0.1 collective-permute-done.15.psi_b
  49.1 0.4 far.1
  49.5 0.1 collective-permute-start.18
  49.6 1.0 %last_adjoint.1 = (bf16[2,16,2,64,256]{4,3,2,1,0:T(8,128)(2,1)S(1)}, f32[2,64,256]{2,1,0:T(8,128)S(1)}, f32[2,64,256]{2,1,0:T(8,128)S(1)}) custom-call(f32[4,2,128,128]{3,2,1,0:T(8,128)S(1)} %copy-done, bf16[2,16,2,64,256]{4,3,2,1,0:T(8,128)(2,1)S(1)} %get-tuple-element.47.phi_ref), custom_call_target="tpu_custom_call" | custom-call | flops 805306368 | bytes 4980736 | tf_op jit(solution)/shard_map/last_adjoint/pallas_call | solution.py:377
  50.6 0.3 collective-permute-done.18.e1_ref
  51.0 4.8 %section.3 = (bf16[2,256,256]{2,1,0:T(8,128)(2,1)S(1)}, f32[128,256]{1,0:T(8,128)S(1)}) custom-call(f32[128,256]{1,0:T(8,128)S(1)} %get-tuple-element.51.e0_ref, f32[128,256]{1,0:T(8,128)S(1)} %collective-permute-done.18.e1_ref, bf16[2,16,2,64,256]{4,3,2,1,0:T(8,128)(2,1)S(1)} %get-tuple-element.52.phi_ref, ...), custom_call_target="tpu_custom_call" | custom-call | flops 3221225472 | bytes 4849664 | tf_op jit(solution)/shard_map/section/pallas_call | solution.py:377
  55.8 0.3 collective-permute-start.19
  56.1 1.0 %apply.2.psi_ref = bf16[2,16,2,64,256]{4,3,2,1,0:T(8,128)(2,1)S(1)} custom-call(bf16[2,256,256]{2,1,0:T(8,128)(2,1)S(1)} %get-tuple-element.57.gate_ref, bf16[2,16,2,64,256]{4,3,2,1,0:T(8,128)(2,1)S(1)} %get-tuple-element.55.psi_ref), custom_call_target="tpu_custom_call" | custom-call | flops 805306368 | bytes 4456448 | tf_op jit(solution)/shard_map/apply/pallas_call | solution.py:377
  57.1 0.2 collective-permute-done.19.e1_ref
  57.2 4.8 %section.4 = (bf16[2,256,256]{2,1,0:T(8,128)(2,1)S(1)}, f32[128,256]{1,0:T(8,128)S(1)}) custom-call(f32[128,256]{1,0:T(8,128)S(1)} %get-tuple-element.56.e0_ref, f32[128,256]{1,0:T(8,128)S(1)} %collective-permute-done.19.e1_ref, bf16[2,16,2,64,256]{4,3,2,1,0:T(8,128)(2,1)S(1)} %get-tuple-element.47.phi_ref, bf16[2,16,2,64,256]{4,3,2,1,0:T(8,128)(2,1)S(1)} %apply.2.psi_ref), custom_call_target="tpu_custom_call" | custom-call | flops 3221225472 | bytes 4849664 | tf_op jit(solution)/shard_map/section/pallas_call | solution.py:377
  62.1 0.2 collective-permute-start.20
  62.3 0.3 collective-permute-start.22
  62.7 1.0 %apply.3.psi_ref = bf16[2,16,2,64,256]{4,3,2,1,0:T(8,128)(2,1)S(1)} custom-call(bf16[2,256,256]{2,1,0:T(8,128)(2,1)S(1)} %get-tuple-element.59.gate_ref, bf16[2,16,2,64,256]{4,3,2,1,0:T(8,128)(2,1)S(1)} %apply.2.psi_ref), custom_call_target="tpu_custom_call" | custom-call | flops 805306368 | bytes 4456448 | tf_op jit(solution)/shard_map/apply/pallas_call | solution.py:377
  63.7 5.1 %section.5 = (bf16[2,256,256]{2,1,0:T(8,128)(2,1)S(1)}, f32[128,256]{1,0:T(8,128)S(1)}) custom-call(f32[128,256]{1,0:T(8,128)S(1)} %get-tuple-element.58.e0_ref, f32[128,256]{1,0:T(8,128)S(1)} %collective-permute-done.20.e1_ref, bf16[2,16,2,64,256]{4,3,2,1,0:T(8,128)(2,1)S(1)} %get-tuple-element.54.phi_ref, bf16[2,16,2,64,256]{4,3,2,1,0:T(8,128)(2,1)S(1)} %apply.3.psi_ref), custom_call_target="tpu_custom_call" | custom-call | flops 3221225472 | bytes 4849664 | tf_op jit(solution)/shard_map/section/pallas_call | solution.py:377
  68.7 0.2 collective-permute-start.21
  69.0 0.4 ends.1
  69.4 0.4 collective-permute-start.23
  69.8 0.0 collective-permute-done.22.got_ref
  69.8 0.1 unpack.1.adjoint_ref
  69.9 0.3 collective-permute-done.21.e1_ref
  70.2 3.5 %last_polar.1 = (f32[256,256]{1,0:T(8,128)S(1)}, f32[2,256,128]{2,1,0:T(8,128)}) custom-call(f32[128,256]{1,0:T(8,128)S(1)} %get-tuple-element.60.e0_ref, f32[128,256]{1,0:T(8,128)S(1)} %collective-permute-done.21.e1_ref, f32[2,256,128]{2,1,0:T(8,128)S(1)} %unpack.1.adjoint_ref), custom_call_target="tpu_custom_call" | custom-call | flops 1610612736 | bytes 1048576 | tf_op jit(solution)/shard_map/last_polar/pallas_call | solution.py:377
  73.6 1.1 %last_apply.1 = f32[2,256,128]{2,1,0:T(8,128)} custom-call(f32[256,256]{1,0:T(8,128)S(1)} %get-tuple-element.65.gate_ref, f32[2,2,64,256]{3,2,1,0:T(8,128)S(1)} %get-tuple-element.67.psi_own, f32[2,2,64,256]{3,2,1,0:T(8,128)S(1)} %collective-permute-done.23.psi_got), custom_call_target="tpu_custom_call" | custom-call | flops 201326592 | bytes 1048576 | tf_op jit(solution)/shard_map/last_apply/pallas_call | solution.py:377
  (13 shorter events, 0.1 us)
Async XLA Ops:
  0.6 1.0 %copy-start.1 = (f32[2,256,128]{2,1,0:T(8,128)S(1)}, f32[2,256,128]{2,1,0:T(8,128)}, u32[]{:S(2)}) copy-start(f32[2,256,128]{2,1,0:T(8,128)} %x_ref.2) | copy-start | bytes 786436
  1.6 36.8 %copy-start = (f32[4,2,128,128]{3,2,1,0:T(8,128)S(1)}, f32[4,2,128,128]{3,2,1,0:T(8,128)}, u32[]{:S(2)}) copy-start(f32[4,2,128,128]{3,2,1,0:T(8,128)} %gates_ref.7) | copy-start | bytes 1572868
  1.7 1.6 %collective-permute-start = (f32[2,64,256]{2,1,0:T(8,128)S(1)}, f32[2,64,256]{2,1,0:T(8,128)S(1)}, u32[]{:S(2)}, u32[]{:S(2)}) collective-permute-start(f32[2,64,256]{2,1,0:T(8,128)S(1)} %get-tuple-element.37), channel_id=1, source_target_pairs={{0,1},{1,0},{2,3},{3,2},{4,5},{5,4},{6,7},{7,6},{8,9},{9,8},{10,11... | collective-permute-start | bytes 393224 | tf_op jit(solution)/shard_map/ppermute | solution.py:413
  2.2 0.9 %copy-start.2 = (f32[2,256,128]{2,1,0:T(8,128)S(1)}, f32[2,256,128]{2,1,0:T(8,128)}, u32[]{:S(2)}) copy-start(f32[2,256,128]{2,1,0:T(8,128)} %x_ref.3) | copy-start | bytes 786436
  3.4 3.2 %collective-permute-start.1 = (f32[2,64,256]{2,1,0:T(8,128)S(1)}, f32[2,64,256]{2,1,0:T(8,128)S(1)}, u32[]{:S(2)}, u32[]{:S(2)}) collective-permute-start(f32[2,64,256]{2,1,0:T(8,128)S(1)} %get-tuple-element.41), channel_id=1, source_target_pairs={{0,1},{1,0},{2,3},{3,2},{4,5},{5,4},{6,7},{7,6},{8,9},{9,8},{10,11... | collective-permute-start | bytes 393224 | tf_op jit(solution)/shard_map/ppermute | solution.py:413
  3.7 9.9 %collective-permute-start.10 = (f32[2,2,64,256]{3,2,1,0:T(8,128)S(1)}, f32[2,2,64,256]{3,2,1,0:T(8,128)S(1)}, u32[]{:S(2)}, u32[]{:S(2)}) collective-permute-start(f32[2,2,64,256]{3,2,1,0:T(8,128)S(1)} %pad_maximum_fusion.refs_0_), channel_id=1, source_target_pairs={{0,2},{1,3},{2,6},{3,7},{4,0},{5,1},{6,10},{7,11},{8,4},{9,5},{10,... | collective-permute-start | bytes 786440 | tf_op jit(solution)/shard_map/ppermute | solution.py:76
  6.5 9.2 %collective-permute-start.9 = (f32[2,2,64,256]{3,2,1,0:T(8,128)S(1)}, f32[2,2,64,256]{3,2,1,0:T(8,128)S(1)}, u32[]{:S(2)}, u32[]{:S(2)}) collective-permute-start(f32[2,2,64,256]{3,2,1,0:T(8,128)S(1)} %pad_maximum_fusion.refs_0_), channel_id=1, source_target_pairs={{0,4},{1,5},{2,0},{3,1},{4,8},{5,9},{6,2},{7,3},{8,12},{9,13},{10,... | collective-permute-start | bytes 786440 | tf_op jit(solution)/shard_map/ppermute | solution.py:76
  6.5 14.7 %collective-permute-start.2 = (f32[2,2,64,256]{3,2,1,0:T(8,128)S(1)}, f32[2,2,64,256]{3,2,1,0:T(8,128)S(1)}, u32[]{:S(2)}, u32[]{:S(2)}) collective-permute-start(f32[2,2,64,256]{3,2,1,0:T(8,128)S(1)} %pad_maximum_fusion.1.refs_0_), channel_id=1, source_target_pairs={{0,4},{1,5},{2,0},{3,1},{4,8},{5,9},{6,2},{7,3},{8,12},{9,13},{10,... | collective-permute-start | bytes 786440 | tf_op jit(solution)/shard_map/ppermute | solution.py:76
  8.6 12.7 %collective-permute-start.6 = (f32[2,2,64,256]{3,2,1,0:T(8,128)S(1)}, f32[2,2,64,256]{3,2,1,0:T(8,128)S(1)}, u32[]{:S(2)}, u32[]{:S(2)}) collective-permute-start(f32[2,2,64,256]{3,2,1,0:T(8,128)S(1)} %pad_maximum_fusion.1.refs_0_), channel_id=1, source_target_pairs={{0,2},{1,3},{2,6},{3,7},{4,0},{5,1},{6,10},{7,11},{8,4},{9,5},{10,... | collective-permute-start | bytes 786440 | tf_op jit(solution)/shard_map/ppermute | solution.py:76
  13.6 11.2 %collective-permute-start.12 = (f32[2,2,64,256]{3,2,1,0:T(8,128)S(1)}, f32[2,2,64,256]{3,2,1,0:T(8,128)S(1)}, u32[]{:S(2)}, u32[]{:S(2)}) collective-permute-start(f32[2,2,64,256]{3,2,1,0:T(8,128)S(1)} %collective-permute-done.10.refs_2_), channel_id=1, source_target_pairs={{0,2},{1,3},{2,6},{3,7},{4,0},{5,1},{6,10},{7,11},{8,4},{9,5},{10,... | collective-permute-start | bytes 786440 | tf_op jit(solution)/shard_map/ppermute | solution.py:76
  15.6 11.2 %collective-permute-start.11 = (f32[2,2,64,256]{3,2,1,0:T(8,128)S(1)}, f32[2,2,64,256]{3,2,1,0:T(8,128)S(1)}, u32[]{:S(2)}, u32[]{:S(2)}) collective-permute-start(f32[2,2,64,256]{3,2,1,0:T(8,128)S(1)} %collective-permute-done.9.refs_1_), channel_id=1, source_target_pairs={{0,4},{1,5},{2,0},{3,1},{4,8},{5,9},{6,2},{7,3},{8,12},{9,13},{10,... | collective-permute-start | bytes 786440 | tf_op jit(solution)/shard_map/ppermute | solution.py:76
  21.3 11.2 %collective-permute-start.3 = (f32[2,2,64,256]{3,2,1,0:T(8,128)S(1)}, f32[2,2,64,256]{3,2,1,0:T(8,128)S(1)}, u32[]{:S(2)}, u32[]{:S(2)}) collective-permute-start(f32[2,2,64,256]{3,2,1,0:T(8,128)S(1)} %collective-permute-done.2.refs_1_), channel_id=1, source_target_pairs={{0,4},{1,5},{2,0},{3,1},{4,8},{5,9},{6,2},{7,3},{8,12},{9,13},{10,... | collective-permute-start | bytes 786440 | tf_op jit(solution)/shard_map/ppermute | solution.py:76
  21.3 11.2 %collective-permute-start.7 = (f32[2,2,64,256]{3,2,1,0:T(8,128)S(1)}, f32[2,2,64,256]{3,2,1,0:T(8,128)S(1)}, u32[]{:S(2)}, u32[]{:S(2)}) collective-permute-start(f32[2,2,64,256]{3,2,1,0:T(8,128)S(1)} %collective-permute-done.6.refs_2_), channel_id=1, source_target_pairs={{0,2},{1,3},{2,6},{3,7},{4,0},{5,1},{6,10},{7,11},{8,4},{9,5},{10,... | collective-permute-start | bytes 786440 | tf_op jit(solution)/shard_map/ppermute | solution.py:76
  24.8 11.4 %collective-permute-start.14 = (f32[2,2,64,256]{3,2,1,0:T(8,128)S(1)}, f32[2,2,64,256]{3,2,1,0:T(8,128)S(1)}, u32[]{:S(2)}, u32[]{:S(2)}) collective-permute-start(f32[2,2,64,256]{3,2,1,0:T(8,128)S(1)} %collective-permute-done.12.refs_4_), channel_id=1, source_target_pairs={{0,2},{1,3},{2,6},{3,7},{4,0},{5,1},{6,10},{7,11},{8,4},{9,5},{10,... | collective-permute-start | bytes 786440 | tf_op jit(solution)/shard_map/ppermute | solution.py:76
  26.9 11.3 %collective-permute-start.13 = (f32[2,2,64,256]{3,2,1,0:T(8,128)S(1)}, f32[2,2,64,256]{3,2,1,0:T(8,128)S(1)}, u32[]{:S(2)}, u32[]{:S(2)}) collective-permute-start(f32[2,2,64,256]{3,2,1,0:T(8,128)S(1)} %collective-permute-done.11.refs_3_), channel_id=1, source_target_pairs={{0,4},{1,5},{2,0},{3,1},{4,8},{5,9},{6,2},{7,3},{8,12},{9,13},{10,... | collective-permute-start | bytes 786440 | tf_op jit(solution)/shard_map/ppermute | solution.py:76
  32.5 11.2 %collective-permute-start.4 = (f32[2,2,64,256]{3,2,1,0:T(8,128)S(1)}, f32[2,2,64,256]{3,2,1,0:T(8,128)S(1)}, u32[]{:S(2)}, u32[]{:S(2)}) collective-permute-start(f32[2,2,64,256]{3,2,1,0:T(8,128)S(1)} %collective-permute-done.3.refs_3_), channel_id=1, source_target_pairs={{0,4},{1,5},{2,0},{3,1},{4,8},{5,9},{6,2},{7,3},{8,12},{9,13},{10,... | collective-permute-start | bytes 786440 | tf_op jit(solution)/shard_map/ppermute | solution.py:76
  32.5 11.4 %collective-permute-start.8 = (f32[2,2,64,256]{3,2,1,0:T(8,128)S(1)}, f32[2,2,64,256]{3,2,1,0:T(8,128)S(1)}, u32[]{:S(2)}, u32[]{:S(2)}) collective-permute-start(f32[2,2,64,256]{3,2,1,0:T(8,128)S(1)} %collective-permute-done.7.refs_4_), channel_id=1, source_target_pairs={{0,2},{1,3},{2,6},{3,7},{4,0},{5,1},{6,10},{7,11},{8,4},{9,5},{10,... | collective-permute-start | bytes 786440 | tf_op jit(solution)/shard_map/ppermute | solution.py:76
  36.2 11.0 %collective-permute-start.17 = (f32[1,2,64,256]{3,2,1,0:T(8,128)S(1)}, f32[1,2,64,256]{3,2,1,0:T(8,128)S(1)}, u32[]{:S(2)}, u32[]{:S(2)}) collective-permute-start(f32[1,2,64,256]{3,2,1,0:T(8,128)S(1)} %slice.19), channel_id=1, source_target_pairs={{0,2},{1,3},{2,6},{3,7},{4,0},{5,1},{6,10},{7,11},{8,4},{9,5},{10,... | collective-permute-start | bytes 393224 | tf_op jit(solution)/shard_map/ppermute | solution.py:82
  38.2 8.9 %collective-permute-start.16 = (f32[1,2,64,256]{3,2,1,0:T(8,128)S(1)}, f32[1,2,64,256]{3,2,1,0:T(8,128)S(1)}, u32[]{:S(2)}, u32[]{:S(2)}) collective-permute-start(f32[1,2,64,256]{3,2,1,0:T(8,128)S(1)} %slice.18), channel_id=1, source_target_pairs={{0,4},{1,5},{2,0},{3,1},{4,8},{5,9},{6,2},{7,3},{8,12},{9,13},{10,... | collective-permute-start | bytes 393224 | tf_op jit(solution)/shard_map/ppermute | solution.py:82
  43.7 5.2 %collective-permute-start.5 = (f32[1,2,64,256]{3,2,1,0:T(8,128)S(1)}, f32[1,2,64,256]{3,2,1,0:T(8,128)S(1)}, u32[]{:S(2)}, u32[]{:S(2)}) collective-permute-start(f32[1,2,64,256]{3,2,1,0:T(8,128)S(1)} %slice.16), channel_id=1, source_target_pairs={{0,4},{1,5},{2,0},{3,1},{4,8},{5,9},{6,2},{7,3},{8,12},{9,13},{10,... | collective-permute-start | bytes 393224 | tf_op jit(solution)/shard_map/ppermute | solution.py:82
  43.9 5.2 %collective-permute-start.15 = (f32[1,2,64,256]{3,2,1,0:T(8,128)S(1)}, f32[1,2,64,256]{3,2,1,0:T(8,128)S(1)}, u32[]{:S(2)}, u32[]{:S(2)}) collective-permute-start(f32[1,2,64,256]{3,2,1,0:T(8,128)S(1)} %slice.17), channel_id=1, source_target_pairs={{0,2},{1,3},{2,6},{3,7},{4,0},{5,1},{6,10},{7,11},{8,4},{9,5},{10,... | collective-permute-start | bytes 393224 | tf_op jit(solution)/shard_map/ppermute | solution.py:82
  49.5 1.4 %collective-permute-start.18 = (f32[128,256]{1,0:T(8,128)S(1)}, f32[128,256]{1,0:T(8,128)S(1)}, u32[]{:S(2)}, u32[]{:S(2)}) collective-permute-start(f32[128,256]{1,0:T(8,128)S(1)} %get-tuple-element.51.e0_ref), channel_id=1, source_target_pairs={{0,1},{1,0},{2,3},{3,2},{4,5},{5,4},{6,7},{7,6},{8,9},{9,8},{10,11... | collective-permute-start | bytes 393224 | tf_op jit(solution)/shard_map/ppermute | solution.py:410
  55.8 1.4 %collective-permute-start.19 = (f32[128,256]{1,0:T(8,128)S(1)}, f32[128,256]{1,0:T(8,128)S(1)}, u32[]{:S(2)}, u32[]{:S(2)}) collective-permute-start(f32[128,256]{1,0:T(8,128)S(1)} %get-tuple-element.56.e0_ref), channel_id=1, source_target_pairs={{0,1},{1,0},{2,3},{3,2},{4,5},{5,4},{6,7},{7,6},{8,9},{9,8},{10,11... | collective-permute-start | bytes 393224 | tf_op jit(solution)/shard_map/ppermute | solution.py:410
  62.1 1.6 %collective-permute-start.20 = (f32[128,256]{1,0:T(8,128)S(1)}, f32[128,256]{1,0:T(8,128)S(1)}, u32[]{:S(2)}, u32[]{:S(2)}) collective-permute-start(f32[128,256]{1,0:T(8,128)S(1)} %get-tuple-element.58.e0_ref), channel_id=1, source_target_pairs={{0,1},{1,0},{2,3},{3,2},{4,5},{5,4},{6,7},{7,6},{8,9},{9,8},{10,11... | collective-permute-start | bytes 393224 | tf_op jit(solution)/shard_map/ppermute | solution.py:410
  62.3 7.4 %collective-permute-start.22 = (f32[2,64,256]{2,1,0:T(8,128)S(1)}, f32[2,64,256]{2,1,0:T(8,128)S(1)}, u32[]{:S(2)}, u32[]{:S(2)}) collective-permute-start(f32[2,64,256]{2,1,0:T(8,128)S(1)} %get-tuple-element.64), channel_id=1, source_target_pairs={{0,1},{1,0},{2,3},{3,2},{4,5},{5,4},{6,7},{7,6},{8,9},{9,8},{10,11... | collective-permute-start | bytes 393224 | tf_op jit(solution)/shard_map/ppermute | solution.py:461
  68.7 1.4 %collective-permute-start.21 = (f32[128,256]{1,0:T(8,128)S(1)}, f32[128,256]{1,0:T(8,128)S(1)}, u32[]{:S(2)}, u32[]{:S(2)}) collective-permute-start(f32[128,256]{1,0:T(8,128)S(1)} %get-tuple-element.60.e0_ref), channel_id=1, source_target_pairs={{0,1},{1,0},{2,3},{3,2},{4,5},{5,4},{6,7},{7,6},{8,9},{9,8},{10,11... | collective-permute-start | bytes 393224 | tf_op jit(solution)/shard_map/ppermute | solution.py:410
  69.4 4.2 %collective-permute-start.23 = (f32[2,2,64,256]{3,2,1,0:T(8,128)S(1)}, f32[2,2,64,256]{3,2,1,0:T(8,128)S(1)}, u32[]{:S(2)}, u32[]{:S(2)}) collective-permute-start(f32[2,2,64,256]{3,2,1,0:T(8,128)S(1)} %get-tuple-element.68), channel_id=1, source_target_pairs={{0,1},{1,0},{2,3},{3,2},{4,5},{5,4},{6,7},{7,6},{8,9},{9,8},{10,11... | collective-permute-start | bytes 786440 | tf_op jit(solution)/shard_map/ppermute | solution.py:472
